TPU v7x, 32 devices: a whole 2x2x4 slice. The times are simulated.
32 devices in a mesh: groups: 2 (over x), pair: 16 (over z, y, core).
Axes of the slice: x: 2, y: 2, z: 4, core: 2. Of those that a mesh axis runs over, the one named last changes fastest.
Arguments:
- right_side: float32 [512, 4096], P(('groups', 'pair')), parts along dimension 0, may hold values from -6 to 6
- pno_energy: float32 [512, 64], P(('groups', 'pair')), parts along dimension 0, may hold values from 1 to 4
- occ_energy: float32 [512], P(('groups', 'pair')), parts along dimension 0, may hold values from -2 to -0.5
- pno_count: int32 [512], P(('groups', 'pair')), parts along dimension 0, may hold values from 32 to 64
- margins: bfloat16 [512, 40, 4096], P(('groups', 'pair')), parts along dimension 0, may hold values from -0.4375 to 0.4375
- partners: int32 [512, 40], P(('groups', 'pair')), parts along dimension 0, may hold values from 0 to 255, as said below
- slot_of: int32 [512], P('groups'), parts along dimension 0, may hold values from 0 to 255, as said below
Outputs:
- solution: float32 [512, 4096], P(('groups', 'pair')), parts along dimension 0
- residual: float32 [512, 4096], P(('groups', 'pair')), parts along dimension 0
There are 2 independent parts, one for each index of `groups`. A program takes and returns all parts, laid end to end along the dimension named above; each array names one. Nothing has to cross between parts.
Inputs may be any that keep to these rules, and one draw needn't show every extreme that they name: slot_of is a permutation of the pair ids; slot s is held by device s // 16 of the pair axis. `partners`: over the rows of one device, at most 54 entries name pairs stored on one device, and in every draw each device has some storing device that it names exactly 54 times.
All inputs are finite; a program needn't handle non-finite values.
Results may differ from a plain program's by a relative error of at most 0.0017.
The roundings to bfloat16 on the way count: a program that leaves them out, or rounds other values in their place, can miss the bound.
Values may be sent and summed in bfloat16 or wider, within the bound.
No kernel may reach another device: no remote copies, remote signals or barrier semaphores. Data moves between devices by JAX's collectives and lax.ppermute only.
A program may use at most 192 MiB of HBM per device.

v0:
```python
import jax
import jax.numpy as jnp
from jax import lax
from jax.sharding import PartitionSpec as P

ITERS = 2


FREQUENCY = 0.25


def pick_rows(blocks, wanted):
    local_pairs = blocks.shape[0]
    selector = (wanted[..., None] == jnp.arange(local_pairs)[None, None, :]).astype(jnp.bfloat16)
    picked = jnp.einsum("dcp,pf->dcf", selector, blocks, preferred_element_type=jnp.float32)
    return picked.astype(jnp.bfloat16)


def shards(right_side, pno_energy, occ_energy, pno_count, margins, partners, slot_of):
    local_pairs = right_side.shape[0]
    width = pno_energy.shape[1]
    partner_count = partners.shape[1]
    devices = lax.axis_size("pair")
    sends = local_pairs * partner_count
    capacity = (4 * sends + 3 * devices - 1) // (3 * devices)
    count_mask = (jnp.arange(width)[None, :] < pno_count[:, None]).astype(jnp.float32)
    mask = (count_mask[:, :, None] * count_mask[:, None, :]).reshape(local_pairs, width * width)
    denom = (pno_energy[:, :, None] + pno_energy[:, None, :]).reshape(local_pairs, width * width)
    denom = denom - occ_energy[:, None] - FREQUENCY
    solution = mask * right_side / denom
    target = jnp.take(slot_of, partners.reshape(-1))
    holder = target // local_pairs
    within = target % local_pairs
    onehot = (holder[:, None] == jnp.arange(devices)[None, :]).astype(jnp.int32)
    position = jnp.sum(jnp.cumsum(onehot, axis=0) * onehot, axis=1) - 1
    requests = jnp.zeros((devices, capacity), jnp.int32).at[holder, position].set(within)
    entry_ids = jnp.arange(sends, dtype=jnp.int32)
    slot_entry = jnp.full((devices, capacity), -1, jnp.int32).at[holder, position].set(entry_ids)
    slot_entry = slot_entry.reshape(devices * capacity)
    slot_used = slot_entry >= 0
    slot_owner = jnp.where(slot_used, jnp.maximum(slot_entry, 0) // partner_count, -1)
    slot_pair = (jnp.arange(local_pairs)[:, None] == slot_owner[None, :]).astype(jnp.float32)
    margin_rows = margins.reshape(sends, width * width)
    slot_tiles = jnp.where(
        slot_used[:, None], margin_rows[jnp.maximum(slot_entry, 0)], jnp.zeros((), jnp.bfloat16)
    )
    slot_tiles = slot_tiles.reshape(devices * capacity, width, width)
    residual = jnp.zeros_like(solution)
    for step in range(ITERS):
        blocks = solution.astype(jnp.bfloat16)
        arrived = lax.all_to_all(
            pick_rows(
                blocks, lax.all_to_all(requests, "pair", split_axis=0, concat_axis=0, tiled=True)
            ),
            "pair",
            split_axis=0,
            concat_axis=0,
            tiled=True,
        )
        arrived = arrived.reshape(devices * capacity, width, width)
        half = jnp.einsum(
            "sab,sbc->sac", slot_tiles, arrived, preferred_element_type=jnp.float32
        ).astype(jnp.bfloat16)
        slot_terms = jnp.einsum(
            "sac,sdc->sad", half, slot_tiles, preferred_element_type=jnp.float32
        ).reshape(devices * capacity, width * width)
        coupled = jnp.dot(
            slot_pair,
            slot_terms,
            precision=lax.Precision.HIGHEST,
            preferred_element_type=jnp.float32,
        )
        residual = mask * (right_side - denom * solution - coupled)
        solution = solution + residual / denom
    return (solution, residual)


def solution(mesh):
    placed = (
        P(("groups", "pair"), None),
        P(("groups", "pair"), None),
        P(("groups", "pair")),
        P(("groups", "pair")),
        P(("groups", "pair"), None, None),
        P(("groups", "pair"), None),
        P("groups"),
    )
    return jax.shard_map(
        shards,
        mesh=mesh,
        in_specs=placed,
        out_specs=(P(("groups", "pair"), None), P(("groups", "pair"), None)),
        check_vma=False,
    )
```

profile of v0, /device:TPU:0, one launch (start us, length us, event | category | flops | bytes accessed | tf_op | source)
XLA Modules:
  0.0 614.0 jit_solution(17423631097846277062)
XLA Ops:
  0.6 0.0 copy-start
  0.6 0.0 copy-start.3
  0.7 0.0 copy-start.2
  0.7 0.8 reshape.299
  1.5 0.8 reshape.301
  2.3 0.8 reshape.300
  3.1 0.0 copy-done
  3.1 4.3 gather_fusion
  7.5 1.4 reduce-window.6
  8.9 0.2 slice_reduce_fusion
  9.2 0.1 fusion.21
  9.4 0.6 broadcast.320
  10.0 89.6 %scatter_fusion.1 = s32[16,54]{1,0:T(8,128)} fusion(s32[16,54]{1,0:T(8,128)} %broadcast.320, s32[640]{0:T(1024)S(1)} %fusion.33, s32[640]{0:T(1024)S(1)} %get-tuple-element.6), kind=kCustom, calls=%fused_computation.3 | custom fusion | bytes 12800 | tf_op jit(solution)/shard_map/scatter | solution.py:36
  99.5 7.2 %all-to-all-start = ((s32[16,1,54]{2,1,0:T(1,128)}), s32[16,1,54]{2,1,0:T(1,128)S(1)}, u32[]{:S(2)}, u32[]{:S(2)}) async-start(s32[16,1,54]{2,1,0:T(1,128)} %bitcast.5), calls=%async_computation | async-start | bytes 16384 | tf_op jit(solution)/shard_map/all_to_all | solution.py:53
  106.8 0.7 fusion.25
  107.5 0.2 broadcast_multiply_fusion
  107.7 1.0 broadcast_add_fusion
  108.7 0.2 mul.38
  108.9 0.2 add.123
  109.1 4.0 all-to-all-done
  113.1 0.0 copy-done.3
  113.1 0.0 copy-done.2
  113.1 5.1 convolution_convert_fusion.1
  118.3 4.9 all-to-all-start.1
  123.2 33.0 %scatter_fusion = s32[16,54]{1,0:T(8,128)S(1)} fusion(s32[16,54]{1,0:T(8,128)S(1)} %broadcast_in_dim.22, s32[640]{0:T(1024)S(1)} %fusion.33, s32[640]{0:T(1024)S(1)} %iota.31), kind=kCustom, calls=%fused_computation.2 | custom fusion | bytes 12800 | tf_op jit(solution)/shard_map/scatter | solution.py:38
  156.2 0.1 and.76
  156.3 0.1 ge.42
  156.4 0.1 div.64
  156.5 0.1 reshape.318
  156.6 18.1 %gather_fusion.1 = bf16[864,4096]{1,0:T(8,128)(2,1)} fusion(bf16[640,4096]{1,0:T(8,128)(2,1)} %bitcast.44, s32[1024]{0:T(1024)S(1)} %pad_clamp_fusion), kind=kCustom, calls=%fused_computation.1 | custom fusion | bytes 14159232 | tf_op jit(solution)/shard_map/gather | solution.py:45
  174.6 10.7 %copy.16 = bf16[864,4096]{0,1:T(8,128)(2,1)} copy(bf16[864,4096]{1,0:T(8,128)(2,1)} %gather_fusion.1) | data formatting | bytes 14155776 | tf_op jit(solution)/shard_map/gather | solution.py:45
  185.4 6.7 %broadcast_select_fusion = bf16[864,64,64]{0,2,1:T(8,128)(2,1)} fusion(bf16[864,64,64]{0,2,1:T(8,128)(2,1)} %bitcast.47, pred[864]{0:T(1024)(128)(4,1)S(1)} %ge.42), kind=kLoop, calls=%fused_computation.10 | loop fusion | flops 3538944 | bytes 14156640 | tf_op jit(solution)/shard_map/jit(_where)/select_n | solution.py:44
  192.0 21.1 %copy.18 = bf16[864,64,64]{2,1,0:T(8,128)(2,1)} copy(bf16[864,64,64]{0,2,1:T(8,128)(2,1)} %broadcast_select_fusion) | data formatting | bytes 14155776 | tf_op jit(solution)/shard_map/jit(_where)/select_n | solution.py:44
  213.2 42.2 %all-to-all-done.1 = bf16[16,54,4096]{2,1,0:T(8,128)(2,1)} async-done(((bf16[16,54,4096]{2,1,0:T(8,128)(2,1)}), bf16[16,54,4096]{2,1,0:T(8,128)(2,1)}, u32[]{:S(2)}, u32[]{:S(2)}) %all-to-all-start.1) | async-done | bytes 7077920 | tf_op jit(solution)/shard_map/all_to_all | solution.py:51
  255.3 19.2 %reshape.304 = bf16[864,64,64]{2,1,0:T(8,128)(2,1)} reshape(bf16[16,54,4096]{2,1,0:T(8,128)(2,1)} %all-to-all-done.1) | data formatting | bytes 14155776 | tf_op jit(solution)/shard_map/reshape | solution.py:60
  274.5 28.3 %fusion.2 = f32[864,64,64]{2,1,0:T(8,128)} fusion(bf16[864,64,64]{2,1,0:T(8,128)(2,1)} %copy.18, bf16[864,64,64]{2,1,0:T(8,128)(2,1)} %reshape.304), kind=kOutput, calls=%fused_computation.6 | convolution fusion | flops 909508608 | bytes 28311552 | tf_op jit(solution)/shard_map/sac,sdc->sad/dot_general | solution.py:64
  302.8 24.0 %copy.20 = f32[864,64,64]{0,2,1:T(8,128)} copy(f32[864,64,64]{2,1,0:T(8,128)} %fusion.2) | data formatting | bytes 28311552 | tf_op jit(solution)/shard_map/sac,sdc->sad/dot_general | solution.py:64
  326.8 9.9 %fusion.11 = f32[16,4096]{1,0:T(8,128)S(1)} fusion(f32[16,4096]{1,0:T(8,128)S(1)} %mul.38, f32[864,4096]{0,1:T(8,128)} %bitcast.46, f32[16,4096]{1,0:T(8,128)S(1)} %copy-done.2, f32[16,4096]{1,0:T(8,128)S(1)} %add.123, f32[16]{0:T(128)S(1)} %copy-done.3, s32[864]{0:T(1024)S(1)} %fusion.28), kind=kOutput, calls=%fused_computation.18 | convolution fusion | flops 680146432 | bytes 15207872 | tf_op jit(solution)/shard_map/dot_general | solution.py:67
  336.8 2.1 convolution_convert_fusion
  338.9 191.8 %all_to_all.20 = bf16[16,54,4096]{2,1,0:T(8,128)(2,1)} all-to-all(bf16[16,54,4096]{2,1,0:T(8,128)(2,1)S(1)} %convolution_convert_fusion), channel_id=1, replica_groups=mesh['groups'=2,'pair'=16] {'pair'}, dimensions={0} | all-to-all | bytes 14155776 | tf_op jit(solution)/shard_map/all_to_all | solution.py:51
  530.7 19.2 %reshape.306 = bf16[864,64,64]{2,1,0:T(8,128)(2,1)} reshape(bf16[16,54,4096]{2,1,0:T(8,128)(2,1)} %all_to_all.20) | data formatting | bytes 14155776 | tf_op jit(solution)/shard_map/reshape | solution.py:60
  549.9 28.3 %fusion = f32[864,64,64]{2,1,0:T(8,128)} fusion(bf16[864,64,64]{2,1,0:T(8,128)(2,1)} %copy.18, bf16[864,64,64]{2,1,0:T(8,128)(2,1)} %reshape.306), kind=kOutput, calls=%fused_computation.4 | convolution fusion | flops 909508608 | bytes 28311552 | tf_op jit(solution)/shard_map/sac,sdc->sad/dot_general | solution.py:64
  578.2 0.0 copy-start.1
  578.2 24.0 %copy.23 = f32[864,64,64]{0,2,1:T(8,128)} copy(f32[864,64,64]{2,1,0:T(8,128)} %fusion) | data formatting | bytes 28311552 | tf_op jit(solution)/shard_map/sac,sdc->sad/dot_general | solution.py:64
  602.2 11.8 %divide_add_fusion = (f32[16,4096]{1,0:T(8,128)}, f32[16,4096]{1,0:T(8,128)}) fusion(f32[16,4096]{1,0:T(8,128)S(1)} %fusion.11, f32[16,4096]{1,0:T(8,128)S(1)} %add.123, f32[16]{0:T(128)S(1)} %copy-done.3, f32[16,4096]{1,0:T(8,128)S(1)} %mul.38, f32[864,4096]{0,1:T(8,128)} %bitcast.45, s32[864]{0:T(1024)S(1)} %fusion.28, f32[16,4096]{1,0:T(8,128)S(1)} %copy-done.2), kind=kOutput, calls=%fused_computation.19 | convolution fusion | flops 680015360 | bytes 15732160 | tf_op jit(solution)/shard_map/dot_general | solution.py:67
  614.0 0.0 copy-done.1
  (14 shorter events, 0.2 us)
Async XLA Ops:
  0.6 2.5 copy-start
  0.6 112.5 %copy-start.3 = (f32[16]{0:T(128)S(1)}, f32[16]{0:T(128)}, u32[]{:S(2)}) copy-start(f32[16]{0:T(128)} %param.9) | copy-start | bytes 196
  0.7 112.5 %copy-start.2 = (f32[16,4096]{1,0:T(8,128)S(1)}, f32[16,4096]{1,0:T(8,128)}, u32[]{:S(2)}) copy-start(f32[16,4096]{1,0:T(8,128)} %param.7) | copy-start | bytes 786436
  99.5 13.6 %all-to-all-start = ((s32[16,1,54]{2,1,0:T(1,128)}), s32[16,1,54]{2,1,0:T(1,128)S(1)}, u32[]{:S(2)}, u32[]{:S(2)}) async-start(s32[16,1,54]{2,1,0:T(1,128)} %bitcast.5), calls=%async_computation | async-start | bytes 16384 | tf_op jit(solution)/shard_map/all_to_all | solution.py:53
  118.3 137.1 %all-to-all-start.1 = ((bf16[16,54,4096]{2,1,0:T(8,128)(2,1)}), bf16[16,54,4096]{2,1,0:T(8,128)(2,1)}, u32[]{:S(2)}, u32[]{:S(2)}) async-start(bf16[16,54,4096]{2,1,0:T(8,128)(2,1)} %convolution_convert_fusion.1), calls=%async_computation.1 | async-start | bytes 14680064 | tf_op jit(solution)/shard_map/all_to_all | solution.py:51
  578.2 35.8 %copy-start.1 = (s32[256]{0:T(256)S(1)}, s32[256]{0:T(256)}, u32[]{:S(2)}) copy-start(s32[256]{0:T(256)} %param.13) | copy-start | bytes 3076
where the time goes:
time: 619 us; the launch traced here: 614 us
  local copies, waits for them, and re-layouts  267 us (43%)
  blocking collectives  192 us (31%)
  matrix products  85.6 us (14%)
  waiting for transfers between devices  46.2 us (7%)
  starting transfers between devices  12.1 us (2%)
  other arithmetic  10.3 us (2%)
    all_to_all x1, blocking collectives, shards(): lax.all_to_all(pick_rows(blocks, lax.all_to_all(requests, 'pair', split_a...  192 us
    scatter x1, local copies, waits for them, and re-layouts, shards(): jnp.zeros((devices, capacity), jnp.int32).at[holder, position].set(within)  89.6 us
    dot_general x2, matrix products, shards(): jnp.einsum('sac,sdc->sad', half, slot_tiles, preferred_element_type=jnp.f...  56.6 us
    dot_general x2, local copies, waits for them, and re-layouts, shards(): jnp.einsum('sac,sdc->sad', half, slot_tiles, preferred_element_type=jnp.f...  48 us
    all_to_all x1, waiting for transfers between devices, shards(): lax.all_to_all(pick_rows(blocks, lax.all_to_all(requests, 'pair', split_a...  42.2 us
    reshape x2, local copies, waits for them, and re-layouts, shards(): arrived = arrived.reshape(devices * capacity, width, width)  38.4 us
    scatter x1, local copies, waits for them, and re-layouts, shards(): jnp.full((devices, capacity), -1, jnp.int32).at[holder, position]  33 us
    gather x2, local copies, waits for them, and re-layouts, shards(): margin_rows[jnp.maximum(slot_entry, 0)]  28.8 us
  transfers between devices with their start and end apart: 2, of which 2 were waited for; matrix products, arithmetic and copies ran while one was open for 15% of the time, Pallas kernels for 0%

commit v1 on v0

v1 whole, which is shorter than its diff:
```python
import functools

import jax
import jax.numpy as jnp
from jax import lax
from jax.experimental import pallas as pl
from jax.experimental.pallas import tpu as pltpu
from jax.sharding import PartitionSpec as P

ITERS = 2
FREQUENCY = 0.25
SLOTS_AT_ONCE = 4
NT = (((1,), (1,)), ((), ()))
VMEM = pl.BlockSpec(memory_space=pltpu.VMEM)
SMEM = pl.BlockSpec(memory_space=pltpu.SMEM)
ANY = pl.BlockSpec(memory_space=pl.ANY)


def left_lanes(width):
    return lax.broadcasted_iota(jnp.int32, (width, 2 * width), 1) < width


def swap_halves(tile):
    width = tile.shape[1] // 2
    return jnp.concatenate([tile[:, width:], tile[:, :width]], axis=1)


def start_kernel(count, occ, right, energy, right_out, denom_out, mask_out, solution_out, blocks_out, rows):
    slots, width = energy.shape
    half = slots // 2
    lanes = 2 * width
    slot = lax.broadcasted_iota(jnp.int32, (slots, lanes), 0)
    for j in range(width // 2):
        part = right[:, j * lanes : (j + 1) * lanes]
        turned = swap_halves(part)
        rows[pl.ds(2 * j, slots, stride=width), :] = jnp.where(slot < half, part, turned)
        rows[pl.ds(2 * j + 1, slots, stride=width), :] = jnp.where(slot < half, turned, part)
    left = left_lanes(width)
    row = lax.broadcasted_iota(jnp.int32, (width, lanes), 0)
    column = lax.broadcasted_iota(jnp.int32, (width, lanes), 1) % width
    across = energy[...]
    down = across.T
    for u in range(half):
        v = u + half
        first = jnp.broadcast_to(down[:, u : u + 1], (width, lanes))
        second = jnp.broadcast_to(down[:, v : v + 1], (width, lanes))
        along = jnp.concatenate([across[u : u + 1], across[v : v + 1]], axis=1)
        shift = jnp.where(left, occ[u], occ[v])
        denom = jnp.where(left, first, second) + along - shift - FREQUENCY
        most = jnp.where(left, count[u], count[v])
        mask = jnp.where((row < most) & (column < most), 1.0, 0.0)
        tile = jnp.where(left, rows[u * width : (u + 1) * width], rows[v * width : (v + 1) * width])
        now = mask * tile / denom
        right_out[u] = tile
        denom_out[u] = denom
        mask_out[u] = mask
        solution_out[u] = now
        blocks_out[u] = now.astype(jnp.bfloat16)


def start(right_side, pno_energy, occ_energy, pno_count):
    slots, width = pno_energy.shape
    tiles = jax.ShapeDtypeStruct((slots // 2, width, 2 * width), jnp.float32)
    return pl.pallas_call(
        start_kernel,
        in_specs=[SMEM, SMEM, VMEM, VMEM],
        out_specs=[VMEM] * 5,
        out_shape=[tiles] * 4 + [jax.ShapeDtypeStruct(tiles.shape, jnp.bfloat16)],
        scratch_shapes=[pltpu.VMEM((slots * width, 2 * width), jnp.float32)],
        name="start",
    )(pno_count, occ_energy, right_side, pno_energy)


def margin_kernel(margins, tiles, rows):
    partners = margins.shape[1]
    width = tiles.shape[2]
    lanes = 2 * width
    even = lax.broadcasted_iota(jnp.int32, (partners, lanes), 0) % 2 == 0
    for j in range(width // 2):
        part = margins[0, :, j * lanes : (j + 1) * lanes].astype(jnp.float32)
        turned = swap_halves(part)
        rows[pl.ds(2 * j, partners, stride=width), :] = jnp.where(even, part, turned)
        rows[pl.ds(2 * j + 1, partners, stride=width), :] = jnp.where(even, turned, part)
    left = left_lanes(width)
    for k in range(partners // 2):
        first = rows[2 * k * width : (2 * k + 1) * width]
        second = rows[(2 * k + 1) * width : (2 * k + 2) * width]
        tiles[0, k] = jnp.where(left, first, second).astype(jnp.bfloat16)


def margin_tiles(margins, width):
    slots, partners, flat = margins.shape
    return pl.pallas_call(
        margin_kernel,
        grid=(slots,),
        in_specs=[pl.BlockSpec((1, partners, flat), lambda s: (s, 0, 0))],
        out_specs=pl.BlockSpec((1, partners // 2, width, 2 * width), lambda s: (s, 0, 0, 0)),
        out_shape=jax.ShapeDtypeStruct((slots, partners // 2, width, 2 * width), jnp.bfloat16),
        scratch_shapes=[pltpu.VMEM((partners * width, 2 * width), jnp.float32)],
        cost_estimate=pl.CostEstimate(flops=0, bytes_accessed=16 * margins.size, transcendentals=0),
        name="margin_tiles",
    )(margins)


def couple_kernel(last, pieces, twist, partners, slot_of, *refs):
    gathered, refs = refs[:pieces], refs[pieces:]
    margins, right, denom, mask, current, solution_out, residual_out = refs[:7]
    blocks_out, refs = (None, refs[7:]) if last else (refs[7], refs[8:])
    expanded, held, halves, coupled, arrived = refs[:5]
    slots, pairs, width, lanes = margins.shape
    half = slots // 2
    count = 2 * pairs

    def fetch(s):
        return pltpu.make_async_copy(margins.at[s], held.at[s], arrived.at[s])

    for s in range(slots):
        fetch(s).start()

    left = left_lanes(width)
    base = 0
    for piece in gathered:
        held_devices = piece.shape[0] // half

        def expand(i, carry, piece=piece, base=base):
            tile = piece[i]
            turned = swap_halves(tile)
            zero = jnp.zeros_like(tile)
            u = (base + i // half) * slots + i % half
            v = u + half
            expanded[2 * u] = jnp.where(left, tile, zero)
            expanded[2 * u + 1] = jnp.where(left, zero, turned)
            expanded[2 * v] = jnp.where(left, turned, zero)
            expanded[2 * v + 1] = jnp.where(left, zero, tile)
            return carry

        lax.fori_loop(0, piece.shape[0], expand, 0, unroll=4)
        base += held_devices

    turn = twist[0] * slots

    def block(s, k):
        target = slot_of[partners[s, k]] ^ turn
        return expanded[2 * target + k % 2]

    zero = jnp.zeros((lanes, lanes), jnp.bfloat16)

    def one_slot(s, at):
        for q in range(pairs // 2):
            upper = jnp.concatenate([block(s, 4 * q), block(s, 4 * q + 1)], axis=0)
            lower = jnp.concatenate([block(s, 4 * q + 2), block(s, 4 * q + 3)], axis=0)
            weights = jnp.concatenate(
                [jnp.concatenate([upper, zero], axis=1), jnp.concatenate([zero, lower], axis=1)], axis=0
            )
            margin = jnp.concatenate([held[s, 2 * q], held[s, 2 * q + 1]], axis=1)
            product = jnp.dot(margin, weights, preferred_element_type=jnp.float32)
            halves[at, :, 2 * q * lanes : 2 * (q + 1) * lanes] = product.astype(jnp.bfloat16)
        margin = jnp.concatenate([held[s, k] for k in range(pairs)], axis=1)
        coupled[s] = lax.dot_general(halves[at], margin, NT, preferred_element_type=jnp.float32)

    def some_slots(i, carry):
        for at in range(SLOTS_AT_ONCE):
            fetch(i * SLOTS_AT_ONCE + at).wait()
        for at in range(SLOTS_AT_ONCE):
            one_slot(i * SLOTS_AT_ONCE + at, at)
        return carry

    lax.fori_loop(0, slots // SLOTS_AT_ONCE, some_slots, 0)

    if last:
        store = refs[5]
    for u in range(half):
        both = jnp.concatenate([coupled[u], coupled[u + half]], axis=1)
        before = current[u]
        residual = mask[u] * (right[u] - denom[u] * before - both)
        after = before + residual / denom[u]
        if last:
            for n, tile in enumerate((after, residual)):
                store[2 * n, u * width : (u + 1) * width] = tile
                store[2 * n + 1, u * width : (u + 1) * width] = swap_halves(tile)
        else:
            solution_out[u] = after
            residual_out[u] = residual
            blocks_out[u] = after.astype(jnp.bfloat16)
    if last:
        keep = lax.broadcasted_iota(jnp.int32, (half, lanes), 1) < width
        for n, out in enumerate((solution_out, residual_out)):
            for j in range(width // 2):
                upper = store[2 * n, pl.ds(2 * j, half, stride=width), :]
                lower = store[2 * n, pl.ds(2 * j + 1, half, stride=width), :]
                upper_turned = store[2 * n + 1, pl.ds(2 * j, half, stride=width), :]
                lower_turned = store[2 * n + 1, pl.ds(2 * j + 1, half, stride=width), :]
                out[:half, j * lanes : (j + 1) * lanes] = jnp.where(keep, upper, lower_turned)
                out[half:, j * lanes : (j + 1) * lanes] = jnp.where(keep, upper_turned, lower)


def couple(last, twist, partners, slot_of, gathered, margins, right, denom, mask, current):
    slots, pairs, width, lanes = margins.shape
    half = slots // 2
    devices = sum(piece.shape[0] for piece in gathered) // half
    packed = jax.ShapeDtypeStruct((half, width, lanes), jnp.float32)
    flat = jax.ShapeDtypeStruct((slots, width * width), jnp.float32)
    blocks = jax.ShapeDtypeStruct((half, width, lanes), jnp.bfloat16)
    outs = [flat, flat] if last else [packed, packed, blocks]
    scratch = [
        pltpu.VMEM((2 * devices * slots, width, lanes), jnp.bfloat16),
        pltpu.VMEM(margins.shape, jnp.bfloat16),
        pltpu.VMEM((SLOTS_AT_ONCE, width, pairs * lanes), jnp.bfloat16),
        pltpu.VMEM((slots, width, width), jnp.float32),
        pltpu.SemaphoreType.DMA((slots,)),
    ]
    if last:
        scratch.append(pltpu.VMEM((4, half * width, lanes), jnp.float32))
    return pl.pallas_call(
        functools.partial(couple_kernel, last, len(gathered)),
        in_specs=[SMEM] * 3 + [VMEM] * len(gathered) + [ANY] + [VMEM] * 4,
        out_specs=[VMEM] * len(outs),
        out_shape=outs,
        scratch_shapes=scratch,
        compiler_params=pltpu.CompilerParams(vmem_limit_bytes=56 * 2**20),
        name="couple",
    )(twist, partners, slot_of, *gathered, margins, right, denom, mask, current)


def gather(blocks, devices):
    if devices != 16:
        return [lax.all_gather(blocks, "pair", axis=0, tiled=True)], jnp.zeros((1,), jnp.int32)

    def swap(piece, other):
        return lax.ppermute(piece, "pair", [(i, i ^ other) for i in range(devices)])

    piece = {0: blocks}
    for other in (2, 4, 12):
        piece[other] = swap(blocks, other)
    piece[8] = swap(piece[12], 4)
    for other in (4, 12, 8):
        piece[other ^ 2] = swap(piece[other], 2)
    for other in (0, 2, 4, 6, 12, 14, 8, 10):
        piece[other ^ 1] = swap(piece[other], 1)
    return [piece[i] for i in range(devices)], lax.axis_index("pair").astype(jnp.int32).reshape(1)


def shards(right_side, pno_energy, occ_energy, pno_count, margins, partners, slot_of):
    devices = lax.axis_size("pair")
    right, denom, mask, current, blocks = start(right_side, pno_energy, occ_energy, pno_count)
    tiles = margin_tiles(margins, pno_energy.shape[1])
    for step in range(ITERS):
        gathered, twist = gather(blocks, devices)
        outs = couple(step == ITERS - 1, twist, partners, slot_of, gathered, tiles, right, denom, mask, current)
        if step < ITERS - 1:
            current, _, blocks = outs
    return tuple(outs)


def solution(mesh):
    placed = (
        P(("groups", "pair"), None),
        P(("groups", "pair"), None),
        P(("groups", "pair")),
        P(("groups", "pair")),
        P(("groups", "pair"), None, None),
        P(("groups", "pair"), None),
        P("groups"),
    )
    return jax.shard_map(
        shards,
        mesh=mesh,
        in_specs=placed,
        out_specs=(P(("groups", "pair"), None), P(("groups", "pair"), None)),
        check_vma=False,
    )
```

time: 619 us -> 93.6 us (0.15)
  local copies, waits for them, and re-layouts: 267 us -> 1.44 us
  blocking collectives: 192 us -> 0 us
  matrix products: 85.6 us -> 0 us
  Pallas kernels: 0 us -> 46.4 us
  waiting for transfers between devices: 46.2 us -> 18.9 us
  starting transfers between devices: 12.1 us -> 25.2 us
  other arithmetic: 10.3 us -> 0 us
    all_to_all x1 -> x0, blocking collectives: 192 us -> none  [shards(): lax.all_to_all(pick_rows(blocks, lax.all_to_all(requests, 'pair', split_a...]
    scatter x2 -> x0, local copies, waits for them, and re-layouts: 123 us -> none  [the longest x1 89.6 us: shards(): jnp.zeros((devices, capacity), jnp.int32).at[holder, position].set(within)]
    dot_general x6 -> x0, matrix products: 85.6 us -> none  [the longest x2 56.6 us: shards(): jnp.einsum('sac,sdc->sad', half, slot_tiles, preferred_element_type=jnp.f...]
    dot_general x2 -> x0, local copies, waits for them, and re-layouts: 48 us -> none  [shards(): jnp.einsum('sac,sdc->sad', half, slot_tiles, preferred_element_type=jnp.f...]
    pallas_call x0 -> x4, Pallas kernels: none -> 46.4 us  [the longest x2 25.2 us: couple(): pl.pallas_call(functools.partial(couple_kernel, last, len(gathered)), in_...]
    all_to_all x2 -> x0, waiting for transfers between devices: 46.2 us -> none  [the longest x1 42.2 us: shards(): lax.all_to_all(pick_rows(blocks, lax.all_to_all(requests, 'pair', split_a...]
    reshape x5 -> x0, local copies, waits for them, and re-layouts: 40.7 us -> none  [the longest x2 38.4 us: shards(): arrived = arrived.reshape(devices * capacity, width, width)]
    gather x3 -> x0, local copies, waits for them, and re-layouts: 33.1 us -> none  [the longest x2 28.8 us: shards(): margin_rows[jnp.maximum(slot_entry, 0)]]
  transfers between devices with their start and end apart: 2 -> 30, of which waited for: 2 -> 11; matrix products, arithmetic and copies ran while one was open for 15% -> 0% of each run, Pallas kernels for 0% -> 20%
where the time goes in v1:
time: 93.6 us; the launch traced here: 93 us
  Pallas kernels  46.4 us (50%)
  starting transfers between devices  25.2 us (27%)
  waiting for transfers between devices  18.9 us (20%)
  local copies, waits for them, and re-layouts  1.44 us (2%)
  between operations  1.03 us (1%)
    ppermute x30, starting transfers between devices, swap(): return lax.ppermute(piece, 'pair', [(i, i ^ other) for i in range(devices)])  25.2 us
    pallas_call x2, Pallas kernels, couple(): pl.pallas_call(functools.partial(couple_kernel, last, len(gathered)), in_...  25.2 us
    ppermute x30, waiting for transfers between devices, swap(): return lax.ppermute(piece, 'pair', [(i, i ^ other) for i in range(devices)])  18.9 us
    pallas_call x1, Pallas kernels, margin_tiles(): pl.pallas_call(margin_kernel, grid=(slots,), in_specs=[pl.BlockSpec((1, p...  18.8 us
    pallas_call x1, Pallas kernels, start(): pl.pallas_call(start_kernel, in_specs=[SMEM, SMEM, VMEM, VMEM], out_specs...  2.42 us
  transfers between devices with their start and end apart: 30, of which 11 were waited for; matrix products, arithmetic and copies ran while one was open for 0% of the time, Pallas kernels for 20%

profile of v1, /device:TPU:0, one launch (start us, length us, event | category | flops | bytes accessed | tf_op | source)
XLA Modules:
  0.0 93.0 jit_solution(2708310110040492141)
XLA Ops:
  0.6 2.4 %start.1 = (f32[8,64,128]{2,1,0:T(8,128)}, f32[8,64,128]{2,1,0:T(8,128)}, f32[8,64,128]{2,1,0:T(8,128)}, f32[8,64,128]{2,1,0:T(8,128)}, bf16[8,64,128]{2,1,0:T(8,128)(2,1)}) custom-call(s32[16]{0:T(128)} %count.1, f32[16]{0:T(128)} %occ.1, f32[16,4096]{1,0:T(8,128)} %right.1, f32[16,64]{1,0:T(8,128)} %energy.1), custom_call_target="tpu_custom_call" | custom-call | tf_op jit(solution)/shard_map/start/pallas_call | solution.py:64
  3.0 5.0 %collective-permute-start.7 = (bf16[8,64,128]{2,1,0:T(8,128)(2,1)}, bf16[8,64,128]{2,1,0:T(8,128)(2,1)S(1)}, u32[]{:S(2)}, u32[]{:S(2)}) collective-permute-start(bf16[8,64,128]{2,1,0:T(8,128)(2,1)} %get-tuple-element.9.refs_0_), channel_id=1, source_target_pairs={{0,12},{1,13},{2,14},{3,15},{4,8},{5,9},{6,10},{7,11},{8,4},{9,5},... | collective-permute-start | bytes 393224 | tf_op jit(solution)/shard_map/ppermute | solution.py:230
  8.1 0.0 collective-permute-start.3
  8.1 1.5 %collective-permute-start.1 = (bf16[8,64,128]{2,1,0:T(8,128)(2,1)}, bf16[8,64,128]{2,1,0:T(8,128)(2,1)S(1)}, u32[]{:S(2)}, u32[]{:S(2)}) collective-permute-start(bf16[8,64,128]{2,1,0:T(8,128)(2,1)} %get-tuple-element.9.refs_0_), channel_id=1, source_target_pairs={{0,2},{1,3},{2,0},{3,1},{4,6},{5,7},{6,4},{7,5},{8,10},{9,11},{10,... | collective-permute-start | bytes 393224 | tf_op jit(solution)/shard_map/ppermute | solution.py:230
  9.6 0.0 collective-permute-start
  9.6 3.1 %collective-permute-done.7.refs_12_ = bf16[8,64,128]{2,1,0:T(8,128)(2,1)S(1)} collective-permute-done((bf16[8,64,128]{2,1,0:T(8,128)(2,1)}, bf16[8,64,128]{2,1,0:T(8,128)(2,1)S(1)}, u32[]{:S(2)}, u32[]{:S(2)}) %collective-permute-start.7) | collective-permute-done | bytes 131104 | tf_op jit(solution)/shard_map/ppermute | solution.py:230
  12.7 1.6 %collective-permute-start.8 = (bf16[8,64,128]{2,1,0:T(8,128)(2,1)S(1)}, bf16[8,64,128]{2,1,0:T(8,128)(2,1)S(1)}, u32[]{:S(2)}, u32[]{:S(2)}) collective-permute-start(bf16[8,64,128]{2,1,0:T(8,128)(2,1)S(1)} %collective-permute-done.7.refs_12_), channel_id=1, source_target_pairs={{0,4},{1,5},{2,6},{3,7},{4,0},{5,1},{6,2},{7,3},{8,12},{9,13},{10,... | collective-permute-start | bytes 393224 | tf_op jit(solution)/shard_map/ppermute | solution.py:230
  14.3 1.5 %collective-permute-start.13 = (bf16[8,64,128]{2,1,0:T(8,128)(2,1)S(1)}, bf16[8,64,128]{2,1,0:T(8,128)(2,1)S(1)}, u32[]{:S(2)}, u32[]{:S(2)}) collective-permute-start(bf16[8,64,128]{2,1,0:T(8,128)(2,1)S(1)} %collective-permute-done.7.refs_12_), channel_id=1, source_target_pairs={{0,2},{1,3},{2,0},{3,1},{4,6},{5,7},{6,4},{7,5},{8,10},{9,11},{10,... | collective-permute-start | bytes 393224 | tf_op jit(solution)/shard_map/ppermute | solution.py:230
  15.9 0.0 collective-permute-done.3.refs_4_
  15.9 0.0 collective-permute-start.12
  15.9 0.0 collective-permute-done.1.refs_2_
  15.9 0.8 collective-permute-start.5
  16.7 0.0 collective-permute-done.refs_1_
  16.7 0.2 collective-permute-start.4
  16.9 0.8 collective-permute-done.8.refs_8_
  17.7 1.7 %collective-permute-start.10 = (bf16[8,64,128]{2,1,0:T(8,128)(2,1)S(1)}, bf16[8,64,128]{2,1,0:T(8,128)(2,1)S(1)}, u32[]{:S(2)}, u32[]{:S(2)}) collective-permute-start(bf16[8,64,128]{2,1,0:T(8,128)(2,1)S(1)} %collective-permute-done.8.refs_8_), channel_id=1, source_target_pairs={{0,2},{1,3},{2,0},{3,1},{4,6},{5,7},{6,4},{7,5},{8,10},{9,11},{10,... | collective-permute-start | bytes 393224 | tf_op jit(solution)/shard_map/ppermute | solution.py:230
  19.4 0.2 collective-permute-done.13.refs_14_
  19.6 0.0 collective-permute-start.2
  19.6 0.0 collective-permute-done.12.refs_13_
  19.6 0.5 collective-permute-start.9
  20.1 2.3 %collective-permute-done.5.refs_6_ = bf16[8,64,128]{2,1,0:T(8,128)(2,1)S(1)} collective-permute-done((bf16[8,64,128]{2,1,0:T(8,128)(2,1)S(1)}, bf16[8,64,128]{2,1,0:T(8,128)(2,1)S(1)}, u32[]{:S(2)}, u32[]{:S(2)}) %collective-permute-start.5) | collective-permute-done | bytes 131104 | tf_op jit(solution)/shard_map/ppermute | solution.py:230
  22.4 0.0 collective-permute-start.14
  22.4 0.0 collective-permute-done.4.refs_5_
  22.4 0.5 collective-permute-start.6
  22.9 2.0 %collective-permute-done.10.refs_10_ = bf16[8,64,128]{2,1,0:T(8,128)(2,1)S(1)} collective-permute-done((bf16[8,64,128]{2,1,0:T(8,128)(2,1)S(1)}, bf16[8,64,128]{2,1,0:T(8,128)(2,1)S(1)}, u32[]{:S(2)}, u32[]{:S(2)}) %collective-permute-start.10) | collective-permute-done | bytes 131104 | tf_op jit(solution)/shard_map/ppermute | solution.py:230
  24.9 0.0 collective-permute-start.11
  24.9 18.8 %margin_tiles.1.refs_16_ = bf16[16,20,64,128]{3,2,1,0:T(8,128)(2,1)} custom-call(bf16[16,40,4096]{2,1,0:T(8,128)(2,1)} %margins.1), custom_call_target="tpu_custom_call" | custom-call | bytes 41943040 | tf_op jit(solution)/shard_map/margin_tiles/pallas_call | solution.py:93
  43.8 0.0 collective-permute-done.2.refs_3_
  43.8 0.0 collective-permute-done.14.refs_15_
  43.8 0.0 collective-permute-done.9.refs_9_
  43.9 0.0 collective-permute-done.11.refs_11_
  43.9 0.6 copy-done.20
  44.4 0.1 copy-done.24
  44.5 0.1 copy-done.22
  44.5 0.1 copy-done.26
  44.6 0.1 copy-done.28
  44.7 12.1 %couple.2 = (f32[8,64,128]{2,1,0:T(8,128)}, f32[8,64,128]{2,1,0:T(8,128)}, bf16[8,64,128]{2,1,0:T(8,128)(2,1)}) custom-call(s32[1]{0:T(128)} %bitcast.twist, s32[16,40]{1,0:T(8,128)} %partners.3, s32[256]{0:T(256)} %slot_of.3, bf16[8,64,128]{2,1,0:T(8,128)(2,1)} %get-tuple-element.9.refs_0_, bf16[8,64,128]{2,1,0:T(8,128)(2,1)} %copy-done.5, ...), custom_call_target="tpu_custom_call" | custom-call | tf_op jit(solution)/shard_map/couple/pallas_call | solution.py:214
  56.8 2.3 %collective-permute-start.22 = (bf16[8,64,128]{2,1,0:T(8,128)(2,1)}, bf16[8,64,128]{2,1,0:T(8,128)(2,1)S(1)}, u32[]{:S(2)}, u32[]{:S(2)}) collective-permute-start(bf16[8,64,128]{2,1,0:T(8,128)(2,1)} %get-tuple-element.14.refs_0_), channel_id=1, source_target_pairs={{0,12},{1,13},{2,14},{3,15},{4,8},{5,9},{6,10},{7,11},{8,4},{9,5},... | collective-permute-start | bytes 393224 | tf_op jit(solution)/shard_map/ppermute | solution.py:230
  59.1 1.1 %collective-permute-start.18 = (bf16[8,64,128]{2,1,0:T(8,128)(2,1)}, bf16[8,64,128]{2,1,0:T(8,128)(2,1)S(1)}, u32[]{:S(2)}, u32[]{:S(2)}) collective-permute-start(bf16[8,64,128]{2,1,0:T(8,128)(2,1)} %get-tuple-element.14.refs_0_), channel_id=1, source_target_pairs={{0,4},{1,5},{2,6},{3,7},{4,0},{5,1},{6,2},{7,3},{8,12},{9,13},{10,... | collective-permute-start | bytes 393224 | tf_op jit(solution)/shard_map/ppermute | solution.py:230
  60.2 1.5 %collective-permute-start.16 = (bf16[8,64,128]{2,1,0:T(8,128)(2,1)}, bf16[8,64,128]{2,1,0:T(8,128)(2,1)S(1)}, u32[]{:S(2)}, u32[]{:S(2)}) collective-permute-start(bf16[8,64,128]{2,1,0:T(8,128)(2,1)} %get-tuple-element.14.refs_0_), channel_id=1, source_target_pairs={{0,2},{1,3},{2,0},{3,1},{4,6},{5,7},{6,4},{7,5},{8,10},{9,11},{10,... | collective-permute-start | bytes 393224 | tf_op jit(solution)/shard_map/ppermute | solution.py:230
  61.7 0.0 collective-permute-start.15
  61.7 3.5 %collective-permute-done.22.refs_12_ = bf16[8,64,128]{2,1,0:T(8,128)(2,1)S(1)} collective-permute-done((bf16[8,64,128]{2,1,0:T(8,128)(2,1)}, bf16[8,64,128]{2,1,0:T(8,128)(2,1)S(1)}, u32[]{:S(2)}, u32[]{:S(2)}) %collective-permute-start.22) | collective-permute-done | bytes 131104 | tf_op jit(solution)/shard_map/ppermute | solution.py:230
  65.2 2.1 %collective-permute-start.23 = (bf16[8,64,128]{2,1,0:T(8,128)(2,1)S(1)}, bf16[8,64,128]{2,1,0:T(8,128)(2,1)S(1)}, u32[]{:S(2)}, u32[]{:S(2)}) collective-permute-start(bf16[8,64,128]{2,1,0:T(8,128)(2,1)S(1)} %collective-permute-done.22.refs_12_), channel_id=1, source_target_pairs={{0,4},{1,5},{2,6},{3,7},{4,0},{5,1},{6,2},{7,3},{8,12},{9,13},{10,... | collective-permute-start | bytes 393224 | tf_op jit(solution)/shard_map/ppermute | solution.py:230
  67.3 1.5 %collective-permute-start.28 = (bf16[8,64,128]{2,1,0:T(8,128)(2,1)S(1)}, bf16[8,64,128]{2,1,0:T(8,128)(2,1)S(1)}, u32[]{:S(2)}, u32[]{:S(2)}) collective-permute-start(bf16[8,64,128]{2,1,0:T(8,128)(2,1)S(1)} %collective-permute-done.22.refs_12_), channel_id=1, source_target_pairs={{0,2},{1,3},{2,0},{3,1},{4,6},{5,7},{6,4},{7,5},{8,10},{9,11},{10,... | collective-permute-start | bytes 393224 | tf_op jit(solution)/shard_map/ppermute | solution.py:230
  68.8 0.0 collective-permute-done.18.refs_4_
  68.8 0.0 collective-permute-start.27
  68.8 0.6 collective-permute-start.20
  69.4 0.2 collective-permute-start.19
  69.6 1.2 %collective-permute-done.23.refs_8_ = bf16[8,64,128]{2,1,0:T(8,128)(2,1)S(1)} collective-permute-done((bf16[8,64,128]{2,1,0:T(8,128)(2,1)S(1)}, bf16[8,64,128]{2,1,0:T(8,128)(2,1)S(1)}, u32[]{:S(2)}, u32[]{:S(2)}) %collective-permute-start.23) | collective-permute-done | bytes 131104 | tf_op jit(solution)/shard_map/ppermute | solution.py:230
  70.8 1.5 %collective-permute-start.25 = (bf16[8,64,128]{2,1,0:T(8,128)(2,1)S(1)}, bf16[8,64,128]{2,1,0:T(8,128)(2,1)S(1)}, u32[]{:S(2)}, u32[]{:S(2)}) collective-permute-start(bf16[8,64,128]{2,1,0:T(8,128)(2,1)S(1)} %collective-permute-done.23.refs_8_), channel_id=1, source_target_pairs={{0,2},{1,3},{2,0},{3,1},{4,6},{5,7},{6,4},{7,5},{8,10},{9,11},{10,... | collective-permute-start | bytes 393224 | tf_op jit(solution)/shard_map/ppermute | solution.py:230
  72.4 0.3 collective-permute-done.28.refs_14_
  72.7 0.0 collective-permute-start.17
  72.7 0.0 collective-permute-done.27.refs_13_
  72.7 0.5 collective-permute-start.24
  73.2 2.3 %collective-permute-done.20.refs_6_ = bf16[8,64,128]{2,1,0:T(8,128)(2,1)S(1)} collective-permute-done((bf16[8,64,128]{2,1,0:T(8,128)(2,1)S(1)}, bf16[8,64,128]{2,1,0:T(8,128)(2,1)S(1)}, u32[]{:S(2)}, u32[]{:S(2)}) %collective-permute-start.20) | collective-permute-done | bytes 131104 | tf_op jit(solution)/shard_map/ppermute | solution.py:230
  75.5 0.5 collective-permute-start.21
  76.0 1.9 %collective-permute-done.25.refs_10_ = bf16[8,64,128]{2,1,0:T(8,128)(2,1)S(1)} collective-permute-done((bf16[8,64,128]{2,1,0:T(8,128)(2,1)S(1)}, bf16[8,64,128]{2,1,0:T(8,128)(2,1)S(1)}, u32[]{:S(2)}, u32[]{:S(2)}) %collective-permute-start.25) | collective-permute-done | bytes 131104 | tf_op jit(solution)/shard_map/ppermute | solution.py:230
  77.9 0.0 collective-permute-start.26
  77.9 0.0 collective-permute-done.17.refs_3_
  78.0 0.0 collective-permute-done.24.refs_9_
  78.0 0.0 collective-permute-done.21.refs_7_
  78.0 1.3 %collective-permute-done.26.refs_11_ = bf16[8,64,128]{2,1,0:T(8,128)(2,1)S(1)} collective-permute-done((bf16[8,64,128]{2,1,0:T(8,128)(2,1)S(1)}, bf16[8,64,128]{2,1,0:T(8,128)(2,1)S(1)}, u32[]{:S(2)}, u32[]{:S(2)}) %collective-permute-start.26) | collective-permute-done | bytes 131104 | tf_op jit(solution)/shard_map/ppermute | solution.py:230
  79.4 0.5 copy-done.29
  79.9 13.1 %couple.3 = (f32[16,4096]{1,0:T(8,128)}, f32[16,4096]{1,0:T(8,128)}) custom-call(s32[1]{0:T(128)} %bitcast.twist, s32[16,40]{1,0:T(8,128)} %partners.3, s32[256]{0:T(256)} %slot_of.3, bf16[8,64,128]{2,1,0:T(8,128)(2,1)} %get-tuple-element.14.refs_0_, bf16[8,64,128]{2,1,0:T(8,128)(2,1)} %copy-done.7, bf16[8,64,128]{2,1,0:T(8,128)(2,1)} %copy-done.6, ...), custom_call_target="tpu_custom_call" | custom-call | tf_op jit(solution)/shard_map/couple/pallas_call | solution.py:214
  (60 shorter events, 0.1 us)
Async XLA Ops:
  3.0 9.6 %collective-permute-start.7 = (bf16[8,64,128]{2,1,0:T(8,128)(2,1)}, bf16[8,64,128]{2,1,0:T(8,128)(2,1)S(1)}, u32[]{:S(2)}, u32[]{:S(2)}) collective-permute-start(bf16[8,64,128]{2,1,0:T(8,128)(2,1)} %get-tuple-element.9.refs_0_), channel_id=1, source_target_pairs={{0,12},{1,13},{2,14},{3,15},{4,8},{5,9},{6,10},{7,11},{8,4},{9,5},... | collective-permute-start | bytes 393224 | tf_op jit(solution)/shard_map/ppermute | solution.py:230
  8.1 7.8 %collective-permute-start.3 = (bf16[8,64,128]{2,1,0:T(8,128)(2,1)}, bf16[8,64,128]{2,1,0:T(8,128)(2,1)S(1)}, u32[]{:S(2)}, u32[]{:S(2)}) collective-permute-start(bf16[8,64,128]{2,1,0:T(8,128)(2,1)} %get-tuple-element.9.refs_0_), channel_id=1, source_target_pairs={{0,4},{1,5},{2,6},{3,7},{4,0},{5,1},{6,2},{7,3},{8,12},{9,13},{10,... | collective-permute-start | bytes 393224 | tf_op jit(solution)/shard_map/ppermute | solution.py:230
  8.1 7.8 %collective-permute-start.1 = (bf16[8,64,128]{2,1,0:T(8,128)(2,1)}, bf16[8,64,128]{2,1,0:T(8,128)(2,1)S(1)}, u32[]{:S(2)}, u32[]{:S(2)}) collective-permute-start(bf16[8,64,128]{2,1,0:T(8,128)(2,1)} %get-tuple-element.9.refs_0_), channel_id=1, source_target_pairs={{0,2},{1,3},{2,0},{3,1},{4,6},{5,7},{6,4},{7,5},{8,10},{9,11},{10,... | collective-permute-start | bytes 393224 | tf_op jit(solution)/shard_map/ppermute | solution.py:230
  9.6 7.1 %collective-permute-start = (bf16[8,64,128]{2,1,0:T(8,128)(2,1)}, bf16[8,64,128]{2,1,0:T(8,128)(2,1)S(1)}, u32[]{:S(2)}, u32[]{:S(2)}) collective-permute-start(bf16[8,64,128]{2,1,0:T(8,128)(2,1)} %get-tuple-element.9.refs_0_), channel_id=1, source_target_pairs={{0,1},{1,0},{2,3},{3,2},{4,5},{5,4},{6,7},{7,6},{8,9},{9,8},{10,11... | collective-permute-start | bytes 393224 | tf_op jit(solution)/shard_map/ppermute | solution.py:230
  12.7 31.0 %copy-start = (bf16[8,64,128]{2,1,0:T(8,128)(2,1)}, bf16[8,64,128]{2,1,0:T(8,128)(2,1)S(1)}, u32[]{:S(2)}) copy-start(bf16[8,64,128]{2,1,0:T(8,128)(2,1)S(1)} %collective-permute-done.7.refs_12_) | copy-start | bytes 393220
  12.7 5.0 %collective-permute-start.8 = (bf16[8,64,128]{2,1,0:T(8,128)(2,1)S(1)}, bf16[8,64,128]{2,1,0:T(8,128)(2,1)S(1)}, u32[]{:S(2)}, u32[]{:S(2)}) collective-permute-start(bf16[8,64,128]{2,1,0:T(8,128)(2,1)S(1)} %collective-permute-done.7.refs_12_), channel_id=1, source_target_pairs={{0,4},{1,5},{2,6},{3,7},{4,0},{5,1},{6,2},{7,3},{8,12},{9,13},{10,... | collective-permute-start | bytes 393224 | tf_op jit(solution)/shard_map/ppermute | solution.py:230
  14.3 5.3 %collective-permute-start.13 = (bf16[8,64,128]{2,1,0:T(8,128)(2,1)S(1)}, bf16[8,64,128]{2,1,0:T(8,128)(2,1)S(1)}, u32[]{:S(2)}, u32[]{:S(2)}) collective-permute-start(bf16[8,64,128]{2,1,0:T(8,128)(2,1)S(1)} %collective-permute-done.7.refs_12_), channel_id=1, source_target_pairs={{0,2},{1,3},{2,0},{3,1},{4,6},{5,7},{6,4},{7,5},{8,10},{9,11},{10,... | collective-permute-start | bytes 393224 | tf_op jit(solution)/shard_map/ppermute | solution.py:230
  15.9 27.8 %copy-start.1 = (bf16[8,64,128]{2,1,0:T(8,128)(2,1)}, bf16[8,64,128]{2,1,0:T(8,128)(2,1)S(1)}, u32[]{:S(2)}) copy-start(bf16[8,64,128]{2,1,0:T(8,128)(2,1)S(1)} %collective-permute-done.3.refs_4_) | copy-start | bytes 393220
  15.9 3.8 %collective-permute-start.12 = (bf16[8,64,128]{2,1,0:T(8,128)(2,1)S(1)}, bf16[8,64,128]{2,1,0:T(8,128)(2,1)S(1)}, u32[]{:S(2)}, u32[]{:S(2)}) collective-permute-start(bf16[8,64,128]{2,1,0:T(8,128)(2,1)S(1)} %collective-permute-done.7.refs_12_), channel_id=1, source_target_pairs={{0,1},{1,0},{2,3},{3,2},{4,5},{5,4},{6,7},{7,6},{8,9},{9,8},{10,11... | collective-permute-start | bytes 393224 | tf_op jit(solution)/shard_map/ppermute | solution.py:230
  15.9 27.8 %copy-start.3 = (bf16[8,64,128]{2,1,0:T(8,128)(2,1)}, bf16[8,64,128]{2,1,0:T(8,128)(2,1)S(1)}, u32[]{:S(2)}) copy-start(bf16[8,64,128]{2,1,0:T(8,128)(2,1)S(1)} %collective-permute-done.1.refs_2_) | copy-start | bytes 393220
  15.9 6.5 %collective-permute-start.5 = (bf16[8,64,128]{2,1,0:T(8,128)(2,1)S(1)}, bf16[8,64,128]{2,1,0:T(8,128)(2,1)S(1)}, u32[]{:S(2)}, u32[]{:S(2)}) collective-permute-start(bf16[8,64,128]{2,1,0:T(8,128)(2,1)S(1)} %collective-permute-done.3.refs_4_), channel_id=1, source_target_pairs={{0,2},{1,3},{2,0},{3,1},{4,6},{5,7},{6,4},{7,5},{8,10},{9,11},{10,... | collective-permute-start | bytes 393224 | tf_op jit(solution)/shard_map/ppermute | solution.py:230
  16.7 27.0 %copy-start.5 = (bf16[8,64,128]{2,1,0:T(8,128)(2,1)}, bf16[8,64,128]{2,1,0:T(8,128)(2,1)S(1)}, u32[]{:S(2)}) copy-start(bf16[8,64,128]{2,1,0:T(8,128)(2,1)S(1)} %collective-permute-done.refs_1_) | copy-start | bytes 393220
  16.7 5.7 %collective-permute-start.4 = (bf16[8,64,128]{2,1,0:T(8,128)(2,1)S(1)}, bf16[8,64,128]{2,1,0:T(8,128)(2,1)S(1)}, u32[]{:S(2)}, u32[]{:S(2)}) collective-permute-start(bf16[8,64,128]{2,1,0:T(8,128)(2,1)S(1)} %collective-permute-done.3.refs_4_), channel_id=1, source_target_pairs={{0,1},{1,0},{2,3},{3,2},{4,5},{5,4},{6,7},{7,6},{8,9},{9,8},{10,11... | collective-permute-start | bytes 393224 | tf_op jit(solution)/shard_map/ppermute | solution.py:230
  17.6 26.1 %copy-start.8 = (bf16[8,64,128]{2,1,0:T(8,128)(2,1)}, bf16[8,64,128]{2,1,0:T(8,128)(2,1)S(1)}, u32[]{:S(2)}) copy-start(bf16[8,64,128]{2,1,0:T(8,128)(2,1)S(1)} %collective-permute-done.8.refs_8_) | copy-start | bytes 393220
  17.7 7.3 %collective-permute-start.10 = (bf16[8,64,128]{2,1,0:T(8,128)(2,1)S(1)}, bf16[8,64,128]{2,1,0:T(8,128)(2,1)S(1)}, u32[]{:S(2)}, u32[]{:S(2)}) collective-permute-start(bf16[8,64,128]{2,1,0:T(8,128)(2,1)S(1)} %collective-permute-done.8.refs_8_), channel_id=1, source_target_pairs={{0,2},{1,3},{2,0},{3,1},{4,6},{5,7},{6,4},{7,5},{8,10},{9,11},{10,... | collective-permute-start | bytes 393224 | tf_op jit(solution)/shard_map/ppermute | solution.py:230
  19.6 24.1 %copy-start.9 = (bf16[8,64,128]{2,1,0:T(8,128)(2,1)}, bf16[8,64,128]{2,1,0:T(8,128)(2,1)S(1)}, u32[]{:S(2)}) copy-start(bf16[8,64,128]{2,1,0:T(8,128)(2,1)S(1)} %collective-permute-done.13.refs_14_) | copy-start | bytes 393220
  19.6 24.2 %collective-permute-start.2 = (bf16[8,64,128]{2,1,0:T(8,128)(2,1)S(1)}, bf16[8,64,128]{2,1,0:T(8,128)(2,1)S(1)}, u32[]{:S(2)}, u32[]{:S(2)}) collective-permute-start(bf16[8,64,128]{2,1,0:T(8,128)(2,1)S(1)} %collective-permute-done.1.refs_2_), channel_id=1, source_target_pairs={{0,1},{1,0},{2,3},{3,2},{4,5},{5,4},{6,7},{7,6},{8,9},{9,8},{10,11... | collective-permute-start | bytes 393224 | tf_op jit(solution)/shard_map/ppermute | solution.py:230
  19.6 24.1 %copy-start.12 = (bf16[8,64,128]{2,1,0:T(8,128)(2,1)}, bf16[8,64,128]{2,1,0:T(8,128)(2,1)S(1)}, u32[]{:S(2)}) copy-start(bf16[8,64,128]{2,1,0:T(8,128)(2,1)S(1)} %collective-permute-done.12.refs_13_) | copy-start | bytes 393220
  19.6 24.2 %collective-permute-start.9 = (bf16[8,64,128]{2,1,0:T(8,128)(2,1)S(1)}, bf16[8,64,128]{2,1,0:T(8,128)(2,1)S(1)}, u32[]{:S(2)}, u32[]{:S(2)}) collective-permute-start(bf16[8,64,128]{2,1,0:T(8,128)(2,1)S(1)} %collective-permute-done.8.refs_8_), channel_id=1, source_target_pairs={{0,1},{1,0},{2,3},{3,2},{4,5},{5,4},{6,7},{7,6},{8,9},{9,8},{10,11... | collective-permute-start | bytes 393224 | tf_op jit(solution)/shard_map/ppermute | solution.py:230
  22.4 21.3 %copy-start.14 = (bf16[8,64,128]{2,1,0:T(8,128)(2,1)}, bf16[8,64,128]{2,1,0:T(8,128)(2,1)S(1)}, u32[]{:S(2)}) copy-start(bf16[8,64,128]{2,1,0:T(8,128)(2,1)S(1)} %collective-permute-done.5.refs_6_) | copy-start | bytes 393220
  22.4 21.4 %collective-permute-start.14 = (bf16[8,64,128]{2,1,0:T(8,128)(2,1)S(1)}, bf16[8,64,128]{2,1,0:T(8,128)(2,1)S(1)}, u32[]{:S(2)}, u32[]{:S(2)}) collective-permute-start(bf16[8,64,128]{2,1,0:T(8,128)(2,1)S(1)} %collective-permute-done.13.refs_14_), channel_id=1, source_target_pairs={{0,1},{1,0},{2,3},{3,2},{4,5},{5,4},{6,7},{7,6},{8,9},{9,8},{10,11... | collective-permute-start | bytes 393224 | tf_op jit(solution)/shard_map/ppermute | solution.py:230
  22.4 21.3 %copy-start.16 = (bf16[8,64,128]{2,1,0:T(8,128)(2,1)}, bf16[8,64,128]{2,1,0:T(8,128)(2,1)S(1)}, u32[]{:S(2)}) copy-start(bf16[8,64,128]{2,1,0:T(8,128)(2,1)S(1)} %collective-permute-done.4.refs_5_) | copy-start | bytes 393220
  22.4 21.4 %collective-permute-start.6 = (bf16[8,64,128]{2,1,0:T(8,128)(2,1)S(1)}, bf16[8,64,128]{2,1,0:T(8,128)(2,1)S(1)}, u32[]{:S(2)}, u32[]{:S(2)}) collective-permute-start(bf16[8,64,128]{2,1,0:T(8,128)(2,1)S(1)} %collective-permute-done.5.refs_6_), channel_id=1, source_target_pairs={{0,1},{1,0},{2,3},{3,2},{4,5},{5,4},{6,7},{7,6},{8,9},{9,8},{10,11... | collective-permute-start | bytes 393224 | tf_op jit(solution)/shard_map/ppermute | solution.py:230
  24.9 18.9 %copy-start.18 = (bf16[8,64,128]{2,1,0:T(8,128)(2,1)}, bf16[8,64,128]{2,1,0:T(8,128)(2,1)S(1)}, u32[]{:S(2)}) copy-start(bf16[8,64,128]{2,1,0:T(8,128)(2,1)S(1)} %collective-permute-done.10.refs_10_) | copy-start | bytes 393220
  24.9 18.9 %collective-permute-start.11 = (bf16[8,64,128]{2,1,0:T(8,128)(2,1)S(1)}, bf16[8,64,128]{2,1,0:T(8,128)(2,1)S(1)}, u32[]{:S(2)}, u32[]{:S(2)}) collective-permute-start(bf16[8,64,128]{2,1,0:T(8,128)(2,1)S(1)} %collective-permute-done.10.refs_10_), channel_id=1, source_target_pairs={{0,1},{1,0},{2,3},{3,2},{4,5},{5,4},{6,7},{7,6},{8,9},{9,8},{10,11... | collective-permute-start | bytes 393224 | tf_op jit(solution)/shard_map/ppermute | solution.py:230
  43.8 0.6 copy-start.20
  43.8 0.7 copy-start.24
  43.8 0.7 copy-start.22
  43.8 0.8 copy-start.26
  43.9 0.8 copy-start.28
  56.8 8.4 %collective-permute-start.22 = (bf16[8,64,128]{2,1,0:T(8,128)(2,1)}, bf16[8,64,128]{2,1,0:T(8,128)(2,1)S(1)}, u32[]{:S(2)}, u32[]{:S(2)}) collective-permute-start(bf16[8,64,128]{2,1,0:T(8,128)(2,1)} %get-tuple-element.14.refs_0_), channel_id=1, source_target_pairs={{0,12},{1,13},{2,14},{3,15},{4,8},{5,9},{6,10},{7,11},{8,4},{9,5},... | collective-permute-start | bytes 393224 | tf_op jit(solution)/shard_map/ppermute | solution.py:230
  59.1 9.7 %collective-permute-start.18 = (bf16[8,64,128]{2,1,0:T(8,128)(2,1)}, bf16[8,64,128]{2,1,0:T(8,128)(2,1)S(1)}, u32[]{:S(2)}, u32[]{:S(2)}) collective-permute-start(bf16[8,64,128]{2,1,0:T(8,128)(2,1)} %get-tuple-element.14.refs_0_), channel_id=1, source_target_pairs={{0,4},{1,5},{2,6},{3,7},{4,0},{5,1},{6,2},{7,3},{8,12},{9,13},{10,... | collective-permute-start | bytes 393224 | tf_op jit(solution)/shard_map/ppermute | solution.py:230
  60.2 8.7 %collective-permute-start.16 = (bf16[8,64,128]{2,1,0:T(8,128)(2,1)}, bf16[8,64,128]{2,1,0:T(8,128)(2,1)S(1)}, u32[]{:S(2)}, u32[]{:S(2)}) collective-permute-start(bf16[8,64,128]{2,1,0:T(8,128)(2,1)} %get-tuple-element.14.refs_0_), channel_id=1, source_target_pairs={{0,2},{1,3},{2,0},{3,1},{4,6},{5,7},{6,4},{7,5},{8,10},{9,11},{10,... | collective-permute-start | bytes 393224 | tf_op jit(solution)/shard_map/ppermute | solution.py:230
  61.7 7.7 %collective-permute-start.15 = (bf16[8,64,128]{2,1,0:T(8,128)(2,1)}, bf16[8,64,128]{2,1,0:T(8,128)(2,1)S(1)}, u32[]{:S(2)}, u32[]{:S(2)}) collective-permute-start(bf16[8,64,128]{2,1,0:T(8,128)(2,1)} %get-tuple-element.14.refs_0_), channel_id=1, source_target_pairs={{0,1},{1,0},{2,3},{3,2},{4,5},{5,4},{6,7},{7,6},{8,9},{9,8},{10,11... | collective-permute-start | bytes 393224 | tf_op jit(solution)/shard_map/ppermute | solution.py:230
  65.2 14.0 %copy-start.2 = (bf16[8,64,128]{2,1,0:T(8,128)(2,1)}, bf16[8,64,128]{2,1,0:T(8,128)(2,1)S(1)}, u32[]{:S(2)}) copy-start(bf16[8,64,128]{2,1,0:T(8,128)(2,1)S(1)} %collective-permute-done.22.refs_12_) | copy-start | bytes 393220
  65.2 5.6 %collective-permute-start.23 = (bf16[8,64,128]{2,1,0:T(8,128)(2,1)S(1)}, bf16[8,64,128]{2,1,0:T(8,128)(2,1)S(1)}, u32[]{:S(2)}, u32[]{:S(2)}) collective-permute-start(bf16[8,64,128]{2,1,0:T(8,128)(2,1)S(1)} %collective-permute-done.22.refs_12_), channel_id=1, source_target_pairs={{0,4},{1,5},{2,6},{3,7},{4,0},{5,1},{6,2},{7,3},{8,12},{9,13},{10,... | collective-permute-start | bytes 393224 | tf_op jit(solution)/shard_map/ppermute | solution.py:230
  67.3 5.4 %collective-permute-start.28 = (bf16[8,64,128]{2,1,0:T(8,128)(2,1)S(1)}, bf16[8,64,128]{2,1,0:T(8,128)(2,1)S(1)}, u32[]{:S(2)}, u32[]{:S(2)}) collective-permute-start(bf16[8,64,128]{2,1,0:T(8,128)(2,1)S(1)} %collective-permute-done.22.refs_12_), channel_id=1, source_target_pairs={{0,2},{1,3},{2,0},{3,1},{4,6},{5,7},{6,4},{7,5},{8,10},{9,11},{10,... | collective-permute-start | bytes 393224 | tf_op jit(solution)/shard_map/ppermute | solution.py:230
  68.8 10.4 %copy-start.4 = (bf16[8,64,128]{2,1,0:T(8,128)(2,1)}, bf16[8,64,128]{2,1,0:T(8,128)(2,1)S(1)}, u32[]{:S(2)}) copy-start(bf16[8,64,128]{2,1,0:T(8,128)(2,1)S(1)} %collective-permute-done.18.refs_4_) | copy-start | bytes 393220
  68.8 3.9 %collective-permute-start.27 = (bf16[8,64,128]{2,1,0:T(8,128)(2,1)S(1)}, bf16[8,64,128]{2,1,0:T(8,128)(2,1)S(1)}, u32[]{:S(2)}, u32[]{:S(2)}) collective-permute-start(bf16[8,64,128]{2,1,0:T(8,128)(2,1)S(1)} %collective-permute-done.22.refs_12_), channel_id=1, source_target_pairs={{0,1},{1,0},{2,3},{3,2},{4,5},{5,4},{6,7},{7,6},{8,9},{9,8},{10,11... | collective-permute-start | bytes 393224 | tf_op jit(solution)/shard_map/ppermute | solution.py:230
  68.8 10.4 %copy-start.6 = (bf16[8,64,128]{2,1,0:T(8,128)(2,1)}, bf16[8,64,128]{2,1,0:T(8,128)(2,1)S(1)}, u32[]{:S(2)}) copy-start(bf16[8,64,128]{2,1,0:T(8,128)(2,1)S(1)} %collective-permute-done.16.refs_2_) | copy-start | bytes 393220
  68.8 6.6 %collective-permute-start.20 = (bf16[8,64,128]{2,1,0:T(8,128)(2,1)S(1)}, bf16[8,64,128]{2,1,0:T(8,128)(2,1)S(1)}, u32[]{:S(2)}, u32[]{:S(2)}) collective-permute-start(bf16[8,64,128]{2,1,0:T(8,128)(2,1)S(1)} %collective-permute-done.18.refs_4_), channel_id=1, source_target_pairs={{0,2},{1,3},{2,0},{3,1},{4,6},{5,7},{6,4},{7,5},{8,10},{9,11},{10,... | collective-permute-start | bytes 393224 | tf_op jit(solution)/shard_map/ppermute | solution.py:230
  69.4 9.9 %copy-start.7 = (bf16[8,64,128]{2,1,0:T(8,128)(2,1)}, bf16[8,64,128]{2,1,0:T(8,128)(2,1)S(1)}, u32[]{:S(2)}) copy-start(bf16[8,64,128]{2,1,0:T(8,128)(2,1)S(1)} %collective-permute-done.15.refs_1_) | copy-start | bytes 393220
  69.4 6.1 %collective-permute-start.19 = (bf16[8,64,128]{2,1,0:T(8,128)(2,1)S(1)}, bf16[8,64,128]{2,1,0:T(8,128)(2,1)S(1)}, u32[]{:S(2)}, u32[]{:S(2)}) collective-permute-start(bf16[8,64,128]{2,1,0:T(8,128)(2,1)S(1)} %collective-permute-done.18.refs_4_), channel_id=1, source_target_pairs={{0,1},{1,0},{2,3},{3,2},{4,5},{5,4},{6,7},{7,6},{8,9},{9,8},{10,11... | collective-permute-start | bytes 393224 | tf_op jit(solution)/shard_map/ppermute | solution.py:230
  70.8 8.5 %copy-start.10 = (bf16[8,64,128]{2,1,0:T(8,128)(2,1)}, bf16[8,64,128]{2,1,0:T(8,128)(2,1)S(1)}, u32[]{:S(2)}) copy-start(bf16[8,64,128]{2,1,0:T(8,128)(2,1)S(1)} %collective-permute-done.23.refs_8_) | copy-start | bytes 393220
  70.8 7.1 %collective-permute-start.25 = (bf16[8,64,128]{2,1,0:T(8,128)(2,1)S(1)}, bf16[8,64,128]{2,1,0:T(8,128)(2,1)S(1)}, u32[]{:S(2)}, u32[]{:S(2)}) collective-permute-start(bf16[8,64,128]{2,1,0:T(8,128)(2,1)S(1)} %collective-permute-done.23.refs_8_), channel_id=1, source_target_pairs={{0,2},{1,3},{2,0},{3,1},{4,6},{5,7},{6,4},{7,5},{8,10},{9,11},{10,... | collective-permute-start | bytes 393224 | tf_op jit(solution)/shard_map/ppermute | solution.py:230
  72.7 6.6 %copy-start.11 = (bf16[8,64,128]{2,1,0:T(8,128)(2,1)}, bf16[8,64,128]{2,1,0:T(8,128)(2,1)S(1)}, u32[]{:S(2)}) copy-start(bf16[8,64,128]{2,1,0:T(8,128)(2,1)S(1)} %collective-permute-done.28.refs_14_) | copy-start | bytes 393220
  72.7 5.2 %collective-permute-start.17 = (bf16[8,64,128]{2,1,0:T(8,128)(2,1)S(1)}, bf16[8,64,128]{2,1,0:T(8,128)(2,1)S(1)}, u32[]{:S(2)}, u32[]{:S(2)}) collective-permute-start(bf16[8,64,128]{2,1,0:T(8,128)(2,1)S(1)} %collective-permute-done.16.refs_2_), channel_id=1, source_target_pairs={{0,1},{1,0},{2,3},{3,2},{4,5},{5,4},{6,7},{7,6},{8,9},{9,8},{10,11... | collective-permute-start | bytes 393224 | tf_op jit(solution)/shard_map/ppermute | solution.py:230
  72.7 6.6 %copy-start.13 = (bf16[8,64,128]{2,1,0:T(8,128)(2,1)}, bf16[8,64,128]{2,1,0:T(8,128)(2,1)S(1)}, u32[]{:S(2)}) copy-start(bf16[8,64,128]{2,1,0:T(8,128)(2,1)S(1)} %collective-permute-done.27.refs_13_) | copy-start | bytes 393220
  72.7 5.3 %collective-permute-start.24 = (bf16[8,64,128]{2,1,0:T(8,128)(2,1)S(1)}, bf16[8,64,128]{2,1,0:T(8,128)(2,1)S(1)}, u32[]{:S(2)}, u32[]{:S(2)}) collective-permute-start(bf16[8,64,128]{2,1,0:T(8,128)(2,1)S(1)} %collective-permute-done.23.refs_8_), channel_id=1, source_target_pairs={{0,1},{1,0},{2,3},{3,2},{4,5},{5,4},{6,7},{7,6},{8,9},{9,8},{10,11... | collective-permute-start | bytes 393224 | tf_op jit(solution)/shard_map/ppermute | solution.py:230
  75.5 3.8 %copy-start.15 = (bf16[8,64,128]{2,1,0:T(8,128)(2,1)}, bf16[8,64,128]{2,1,0:T(8,128)(2,1)S(1)}, u32[]{:S(2)}) copy-start(bf16[8,64,128]{2,1,0:T(8,128)(2,1)S(1)} %collective-permute-done.20.refs_6_) | copy-start | bytes 393220
  75.5 2.4 %collective-permute-start.29 = (bf16[8,64,128]{2,1,0:T(8,128)(2,1)S(1)}, bf16[8,64,128]{2,1,0:T(8,128)(2,1)S(1)}, u32[]{:S(2)}, u32[]{:S(2)}) collective-permute-start(bf16[8,64,128]{2,1,0:T(8,128)(2,1)S(1)} %collective-permute-done.28.refs_14_), channel_id=1, source_target_pairs={{0,1},{1,0},{2,3},{3,2},{4,5},{5,4},{6,7},{7,6},{8,9},{9,8},{10,11... | collective-permute-start | bytes 393224 | tf_op jit(solution)/shard_map/ppermute | solution.py:230
  75.5 3.8 %copy-start.17 = (bf16[8,64,128]{2,1,0:T(8,128)(2,1)}, bf16[8,64,128]{2,1,0:T(8,128)(2,1)S(1)}, u32[]{:S(2)}) copy-start(bf16[8,64,128]{2,1,0:T(8,128)(2,1)S(1)} %collective-permute-done.19.refs_5_) | copy-start | bytes 393220
  75.5 2.5 %collective-permute-start.21 = (bf16[8,64,128]{2,1,0:T(8,128)(2,1)S(1)}, bf16[8,64,128]{2,1,0:T(8,128)(2,1)S(1)}, u32[]{:S(2)}, u32[]{:S(2)}) collective-permute-start(bf16[8,64,128]{2,1,0:T(8,128)(2,1)S(1)} %collective-permute-done.20.refs_6_), channel_id=1, source_target_pairs={{0,1},{1,0},{2,3},{3,2},{4,5},{5,4},{6,7},{7,6},{8,9},{9,8},{10,11... | collective-permute-start | bytes 393224 | tf_op jit(solution)/shard_map/ppermute | solution.py:230
  77.9 1.4 %copy-start.19 = (bf16[8,64,128]{2,1,0:T(8,128)(2,1)}, bf16[8,64,128]{2,1,0:T(8,128)(2,1)S(1)}, u32[]{:S(2)}) copy-start(bf16[8,64,128]{2,1,0:T(8,128)(2,1)S(1)} %collective-permute-done.25.refs_10_) | copy-start | bytes 393220
  77.9 1.3 %collective-permute-start.26 = (bf16[8,64,128]{2,1,0:T(8,128)(2,1)S(1)}, bf16[8,64,128]{2,1,0:T(8,128)(2,1)S(1)}, u32[]{:S(2)}, u32[]{:S(2)}) collective-permute-start(bf16[8,64,128]{2,1,0:T(8,128)(2,1)S(1)} %collective-permute-done.25.refs_10_), channel_id=1, source_target_pairs={{0,1},{1,0},{2,3},{3,2},{4,5},{5,4},{6,7},{7,6},{8,9},{9,8},{10,11... | collective-permute-start | bytes 393224 | tf_op jit(solution)/shard_map/ppermute | solution.py:230
  77.9 1.4 %copy-start.21 = (bf16[8,64,128]{2,1,0:T(8,128)(2,1)}, bf16[8,64,128]{2,1,0:T(8,128)(2,1)S(1)}, u32[]{:S(2)}) copy-start(bf16[8,64,128]{2,1,0:T(8,128)(2,1)S(1)} %collective-permute-done.17.refs_3_) | copy-start | bytes 393220
  77.9 1.4 %copy-start.25 = (bf16[8,64,128]{2,1,0:T(8,128)(2,1)}, bf16[8,64,128]{2,1,0:T(8,128)(2,1)S(1)}, u32[]{:S(2)}) copy-start(bf16[8,64,128]{2,1,0:T(8,128)(2,1)S(1)} %collective-permute-done.29.refs_15_) | copy-start | bytes 393220
  78.0 1.4 %copy-start.23 = (bf16[8,64,128]{2,1,0:T(8,128)(2,1)}, bf16[8,64,128]{2,1,0:T(8,128)(2,1)S(1)}, u32[]{:S(2)}) copy-start(bf16[8,64,128]{2,1,0:T(8,128)(2,1)S(1)} %collective-permute-done.24.refs_9_) | copy-start | bytes 393220
  78.0 1.4 %copy-start.27 = (bf16[8,64,128]{2,1,0:T(8,128)(2,1)}, bf16[8,64,128]{2,1,0:T(8,128)(2,1)S(1)}, u32[]{:S(2)}) copy-start(bf16[8,64,128]{2,1,0:T(8,128)(2,1)S(1)} %collective-permute-done.21.refs_7_) | copy-start | bytes 393220
  79.3 0.7 copy-start.29

commit v2 on v1

--- a/solution.py
+++ b/solution.py
@@ -1,7 +1,9 @@
 import functools
+import math
 
 import jax
 import jax.numpy as jnp
+import numpy as np
 from jax import lax
 from jax.experimental import pallas as pl
 from jax.experimental.pallas import tpu as pltpu
@@ -10,6 +12,9 @@
 ITERS = 2
 FREQUENCY = 0.25
 SLOTS_AT_ONCE = 4
+ENTRIES = 16
+TILES = 8
+PARTS = 4
 NT = (((1,), (1,)), ((), ()))
 VMEM = pl.BlockSpec(memory_space=pltpu.VMEM)
 SMEM = pl.BlockSpec(memory_space=pltpu.SMEM)
@@ -71,51 +76,82 @@
     )(pno_count, occ_energy, right_side, pno_energy)
 
 
-def margin_kernel(margins, tiles, rows):
-    partners = margins.shape[1]
-    width = tiles.shape[2]
-    lanes = 2 * width
-    even = lax.broadcasted_iota(jnp.int32, (partners, lanes), 0) % 2 == 0
-    for j in range(width // 2):
-        part = margins[0, :, j * lanes : (j + 1) * lanes].astype(jnp.float32)
-        turned = swap_halves(part)
-        rows[pl.ds(2 * j, partners, stride=width), :] = jnp.where(even, part, turned)
-        rows[pl.ds(2 * j + 1, partners, stride=width), :] = jnp.where(even, turned, part)
-    left = left_lanes(width)
-    for k in range(partners // 2):
-        first = rows[2 * k * width : (2 * k + 1) * width]
-        second = rows[(2 * k + 1) * width : (2 * k + 2) * width]
-        tiles[0, k] = jnp.where(left, first, second).astype(jnp.bfloat16)
+def picker():
+    pair, line = np.divmod(np.arange(ENTRIES * TILES), 2 * TILES)
+    ones = np.zeros((ENTRIES * TILES, 2 * TILES * ENTRIES), np.float32)
+    for side in range(2):
+        ones[np.arange(ENTRIES * TILES), (line % 2) * TILES * ENTRIES + (line // 2) * ENTRIES + 2 * pair + side] = 1
+    return jnp.asarray(ones, jnp.bfloat16)
+
+
+def margin_kernel(pick, margins, tiles):
+    width, lanes = tiles.shape[1:]
+    left = lax.broadcasted_iota(jnp.int32, (ENTRIES, lanes), 1) < width
+    even = lax.broadcasted_iota(jnp.int32, (ENTRIES, lanes), 0) % 2 == 0
+    ones = pick[...]
+    for group in range(margins.shape[0] // ENTRIES):
+        rows = slice(group * ENTRIES, (group + 1) * ENTRIES)
+        for n in range(0, width // 2, 2 * TILES):
+            sides = []
+            for part in (n, n + TILES):
+                upper, lower = [], []
+                for j in range(part, part + TILES):
+                    here = margins[rows, j * lanes : (j + 1) * lanes]
+                    turned = swap_halves(here)
+                    zero = jnp.zeros_like(here)
+                    upper.append(jnp.where(left & even, here, jnp.where(left | even, zero, turned)))
+                    lower.append(jnp.where(left & even, turned, jnp.where(left | even, zero, here)))
+                sides.append(jnp.concatenate(upper + lower, axis=0))
+            both = jnp.concatenate(sides, axis=1)
+            found = jnp.dot(ones, both, preferred_element_type=jnp.float32).astype(jnp.bfloat16)
+            for pair in range(ENTRIES // 2):
+                for side in range(2):
+                    line = 2 * (n + side * TILES)
+                    tiles[group * ENTRIES // 2 + pair, line : line + 2 * TILES] = found[
+                        pair * 2 * TILES : (pair + 1) * 2 * TILES, side * lanes : (side + 1) * lanes
+                    ]
 
 
 def margin_tiles(margins, width):
     slots, partners, flat = margins.shape
-    return pl.pallas_call(
-        margin_kernel,
-        grid=(slots,),
-        in_specs=[pl.BlockSpec((1, partners, flat), lambda s: (s, 0, 0))],
-        out_specs=pl.BlockSpec((1, partners // 2, width, 2 * width), lambda s: (s, 0, 0, 0)),
-        out_shape=jax.ShapeDtypeStruct((slots, partners // 2, width, 2 * width), jnp.bfloat16),
-        scratch_shapes=[pltpu.VMEM((partners * width, 2 * width), jnp.float32)],
-        cost_estimate=pl.CostEstimate(flops=0, bytes_accessed=16 * margins.size, transcendentals=0),
-        name="margin_tiles",
-    )(margins)
+    rows = margins.reshape(slots * partners, flat)
+    step = ENTRIES * math.lcm(partners, ENTRIES) // ENTRIES
+    part = slots * partners // PARTS
+    pick = picker()
+    parts = []
+    for n in range(PARTS):
+        tiles = pl.pallas_call(
+            margin_kernel,
+            grid=(part // step,),
+            in_specs=[
+                pl.BlockSpec(pick.shape, lambda i: (0, 0)),
+                pl.BlockSpec((step, flat), lambda i, n=n: (n * (part // step) + i, 0)),
+            ],
+            out_specs=pl.BlockSpec((step // 2, width, 2 * width), lambda i: (i, 0, 0)),
+            out_shape=jax.ShapeDtypeStruct((part // 2, width, 2 * width), jnp.bfloat16),
+            cost_estimate=pl.CostEstimate(flops=0, bytes_accessed=4 * part * flat, transcendentals=0),
+            compiler_params=pltpu.CompilerParams(vmem_limit_bytes=16 * 2**20),
+            name="margin_tiles",
+        )(pick, rows)
+        parts.append(tiles.reshape(slots // PARTS, partners // 2, width, 2 * width))
+    return parts
 
 
 def couple_kernel(last, pieces, twist, partners, slot_of, *refs):
     gathered, refs = refs[:pieces], refs[pieces:]
-    margins, right, denom, mask, current, solution_out, residual_out = refs[:7]
-    blocks_out, refs = (None, refs[7:]) if last else (refs[7], refs[8:])
+    margins, refs = refs[:PARTS], refs[PARTS:]
+    right, denom, mask, current = refs[:4]
+    outs, refs = refs[4:6], refs[6:]
     expanded, held, halves, coupled, arrived = refs[:5]
-    slots, pairs, width, lanes = margins.shape
+    slots, pairs, width, lanes = held.shape
     half = slots // 2
-    count = 2 * pairs
-
-    def fetch(s):
-        return pltpu.make_async_copy(margins.at[s], held.at[s], arrived.at[s])
-
-    for s in range(slots):
-        fetch(s).start()
+    share = slots // PARTS
+
+    def fetch(part):
+        return pltpu.make_async_copy(margins[part], held.at[pl.ds(part * share, share)], arrived.at[part])
+
+    for part in range(PARTS):
+        fetch(part).start()
 
     left = left_lanes(width)
     base = 0
@@ -160,11 +196,11 @@
 
     def some_slots(i, carry):
         for at in range(SLOTS_AT_ONCE):
-            fetch(i * SLOTS_AT_ONCE + at).wait()
-        for at in range(SLOTS_AT_ONCE):
             one_slot(i * SLOTS_AT_ONCE + at, at)
         return carry
 
+    for part in range(PARTS):
+        fetch(part).wait()
     lax.fori_loop(0, slots // SLOTS_AT_ONCE, some_slots, 0)
 
     if last:
@@ -179,12 +215,11 @@
                 store[2 * n, u * width : (u + 1) * width] = tile
                 store[2 * n + 1, u * width : (u + 1) * width] = swap_halves(tile)
         else:
-            solution_out[u] = after
-            residual_out[u] = residual
-            blocks_out[u] = after.astype(jnp.bfloat16)
+            outs[0][u] = after
+            outs[1][u] = after.astype(jnp.bfloat16)
     if last:
         keep = lax.broadcasted_iota(jnp.int32, (half, lanes), 1) < width
-        for n, out in enumerate((solution_out, residual_out)):
+        for n, out in enumerate(outs):
             for j in range(width // 2):
                 upper = store[2 * n, pl.ds(2 * j, half, stride=width), :]
                 lower = store[2 * n, pl.ds(2 * j + 1, half, stride=width), :]
@@ -195,34 +230,35 @@
 
 
 def couple(last, twist, partners, slot_of, gathered, margins, right, denom, mask, current):
-    slots, pairs, width, lanes = margins.shape
+    share, pairs, width, lanes = margins[0].shape
+    slots = share * len(margins)
     half = slots // 2
     devices = sum(piece.shape[0] for piece in gathered) // half
     packed = jax.ShapeDtypeStruct((half, width, lanes), jnp.float32)
     flat = jax.ShapeDtypeStruct((slots, width * width), jnp.float32)
     blocks = jax.ShapeDtypeStruct((half, width, lanes), jnp.bfloat16)
-    outs = [flat, flat] if last else [packed, packed, blocks]
+    outs = [flat, flat] if last else [packed, blocks]
     scratch = [
         pltpu.VMEM((2 * devices * slots, width, lanes), jnp.bfloat16),
-        pltpu.VMEM(margins.shape, jnp.bfloat16),
+        pltpu.VMEM((slots, pairs, width, lanes), jnp.bfloat16),
         pltpu.VMEM((SLOTS_AT_ONCE, width, pairs * lanes), jnp.bfloat16),
         pltpu.VMEM((slots, width, width), jnp.float32),
-        pltpu.SemaphoreType.DMA((slots,)),
+        pltpu.SemaphoreType.DMA((len(margins),)),
     ]
     if last:
         scratch.append(pltpu.VMEM((4, half * width, lanes), jnp.float32))
     return pl.pallas_call(
         functools.partial(couple_kernel, last, len(gathered)),
-        in_specs=[SMEM] * 3 + [VMEM] * len(gathered) + [ANY] + [VMEM] * 4,
+        in_specs=[SMEM] * 3 + [VMEM] * len(gathered) + [ANY] * len(margins) + [VMEM] * 4,
         out_specs=[VMEM] * len(outs),
         out_shape=outs,
         scratch_shapes=scratch,
         compiler_params=pltpu.CompilerParams(vmem_limit_bytes=56 * 2**20),
         name="couple",
-    )(twist, partners, slot_of, *gathered, margins, right, denom, mask, current)
-
-
-def gather(blocks, devices):
+    )(twist, partners, slot_of, *gathered, *margins, right, denom, mask, current)
+
+
+def gather(blocks, devices, meanwhile):
     if devices != 16:
         return [lax.all_gather(blocks, "pair", axis=0, tiled=True)], jnp.zeros((1,), jnp.int32)
 
@@ -232,10 +268,15 @@
     piece = {0: blocks}
     for other in (2, 4, 12):
         piece[other] = swap(blocks, other)
+    piece[12], meanwhile[:2] = lax.optimization_barrier((piece[12], meanwhile[:2]))
     piece[8] = swap(piece[12], 4)
-    for other in (4, 12, 8):
-        piece[other ^ 2] = swap(piece[other], 2)
-    for other in (0, 2, 4, 6, 12, 14, 8, 10):
+    piece[14] = swap(piece[12], 2)
+    piece[10] = swap(piece[12], 6)
+    piece[6] = swap(piece[4], 2)
+    for other in (0, 2, 4, 12):
+        piece[other ^ 1] = swap(piece[other], 1)
+    for other in (6, 14, 8, 10):
+        piece[other], meanwhile[2:] = lax.optimization_barrier((piece[other], meanwhile[2:]))
         piece[other ^ 1] = swap(piece[other], 1)
     return [piece[i] for i in range(devices)], lax.axis_index("pair").astype(jnp.int32).reshape(1)
 
@@ -245,10 +286,10 @@
     right, denom, mask, current, blocks = start(right_side, pno_energy, occ_energy, pno_count)
     tiles = margin_tiles(margins, pno_energy.shape[1])
     for step in range(ITERS):
-        gathered, twist = gather(blocks, devices)
+        gathered, twist = gather(blocks, devices, tiles if step == 0 else [])
         outs = couple(step == ITERS - 1, twist, partners, slot_of, gathered, tiles, right, denom, mask, current)
         if step < ITERS - 1:
-            current, _, blocks = outs
+            current, blocks = outs
     return tuple(outs)
 
 

time: 93.6 us -> 81.3 us (0.87)
  Pallas kernels: 46.4 us -> 31.1 us
  local copies, waits for them, and re-layouts: 1.44 us -> 8.87 us
  starting transfers between devices: 25.2 us -> 20.3 us
    pallas_call x1 -> x4, Pallas kernels: 18.8 us -> 3.76 us  [margin_tiles(): pl.pallas_call(margin_kernel, grid=(part // step,), in_specs=[pl.BlockSpe...]
    unnamed x60 -> x74, local copies, waits for them, and re-layouts: 1.44 us -> 8.87 us
    ppermute x30, starting transfers between devices: 25.2 us -> 20.3 us  [swap(): return lax.ppermute(piece, 'pair', [(i, i ^ other) for i in range(devices)])]
  transfers between devices with their start and end apart: 30 -> 30, of which waited for: 11 -> 13; matrix products, arithmetic and copies ran while one was open for 0% -> 0% of each run, Pallas kernels for 20% -> 5%
where the time goes in v2:
time: 81.3 us; the launch traced here: 81 us
  Pallas kernels  31.1 us (38%)
  starting transfers between devices  20.3 us (25%)
  waiting for transfers between devices  19.8 us (24%)
  local copies, waits for them, and re-layouts  8.87 us (11%)
  between operations  0.92 us (1%)
    pallas_call x2, Pallas kernels, couple(): pl.pallas_call(functools.partial(couple_kernel, last, len(gathered)), in_...  24.9 us
    ppermute x30, starting transfers between devices, swap(): return lax.ppermute(piece, 'pair', [(i, i ^ other) for i in range(devices)])  20.3 us
    ppermute x30, waiting for transfers between devices, swap(): return lax.ppermute(piece, 'pair', [(i, i ^ other) for i in range(devices)])  19.8 us
    unnamed x74, local copies, waits for them, and re-layouts  8.87 us
    pallas_call x4, Pallas kernels, margin_tiles(): pl.pallas_call(margin_kernel, grid=(part // step,), in_specs=[pl.BlockSpe...  3.76 us
    pallas_call x1, Pallas kernels, start(): pl.pallas_call(start_kernel, in_specs=[SMEM, SMEM, VMEM, VMEM], out_specs...  2.43 us
  transfers between devices with their start and end apart: 30, of which 13 were waited for; matrix products, arithmetic and copies ran while one was open for 0% of the time, Pallas kernels for 5%

profile of v2, /device:TPU:0, one launch (start us, length us, event | category | flops | bytes accessed | tf_op | source)
XLA Modules:
  0.0 81.0 jit_solution(11260325959767998505)
XLA Ops:
  0.6 2.4 %start.1 = (f32[8,64,128]{2,1,0:T(8,128)}, f32[8,64,128]{2,1,0:T(8,128)}, f32[8,64,128]{2,1,0:T(8,128)}, f32[8,64,128]{2,1,0:T(8,128)}, bf16[8,64,128]{2,1,0:T(8,128)(2,1)}) custom-call(s32[16]{0:T(128)} %count.1, f32[16]{0:T(128)} %occ.1, f32[16,4096]{1,0:T(8,128)} %right.1, f32[16,64]{1,0:T(8,128)} %energy.1), custom_call_target="tpu_custom_call" | custom-call | tf_op jit(solution)/shard_map/start/pallas_call | solution.py:69
  3.1 3.0 %collective-permute-start.3 = (bf16[8,64,128]{2,1,0:T(8,128)(2,1)}, bf16[8,64,128]{2,1,0:T(8,128)(2,1)S(1)}, u32[]{:S(2)}, u32[]{:S(2)}) collective-permute-start(bf16[8,64,128]{2,1,0:T(8,128)(2,1)} %get-tuple-element.24.refs_0_), channel_id=1, source_target_pairs={{0,4},{1,5},{2,6},{3,7},{4,0},{5,1},{6,2},{7,3},{8,12},{9,13},{10,... | collective-permute-start | bytes 393224 | tf_op jit(solution)/shard_map/ppermute | solution.py:266
  6.1 2.5 %collective-permute-start.7 = (bf16[8,64,128]{2,1,0:T(8,128)(2,1)}, bf16[8,64,128]{2,1,0:T(8,128)(2,1)S(1)}, u32[]{:S(2)}, u32[]{:S(2)}) collective-permute-start(bf16[8,64,128]{2,1,0:T(8,128)(2,1)} %get-tuple-element.24.refs_0_), channel_id=1, source_target_pairs={{0,12},{1,13},{2,14},{3,15},{4,8},{5,9},{6,10},{7,11},{8,4},{9,5},... | collective-permute-start | bytes 393224 | tf_op jit(solution)/shard_map/ppermute | solution.py:266
  8.6 1.5 %collective-permute-start.1 = (bf16[8,64,128]{2,1,0:T(8,128)(2,1)}, bf16[8,64,128]{2,1,0:T(8,128)(2,1)S(1)}, u32[]{:S(2)}, u32[]{:S(2)}) collective-permute-start(bf16[8,64,128]{2,1,0:T(8,128)(2,1)} %get-tuple-element.24.refs_0_), channel_id=1, source_target_pairs={{0,2},{1,3},{2,0},{3,1},{4,6},{5,7},{6,4},{7,5},{8,10},{9,11},{10,... | collective-permute-start | bytes 393224 | tf_op jit(solution)/shard_map/ppermute | solution.py:266
  10.1 2.5 %copy-done = bf16[16,40,4096]{2,1,0:T(8,128)(2,1)S(1)} copy-done((bf16[16,40,4096]{2,1,0:T(8,128)(2,1)S(1)}, bf16[16,40,4096]{2,1,0:T(8,128)(2,1)}, u32[]{:S(2)}) %copy-start) | copy-done | bytes 5242904
  12.6 0.8 %copy-done.5 = bf16[128,256]{1,0:T(8,128)(2,1)S(1)} copy-done((bf16[128,256]{1,0:T(8,128)(2,1)S(1)}, bf16[128,256]{1,0:T(8,128)(2,1)}, u32[]{:S(2)}) %copy-start.5) | copy-done | bytes 65560
  13.4 0.9 %margin_tiles.7 = bf16[80,64,128]{2,1,0:T(8,128)(2,1)S(1)} custom-call(bf16[128,256]{1,0:T(8,128)(2,1)S(1)} %copy-done.5, bf16[640,4096]{1,0:T(8,128)(2,1)S(1)} %bitcast.6), custom_call_target="tpu_custom_call" | custom-call | bytes 2621440 | tf_op jit(solution)/shard_map/margin_tiles/pallas_call | solution.py:123
  14.4 1.1 %copy-done.1 = bf16[80,64,128]{2,1,0:T(8,128)(2,1)} copy-done((bf16[80,64,128]{2,1,0:T(8,128)(2,1)}, bf16[80,64,128]{2,1,0:T(8,128)(2,1)S(1)}, u32[]{:S(2)}) %copy-start.1) | copy-done | bytes 1310744
  15.4 0.9 %margin_tiles.6 = bf16[80,64,128]{2,1,0:T(8,128)(2,1)S(1)} custom-call(bf16[128,256]{1,0:T(8,128)(2,1)S(1)} %copy-done.5, bf16[640,4096]{1,0:T(8,128)(2,1)S(1)} %bitcast.7), custom_call_target="tpu_custom_call" | custom-call | bytes 2621440 | tf_op jit(solution)/shard_map/margin_tiles/pallas_call | solution.py:123
  16.4 1.1 %copy-done.2 = bf16[80,64,128]{2,1,0:T(8,128)(2,1)} copy-done((bf16[80,64,128]{2,1,0:T(8,128)(2,1)}, bf16[80,64,128]{2,1,0:T(8,128)(2,1)S(1)}, u32[]{:S(2)}) %copy-start.2) | copy-done | bytes 1310744
  17.5 0.0 collective-permute-done.3.refs_4_
  17.5 0.5 collective-permute-start.5
  18.0 1.5 %collective-permute-start.9 = (bf16[8,64,128]{2,1,0:T(8,128)(2,1)S(1)}, bf16[8,64,128]{2,1,0:T(8,128)(2,1)S(1)}, u32[]{:S(2)}, u32[]{:S(2)}) collective-permute-start(bf16[8,64,128]{2,1,0:T(8,128)(2,1)S(1)} %collective-permute-done.7.refs_12_), channel_id=1, source_target_pairs={{0,2},{1,3},{2,0},{3,1},{4,6},{5,7},{6,4},{7,5},{8,10},{9,11},{10,... | collective-permute-start | bytes 393224 | tf_op jit(solution)/shard_map/ppermute | solution.py:266
  19.5 0.7 collective-permute-start.8
  20.2 1.3 %collective-permute-start.11 = (bf16[8,64,128]{2,1,0:T(8,128)(2,1)S(1)}, bf16[8,64,128]{2,1,0:T(8,128)(2,1)S(1)}, u32[]{:S(2)}, u32[]{:S(2)}) collective-permute-start(bf16[8,64,128]{2,1,0:T(8,128)(2,1)S(1)} %collective-permute-done.7.refs_12_), channel_id=1, source_target_pairs={{0,6},{1,7},{2,4},{3,5},{4,2},{5,3},{6,0},{7,1},{8,14},{9,15},{10,... | collective-permute-start | bytes 393224 | tf_op jit(solution)/shard_map/ppermute | solution.py:266
  21.5 0.1 collective-permute-start
  21.6 3.1 %collective-permute-done.5.refs_6_ = bf16[8,64,128]{2,1,0:T(8,128)(2,1)S(1)} collective-permute-done((bf16[8,64,128]{2,1,0:T(8,128)(2,1)S(1)}, bf16[8,64,128]{2,1,0:T(8,128)(2,1)S(1)}, u32[]{:S(2)}, u32[]{:S(2)}) %collective-permute-start.5) | collective-permute-done | bytes 131104 | tf_op jit(solution)/shard_map/ppermute | solution.py:266
  24.7 0.0 collective-permute-start.4
  24.7 2.8 %collective-permute-done.9.refs_14_ = bf16[8,64,128]{2,1,0:T(8,128)(2,1)S(1)} collective-permute-done((bf16[8,64,128]{2,1,0:T(8,128)(2,1)S(1)}, bf16[8,64,128]{2,1,0:T(8,128)(2,1)S(1)}, u32[]{:S(2)}, u32[]{:S(2)}) %collective-permute-start.9) | collective-permute-done | bytes 131104 | tf_op jit(solution)/shard_map/ppermute | solution.py:266
  27.5 0.9 %margin_tiles.5 = bf16[80,64,128]{2,1,0:T(8,128)(2,1)S(1)} custom-call(bf16[128,256]{1,0:T(8,128)(2,1)S(1)} %copy-done.5, bf16[640,4096]{1,0:T(8,128)(2,1)S(1)} %bitcast.8), custom_call_target="tpu_custom_call" | custom-call | bytes 2621440 | tf_op jit(solution)/shard_map/margin_tiles/pallas_call | solution.py:123
  28.5 1.1 %copy-done.3 = bf16[80,64,128]{2,1,0:T(8,128)(2,1)} copy-done((bf16[80,64,128]{2,1,0:T(8,128)(2,1)}, bf16[80,64,128]{2,1,0:T(8,128)(2,1)S(1)}, u32[]{:S(2)}) %copy-start.3) | copy-done | bytes 1310744
  29.5 0.9 %margin_tiles.4 = bf16[80,64,128]{2,1,0:T(8,128)(2,1)S(1)} custom-call(bf16[128,256]{1,0:T(8,128)(2,1)S(1)} %copy-done.5, bf16[640,4096]{1,0:T(8,128)(2,1)S(1)} %bitcast.9), custom_call_target="tpu_custom_call" | custom-call | bytes 2621440 | tf_op jit(solution)/shard_map/margin_tiles/pallas_call | solution.py:123
  30.5 1.1 %copy-done.4 = bf16[80,64,128]{2,1,0:T(8,128)(2,1)} copy-done((bf16[80,64,128]{2,1,0:T(8,128)(2,1)}, bf16[80,64,128]{2,1,0:T(8,128)(2,1)S(1)}, u32[]{:S(2)}) %copy-start.4) | copy-done | bytes 1310744
  31.6 0.0 collective-permute-done.8.refs_8_
  31.6 0.6 collective-permute-start.13
  32.1 0.1 collective-permute-start.12
  32.2 0.4 collective-permute-start.10
  32.7 0.0 collective-permute-done.4.refs_5_
  32.7 0.2 collective-permute-start.14
  32.8 0.5 collective-permute-start.6
  33.3 0.0 collective-permute-done.13.refs_13_
  33.3 0.2 collective-permute-done.12.refs_11_
  33.5 0.2 collective-permute-done.10.refs_9_
  33.7 0.4 collective-permute-done.14.refs_15_
  34.1 0.2 collective-permute-done.6.refs_7_
  34.4 0.4 copy-done.34
  34.7 0.2 copy-done.36
  35.0 11.9 %couple.2 = (f32[8,64,128]{2,1,0:T(8,128)}, bf16[8,64,128]{2,1,0:T(8,128)(2,1)}) custom-call(s32[1]{0:T(128)} %bitcast.twist, s32[16,40]{1,0:T(8,128)} %partners.3, s32[256]{0:T(256)} %slot_of.3, bf16[8,64,128]{2,1,0:T(8,128)(2,1)} %get-tuple-element.24.refs_0_, bf16[8,64,128]{2,1,0:T(8,128)(2,1)} %copy-done.21, bf16[8,64,128]{2,1,0:T(8,128)(2,1)} %copy-done.10, ...), custom_call_target="tpu_custom_call" | custom-call | tf_op jit(solution)/shard_map/couple/pallas_call | solution.py:250
  46.9 1.4 %collective-permute-start.22 = (bf16[8,64,128]{2,1,0:T(8,128)(2,1)}, bf16[8,64,128]{2,1,0:T(8,128)(2,1)S(1)}, u32[]{:S(2)}, u32[]{:S(2)}) collective-permute-start(bf16[8,64,128]{2,1,0:T(8,128)(2,1)} %get-tuple-element.44.refs_0_), channel_id=1, source_target_pairs={{0,12},{1,13},{2,14},{3,15},{4,8},{5,9},{6,10},{7,11},{8,4},{9,5},... | collective-permute-start | bytes 393224 | tf_op jit(solution)/shard_map/ppermute | solution.py:266
  48.3 0.0 collective-permute-start.18
  48.3 0.5 collective-permute-start.16
  48.8 6.5 %collective-permute-done.22.refs_12_ = bf16[8,64,128]{2,1,0:T(8,128)(2,1)S(1)} collective-permute-done((bf16[8,64,128]{2,1,0:T(8,128)(2,1)}, bf16[8,64,128]{2,1,0:T(8,128)(2,1)S(1)}, u32[]{:S(2)}, u32[]{:S(2)}) %collective-permute-start.22) | collective-permute-done | bytes 131104 | tf_op jit(solution)/shard_map/ppermute | solution.py:266
  55.3 0.5 collective-permute-start.28
  55.8 2.0 %collective-permute-start.25 = (bf16[8,64,128]{2,1,0:T(8,128)(2,1)S(1)}, bf16[8,64,128]{2,1,0:T(8,128)(2,1)S(1)}, u32[]{:S(2)}, u32[]{:S(2)}) collective-permute-start(bf16[8,64,128]{2,1,0:T(8,128)(2,1)S(1)} %collective-permute-done.22.refs_12_), channel_id=1, source_target_pairs={{0,6},{1,7},{2,4},{3,5},{4,2},{5,3},{6,0},{7,1},{8,14},{9,15},{10,... | collective-permute-start | bytes 393224 | tf_op jit(solution)/shard_map/ppermute | solution.py:266
  57.9 1.0 %collective-permute-start.23 = (bf16[8,64,128]{2,1,0:T(8,128)(2,1)S(1)}, bf16[8,64,128]{2,1,0:T(8,128)(2,1)S(1)}, u32[]{:S(2)}, u32[]{:S(2)}) collective-permute-start(bf16[8,64,128]{2,1,0:T(8,128)(2,1)S(1)} %collective-permute-done.22.refs_12_), channel_id=1, source_target_pairs={{0,4},{1,5},{2,6},{3,7},{4,0},{5,1},{6,2},{7,3},{8,12},{9,13},{10,... | collective-permute-start | bytes 393224 | tf_op jit(solution)/shard_map/ppermute | solution.py:266
  58.8 0.0 collective-permute-done.18.refs_4_
  58.8 0.5 collective-permute-start.20
  59.3 0.0 collective-permute-done.16.refs_2_
  59.3 0.0 collective-permute-start.15
  59.3 4.5 %collective-permute-done.28.refs_14_ = bf16[8,64,128]{2,1,0:T(8,128)(2,1)S(1)} collective-permute-done((bf16[8,64,128]{2,1,0:T(8,128)(2,1)S(1)}, bf16[8,64,128]{2,1,0:T(8,128)(2,1)S(1)}, u32[]{:S(2)}, u32[]{:S(2)}) %collective-permute-start.28) | collective-permute-done | bytes 131104 | tf_op jit(solution)/shard_map/ppermute | solution.py:266
  63.8 0.5 collective-permute-start.19
  64.3 0.1 collective-permute-start.17
  64.4 0.9 %collective-permute-done.20.refs_6_ = bf16[8,64,128]{2,1,0:T(8,128)(2,1)S(1)} collective-permute-done((bf16[8,64,128]{2,1,0:T(8,128)(2,1)S(1)}, bf16[8,64,128]{2,1,0:T(8,128)(2,1)S(1)}, u32[]{:S(2)}, u32[]{:S(2)}) %collective-permute-start.20) | collective-permute-done | bytes 131104 | tf_op jit(solution)/shard_map/ppermute | solution.py:266
  65.3 0.5 collective-permute-start.26
  65.8 0.1 collective-permute-start.24
  65.9 0.4 collective-permute-start.21
  66.4 0.3 collective-permute-done.29.refs_15_
  66.7 0.2 collective-permute-done.26.refs_11_
  66.9 0.3 collective-permute-done.24.refs_9_
  67.2 0.2 collective-permute-done.21.refs_7_
  67.5 0.0 copy-done.31
  67.5 0.3 copy-done.33
  67.8 0.2 copy-done.35
  68.1 13.0 %couple.3 = (f32[16,4096]{1,0:T(8,128)}, f32[16,4096]{1,0:T(8,128)}) custom-call(s32[1]{0:T(128)} %bitcast.twist, s32[16,40]{1,0:T(8,128)} %partners.3, s32[256]{0:T(256)} %slot_of.3, bf16[8,64,128]{2,1,0:T(8,128)(2,1)} %get-tuple-element.44.refs_0_, bf16[8,64,128]{2,1,0:T(8,128)(2,1)} %copy-done.22, bf16[8,64,128]{2,1,0:T(8,128)(2,1)} %copy-done.12, ...), custom_call_target="tpu_custom_call" | custom-call | tf_op jit(solution)/shard_map/couple/pallas_call | solution.py:250
  (77 shorter events, 0.2 us)
Async XLA Ops:
  3.1 14.4 %collective-permute-start.3 = (bf16[8,64,128]{2,1,0:T(8,128)(2,1)}, bf16[8,64,128]{2,1,0:T(8,128)(2,1)S(1)}, u32[]{:S(2)}, u32[]{:S(2)}) collective-permute-start(bf16[8,64,128]{2,1,0:T(8,128)(2,1)} %get-tuple-element.24.refs_0_), channel_id=1, source_target_pairs={{0,4},{1,5},{2,6},{3,7},{4,0},{5,1},{6,2},{7,3},{8,12},{9,13},{10,... | collective-permute-start | bytes 393224 | tf_op jit(solution)/shard_map/ppermute | solution.py:266
  6.1 11.9 %collective-permute-start.7 = (bf16[8,64,128]{2,1,0:T(8,128)(2,1)}, bf16[8,64,128]{2,1,0:T(8,128)(2,1)S(1)}, u32[]{:S(2)}, u32[]{:S(2)}) collective-permute-start(bf16[8,64,128]{2,1,0:T(8,128)(2,1)} %get-tuple-element.24.refs_0_), channel_id=1, source_target_pairs={{0,12},{1,13},{2,14},{3,15},{4,8},{5,9},{6,10},{7,11},{8,4},{9,5},... | collective-permute-start | bytes 393224 | tf_op jit(solution)/shard_map/ppermute | solution.py:266
  8.6 12.9 %collective-permute-start.1 = (bf16[8,64,128]{2,1,0:T(8,128)(2,1)}, bf16[8,64,128]{2,1,0:T(8,128)(2,1)S(1)}, u32[]{:S(2)}, u32[]{:S(2)}) collective-permute-start(bf16[8,64,128]{2,1,0:T(8,128)(2,1)} %get-tuple-element.24.refs_0_), channel_id=1, source_target_pairs={{0,2},{1,3},{2,0},{3,1},{4,6},{5,7},{6,4},{7,5},{8,10},{9,11},{10,... | collective-permute-start | bytes 393224 | tf_op jit(solution)/shard_map/ppermute | solution.py:266
  10.1 2.5 %copy-start = (bf16[16,40,4096]{2,1,0:T(8,128)(2,1)S(1)}, bf16[16,40,4096]{2,1,0:T(8,128)(2,1)}, u32[]{:S(2)}) copy-start(bf16[16,40,4096]{2,1,0:T(8,128)(2,1)} %param.12) | copy-start | bytes 15728644
  12.6 0.8 %copy-start.5 = (bf16[128,256]{1,0:T(8,128)(2,1)S(1)}, bf16[128,256]{1,0:T(8,128)(2,1)}, u32[]{:S(2)}) copy-start(bf16[128,256]{1,0:T(8,128)(2,1)} %constant.6.clone.pick) | copy-start | bytes 196612
  14.4 1.1 %copy-start.1 = (bf16[80,64,128]{2,1,0:T(8,128)(2,1)}, bf16[80,64,128]{2,1,0:T(8,128)(2,1)S(1)}, u32[]{:S(2)}) copy-start(bf16[80,64,128]{2,1,0:T(8,128)(2,1)S(1)} %margin_tiles.7) | copy-start | bytes 3932164
  15.4 6.1 %copy-start.6 = (bf16[8,64,128]{2,1,0:T(8,128)(2,1)S(1)}, bf16[8,64,128]{2,1,0:T(8,128)(2,1)}, u32[]{:S(2)}) copy-start(bf16[8,64,128]{2,1,0:T(8,128)(2,1)} %get-tuple-element.24.refs_0_) | copy-start | bytes 393220
  16.4 1.1 %copy-start.2 = (bf16[80,64,128]{2,1,0:T(8,128)(2,1)}, bf16[80,64,128]{2,1,0:T(8,128)(2,1)S(1)}, u32[]{:S(2)}) copy-start(bf16[80,64,128]{2,1,0:T(8,128)(2,1)S(1)} %margin_tiles.6) | copy-start | bytes 3932164
  17.5 11.0 %copy-start.7 = (bf16[8,64,128]{2,1,0:T(8,128)(2,1)}, bf16[8,64,128]{2,1,0:T(8,128)(2,1)S(1)}, u32[]{:S(2)}) copy-start(bf16[8,64,128]{2,1,0:T(8,128)(2,1)S(1)} %collective-permute-done.3.refs_4_) | copy-start | bytes 393220
  17.5 7.2 %collective-permute-start.5 = (bf16[8,64,128]{2,1,0:T(8,128)(2,1)S(1)}, bf16[8,64,128]{2,1,0:T(8,128)(2,1)S(1)}, u32[]{:S(2)}, u32[]{:S(2)}) collective-permute-start(bf16[8,64,128]{2,1,0:T(8,128)(2,1)S(1)} %collective-permute-done.3.refs_4_), channel_id=1, source_target_pairs={{0,2},{1,3},{2,0},{3,1},{4,6},{5,7},{6,4},{7,5},{8,10},{9,11},{10,... | collective-permute-start | bytes 393224 | tf_op jit(solution)/shard_map/ppermute | solution.py:266
  18.0 13.6 %copy-start.8 = (bf16[8,64,128]{2,1,0:T(8,128)(2,1)}, bf16[8,64,128]{2,1,0:T(8,128)(2,1)S(1)}, u32[]{:S(2)}) copy-start(bf16[8,64,128]{2,1,0:T(8,128)(2,1)S(1)} %collective-permute-done.7.refs_12_) | copy-start | bytes 393220
  18.0 9.5 %collective-permute-start.9 = (bf16[8,64,128]{2,1,0:T(8,128)(2,1)S(1)}, bf16[8,64,128]{2,1,0:T(8,128)(2,1)S(1)}, u32[]{:S(2)}, u32[]{:S(2)}) collective-permute-start(bf16[8,64,128]{2,1,0:T(8,128)(2,1)S(1)} %collective-permute-done.7.refs_12_), channel_id=1, source_target_pairs={{0,2},{1,3},{2,0},{3,1},{4,6},{5,7},{6,4},{7,5},{8,10},{9,11},{10,... | collective-permute-start | bytes 393224 | tf_op jit(solution)/shard_map/ppermute | solution.py:266
  19.5 12.1 %collective-permute-start.8 = (bf16[8,64,128]{2,1,0:T(8,128)(2,1)S(1)}, bf16[8,64,128]{2,1,0:T(8,128)(2,1)S(1)}, u32[]{:S(2)}, u32[]{:S(2)}) collective-permute-start(bf16[8,64,128]{2,1,0:T(8,128)(2,1)S(1)} %collective-permute-done.7.refs_12_), channel_id=1, source_target_pairs={{0,4},{1,5},{2,6},{3,7},{4,0},{5,1},{6,2},{7,3},{8,12},{9,13},{10,... | collective-permute-start | bytes 393224 | tf_op jit(solution)/shard_map/ppermute | solution.py:266
  20.2 12.0 %collective-permute-start.11 = (bf16[8,64,128]{2,1,0:T(8,128)(2,1)S(1)}, bf16[8,64,128]{2,1,0:T(8,128)(2,1)S(1)}, u32[]{:S(2)}, u32[]{:S(2)}) collective-permute-start(bf16[8,64,128]{2,1,0:T(8,128)(2,1)S(1)} %collective-permute-done.7.refs_12_), channel_id=1, source_target_pairs={{0,6},{1,7},{2,4},{3,5},{4,2},{5,3},{6,0},{7,1},{8,14},{9,15},{10,... | collective-permute-start | bytes 393224 | tf_op jit(solution)/shard_map/ppermute | solution.py:266
  21.5 7.0 %copy-start.10 = (bf16[8,64,128]{2,1,0:T(8,128)(2,1)}, bf16[8,64,128]{2,1,0:T(8,128)(2,1)S(1)}, u32[]{:S(2)}) copy-start(bf16[8,64,128]{2,1,0:T(8,128)(2,1)S(1)} %collective-permute-done.1.refs_2_) | copy-start | bytes 393220
  21.5 10.8 %collective-permute-start = (bf16[8,64,128]{2,1,0:T(8,128)(2,1)S(1)}, bf16[8,64,128]{2,1,0:T(8,128)(2,1)S(1)}, u32[]{:S(2)}, u32[]{:S(2)}) collective-permute-start(bf16[8,64,128]{2,1,0:T(8,128)(2,1)S(1)} %copy-done.6), channel_id=1, source_target_pairs={{0,1},{1,0},{2,3},{3,2},{4,5},{5,4},{6,7},{7,6},{8,9},{9,8},{10,11... | collective-permute-start | bytes 393224 | tf_op jit(solution)/shard_map/ppermute | solution.py:266
  24.7 8.1 %copy-start.13 = (bf16[8,64,128]{2,1,0:T(8,128)(2,1)}, bf16[8,64,128]{2,1,0:T(8,128)(2,1)S(1)}, u32[]{:S(2)}) copy-start(bf16[8,64,128]{2,1,0:T(8,128)(2,1)S(1)} %collective-permute-done.5.refs_6_) | copy-start | bytes 393220
  24.7 8.0 %collective-permute-start.4 = (bf16[8,64,128]{2,1,0:T(8,128)(2,1)S(1)}, bf16[8,64,128]{2,1,0:T(8,128)(2,1)S(1)}, u32[]{:S(2)}, u32[]{:S(2)}) collective-permute-start(bf16[8,64,128]{2,1,0:T(8,128)(2,1)S(1)} %collective-permute-done.3.refs_4_), channel_id=1, source_target_pairs={{0,1},{1,0},{2,3},{3,2},{4,5},{5,4},{6,7},{7,6},{8,9},{9,8},{10,11... | collective-permute-start | bytes 393224 | tf_op jit(solution)/shard_map/ppermute | solution.py:266
  27.5 5.2 %copy-start.16 = (bf16[8,64,128]{2,1,0:T(8,128)(2,1)}, bf16[8,64,128]{2,1,0:T(8,128)(2,1)S(1)}, u32[]{:S(2)}) copy-start(bf16[8,64,128]{2,1,0:T(8,128)(2,1)S(1)} %collective-permute-done.9.refs_14_) | copy-start | bytes 393220
  27.5 5.3 %collective-permute-start.2 = (bf16[8,64,128]{2,1,0:T(8,128)(2,1)S(1)}, bf16[8,64,128]{2,1,0:T(8,128)(2,1)S(1)}, u32[]{:S(2)}, u32[]{:S(2)}) collective-permute-start(bf16[8,64,128]{2,1,0:T(8,128)(2,1)S(1)} %collective-permute-done.1.refs_2_), channel_id=1, source_target_pairs={{0,1},{1,0},{2,3},{3,2},{4,5},{5,4},{6,7},{7,6},{8,9},{9,8},{10,11... | collective-permute-start | bytes 393224 | tf_op jit(solution)/shard_map/ppermute | solution.py:266
  28.5 1.1 %copy-start.3 = (bf16[80,64,128]{2,1,0:T(8,128)(2,1)}, bf16[80,64,128]{2,1,0:T(8,128)(2,1)S(1)}, u32[]{:S(2)}) copy-start(bf16[80,64,128]{2,1,0:T(8,128)(2,1)S(1)} %margin_tiles.5) | copy-start | bytes 3932164
  30.5 1.1 %copy-start.4 = (bf16[80,64,128]{2,1,0:T(8,128)(2,1)}, bf16[80,64,128]{2,1,0:T(8,128)(2,1)S(1)}, u32[]{:S(2)}) copy-start(bf16[80,64,128]{2,1,0:T(8,128)(2,1)S(1)} %margin_tiles.4) | copy-start | bytes 3932164
  31.6 2.7 %copy-start.18 = (bf16[8,64,128]{2,1,0:T(8,128)(2,1)}, bf16[8,64,128]{2,1,0:T(8,128)(2,1)S(1)}, u32[]{:S(2)}) copy-start(bf16[8,64,128]{2,1,0:T(8,128)(2,1)S(1)} %collective-permute-done.8.refs_8_) | copy-start | bytes 393220
  31.6 1.7 %collective-permute-start.13 = (bf16[8,64,128]{2,1,0:T(8,128)(2,1)S(1)}, bf16[8,64,128]{2,1,0:T(8,128)(2,1)S(1)}, u32[]{:S(2)}, u32[]{:S(2)}) collective-permute-start(bf16[8,64,128]{2,1,0:T(8,128)(2,1)S(1)} %collective-permute-done.7.refs_12_), channel_id=1, source_target_pairs={{0,1},{1,0},{2,3},{3,2},{4,5},{5,4},{6,7},{7,6},{8,9},{9,8},{10,11... | collective-permute-start | bytes 393224 | tf_op jit(solution)/shard_map/ppermute | solution.py:266
  32.1 2.2 %copy-start.19 = (bf16[8,64,128]{2,1,0:T(8,128)(2,1)}, bf16[8,64,128]{2,1,0:T(8,128)(2,1)S(1)}, u32[]{:S(2)}) copy-start(bf16[8,64,128]{2,1,0:T(8,128)(2,1)S(1)} %collective-permute-done.11.refs_10_) | copy-start | bytes 393220
  32.1 1.3 %collective-permute-start.12 = (bf16[8,64,128]{2,1,0:T(8,128)(2,1)S(1)}, bf16[8,64,128]{2,1,0:T(8,128)(2,1)S(1)}, u32[]{:S(2)}, u32[]{:S(2)}) collective-permute-start(bf16[8,64,128]{2,1,0:T(8,128)(2,1)S(1)} %collective-permute-done.11.refs_10_), channel_id=1, source_target_pairs={{0,1},{1,0},{2,3},{3,2},{4,5},{5,4},{6,7},{7,6},{8,9},{9,8},{10,11... | collective-permute-start | bytes 393224 | tf_op jit(solution)/shard_map/ppermute | solution.py:266
  32.2 2.1 %copy-start.21 = (bf16[8,64,128]{2,1,0:T(8,128)(2,1)}, bf16[8,64,128]{2,1,0:T(8,128)(2,1)S(1)}, u32[]{:S(2)}) copy-start(bf16[8,64,128]{2,1,0:T(8,128)(2,1)S(1)} %collective-permute-done.refs_1_) | copy-start | bytes 393220
  32.2 1.4 %collective-permute-start.10 = (bf16[8,64,128]{2,1,0:T(8,128)(2,1)S(1)}, bf16[8,64,128]{2,1,0:T(8,128)(2,1)S(1)}, u32[]{:S(2)}, u32[]{:S(2)}) collective-permute-start(bf16[8,64,128]{2,1,0:T(8,128)(2,1)S(1)} %collective-permute-done.8.refs_8_), channel_id=1, source_target_pairs={{0,1},{1,0},{2,3},{3,2},{4,5},{5,4},{6,7},{7,6},{8,9},{9,8},{10,11... | collective-permute-start | bytes 393224 | tf_op jit(solution)/shard_map/ppermute | solution.py:266
  32.7 1.6 %copy-start.23 = (bf16[8,64,128]{2,1,0:T(8,128)(2,1)}, bf16[8,64,128]{2,1,0:T(8,128)(2,1)S(1)}, u32[]{:S(2)}) copy-start(bf16[8,64,128]{2,1,0:T(8,128)(2,1)S(1)} %collective-permute-done.4.refs_5_) | copy-start | bytes 393220
  32.7 1.4 %collective-permute-start.14 = (bf16[8,64,128]{2,1,0:T(8,128)(2,1)S(1)}, bf16[8,64,128]{2,1,0:T(8,128)(2,1)S(1)}, u32[]{:S(2)}, u32[]{:S(2)}) collective-permute-start(bf16[8,64,128]{2,1,0:T(8,128)(2,1)S(1)} %collective-permute-done.9.refs_14_), channel_id=1, source_target_pairs={{0,1},{1,0},{2,3},{3,2},{4,5},{5,4},{6,7},{7,6},{8,9},{9,8},{10,11... | collective-permute-start | bytes 393224 | tf_op jit(solution)/shard_map/ppermute | solution.py:266
  32.8 1.5 %copy-start.25 = (bf16[8,64,128]{2,1,0:T(8,128)(2,1)}, bf16[8,64,128]{2,1,0:T(8,128)(2,1)S(1)}, u32[]{:S(2)}) copy-start(bf16[8,64,128]{2,1,0:T(8,128)(2,1)S(1)} %collective-permute-done.2.refs_3_) | copy-start | bytes 393220
  32.8 1.5 %collective-permute-start.6 = (bf16[8,64,128]{2,1,0:T(8,128)(2,1)S(1)}, bf16[8,64,128]{2,1,0:T(8,128)(2,1)S(1)}, u32[]{:S(2)}, u32[]{:S(2)}) collective-permute-start(bf16[8,64,128]{2,1,0:T(8,128)(2,1)S(1)} %collective-permute-done.5.refs_6_), channel_id=1, source_target_pairs={{0,1},{1,0},{2,3},{3,2},{4,5},{5,4},{6,7},{7,6},{8,9},{9,8},{10,11... | collective-permute-start | bytes 393224 | tf_op jit(solution)/shard_map/ppermute | solution.py:266
  33.3 1.0 %copy-start.28 = (bf16[8,64,128]{2,1,0:T(8,128)(2,1)}, bf16[8,64,128]{2,1,0:T(8,128)(2,1)S(1)}, u32[]{:S(2)}) copy-start(bf16[8,64,128]{2,1,0:T(8,128)(2,1)S(1)} %collective-permute-done.13.refs_13_) | copy-start | bytes 393220
  33.5 0.8 %copy-start.30 = (bf16[8,64,128]{2,1,0:T(8,128)(2,1)}, bf16[8,64,128]{2,1,0:T(8,128)(2,1)S(1)}, u32[]{:S(2)}) copy-start(bf16[8,64,128]{2,1,0:T(8,128)(2,1)S(1)} %collective-permute-done.12.refs_11_) | copy-start | bytes 393220
  33.7 0.7 copy-start.32
  46.9 8.5 %collective-permute-start.22 = (bf16[8,64,128]{2,1,0:T(8,128)(2,1)}, bf16[8,64,128]{2,1,0:T(8,128)(2,1)S(1)}, u32[]{:S(2)}, u32[]{:S(2)}) collective-permute-start(bf16[8,64,128]{2,1,0:T(8,128)(2,1)} %get-tuple-element.44.refs_0_), channel_id=1, source_target_pairs={{0,12},{1,13},{2,14},{3,15},{4,8},{5,9},{6,10},{7,11},{8,4},{9,5},... | collective-permute-start | bytes 393224 | tf_op jit(solution)/shard_map/ppermute | solution.py:266
  48.3 10.5 %collective-permute-start.18 = (bf16[8,64,128]{2,1,0:T(8,128)(2,1)}, bf16[8,64,128]{2,1,0:T(8,128)(2,1)S(1)}, u32[]{:S(2)}, u32[]{:S(2)}) collective-permute-start(bf16[8,64,128]{2,1,0:T(8,128)(2,1)} %get-tuple-element.44.refs_0_), channel_id=1, source_target_pairs={{0,4},{1,5},{2,6},{3,7},{4,0},{5,1},{6,2},{7,3},{8,12},{9,13},{10,... | collective-permute-start | bytes 393224 | tf_op jit(solution)/shard_map/ppermute | solution.py:266
  48.3 11.0 %collective-permute-start.16 = (bf16[8,64,128]{2,1,0:T(8,128)(2,1)}, bf16[8,64,128]{2,1,0:T(8,128)(2,1)S(1)}, u32[]{:S(2)}, u32[]{:S(2)}) collective-permute-start(bf16[8,64,128]{2,1,0:T(8,128)(2,1)} %get-tuple-element.44.refs_0_), channel_id=1, source_target_pairs={{0,2},{1,3},{2,0},{3,1},{4,6},{5,7},{6,4},{7,5},{8,10},{9,11},{10,... | collective-permute-start | bytes 393224 | tf_op jit(solution)/shard_map/ppermute | solution.py:266
  55.3 12.1 %copy-start.9 = (bf16[8,64,128]{2,1,0:T(8,128)(2,1)}, bf16[8,64,128]{2,1,0:T(8,128)(2,1)S(1)}, u32[]{:S(2)}) copy-start(bf16[8,64,128]{2,1,0:T(8,128)(2,1)S(1)} %collective-permute-done.22.refs_12_) | copy-start | bytes 393220
  55.3 8.5 %collective-permute-start.28 = (bf16[8,64,128]{2,1,0:T(8,128)(2,1)S(1)}, bf16[8,64,128]{2,1,0:T(8,128)(2,1)S(1)}, u32[]{:S(2)}, u32[]{:S(2)}) collective-permute-start(bf16[8,64,128]{2,1,0:T(8,128)(2,1)S(1)} %collective-permute-done.22.refs_12_), channel_id=1, source_target_pairs={{0,2},{1,3},{2,0},{3,1},{4,6},{5,7},{6,4},{7,5},{8,10},{9,11},{10,... | collective-permute-start | bytes 393224 | tf_op jit(solution)/shard_map/ppermute | solution.py:266
  55.8 8.0 %collective-permute-start.25 = (bf16[8,64,128]{2,1,0:T(8,128)(2,1)S(1)}, bf16[8,64,128]{2,1,0:T(8,128)(2,1)S(1)}, u32[]{:S(2)}, u32[]{:S(2)}) collective-permute-start(bf16[8,64,128]{2,1,0:T(8,128)(2,1)S(1)} %collective-permute-done.22.refs_12_), channel_id=1, source_target_pairs={{0,6},{1,7},{2,4},{3,5},{4,2},{5,3},{6,0},{7,1},{8,14},{9,15},{10,... | collective-permute-start | bytes 393224 | tf_op jit(solution)/shard_map/ppermute | solution.py:266
  57.9 6.5 %collective-permute-start.23 = (bf16[8,64,128]{2,1,0:T(8,128)(2,1)S(1)}, bf16[8,64,128]{2,1,0:T(8,128)(2,1)S(1)}, u32[]{:S(2)}, u32[]{:S(2)}) collective-permute-start(bf16[8,64,128]{2,1,0:T(8,128)(2,1)S(1)} %collective-permute-done.22.refs_12_), channel_id=1, source_target_pairs={{0,4},{1,5},{2,6},{3,7},{4,0},{5,1},{6,2},{7,3},{8,12},{9,13},{10,... | collective-permute-start | bytes 393224 | tf_op jit(solution)/shard_map/ppermute | solution.py:266
  58.8 8.6 %copy-start.11 = (bf16[8,64,128]{2,1,0:T(8,128)(2,1)}, bf16[8,64,128]{2,1,0:T(8,128)(2,1)S(1)}, u32[]{:S(2)}) copy-start(bf16[8,64,128]{2,1,0:T(8,128)(2,1)S(1)} %collective-permute-done.18.refs_4_) | copy-start | bytes 393220
  58.8 6.5 %collective-permute-start.20 = (bf16[8,64,128]{2,1,0:T(8,128)(2,1)S(1)}, bf16[8,64,128]{2,1,0:T(8,128)(2,1)S(1)}, u32[]{:S(2)}, u32[]{:S(2)}) collective-permute-start(bf16[8,64,128]{2,1,0:T(8,128)(2,1)S(1)} %collective-permute-done.18.refs_4_), channel_id=1, source_target_pairs={{0,2},{1,3},{2,0},{3,1},{4,6},{5,7},{6,4},{7,5},{8,10},{9,11},{10,... | collective-permute-start | bytes 393224 | tf_op jit(solution)/shard_map/ppermute | solution.py:266
  59.3 8.1 %copy-start.12 = (bf16[8,64,128]{2,1,0:T(8,128)(2,1)}, bf16[8,64,128]{2,1,0:T(8,128)(2,1)S(1)}, u32[]{:S(2)}) copy-start(bf16[8,64,128]{2,1,0:T(8,128)(2,1)S(1)} %collective-permute-done.16.refs_2_) | copy-start | bytes 393220
  59.3 6.0 %collective-permute-start.15 = (bf16[8,64,128]{2,1,0:T(8,128)(2,1)}, bf16[8,64,128]{2,1,0:T(8,128)(2,1)S(1)}, u32[]{:S(2)}, u32[]{:S(2)}) collective-permute-start(bf16[8,64,128]{2,1,0:T(8,128)(2,1)} %get-tuple-element.44.refs_0_), channel_id=1, source_target_pairs={{0,1},{1,0},{2,3},{3,2},{4,5},{5,4},{6,7},{7,6},{8,9},{9,8},{10,11... | collective-permute-start | bytes 393224 | tf_op jit(solution)/shard_map/ppermute | solution.py:266
  63.8 3.6 %copy-start.14 = (bf16[8,64,128]{2,1,0:T(8,128)(2,1)}, bf16[8,64,128]{2,1,0:T(8,128)(2,1)S(1)}, u32[]{:S(2)}) copy-start(bf16[8,64,128]{2,1,0:T(8,128)(2,1)S(1)} %collective-permute-done.28.refs_14_) | copy-start | bytes 393220
  63.8 2.0 %collective-permute-start.27 = (bf16[8,64,128]{2,1,0:T(8,128)(2,1)S(1)}, bf16[8,64,128]{2,1,0:T(8,128)(2,1)S(1)}, u32[]{:S(2)}, u32[]{:S(2)}) collective-permute-start(bf16[8,64,128]{2,1,0:T(8,128)(2,1)S(1)} %collective-permute-done.22.refs_12_), channel_id=1, source_target_pairs={{0,1},{1,0},{2,3},{3,2},{4,5},{5,4},{6,7},{7,6},{8,9},{9,8},{10,11... | collective-permute-start | bytes 393224 | tf_op jit(solution)/shard_map/ppermute | solution.py:266
  63.8 3.6 %copy-start.15 = (bf16[8,64,128]{2,1,0:T(8,128)(2,1)}, bf16[8,64,128]{2,1,0:T(8,128)(2,1)S(1)}, u32[]{:S(2)}) copy-start(bf16[8,64,128]{2,1,0:T(8,128)(2,1)S(1)} %collective-permute-done.25.refs_10_) | copy-start | bytes 393220
  63.8 2.1 %collective-permute-start.19 = (bf16[8,64,128]{2,1,0:T(8,128)(2,1)S(1)}, bf16[8,64,128]{2,1,0:T(8,128)(2,1)S(1)}, u32[]{:S(2)}, u32[]{:S(2)}) collective-permute-start(bf16[8,64,128]{2,1,0:T(8,128)(2,1)S(1)} %collective-permute-done.18.refs_4_), channel_id=1, source_target_pairs={{0,1},{1,0},{2,3},{3,2},{4,5},{5,4},{6,7},{7,6},{8,9},{9,8},{10,11... | collective-permute-start | bytes 393224 | tf_op jit(solution)/shard_map/ppermute | solution.py:266
  64.3 3.1 %copy-start.17 = (bf16[8,64,128]{2,1,0:T(8,128)(2,1)}, bf16[8,64,128]{2,1,0:T(8,128)(2,1)S(1)}, u32[]{:S(2)}) copy-start(bf16[8,64,128]{2,1,0:T(8,128)(2,1)S(1)} %collective-permute-done.23.refs_8_) | copy-start | bytes 393220
  64.3 2.0 %collective-permute-start.17 = (bf16[8,64,128]{2,1,0:T(8,128)(2,1)S(1)}, bf16[8,64,128]{2,1,0:T(8,128)(2,1)S(1)}, u32[]{:S(2)}, u32[]{:S(2)}) collective-permute-start(bf16[8,64,128]{2,1,0:T(8,128)(2,1)S(1)} %collective-permute-done.16.refs_2_), channel_id=1, source_target_pairs={{0,1},{1,0},{2,3},{3,2},{4,5},{5,4},{6,7},{7,6},{8,9},{9,8},{10,11... | collective-permute-start | bytes 393224 | tf_op jit(solution)/shard_map/ppermute | solution.py:266
  65.3 2.1 %copy-start.20 = (bf16[8,64,128]{2,1,0:T(8,128)(2,1)}, bf16[8,64,128]{2,1,0:T(8,128)(2,1)S(1)}, u32[]{:S(2)}) copy-start(bf16[8,64,128]{2,1,0:T(8,128)(2,1)S(1)} %collective-permute-done.20.refs_6_) | copy-start | bytes 393220
  65.3 1.3 %collective-permute-start.29 = (bf16[8,64,128]{2,1,0:T(8,128)(2,1)S(1)}, bf16[8,64,128]{2,1,0:T(8,128)(2,1)S(1)}, u32[]{:S(2)}, u32[]{:S(2)}) collective-permute-start(bf16[8,64,128]{2,1,0:T(8,128)(2,1)S(1)} %collective-permute-done.28.refs_14_), channel_id=1, source_target_pairs={{0,1},{1,0},{2,3},{3,2},{4,5},{5,4},{6,7},{7,6},{8,9},{9,8},{10,11... | collective-permute-start | bytes 393224 | tf_op jit(solution)/shard_map/ppermute | solution.py:266
  65.3 2.1 %copy-start.22 = (bf16[8,64,128]{2,1,0:T(8,128)(2,1)}, bf16[8,64,128]{2,1,0:T(8,128)(2,1)S(1)}, u32[]{:S(2)}) copy-start(bf16[8,64,128]{2,1,0:T(8,128)(2,1)S(1)} %collective-permute-done.15.refs_1_) | copy-start | bytes 393220
  65.3 1.5 %collective-permute-start.26 = (bf16[8,64,128]{2,1,0:T(8,128)(2,1)S(1)}, bf16[8,64,128]{2,1,0:T(8,128)(2,1)S(1)}, u32[]{:S(2)}, u32[]{:S(2)}) collective-permute-start(bf16[8,64,128]{2,1,0:T(8,128)(2,1)S(1)} %collective-permute-done.25.refs_10_), channel_id=1, source_target_pairs={{0,1},{1,0},{2,3},{3,2},{4,5},{5,4},{6,7},{7,6},{8,9},{9,8},{10,11... | collective-permute-start | bytes 393224 | tf_op jit(solution)/shard_map/ppermute | solution.py:266
  65.8 1.6 %copy-start.24 = (bf16[8,64,128]{2,1,0:T(8,128)(2,1)}, bf16[8,64,128]{2,1,0:T(8,128)(2,1)S(1)}, u32[]{:S(2)}) copy-start(bf16[8,64,128]{2,1,0:T(8,128)(2,1)S(1)} %collective-permute-done.27.refs_13_) | copy-start | bytes 393220
  65.8 1.3 %collective-permute-start.24 = (bf16[8,64,128]{2,1,0:T(8,128)(2,1)S(1)}, bf16[8,64,128]{2,1,0:T(8,128)(2,1)S(1)}, u32[]{:S(2)}, u32[]{:S(2)}) collective-permute-start(bf16[8,64,128]{2,1,0:T(8,128)(2,1)S(1)} %collective-permute-done.23.refs_8_), channel_id=1, source_target_pairs={{0,1},{1,0},{2,3},{3,2},{4,5},{5,4},{6,7},{7,6},{8,9},{9,8},{10,11... | collective-permute-start | bytes 393224 | tf_op jit(solution)/shard_map/ppermute | solution.py:266
  65.9 1.5 %copy-start.26 = (bf16[8,64,128]{2,1,0:T(8,128)(2,1)}, bf16[8,64,128]{2,1,0:T(8,128)(2,1)S(1)}, u32[]{:S(2)}) copy-start(bf16[8,64,128]{2,1,0:T(8,128)(2,1)S(1)} %collective-permute-done.19.refs_5_) | copy-start | bytes 393220
  65.9 1.4 %collective-permute-start.21 = (bf16[8,64,128]{2,1,0:T(8,128)(2,1)S(1)}, bf16[8,64,128]{2,1,0:T(8,128)(2,1)S(1)}, u32[]{:S(2)}, u32[]{:S(2)}) collective-permute-start(bf16[8,64,128]{2,1,0:T(8,128)(2,1)S(1)} %collective-permute-done.20.refs_6_), channel_id=1, source_target_pairs={{0,1},{1,0},{2,3},{3,2},{4,5},{5,4},{6,7},{7,6},{8,9},{9,8},{10,11... | collective-permute-start | bytes 393224 | tf_op jit(solution)/shard_map/ppermute | solution.py:266
  66.4 1.1 %copy-start.27 = (bf16[8,64,128]{2,1,0:T(8,128)(2,1)}, bf16[8,64,128]{2,1,0:T(8,128)(2,1)S(1)}, u32[]{:S(2)}) copy-start(bf16[8,64,128]{2,1,0:T(8,128)(2,1)S(1)} %collective-permute-done.17.refs_3_) | copy-start | bytes 393220
  66.7 0.8 copy-start.29
  66.9 0.7 copy-start.31
  67.4 0.7 copy-start.35
  (3 other events, 2.0 us)

commit v3 on v2

--- a/solution.py
+++ b/solution.py
@@ -14,7 +14,6 @@
 SLOTS_AT_ONCE = 4
 ENTRIES = 16
 TILES = 8
-PARTS = 4
 NT = (((1,), (1,)), ((), ()))
 VMEM = pl.BlockSpec(memory_space=pltpu.VMEM)
 SMEM = pl.BlockSpec(memory_space=pltpu.SMEM)
@@ -84,90 +83,86 @@
     return jnp.asarray(ones, jnp.bfloat16)
 
 
-def margin_kernel(pick, margins, tiles):
+def margin_kernel(pick, margins, tiles, held, arrived):
     width, lanes = tiles.shape[1:]
+    steps, step = held.shape[:2]
     left = lax.broadcasted_iota(jnp.int32, (ENTRIES, lanes), 1) < width
     even = lax.broadcasted_iota(jnp.int32, (ENTRIES, lanes), 0) % 2 == 0
+
+    def fetch(i):
+        return pltpu.make_async_copy(margins.at[pl.ds(i * step, step)], held.at[i], arrived.at[i])
+
+    for i in range(steps):
+        fetch(i).start()
     ones = pick[...]
-    for group in range(margins.shape[0] // ENTRIES):
-        rows = slice(group * ENTRIES, (group + 1) * ENTRIES)
-        for n in range(0, width // 2, 2 * TILES):
-            sides = []
-            for part in (n, n + TILES):
-                upper, lower = [], []
-                for j in range(part, part + TILES):
-                    here = margins[rows, j * lanes : (j + 1) * lanes]
-                    turned = swap_halves(here)
-                    zero = jnp.zeros_like(here)
-                    upper.append(jnp.where(left & even, here, jnp.where(left | even, zero, turned)))
-                    lower.append(jnp.where(left & even, turned, jnp.where(left | even, zero, here)))
-                sides.append(jnp.concatenate(upper + lower, axis=0))
-            both = jnp.concatenate(sides, axis=1)
-            found = jnp.dot(ones, both, preferred_element_type=jnp.float32).astype(jnp.bfloat16)
-            for pair in range(ENTRIES // 2):
-                for side in range(2):
-                    line = 2 * (n + side * TILES)
-                    tiles[group * ENTRIES // 2 + pair, line : line + 2 * TILES] = found[
-                        pair * 2 * TILES : (pair + 1) * 2 * TILES, side * lanes : (side + 1) * lanes
-                    ]
+
+    def some(i, carry):
+        fetch(i).wait()
+        for group in range(step // ENTRIES):
+            rows = slice(group * ENTRIES, (group + 1) * ENTRIES)
+            for n in range(0, width // 2, 2 * TILES):
+                sides = []
+                for part in (n, n + TILES):
+                    upper, lower = [], []
+                    for j in range(part, part + TILES):
+                        here = held[i, rows, j * lanes : (j + 1) * lanes]
+                        turned = swap_halves(here)
+                        zero = jnp.zeros_like(here)
+                        upper.append(jnp.where(left & even, here, jnp.where(left | even, zero, turned)))
+                        lower.append(jnp.where(left & even, turned, jnp.where(left | even, zero, here)))
+                    sides.append(jnp.concatenate(upper + lower, axis=0))
+                both = jnp.concatenate(sides, axis=1)
+                found = jnp.dot(ones, both, preferred_element_type=jnp.float32).astype(jnp.bfloat16)
+                for pair in range(ENTRIES // 2):
+                    for side in range(2):
+                        line = 2 * (n + side * TILES)
+                        tiles[i * (step // 2) + group * (ENTRIES // 2) + pair, line : line + 2 * TILES] = found[
+                            pair * 2 * TILES : (pair + 1) * 2 * TILES, side * lanes : (side + 1) * lanes
+                        ]
+        return carry
+
+    lax.fori_loop(0, steps, some, 0)
 
 
 def margin_tiles(margins, width):
     slots, partners, flat = margins.shape
-    rows = margins.reshape(slots * partners, flat)
-    step = ENTRIES * math.lcm(partners, ENTRIES) // ENTRIES
-    part = slots * partners // PARTS
-    pick = picker()
-    parts = []
-    for n in range(PARTS):
-        tiles = pl.pallas_call(
-            margin_kernel,
-            grid=(part // step,),
-            in_specs=[
-                pl.BlockSpec(pick.shape, lambda i: (0, 0)),
-                pl.BlockSpec((step, flat), lambda i, n=n: (n * (part // step) + i, 0)),
-            ],
-            out_specs=pl.BlockSpec((step // 2, width, 2 * width), lambda i: (i, 0, 0)),
-            out_shape=jax.ShapeDtypeStruct((part // 2, width, 2 * width), jnp.bfloat16),
-            cost_estimate=pl.CostEstimate(flops=0, bytes_accessed=4 * part * flat, transcendentals=0),
-            compiler_params=pltpu.CompilerParams(vmem_limit_bytes=16 * 2**20),
-            name="margin_tiles",
-        )(pick, rows)
-        parts.append(tiles.reshape(slots // PARTS, partners // 2, width, 2 * width))
-    return parts
+    entries = slots * partners
+    step = math.lcm(partners, ENTRIES)
+    tiles = pl.pallas_call(
+        margin_kernel,
+        in_specs=[VMEM, ANY],
+        out_specs=VMEM,
+        out_shape=jax.ShapeDtypeStruct((entries // 2, width, 2 * width), jnp.bfloat16),
+        scratch_shapes=[
+            pltpu.VMEM((entries // step, step, flat), jnp.bfloat16),
+            pltpu.SemaphoreType.DMA((entries // step,)),
+        ],
+        cost_estimate=pl.CostEstimate(flops=0, bytes_accessed=4 * margins.size, transcendentals=0),
+        compiler_params=pltpu.CompilerParams(vmem_limit_bytes=12 * 2**20),
+        name="margin_tiles",
+    )(picker(), margins.reshape(entries, flat))
+    return tiles.reshape(slots, partners // 2, width, 2 * width)
 
 
 def couple_kernel(last, pieces, twist, partners, slot_of, *refs):
     gathered, refs = refs[:pieces], refs[pieces:]
-    margins, refs = refs[:PARTS], refs[PARTS:]
-    right, denom, mask, current = refs[:4]
-    outs, refs = refs[4:6], refs[6:]
-    expanded, held, halves, coupled, arrived = refs[:5]
+    held, right, denom, mask, current = refs[:5]
+    outs, refs = refs[5:7], refs[7:]
+    expanded, halves, coupled = refs[:3]
     slots, pairs, width, lanes = held.shape
     half = slots // 2
-    share = slots // PARTS
-
-    def fetch(part):
-        return pltpu.make_async_copy(margins[part], held.at[pl.ds(part * share, share)], arrived.at[part])
-
-    for part in range(PARTS):
-        fetch(part).start()
 
     left = left_lanes(width)
+    right_half = jnp.logical_not(left)
     base = 0
     for piece in gathered:
         held_devices = piece.shape[0] // half
 
         def expand(i, carry, piece=piece, base=base):
             tile = piece[i]
-            turned = swap_halves(tile)
-            zero = jnp.zeros_like(tile)
-            u = (base + i // half) * slots + i % half
-            v = u + half
-            expanded[2 * u] = jnp.where(left, tile, zero)
-            expanded[2 * u + 1] = jnp.where(left, zero, turned)
-            expanded[2 * v] = jnp.where(left, turned, zero)
-            expanded[2 * v + 1] = jnp.where(left, zero, tile)
+            at = 2 * (base * half + i)
+            expanded[at] = tile
+            expanded[at + 1] = swap_halves(tile)
             return carry
 
         lax.fori_loop(0, piece.shape[0], expand, 0, unroll=4)
@@ -177,7 +172,10 @@
 
     def block(s, k):
         target = slot_of[partners[s, k]] ^ turn
-        return expanded[2 * target + k % 2]
+        device, slot = target // slots, target % slots
+        side = jnp.where(slot >= half, 1, 0)
+        tile = expanded[2 * (device * half + slot - half * side) + (side ^ (k % 2))]
+        return jnp.where(left if k % 2 == 0 else right_half, tile, jnp.zeros_like(tile))
 
     zero = jnp.zeros((lanes, lanes), jnp.bfloat16)
 
@@ -199,12 +197,10 @@
             one_slot(i * SLOTS_AT_ONCE + at, at)
         return carry
 
-    for part in range(PARTS):
-        fetch(part).wait()
     lax.fori_loop(0, slots // SLOTS_AT_ONCE, some_slots, 0)
 
     if last:
-        store = refs[5]
+        store = refs[3]
     for u in range(half):
         both = jnp.concatenate([coupled[u], coupled[u + half]], axis=1)
         before = current[u]
@@ -230,8 +226,7 @@
 
 
 def couple(last, twist, partners, slot_of, gathered, margins, right, denom, mask, current):
-    share, pairs, width, lanes = margins[0].shape
-    slots = share * len(margins)
+    slots, pairs, width, lanes = margins.shape
     half = slots // 2
     devices = sum(piece.shape[0] for piece in gathered) // half
     packed = jax.ShapeDtypeStruct((half, width, lanes), jnp.float32)
@@ -239,28 +234,28 @@
     blocks = jax.ShapeDtypeStruct((half, width, lanes), jnp.bfloat16)
     outs = [flat, flat] if last else [packed, blocks]
     scratch = [
-        pltpu.VMEM((2 * devices * slots, width, lanes), jnp.bfloat16),
-        pltpu.VMEM((slots, pairs, width, lanes), jnp.bfloat16),
+        pltpu.VMEM((devices * slots, width, lanes), jnp.bfloat16),
         pltpu.VMEM((SLOTS_AT_ONCE, width, pairs * lanes), jnp.bfloat16),
         pltpu.VMEM((slots, width, width), jnp.float32),
-        pltpu.SemaphoreType.DMA((len(margins),)),
     ]
     if last:
         scratch.append(pltpu.VMEM((4, half * width, lanes), jnp.float32))
+    operands = [*gathered, margins, right, denom, mask, current]
+    size = sum(math.prod(x.shape) * x.dtype.itemsize for x in operands + outs + scratch)
     return pl.pallas_call(
         functools.partial(couple_kernel, last, len(gathered)),
-        in_specs=[SMEM] * 3 + [VMEM] * len(gathered) + [ANY] * len(margins) + [VMEM] * 4,
+        in_specs=[SMEM] * 3 + [VMEM] * len(operands),
         out_specs=[VMEM] * len(outs),
         out_shape=outs,
         scratch_shapes=scratch,
-        compiler_params=pltpu.CompilerParams(vmem_limit_bytes=56 * 2**20),
+        compiler_params=pltpu.CompilerParams(vmem_limit_bytes=size + 4 * 2**20),
         name="couple",
-    )(twist, partners, slot_of, *gathered, *margins, right, denom, mask, current)
+    )(twist, partners, slot_of, *operands)
 
 
 def gather(blocks, devices, meanwhile):
     if devices != 16:
-        return [lax.all_gather(blocks, "pair", axis=0, tiled=True)], jnp.zeros((1,), jnp.int32)
+        return [lax.all_gather(blocks, "pair", axis=0, tiled=True)], jnp.zeros((1,), jnp.int32), meanwhile
 
     def swap(piece, other):
         return lax.ppermute(piece, "pair", [(i, i ^ other) for i in range(devices)])
@@ -268,17 +263,16 @@
     piece = {0: blocks}
     for other in (2, 4, 12):
         piece[other] = swap(blocks, other)
-    piece[12], meanwhile[:2] = lax.optimization_barrier((piece[12], meanwhile[:2]))
+    piece[6] = swap(piece[4], 2)
+    piece[12], piece[6], meanwhile = lax.optimization_barrier((piece[12], piece[6], meanwhile))
     piece[8] = swap(piece[12], 4)
     piece[14] = swap(piece[12], 2)
     piece[10] = swap(piece[12], 6)
-    piece[6] = swap(piece[4], 2)
     for other in (0, 2, 4, 12):
         piece[other ^ 1] = swap(piece[other], 1)
     for other in (6, 14, 8, 10):
-        piece[other], meanwhile[2:] = lax.optimization_barrier((piece[other], meanwhile[2:]))
         piece[other ^ 1] = swap(piece[other], 1)
-    return [piece[i] for i in range(devices)], lax.axis_index("pair").astype(jnp.int32).reshape(1)
+    return [piece[i] for i in range(devices)], lax.axis_index("pair").astype(jnp.int32).reshape(1), meanwhile
 
 
 def shards(right_side, pno_energy, occ_energy, pno_count, margins, partners, slot_of):
@@ -286,7 +280,7 @@
     right, denom, mask, current, blocks = start(right_side, pno_energy, occ_energy, pno_count)
     tiles = margin_tiles(margins, pno_energy.shape[1])
     for step in range(ITERS):
-        gathered, twist = gather(blocks, devices, tiles if step == 0 else [])
+        gathered, twist, tiles = gather(blocks, devices, tiles)
         outs = couple(step == ITERS - 1, twist, partners, slot_of, gathered, tiles, right, denom, mask, current)
         if step < ITERS - 1:
             current, blocks = outs

time: 81.3 us -> 87.5 us (1.076)
  the two profiles are of different devices: /device:TPU:0 before, /device:TPU:19 now
where the time goes in v3:
time: 87.5 us; the launch traced here: 87.3 us
  starting transfers between devices  37.1 us (42%)
  Pallas kernels  32.6 us (37%)
  waiting for transfers between devices  8.7 us (10%)
  local copies, waits for them, and re-layouts  8.15 us (9%)
    ppermute x30, starting transfers between devices, swap(): return lax.ppermute(piece, 'pair', [(i, i ^ other) for i in range(devices)])  37.1 us
    pallas_call x2, Pallas kernels, couple(): pl.pallas_call(functools.partial(couple_kernel, last, len(gathered)), in_...  24.7 us
    ppermute x30, waiting for transfers between devices, swap(): return lax.ppermute(piece, 'pair', [(i, i ^ other) for i in range(devices)])  8.7 us
    unnamed x24, local copies, waits for them, and re-layouts  8.15 us
    pallas_call x1, Pallas kernels, margin_tiles(): pl.pallas_call(margin_kernel, in_specs=[VMEM, ANY], out_specs=VMEM, out_s...  5.46 us
    pallas_call x1, Pallas kernels, start(): pl.pallas_call(start_kernel, in_specs=[SMEM, SMEM, VMEM, VMEM], out_specs...  2.42 us
  transfers between devices with their start and end apart: 30, of which 8 were waited for; matrix products, arithmetic and copies ran while one was open for 0% of the time, Pallas kernels for 6%

profile of v3, /device:TPU:19, one launch (start us, length us, event | category | flops | bytes accessed | tf_op | source)
XLA Modules:
  0.0 87.3 jit_solution(18093976881487642468)
XLA Ops:
  0.6 2.4 %start.1 = (f32[8,64,128]{2,1,0:T(8,128)}, f32[8,64,128]{2,1,0:T(8,128)}, f32[8,64,128]{2,1,0:T(8,128)}, f32[8,64,128]{2,1,0:T(8,128)}, bf16[8,64,128]{2,1,0:T(8,128)(2,1)}) custom-call(s32[16]{0:T(128)} %count.1, f32[16]{0:T(128)} %occ.1, f32[16,4096]{1,0:T(8,128)} %right.1, f32[16,64]{1,0:T(8,128)} %energy.1), custom_call_target="tpu_custom_call" | custom-call | tf_op jit(solution)/shard_map/start/pallas_call | solution.py:68
  3.0 1.3 %collective-permute-start.3 = (bf16[8,64,128]{2,1,0:T(8,128)(2,1)}, bf16[8,64,128]{2,1,0:T(8,128)(2,1)S(1)}, u32[]{:S(2)}, u32[]{:S(2)}) collective-permute-start(bf16[8,64,128]{2,1,0:T(8,128)(2,1)} %get-tuple-element.15.refs_0_), channel_id=1, source_target_pairs={{0,4},{1,5},{2,6},{3,7},{4,0},{5,1},{6,2},{7,3},{8,12},{9,13},{10,... | collective-permute-start | bytes 393224 | tf_op jit(solution)/shard_map/ppermute | solution.py:261
  4.3 1.2 %collective-permute-start.1 = (bf16[8,64,128]{2,1,0:T(8,128)(2,1)}, bf16[8,64,128]{2,1,0:T(8,128)(2,1)S(1)}, u32[]{:S(2)}, u32[]{:S(2)}) collective-permute-start(bf16[8,64,128]{2,1,0:T(8,128)(2,1)} %get-tuple-element.15.refs_0_), channel_id=1, source_target_pairs={{0,2},{1,3},{2,0},{3,1},{4,6},{5,7},{6,4},{7,5},{8,10},{9,11},{10,... | collective-permute-start | bytes 393224 | tf_op jit(solution)/shard_map/ppermute | solution.py:261
  5.6 0.0 collective-permute-start.5
  5.6 2.0 %collective-permute-done.3.refs_4_ = bf16[8,64,128]{2,1,0:T(8,128)(2,1)S(1)} collective-permute-done((bf16[8,64,128]{2,1,0:T(8,128)(2,1)}, bf16[8,64,128]{2,1,0:T(8,128)(2,1)S(1)}, u32[]{:S(2)}, u32[]{:S(2)}) %collective-permute-start.3) | collective-permute-done | bytes 131104 | tf_op jit(solution)/shard_map/ppermute | solution.py:261
  7.6 1.2 %collective-permute-start.6 = (bf16[8,64,128]{2,1,0:T(8,128)(2,1)S(1)}, bf16[8,64,128]{2,1,0:T(8,128)(2,1)S(1)}, u32[]{:S(2)}, u32[]{:S(2)}) collective-permute-start(bf16[8,64,128]{2,1,0:T(8,128)(2,1)S(1)} %collective-permute-done.3.refs_4_), channel_id=1, source_target_pairs={{0,2},{1,3},{2,0},{3,1},{4,6},{5,7},{6,4},{7,5},{8,10},{9,11},{10,... | collective-permute-start | bytes 393224 | tf_op jit(solution)/shard_map/ppermute | solution.py:261
  8.9 3.0 %collective-permute-start = (bf16[8,64,128]{2,1,0:T(8,128)(2,1)}, bf16[8,64,128]{2,1,0:T(8,128)(2,1)S(1)}, u32[]{:S(2)}, u32[]{:S(2)}) collective-permute-start(bf16[8,64,128]{2,1,0:T(8,128)(2,1)} %get-tuple-element.15.refs_0_), channel_id=1, source_target_pairs={{0,1},{1,0},{2,3},{3,2},{4,5},{5,4},{6,7},{7,6},{8,9},{9,8},{10,11... | collective-permute-start | bytes 393224 | tf_op jit(solution)/shard_map/ppermute | solution.py:261
  11.8 2.5 %copy-done.3 = bf16[16,40,4096]{2,1,0:T(8,128)(2,1)S(1)} copy-done((bf16[16,40,4096]{2,1,0:T(8,128)(2,1)S(1)}, bf16[16,40,4096]{2,1,0:T(8,128)(2,1)}, u32[]{:S(2)}) %copy-start.3) | copy-done | bytes 5242904
  14.3 0.8 copy-done.9
  15.2 0.0 copy-start.10
  15.2 0.0 copy-start.11
  15.2 5.5 %margin_tiles.1 = bf16[320,64,128]{2,1,0:T(8,128)(2,1)S(1)} custom-call(bf16[128,256]{1,0:T(8,128)(2,1)S(1)} %copy-done.9, bf16[640,4096]{1,0:T(8,128)(2,1)S(1)} %bitcast.5), custom_call_target="tpu_custom_call" | custom-call | bytes 10485760 | tf_op jit(solution)/shard_map/margin_tiles/pallas_call | solution.py:131
  20.7 2.3 %copy-done = bf16[320,64,128]{2,1,0:T(8,128)(2,1)} copy-done((bf16[320,64,128]{2,1,0:T(8,128)(2,1)}, bf16[320,64,128]{2,1,0:T(8,128)(2,1)S(1)}, u32[]{:S(2)}) %copy-start) | copy-done | bytes 5242904
  23.0 0.0 collective-permute-start.4
  23.0 0.0 collective-permute-done.1.refs_2_
  23.0 0.5 collective-permute-start.2
  23.5 0.0 collective-permute-done.5.refs_12_
  23.5 0.0 collective-permute-done.6.refs_6_
  23.5 0.0 collective-permute-start.13
  23.5 4.2 %collective-permute-start.10 = (bf16[8,64,128]{2,1,0:T(8,128)(2,1)S(1)}, bf16[8,64,128]{2,1,0:T(8,128)(2,1)S(1)}, u32[]{:S(2)}, u32[]{:S(2)}) collective-permute-start(bf16[8,64,128]{2,1,0:T(8,128)(2,1)S(1)} %collective-permute-done.5.refs_12_), channel_id=1, source_target_pairs={{0,6},{1,7},{2,4},{3,5},{4,2},{5,3},{6,0},{7,1},{8,14},{9,15},{10,... | collective-permute-start | bytes 393224 | tf_op jit(solution)/shard_map/ppermute | solution.py:261
  27.7 0.0 collective-permute-done.refs_1_
  27.7 0.0 collective-permute-start.8
  27.7 0.0 collective-permute-done.4.refs_5_
  27.7 0.7 collective-permute-start.12
  28.4 0.0 collective-permute-done.2.refs_3_
  28.4 0.1 collective-permute-start.7
  28.5 0.1 collective-permute-done.13.refs_14_
  28.6 3.3 %collective-permute-start.14 = (bf16[8,64,128]{2,1,0:T(8,128)(2,1)S(1)}, bf16[8,64,128]{2,1,0:T(8,128)(2,1)S(1)}, u32[]{:S(2)}, u32[]{:S(2)}) collective-permute-start(bf16[8,64,128]{2,1,0:T(8,128)(2,1)S(1)} %collective-permute-done.13.refs_14_), channel_id=1, source_target_pairs={{0,1},{1,0},{2,3},{3,2},{4,5},{5,4},{6,7},{7,6},{8,9},{9,8},{10,11... | collective-permute-start | bytes 393224 | tf_op jit(solution)/shard_map/ppermute | solution.py:261
  31.9 0.0 collective-permute-done.10.refs_10_
  31.9 0.7 collective-permute-start.11
  32.6 0.5 collective-permute-done.8.refs_8_
  33.1 1.2 %collective-permute-start.9 = (bf16[8,64,128]{2,1,0:T(8,128)(2,1)S(1)}, bf16[8,64,128]{2,1,0:T(8,128)(2,1)S(1)}, u32[]{:S(2)}, u32[]{:S(2)}) collective-permute-start(bf16[8,64,128]{2,1,0:T(8,128)(2,1)S(1)} %collective-permute-done.8.refs_8_), channel_id=1, source_target_pairs={{0,1},{1,0},{2,3},{3,2},{4,5},{5,4},{6,7},{7,6},{8,9},{9,8},{10,11... | collective-permute-start | bytes 393224 | tf_op jit(solution)/shard_map/ppermute | solution.py:261
  34.3 0.0 collective-permute-done.11.refs_11_
  34.3 1.0 %collective-permute-done.9.refs_9_ = bf16[8,64,128]{2,1,0:T(8,128)(2,1)S(1)} collective-permute-done((bf16[8,64,128]{2,1,0:T(8,128)(2,1)S(1)}, bf16[8,64,128]{2,1,0:T(8,128)(2,1)S(1)}, u32[]{:S(2)}, u32[]{:S(2)}) %collective-permute-start.9) | collective-permute-done | bytes 131104 | tf_op jit(solution)/shard_map/ppermute | solution.py:261
  35.3 2.5 %copy-done.1 = bf16[320,64,128]{2,1,0:T(8,128)(2,1)S(1)} copy-done((bf16[320,64,128]{2,1,0:T(8,128)(2,1)S(1)}, bf16[320,64,128]{2,1,0:T(8,128)(2,1)}, u32[]{:S(2)}) %copy-start.1) | copy-done | bytes 5242904
  37.8 11.5 %couple.2 = (f32[8,64,128]{2,1,0:T(8,128)S(1)}, bf16[8,64,128]{2,1,0:T(8,128)(2,1)S(1)}) custom-call(s32[1]{0:T(128)} %bitcast.twist, s32[16,40]{1,0:T(8,128)S(1)} %copy-done.10, s32[256]{0:T(256)S(1)} %copy-done.11, bf16[8,64,128]{2,1,0:T(8,128)(2,1)S(1)} %copy-done.8, bf16[8,64,128]{2,1,0:T(8,128)(2,1)S(1)} %collective-permute-done.refs_1_, ...), custom_call_target="tpu_custom_call" | custom-call | tf_op jit(solution)/shard_map/couple/pallas_call | solution.py:245
  49.2 2.3 %collective-permute-start.18 = (bf16[8,64,128]{2,1,0:T(8,128)(2,1)S(1)}, bf16[8,64,128]{2,1,0:T(8,128)(2,1)S(1)}, u32[]{:S(2)}, u32[]{:S(2)}) collective-permute-start(bf16[8,64,128]{2,1,0:T(8,128)(2,1)S(1)} %get-tuple-element.23.refs_0_), channel_id=1, source_target_pairs={{0,4},{1,5},{2,6},{3,7},{4,0},{5,1},{6,2},{7,3},{8,12},{9,13},{10,... | collective-permute-start | bytes 393224 | tf_op jit(solution)/shard_map/ppermute | solution.py:261
  51.5 0.1 collective-permute-start.16
  51.6 0.0 collective-permute-start.20
  51.6 3.5 %collective-permute-done.18.refs_4_ = bf16[8,64,128]{2,1,0:T(8,128)(2,1)S(1)} collective-permute-done((bf16[8,64,128]{2,1,0:T(8,128)(2,1)S(1)}, bf16[8,64,128]{2,1,0:T(8,128)(2,1)S(1)}, u32[]{:S(2)}, u32[]{:S(2)}) %collective-permute-start.18) | collective-permute-done | bytes 131104 | tf_op jit(solution)/shard_map/ppermute | solution.py:261
  55.1 0.0 collective-permute-start.21
  55.1 3.0 %collective-permute-start.15 = (bf16[8,64,128]{2,1,0:T(8,128)(2,1)S(1)}, bf16[8,64,128]{2,1,0:T(8,128)(2,1)S(1)}, u32[]{:S(2)}, u32[]{:S(2)}) collective-permute-start(bf16[8,64,128]{2,1,0:T(8,128)(2,1)S(1)} %get-tuple-element.23.refs_0_), channel_id=1, source_target_pairs={{0,1},{1,0},{2,3},{3,2},{4,5},{5,4},{6,7},{7,6},{8,9},{9,8},{10,11... | collective-permute-start | bytes 393224 | tf_op jit(solution)/shard_map/ppermute | solution.py:261
  58.1 0.0 collective-permute-start.19
  58.1 0.5 collective-permute-start.17
  58.6 0.3 collective-permute-done.20.refs_12_
  58.9 0.3 collective-permute-done.21.refs_6_
  59.2 1.3 %collective-permute-start.28 = (bf16[8,64,128]{2,1,0:T(8,128)(2,1)S(1)}, bf16[8,64,128]{2,1,0:T(8,128)(2,1)S(1)}, u32[]{:S(2)}, u32[]{:S(2)}) collective-permute-start(bf16[8,64,128]{2,1,0:T(8,128)(2,1)S(1)} %collective-permute-done.20.refs_12_), channel_id=1, source_target_pairs={{0,2},{1,3},{2,0},{3,1},{4,6},{5,7},{6,4},{7,5},{8,10},{9,11},{10,... | collective-permute-start | bytes 393224 | tf_op jit(solution)/shard_map/ppermute | solution.py:261
  60.4 1.8 %collective-permute-start.25 = (bf16[8,64,128]{2,1,0:T(8,128)(2,1)S(1)}, bf16[8,64,128]{2,1,0:T(8,128)(2,1)S(1)}, u32[]{:S(2)}, u32[]{:S(2)}) collective-permute-start(bf16[8,64,128]{2,1,0:T(8,128)(2,1)S(1)} %collective-permute-done.20.refs_12_), channel_id=1, source_target_pairs={{0,6},{1,7},{2,4},{3,5},{4,2},{5,3},{6,0},{7,1},{8,14},{9,15},{10,... | collective-permute-start | bytes 393224 | tf_op jit(solution)/shard_map/ppermute | solution.py:261
  62.3 0.0 collective-permute-done.15.refs_1_
  62.3 0.2 collective-permute-start.23
  62.5 5.7 %collective-permute-start.27 = (bf16[8,64,128]{2,1,0:T(8,128)(2,1)S(1)}, bf16[8,64,128]{2,1,0:T(8,128)(2,1)S(1)}, u32[]{:S(2)}, u32[]{:S(2)}) collective-permute-start(bf16[8,64,128]{2,1,0:T(8,128)(2,1)S(1)} %collective-permute-done.20.refs_12_), channel_id=1, source_target_pairs={{0,1},{1,0},{2,3},{3,2},{4,5},{5,4},{6,7},{7,6},{8,9},{9,8},{10,11... | collective-permute-start | bytes 393224 | tf_op jit(solution)/shard_map/ppermute | solution.py:261
  68.2 0.0 collective-permute-done.17.refs_3_
  68.2 0.1 collective-permute-start.22
  68.2 0.0 collective-permute-done.28.refs_14_
  68.3 0.5 collective-permute-start.29
  68.8 0.0 collective-permute-done.25.refs_10_
  68.8 2.2 %collective-permute-start.26 = (bf16[8,64,128]{2,1,0:T(8,128)(2,1)S(1)}, bf16[8,64,128]{2,1,0:T(8,128)(2,1)S(1)}, u32[]{:S(2)}, u32[]{:S(2)}) collective-permute-start(bf16[8,64,128]{2,1,0:T(8,128)(2,1)S(1)} %collective-permute-done.25.refs_10_), channel_id=1, source_target_pairs={{0,1},{1,0},{2,3},{3,2},{4,5},{5,4},{6,7},{7,6},{8,9},{9,8},{10,11... | collective-permute-start | bytes 393224 | tf_op jit(solution)/shard_map/ppermute | solution.py:261
  71.0 2.0 %collective-permute-start.24 = (bf16[8,64,128]{2,1,0:T(8,128)(2,1)S(1)}, bf16[8,64,128]{2,1,0:T(8,128)(2,1)S(1)}, u32[]{:S(2)}, u32[]{:S(2)}) collective-permute-start(bf16[8,64,128]{2,1,0:T(8,128)(2,1)S(1)} %collective-permute-done.23.refs_8_), channel_id=1, source_target_pairs={{0,1},{1,0},{2,3},{3,2},{4,5},{5,4},{6,7},{7,6},{8,9},{9,8},{10,11... | collective-permute-start | bytes 393224 | tf_op jit(solution)/shard_map/ppermute | solution.py:261
  73.1 0.0 collective-permute-done.22.refs_7_
  73.1 0.0 collective-permute-done.27.refs_13_
  73.1 0.0 collective-permute-done.29.refs_15_
  73.1 0.0 collective-permute-done.26.refs_11_
  73.1 1.0 %collective-permute-done.24.refs_9_ = bf16[8,64,128]{2,1,0:T(8,128)(2,1)S(1)} collective-permute-done((bf16[8,64,128]{2,1,0:T(8,128)(2,1)S(1)}, bf16[8,64,128]{2,1,0:T(8,128)(2,1)S(1)}, u32[]{:S(2)}, u32[]{:S(2)}) %collective-permute-start.24) | collective-permute-done | bytes 131104 | tf_op jit(solution)/shard_map/ppermute | solution.py:261
  74.0 13.2 %couple.3 = (f32[16,4096]{1,0:T(8,128)}, f32[16,4096]{1,0:T(8,128)}) custom-call(s32[1]{0:T(128)} %bitcast.twist, s32[16,40]{1,0:T(8,128)S(1)} %copy-done.10, s32[256]{0:T(256)S(1)} %copy-done.11, bf16[8,64,128]{2,1,0:T(8,128)(2,1)S(1)} %get-tuple-element.23.refs_0_, bf16[8,64,128]{2,1,0:T(8,128)(2,1)S(1)} %collective-permute-done.15.refs_1_, ...), custom_call_target="tpu_custom_call" | custom-call | tf_op jit(solution)/shard_map/couple/pallas_call | solution.py:245
  (24 shorter events, 0.0 us)
Async XLA Ops:
  3.0 4.6 %collective-permute-start.3 = (bf16[8,64,128]{2,1,0:T(8,128)(2,1)}, bf16[8,64,128]{2,1,0:T(8,128)(2,1)S(1)}, u32[]{:S(2)}, u32[]{:S(2)}) collective-permute-start(bf16[8,64,128]{2,1,0:T(8,128)(2,1)} %get-tuple-element.15.refs_0_), channel_id=1, source_target_pairs={{0,4},{1,5},{2,6},{3,7},{4,0},{5,1},{6,2},{7,3},{8,12},{9,13},{10,... | collective-permute-start | bytes 393224 | tf_op jit(solution)/shard_map/ppermute | solution.py:261
  4.3 18.7 %collective-permute-start.1 = (bf16[8,64,128]{2,1,0:T(8,128)(2,1)}, bf16[8,64,128]{2,1,0:T(8,128)(2,1)S(1)}, u32[]{:S(2)}, u32[]{:S(2)}) collective-permute-start(bf16[8,64,128]{2,1,0:T(8,128)(2,1)} %get-tuple-element.15.refs_0_), channel_id=1, source_target_pairs={{0,2},{1,3},{2,0},{3,1},{4,6},{5,7},{6,4},{7,5},{8,10},{9,11},{10,... | collective-permute-start | bytes 393224 | tf_op jit(solution)/shard_map/ppermute | solution.py:261
  5.6 17.9 %collective-permute-start.5 = (bf16[8,64,128]{2,1,0:T(8,128)(2,1)}, bf16[8,64,128]{2,1,0:T(8,128)(2,1)S(1)}, u32[]{:S(2)}, u32[]{:S(2)}) collective-permute-start(bf16[8,64,128]{2,1,0:T(8,128)(2,1)} %get-tuple-element.15.refs_0_), channel_id=1, source_target_pairs={{0,12},{1,13},{2,14},{3,15},{4,8},{5,9},{6,10},{7,11},{8,4},{9,5},... | collective-permute-start | bytes 393224 | tf_op jit(solution)/shard_map/ppermute | solution.py:261
  7.6 15.9 %collective-permute-start.6 = (bf16[8,64,128]{2,1,0:T(8,128)(2,1)S(1)}, bf16[8,64,128]{2,1,0:T(8,128)(2,1)S(1)}, u32[]{:S(2)}, u32[]{:S(2)}) collective-permute-start(bf16[8,64,128]{2,1,0:T(8,128)(2,1)S(1)} %collective-permute-done.3.refs_4_), channel_id=1, source_target_pairs={{0,2},{1,3},{2,0},{3,1},{4,6},{5,7},{6,4},{7,5},{8,10},{9,11},{10,... | collective-permute-start | bytes 393224 | tf_op jit(solution)/shard_map/ppermute | solution.py:261
  8.9 18.8 %collective-permute-start = (bf16[8,64,128]{2,1,0:T(8,128)(2,1)}, bf16[8,64,128]{2,1,0:T(8,128)(2,1)S(1)}, u32[]{:S(2)}, u32[]{:S(2)}) collective-permute-start(bf16[8,64,128]{2,1,0:T(8,128)(2,1)} %get-tuple-element.15.refs_0_), channel_id=1, source_target_pairs={{0,1},{1,0},{2,3},{3,2},{4,5},{5,4},{6,7},{7,6},{8,9},{9,8},{10,11... | collective-permute-start | bytes 393224 | tf_op jit(solution)/shard_map/ppermute | solution.py:261
  11.8 2.5 %copy-start.3 = (bf16[16,40,4096]{2,1,0:T(8,128)(2,1)S(1)}, bf16[16,40,4096]{2,1,0:T(8,128)(2,1)}, u32[]{:S(2)}) copy-start(bf16[16,40,4096]{2,1,0:T(8,128)(2,1)} %param.12) | copy-start | bytes 15728644
  14.3 0.8 copy-start.9
  15.2 20.1 %copy-start.4 = (f32[8,64,128]{2,1,0:T(8,128)S(1)}, f32[8,64,128]{2,1,0:T(8,128)}, u32[]{:S(2)}) copy-start(f32[8,64,128]{2,1,0:T(8,128)} %get-tuple-element.19.refs_17_) | copy-start | bytes 786436
  15.2 20.1 %copy-start.5 = (f32[8,64,128]{2,1,0:T(8,128)S(1)}, f32[8,64,128]{2,1,0:T(8,128)}, u32[]{:S(2)}) copy-start(f32[8,64,128]{2,1,0:T(8,128)} %get-tuple-element.20.refs_18_) | copy-start | bytes 786436
  15.2 20.1 %copy-start.6 = (f32[8,64,128]{2,1,0:T(8,128)S(1)}, f32[8,64,128]{2,1,0:T(8,128)}, u32[]{:S(2)}) copy-start(f32[8,64,128]{2,1,0:T(8,128)} %get-tuple-element.21.refs_19_) | copy-start | bytes 786436
  15.2 20.1 %copy-start.7 = (f32[8,64,128]{2,1,0:T(8,128)S(1)}, f32[8,64,128]{2,1,0:T(8,128)}, u32[]{:S(2)}) copy-start(f32[8,64,128]{2,1,0:T(8,128)} %get-tuple-element.22.refs_20_) | copy-start | bytes 786436
  15.2 20.1 %copy-start.8 = (bf16[8,64,128]{2,1,0:T(8,128)(2,1)S(1)}, bf16[8,64,128]{2,1,0:T(8,128)(2,1)}, u32[]{:S(2)}) copy-start(bf16[8,64,128]{2,1,0:T(8,128)(2,1)} %get-tuple-element.15.refs_0_) | copy-start | bytes 393220
  15.2 20.1 %copy-start.10 = (s32[16,40]{1,0:T(8,128)S(1)}, s32[16,40]{1,0:T(8,128)}, u32[]{:S(2)}) copy-start(s32[16,40]{1,0:T(8,128)} %partners.3) | copy-start | bytes 7684
  15.2 20.1 %copy-start.11 = (s32[256]{0:T(256)S(1)}, s32[256]{0:T(256)}, u32[]{:S(2)}) copy-start(s32[256]{0:T(256)} %slot_of.3) | copy-start | bytes 3076
  20.7 2.3 %copy-start = (bf16[320,64,128]{2,1,0:T(8,128)(2,1)}, bf16[320,64,128]{2,1,0:T(8,128)(2,1)S(1)}, u32[]{:S(2)}) copy-start(bf16[320,64,128]{2,1,0:T(8,128)(2,1)S(1)} %margin_tiles.1) | copy-start | bytes 15728644
  23.0 4.7 %collective-permute-start.4 = (bf16[8,64,128]{2,1,0:T(8,128)(2,1)S(1)}, bf16[8,64,128]{2,1,0:T(8,128)(2,1)S(1)}, u32[]{:S(2)}, u32[]{:S(2)}) collective-permute-start(bf16[8,64,128]{2,1,0:T(8,128)(2,1)S(1)} %collective-permute-done.3.refs_4_), channel_id=1, source_target_pairs={{0,1},{1,0},{2,3},{3,2},{4,5},{5,4},{6,7},{7,6},{8,9},{9,8},{10,11... | collective-permute-start | bytes 393224 | tf_op jit(solution)/shard_map/ppermute | solution.py:261
  23.0 5.4 %collective-permute-start.2 = (bf16[8,64,128]{2,1,0:T(8,128)(2,1)S(1)}, bf16[8,64,128]{2,1,0:T(8,128)(2,1)S(1)}, u32[]{:S(2)}, u32[]{:S(2)}) collective-permute-start(bf16[8,64,128]{2,1,0:T(8,128)(2,1)S(1)} %collective-permute-done.1.refs_2_), channel_id=1, source_target_pairs={{0,1},{1,0},{2,3},{3,2},{4,5},{5,4},{6,7},{7,6},{8,9},{9,8},{10,11... | collective-permute-start | bytes 393224 | tf_op jit(solution)/shard_map/ppermute | solution.py:261
  23.5 5.1 %collective-permute-start.13 = (bf16[8,64,128]{2,1,0:T(8,128)(2,1)S(1)}, bf16[8,64,128]{2,1,0:T(8,128)(2,1)S(1)}, u32[]{:S(2)}, u32[]{:S(2)}) collective-permute-start(bf16[8,64,128]{2,1,0:T(8,128)(2,1)S(1)} %collective-permute-done.5.refs_12_), channel_id=1, source_target_pairs={{0,2},{1,3},{2,0},{3,1},{4,6},{5,7},{6,4},{7,5},{8,10},{9,11},{10,... | collective-permute-start | bytes 393224 | tf_op jit(solution)/shard_map/ppermute | solution.py:261
  23.5 8.4 %collective-permute-start.10 = (bf16[8,64,128]{2,1,0:T(8,128)(2,1)S(1)}, bf16[8,64,128]{2,1,0:T(8,128)(2,1)S(1)}, u32[]{:S(2)}, u32[]{:S(2)}) collective-permute-start(bf16[8,64,128]{2,1,0:T(8,128)(2,1)S(1)} %collective-permute-done.5.refs_12_), channel_id=1, source_target_pairs={{0,6},{1,7},{2,4},{3,5},{4,2},{5,3},{6,0},{7,1},{8,14},{9,15},{10,... | collective-permute-start | bytes 393224 | tf_op jit(solution)/shard_map/ppermute | solution.py:261
  27.7 5.4 %collective-permute-start.8 = (bf16[8,64,128]{2,1,0:T(8,128)(2,1)S(1)}, bf16[8,64,128]{2,1,0:T(8,128)(2,1)S(1)}, u32[]{:S(2)}, u32[]{:S(2)}) collective-permute-start(bf16[8,64,128]{2,1,0:T(8,128)(2,1)S(1)} %collective-permute-done.5.refs_12_), channel_id=1, source_target_pairs={{0,4},{1,5},{2,6},{3,7},{4,0},{5,1},{6,2},{7,3},{8,12},{9,13},{10,... | collective-permute-start | bytes 393224 | tf_op jit(solution)/shard_map/ppermute | solution.py:261
  27.7 6.6 %collective-permute-start.12 = (bf16[8,64,128]{2,1,0:T(8,128)(2,1)S(1)}, bf16[8,64,128]{2,1,0:T(8,128)(2,1)S(1)}, u32[]{:S(2)}, u32[]{:S(2)}) collective-permute-start(bf16[8,64,128]{2,1,0:T(8,128)(2,1)S(1)} %collective-permute-done.5.refs_12_), channel_id=1, source_target_pairs={{0,1},{1,0},{2,3},{3,2},{4,5},{5,4},{6,7},{7,6},{8,9},{9,8},{10,11... | collective-permute-start | bytes 393224 | tf_op jit(solution)/shard_map/ppermute | solution.py:261
  28.4 5.9 %collective-permute-start.7 = (bf16[8,64,128]{2,1,0:T(8,128)(2,1)S(1)}, bf16[8,64,128]{2,1,0:T(8,128)(2,1)S(1)}, u32[]{:S(2)}, u32[]{:S(2)}) collective-permute-start(bf16[8,64,128]{2,1,0:T(8,128)(2,1)S(1)} %collective-permute-done.6.refs_6_), channel_id=1, source_target_pairs={{0,1},{1,0},{2,3},{3,2},{4,5},{5,4},{6,7},{7,6},{8,9},{9,8},{10,11... | collective-permute-start | bytes 393224 | tf_op jit(solution)/shard_map/ppermute | solution.py:261
  28.6 5.7 %collective-permute-start.14 = (bf16[8,64,128]{2,1,0:T(8,128)(2,1)S(1)}, bf16[8,64,128]{2,1,0:T(8,128)(2,1)S(1)}, u32[]{:S(2)}, u32[]{:S(2)}) collective-permute-start(bf16[8,64,128]{2,1,0:T(8,128)(2,1)S(1)} %collective-permute-done.13.refs_14_), channel_id=1, source_target_pairs={{0,1},{1,0},{2,3},{3,2},{4,5},{5,4},{6,7},{7,6},{8,9},{9,8},{10,11... | collective-permute-start | bytes 393224 | tf_op jit(solution)/shard_map/ppermute | solution.py:261
  31.9 2.4 %collective-permute-start.11 = (bf16[8,64,128]{2,1,0:T(8,128)(2,1)S(1)}, bf16[8,64,128]{2,1,0:T(8,128)(2,1)S(1)}, u32[]{:S(2)}, u32[]{:S(2)}) collective-permute-start(bf16[8,64,128]{2,1,0:T(8,128)(2,1)S(1)} %collective-permute-done.10.refs_10_), channel_id=1, source_target_pairs={{0,1},{1,0},{2,3},{3,2},{4,5},{5,4},{6,7},{7,6},{8,9},{9,8},{10,11... | collective-permute-start | bytes 393224 | tf_op jit(solution)/shard_map/ppermute | solution.py:261
  33.1 2.2 %collective-permute-start.9 = (bf16[8,64,128]{2,1,0:T(8,128)(2,1)S(1)}, bf16[8,64,128]{2,1,0:T(8,128)(2,1)S(1)}, u32[]{:S(2)}, u32[]{:S(2)}) collective-permute-start(bf16[8,64,128]{2,1,0:T(8,128)(2,1)S(1)} %collective-permute-done.8.refs_8_), channel_id=1, source_target_pairs={{0,1},{1,0},{2,3},{3,2},{4,5},{5,4},{6,7},{7,6},{8,9},{9,8},{10,11... | collective-permute-start | bytes 393224 | tf_op jit(solution)/shard_map/ppermute | solution.py:261
  35.3 2.5 %copy-start.1 = (bf16[320,64,128]{2,1,0:T(8,128)(2,1)S(1)}, bf16[320,64,128]{2,1,0:T(8,128)(2,1)}, u32[]{:S(2)}) copy-start(bf16[320,64,128]{2,1,0:T(8,128)(2,1)} %copy-done) | copy-start | bytes 15728644
  37.8 36.3 %copy-start.2 = (bf16[320,64,128]{2,1,0:T(8,128)(2,1)S(1)}, bf16[320,64,128]{2,1,0:T(8,128)(2,1)}, u32[]{:S(2)}) copy-start(bf16[320,64,128]{2,1,0:T(8,128)(2,1)} %copy-done) | copy-start | bytes 15728644
  49.2 5.8 %collective-permute-start.18 = (bf16[8,64,128]{2,1,0:T(8,128)(2,1)S(1)}, bf16[8,64,128]{2,1,0:T(8,128)(2,1)S(1)}, u32[]{:S(2)}, u32[]{:S(2)}) collective-permute-start(bf16[8,64,128]{2,1,0:T(8,128)(2,1)S(1)} %get-tuple-element.23.refs_0_), channel_id=1, source_target_pairs={{0,4},{1,5},{2,6},{3,7},{4,0},{5,1},{6,2},{7,3},{8,12},{9,13},{10,... | collective-permute-start | bytes 393224 | tf_op jit(solution)/shard_map/ppermute | solution.py:261
  51.5 6.6 %collective-permute-start.16 = (bf16[8,64,128]{2,1,0:T(8,128)(2,1)S(1)}, bf16[8,64,128]{2,1,0:T(8,128)(2,1)S(1)}, u32[]{:S(2)}, u32[]{:S(2)}) collective-permute-start(bf16[8,64,128]{2,1,0:T(8,128)(2,1)S(1)} %get-tuple-element.23.refs_0_), channel_id=1, source_target_pairs={{0,2},{1,3},{2,0},{3,1},{4,6},{5,7},{6,4},{7,5},{8,10},{9,11},{10,... | collective-permute-start | bytes 393224 | tf_op jit(solution)/shard_map/ppermute | solution.py:261
  51.6 7.3 %collective-permute-start.20 = (bf16[8,64,128]{2,1,0:T(8,128)(2,1)S(1)}, bf16[8,64,128]{2,1,0:T(8,128)(2,1)S(1)}, u32[]{:S(2)}, u32[]{:S(2)}) collective-permute-start(bf16[8,64,128]{2,1,0:T(8,128)(2,1)S(1)} %get-tuple-element.23.refs_0_), channel_id=1, source_target_pairs={{0,12},{1,13},{2,14},{3,15},{4,8},{5,9},{6,10},{7,11},{8,4},{9,5},... | collective-permute-start | bytes 393224 | tf_op jit(solution)/shard_map/ppermute | solution.py:261
  55.1 4.1 %collective-permute-start.21 = (bf16[8,64,128]{2,1,0:T(8,128)(2,1)S(1)}, bf16[8,64,128]{2,1,0:T(8,128)(2,1)S(1)}, u32[]{:S(2)}, u32[]{:S(2)}) collective-permute-start(bf16[8,64,128]{2,1,0:T(8,128)(2,1)S(1)} %collective-permute-done.18.refs_4_), channel_id=1, source_target_pairs={{0,2},{1,3},{2,0},{3,1},{4,6},{5,7},{6,4},{7,5},{8,10},{9,11},{10,... | collective-permute-start | bytes 393224 | tf_op jit(solution)/shard_map/ppermute | solution.py:261
  55.1 7.2 %collective-permute-start.15 = (bf16[8,64,128]{2,1,0:T(8,128)(2,1)S(1)}, bf16[8,64,128]{2,1,0:T(8,128)(2,1)S(1)}, u32[]{:S(2)}, u32[]{:S(2)}) collective-permute-start(bf16[8,64,128]{2,1,0:T(8,128)(2,1)S(1)} %get-tuple-element.23.refs_0_), channel_id=1, source_target_pairs={{0,1},{1,0},{2,3},{3,2},{4,5},{5,4},{6,7},{7,6},{8,9},{9,8},{10,11... | collective-permute-start | bytes 393224 | tf_op jit(solution)/shard_map/ppermute | solution.py:261
  58.1 4.4 %collective-permute-start.19 = (bf16[8,64,128]{2,1,0:T(8,128)(2,1)S(1)}, bf16[8,64,128]{2,1,0:T(8,128)(2,1)S(1)}, u32[]{:S(2)}, u32[]{:S(2)}) collective-permute-start(bf16[8,64,128]{2,1,0:T(8,128)(2,1)S(1)} %collective-permute-done.18.refs_4_), channel_id=1, source_target_pairs={{0,1},{1,0},{2,3},{3,2},{4,5},{5,4},{6,7},{7,6},{8,9},{9,8},{10,11... | collective-permute-start | bytes 393224 | tf_op jit(solution)/shard_map/ppermute | solution.py:261
  58.1 10.1 %collective-permute-start.17 = (bf16[8,64,128]{2,1,0:T(8,128)(2,1)S(1)}, bf16[8,64,128]{2,1,0:T(8,128)(2,1)S(1)}, u32[]{:S(2)}, u32[]{:S(2)}) collective-permute-start(bf16[8,64,128]{2,1,0:T(8,128)(2,1)S(1)} %collective-permute-done.16.refs_2_), channel_id=1, source_target_pairs={{0,1},{1,0},{2,3},{3,2},{4,5},{5,4},{6,7},{7,6},{8,9},{9,8},{10,11... | collective-permute-start | bytes 393224 | tf_op jit(solution)/shard_map/ppermute | solution.py:261
  59.2 9.1 %collective-permute-start.28 = (bf16[8,64,128]{2,1,0:T(8,128)(2,1)S(1)}, bf16[8,64,128]{2,1,0:T(8,128)(2,1)S(1)}, u32[]{:S(2)}, u32[]{:S(2)}) collective-permute-start(bf16[8,64,128]{2,1,0:T(8,128)(2,1)S(1)} %collective-permute-done.20.refs_12_), channel_id=1, source_target_pairs={{0,2},{1,3},{2,0},{3,1},{4,6},{5,7},{6,4},{7,5},{8,10},{9,11},{10,... | collective-permute-start | bytes 393224 | tf_op jit(solution)/shard_map/ppermute | solution.py:261
  60.4 8.3 %collective-permute-start.25 = (bf16[8,64,128]{2,1,0:T(8,128)(2,1)S(1)}, bf16[8,64,128]{2,1,0:T(8,128)(2,1)S(1)}, u32[]{:S(2)}, u32[]{:S(2)}) collective-permute-start(bf16[8,64,128]{2,1,0:T(8,128)(2,1)S(1)} %collective-permute-done.20.refs_12_), channel_id=1, source_target_pairs={{0,6},{1,7},{2,4},{3,5},{4,2},{5,3},{6,0},{7,1},{8,14},{9,15},{10,... | collective-permute-start | bytes 393224 | tf_op jit(solution)/shard_map/ppermute | solution.py:261
  62.3 8.7 %collective-permute-start.23 = (bf16[8,64,128]{2,1,0:T(8,128)(2,1)S(1)}, bf16[8,64,128]{2,1,0:T(8,128)(2,1)S(1)}, u32[]{:S(2)}, u32[]{:S(2)}) collective-permute-start(bf16[8,64,128]{2,1,0:T(8,128)(2,1)S(1)} %collective-permute-done.20.refs_12_), channel_id=1, source_target_pairs={{0,4},{1,5},{2,6},{3,7},{4,0},{5,1},{6,2},{7,3},{8,12},{9,13},{10,... | collective-permute-start | bytes 393224 | tf_op jit(solution)/shard_map/ppermute | solution.py:261
  62.5 10.6 %collective-permute-start.27 = (bf16[8,64,128]{2,1,0:T(8,128)(2,1)S(1)}, bf16[8,64,128]{2,1,0:T(8,128)(2,1)S(1)}, u32[]{:S(2)}, u32[]{:S(2)}) collective-permute-start(bf16[8,64,128]{2,1,0:T(8,128)(2,1)S(1)} %collective-permute-done.20.refs_12_), channel_id=1, source_target_pairs={{0,1},{1,0},{2,3},{3,2},{4,5},{5,4},{6,7},{7,6},{8,9},{9,8},{10,11... | collective-permute-start | bytes 393224 | tf_op jit(solution)/shard_map/ppermute | solution.py:261
  68.2 4.9 %collective-permute-start.22 = (bf16[8,64,128]{2,1,0:T(8,128)(2,1)S(1)}, bf16[8,64,128]{2,1,0:T(8,128)(2,1)S(1)}, u32[]{:S(2)}, u32[]{:S(2)}) collective-permute-start(bf16[8,64,128]{2,1,0:T(8,128)(2,1)S(1)} %collective-permute-done.21.refs_6_), channel_id=1, source_target_pairs={{0,1},{1,0},{2,3},{3,2},{4,5},{5,4},{6,7},{7,6},{8,9},{9,8},{10,11... | collective-permute-start | bytes 393224 | tf_op jit(solution)/shard_map/ppermute | solution.py:261
  68.3 4.8 %collective-permute-start.29 = (bf16[8,64,128]{2,1,0:T(8,128)(2,1)S(1)}, bf16[8,64,128]{2,1,0:T(8,128)(2,1)S(1)}, u32[]{:S(2)}, u32[]{:S(2)}) collective-permute-start(bf16[8,64,128]{2,1,0:T(8,128)(2,1)S(1)} %collective-permute-done.28.refs_14_), channel_id=1, source_target_pairs={{0,1},{1,0},{2,3},{3,2},{4,5},{5,4},{6,7},{7,6},{8,9},{9,8},{10,11... | collective-permute-start | bytes 393224 | tf_op jit(solution)/shard_map/ppermute | solution.py:261
  68.8 4.3 %collective-permute-start.26 = (bf16[8,64,128]{2,1,0:T(8,128)(2,1)S(1)}, bf16[8,64,128]{2,1,0:T(8,128)(2,1)S(1)}, u32[]{:S(2)}, u32[]{:S(2)}) collective-permute-start(bf16[8,64,128]{2,1,0:T(8,128)(2,1)S(1)} %collective-permute-done.25.refs_10_), channel_id=1, source_target_pairs={{0,1},{1,0},{2,3},{3,2},{4,5},{5,4},{6,7},{7,6},{8,9},{9,8},{10,11... | collective-permute-start | bytes 393224 | tf_op jit(solution)/shard_map/ppermute | solution.py:261
  71.0 3.0 %collective-permute-start.24 = (bf16[8,64,128]{2,1,0:T(8,128)(2,1)S(1)}, bf16[8,64,128]{2,1,0:T(8,128)(2,1)S(1)}, u32[]{:S(2)}, u32[]{:S(2)}) collective-permute-start(bf16[8,64,128]{2,1,0:T(8,128)(2,1)S(1)} %collective-permute-done.23.refs_8_), channel_id=1, source_target_pairs={{0,1},{1,0},{2,3},{3,2},{4,5},{5,4},{6,7},{7,6},{8,9},{9,8},{10,11... | collective-permute-start | bytes 393224 | tf_op jit(solution)/shard_map/ppermute | solution.py:261

commit v4 on v3

--- a/solution.py
+++ b/solution.py
@@ -11,13 +11,13 @@
 
 ITERS = 2
 FREQUENCY = 0.25
-SLOTS_AT_ONCE = 4
+SLOTS_AT_ONCE = 8
 ENTRIES = 16
 TILES = 8
 NT = (((1,), (1,)), ((), ()))
 VMEM = pl.BlockSpec(memory_space=pltpu.VMEM)
 SMEM = pl.BlockSpec(memory_space=pltpu.SMEM)
-ANY = pl.BlockSpec(memory_space=pl.ANY)
+HBM = pl.BlockSpec(memory_space=pltpu.HBM)
 
 
 def left_lanes(width):
@@ -29,7 +29,7 @@
     return jnp.concatenate([tile[:, width:], tile[:, :width]], axis=1)
 
 
-def start_kernel(count, occ, right, energy, right_out, denom_out, mask_out, solution_out, blocks_out, rows):
+def begin(count, occ, right, energy, rows):
     slots, width = energy.shape
     half = slots // 2
     lanes = 2 * width
@@ -53,26 +53,59 @@
         denom = jnp.where(left, first, second) + along - shift - FREQUENCY
         most = jnp.where(left, count[u], count[v])
         mask = jnp.where((row < most) & (column < most), 1.0, 0.0)
-        tile = jnp.where(left, rows[u * width : (u + 1) * width], rows[v * width : (v + 1) * width])
-        now = mask * tile / denom
+        yield u, jnp.where(left, rows[u * width : (u + 1) * width], rows[v * width : (v + 1) * width]), denom, mask
+
+
+def start_kernel(count, occ, right, energy, blocks_out, rows):
+    for u, tile, denom, mask in begin(count, occ, right, energy, rows):
+        blocks_out[u] = (mask * tile / denom).astype(jnp.bfloat16)
+
+
+def state_kernel(count, occ, twist, partners, slot_of, right, energy, right_out, denom_out, mask_out, solution_out, place_out, rows):
+    for u, tile, denom, mask in begin(count, occ, right, energy, rows):
         right_out[u] = tile
         denom_out[u] = denom
         mask_out[u] = mask
-        solution_out[u] = now
-        blocks_out[u] = now.astype(jnp.bfloat16)
+        solution_out[u] = mask * tile / denom
+    slots, entries = partners.shape
+    half = slots // 2
+
+    def places(s, carry):
+        for k in range(entries):
+            target = slot_of[partners[s, k]] ^ (twist[0] * slots)
+            slot = lax.rem(target, slots)
+            side = lax.div(slot, half)
+            tile = lax.div(target, slots) * half + slot - side * half
+            place_out[s, k] = 4 * tile + 2 * side + k % 2
+        return carry
+
+    lax.fori_loop(0, slots, places, 0)
 
 
 def start(right_side, pno_energy, occ_energy, pno_count):
+    slots, width = pno_energy.shape
+    return pl.pallas_call(
+        start_kernel,
+        in_specs=[SMEM, SMEM, VMEM, VMEM],
+        out_specs=VMEM,
+        out_shape=jax.ShapeDtypeStruct((slots // 2, width, 2 * width), jnp.bfloat16),
+        scratch_shapes=[pltpu.VMEM((slots * width, 2 * width), jnp.float32)],
+        name="start",
+    )(pno_count, occ_energy, right_side, pno_energy)
+
+
+def state(twist, partners, slot_of, right_side, pno_energy, occ_energy, pno_count):
     slots, width = pno_energy.shape
     tiles = jax.ShapeDtypeStruct((slots // 2, width, 2 * width), jnp.float32)
     return pl.pallas_call(
-        start_kernel,
-        in_specs=[SMEM, SMEM, VMEM, VMEM],
-        out_specs=[VMEM] * 5,
-        out_shape=[tiles] * 4 + [jax.ShapeDtypeStruct(tiles.shape, jnp.bfloat16)],
+        state_kernel,
+        in_specs=[SMEM] * 5 + [VMEM] * 2,
+        out_specs=[VMEM] * 4 + [SMEM],
+        out_shape=[tiles] * 4 + [jax.ShapeDtypeStruct(partners.shape, jnp.int32)],
         scratch_shapes=[pltpu.VMEM((slots * width, 2 * width), jnp.float32)],
-        name="start",
-    )(pno_count, occ_energy, right_side, pno_energy)
+        cost_estimate=pl.CostEstimate(flops=0, bytes_accessed=32 * right_side.size, transcendentals=0),
+        name="state",
+    )(pno_count, occ_energy, twist, partners, slot_of, right_side, pno_energy)
 
 
 def picker():
@@ -83,7 +116,7 @@
     return jnp.asarray(ones, jnp.bfloat16)
 
 
-def margin_kernel(pick, margins, tiles, held, arrived):
+def margin_kernel(pick, margins, tiles, held, made, arrived, left_for):
     width, lanes = tiles.shape[1:]
     steps, step = held.shape[:2]
     left = lax.broadcasted_iota(jnp.int32, (ENTRIES, lanes), 1) < width
@@ -91,6 +124,9 @@
 
     def fetch(i):
         return pltpu.make_async_copy(margins.at[pl.ds(i * step, step)], held.at[i], arrived.at[i])
+
+    def store(i):
+        return pltpu.make_async_copy(made.at[i], tiles.at[pl.ds(i * (step // 2), step // 2)], left_for.at[i])
 
     for i in range(steps):
         fetch(i).start()
@@ -116,12 +152,15 @@
                 for pair in range(ENTRIES // 2):
                     for side in range(2):
                         line = 2 * (n + side * TILES)
-                        tiles[i * (step // 2) + group * (ENTRIES // 2) + pair, line : line + 2 * TILES] = found[
+                        made[i, group * (ENTRIES // 2) + pair, line : line + 2 * TILES] = found[
                             pair * 2 * TILES : (pair + 1) * 2 * TILES, side * lanes : (side + 1) * lanes
                         ]
+        store(i).start()
         return carry
 
     lax.fori_loop(0, steps, some, 0)
+    for i in range(steps):
+        store(i).wait()
 
 
 def margin_tiles(margins, width):
@@ -130,69 +169,63 @@
     step = math.lcm(partners, ENTRIES)
     tiles = pl.pallas_call(
         margin_kernel,
-        in_specs=[VMEM, ANY],
-        out_specs=VMEM,
+        in_specs=[VMEM, HBM],
+        out_specs=HBM,
         out_shape=jax.ShapeDtypeStruct((entries // 2, width, 2 * width), jnp.bfloat16),
         scratch_shapes=[
             pltpu.VMEM((entries // step, step, flat), jnp.bfloat16),
+            pltpu.VMEM((entries // step, step // 2, width, 2 * width), jnp.bfloat16),
+            pltpu.SemaphoreType.DMA((entries // step,)),
             pltpu.SemaphoreType.DMA((entries // step,)),
         ],
         cost_estimate=pl.CostEstimate(flops=0, bytes_accessed=4 * margins.size, transcendentals=0),
-        compiler_params=pltpu.CompilerParams(vmem_limit_bytes=12 * 2**20),
+        compiler_params=pltpu.CompilerParams(vmem_limit_bytes=4 * margins.size + 2**20),
         name="margin_tiles",
     )(picker(), margins.reshape(entries, flat))
     return tiles.reshape(slots, partners // 2, width, 2 * width)
 
 
-def couple_kernel(last, pieces, twist, partners, slot_of, *refs):
+def couple_kernel(last, pieces, place, *refs):
     gathered, refs = refs[:pieces], refs[pieces:]
-    held, right, denom, mask, current = refs[:5]
+    margins, right, denom, mask, current = refs[:5]
     outs, refs = refs[5:7], refs[7:]
-    expanded, halves, coupled = refs[:3]
+    expanded, held, halves, coupled, arrived = refs[-5:]
     slots, pairs, width, lanes = held.shape
     half = slots // 2
 
+    def fetch(i):
+        some = pl.ds(i * SLOTS_AT_ONCE, SLOTS_AT_ONCE)
+        return pltpu.make_async_copy(margins.at[some], held.at[some], arrived.at[i])
+
+    for i in range(slots // SLOTS_AT_ONCE):
+        fetch(i).start()
+
     left = left_lanes(width)
-    right_half = jnp.logical_not(left)
-    base = 0
+    at = 0
     for piece in gathered:
-        held_devices = piece.shape[0] // half
-
-        def expand(i, carry, piece=piece, base=base):
+
+        def expand(i, at, piece=piece):
             tile = piece[i]
-            at = 2 * (base * half + i)
-            expanded[at] = tile
-            expanded[at + 1] = swap_halves(tile)
-            return carry
-
-        lax.fori_loop(0, piece.shape[0], expand, 0, unroll=4)
-        base += held_devices
-
-    turn = twist[0] * slots
-
-    def block(s, k):
-        target = slot_of[partners[s, k]] ^ turn
-        device, slot = target // slots, target % slots
-        side = jnp.where(slot >= half, 1, 0)
-        tile = expanded[2 * (device * half + slot - half * side) + (side ^ (k % 2))]
-        return jnp.where(left if k % 2 == 0 else right_half, tile, jnp.zeros_like(tile))
-
-    zero = jnp.zeros((lanes, lanes), jnp.bfloat16)
+            turned = swap_halves(tile)
+            zero = jnp.zeros_like(tile)
+            expanded[at] = jnp.where(left, tile, zero)
+            expanded[at + 1] = jnp.where(left, zero, turned)
+            expanded[at + 2] = jnp.where(left, turned, zero)
+            expanded[at + 3] = jnp.where(left, zero, tile)
+            return at + 4
+
+        at = lax.fori_loop(0, piece.shape[0], expand, at, unroll=half)
 
     def one_slot(s, at):
-        for q in range(pairs // 2):
-            upper = jnp.concatenate([block(s, 4 * q), block(s, 4 * q + 1)], axis=0)
-            lower = jnp.concatenate([block(s, 4 * q + 2), block(s, 4 * q + 3)], axis=0)
-            weights = jnp.concatenate(
-                [jnp.concatenate([upper, zero], axis=1), jnp.concatenate([zero, lower], axis=1)], axis=0
-            )
-            margin = jnp.concatenate([held[s, 2 * q], held[s, 2 * q + 1]], axis=1)
-            product = jnp.dot(margin, weights, preferred_element_type=jnp.float32)
-            halves[at, :, 2 * q * lanes : 2 * (q + 1) * lanes] = product.astype(jnp.bfloat16)
+        for k in range(pairs):
+            weights = jnp.concatenate([expanded[place[s, 2 * k]], expanded[place[s, 2 * k + 1]]], axis=0)
+            product = jnp.dot(held[s, k], weights, preferred_element_type=jnp.float32)
+            halves[at, :, k * lanes : (k + 1) * lanes] = product.astype(jnp.bfloat16)
         margin = jnp.concatenate([held[s, k] for k in range(pairs)], axis=1)
         coupled[s] = lax.dot_general(halves[at], margin, NT, preferred_element_type=jnp.float32)
 
     def some_slots(i, carry):
+        fetch(i).wait()
         for at in range(SLOTS_AT_ONCE):
             one_slot(i * SLOTS_AT_ONCE + at, at)
         return carry
@@ -200,7 +233,7 @@
     lax.fori_loop(0, slots // SLOTS_AT_ONCE, some_slots, 0)
 
     if last:
-        store = refs[3]
+        store = refs[0]
     for u in range(half):
         both = jnp.concatenate([coupled[u], coupled[u + half]], axis=1)
         before = current[u]
@@ -225,7 +258,7 @@
                 out[half:, j * lanes : (j + 1) * lanes] = jnp.where(keep, upper_turned, lower)
 
 
-def couple(last, twist, partners, slot_of, gathered, margins, right, denom, mask, current):
+def couple(last, place, gathered, margins, right, denom, mask, current):
     slots, pairs, width, lanes = margins.shape
     half = slots // 2
     devices = sum(piece.shape[0] for piece in gathered) // half
@@ -234,56 +267,65 @@
     blocks = jax.ShapeDtypeStruct((half, width, lanes), jnp.bfloat16)
     outs = [flat, flat] if last else [packed, blocks]
     scratch = [
-        pltpu.VMEM((devices * slots, width, lanes), jnp.bfloat16),
+        pltpu.VMEM((2 * devices * slots, width, lanes), jnp.bfloat16),
+        pltpu.VMEM((slots, pairs, width, lanes), jnp.bfloat16),
         pltpu.VMEM((SLOTS_AT_ONCE, width, pairs * lanes), jnp.bfloat16),
         pltpu.VMEM((slots, width, width), jnp.float32),
     ]
     if last:
-        scratch.append(pltpu.VMEM((4, half * width, lanes), jnp.float32))
+        scratch.insert(0, pltpu.VMEM((4, half * width, lanes), jnp.float32))
     operands = [*gathered, margins, right, denom, mask, current]
     size = sum(math.prod(x.shape) * x.dtype.itemsize for x in operands + outs + scratch)
+    scratch.append(pltpu.SemaphoreType.DMA((slots // SLOTS_AT_ONCE,)))
     return pl.pallas_call(
         functools.partial(couple_kernel, last, len(gathered)),
-        in_specs=[SMEM] * 3 + [VMEM] * len(operands),
+        in_specs=[SMEM] + [VMEM] * len(gathered) + [HBM] + [VMEM] * 4,
         out_specs=[VMEM] * len(outs),
         out_shape=outs,
         scratch_shapes=scratch,
         compiler_params=pltpu.CompilerParams(vmem_limit_bytes=size + 4 * 2**20),
         name="couple",
-    )(twist, partners, slot_of, *operands)
+    )(place, *operands)
 
 
 def gather(blocks, devices, meanwhile):
     if devices != 16:
-        return [lax.all_gather(blocks, "pair", axis=0, tiled=True)], jnp.zeros((1,), jnp.int32), meanwhile
+        return [lax.all_gather(blocks, "pair", axis=0, tiled=True)], meanwhile
 
     def swap(piece, other):
         return lax.ppermute(piece, "pair", [(i, i ^ other) for i in range(devices)])
 
+    first, second = meanwhile
     piece = {0: blocks}
     for other in (2, 4, 12):
         piece[other] = swap(blocks, other)
     piece[6] = swap(piece[4], 2)
-    piece[12], piece[6], meanwhile = lax.optimization_barrier((piece[12], piece[6], meanwhile))
+    piece[12], piece[6], first = lax.optimization_barrier((piece[12], piece[6], first))
     piece[8] = swap(piece[12], 4)
     piece[14] = swap(piece[12], 2)
     piece[10] = swap(piece[12], 6)
-    for other in (0, 2, 4, 12):
+    for other in (0, 2, 4, 12, 6):
         piece[other ^ 1] = swap(piece[other], 1)
-    for other in (6, 14, 8, 10):
+    piece[14], second = lax.optimization_barrier((piece[14], second))
+    for other in (14, 8, 10):
         piece[other ^ 1] = swap(piece[other], 1)
-    return [piece[i] for i in range(devices)], lax.axis_index("pair").astype(jnp.int32).reshape(1), meanwhile
+    return [piece[i] for i in range(devices)], (first, second)
 
 
 def shards(right_side, pno_energy, occ_energy, pno_count, margins, partners, slot_of):
     devices = lax.axis_size("pair")
-    right, denom, mask, current, blocks = start(right_side, pno_energy, occ_energy, pno_count)
+    twist = lax.axis_index("pair") if devices == 16 else 0
+    twist = jnp.full((1,), twist, jnp.int32)
+    blocks = start(right_side, pno_energy, occ_energy, pno_count)
     tiles = margin_tiles(margins, pno_energy.shape[1])
+    states = state(twist, partners, slot_of, right_side, pno_energy, occ_energy, pno_count)
     for step in range(ITERS):
-        gathered, twist, tiles = gather(blocks, devices, tiles)
-        outs = couple(step == ITERS - 1, twist, partners, slot_of, gathered, tiles, right, denom, mask, current)
+        gathered, (tiles, states) = gather(blocks, devices, (tiles, states))
+        right, denom, mask, current, place = states
+        outs = couple(step == ITERS - 1, place, gathered, tiles, right, denom, mask, current)
         if step < ITERS - 1:
             current, blocks = outs
+            states = right, denom, mask, current, place
     return tuple(outs)
 
 

time: 87.5 us -> 96.6 us (1.10)
  the two profiles are of different devices: /device:TPU:19 before, /device:TPU:25 now
where the time goes in v4:
time: 96.6 us; the launch traced here: 96.1 us
  Pallas kernels  33.2 us (34%)
  starting transfers between devices  28.9 us (30%)
  waiting for transfers between devices  20.6 us (21%)
  local copies, waits for them, and re-layouts  12.6 us (13%)
    ppermute x30, starting transfers between devices, swap(): return lax.ppermute(piece, 'pair', [(i, i ^ other) for i in range(devices)])  28.9 us
    ppermute x30, waiting for transfers between devices, swap(): return lax.ppermute(piece, 'pair', [(i, i ^ other) for i in range(devices)])  20.6 us
    pallas_call x2, Pallas kernels, couple(): pl.pallas_call(functools.partial(couple_kernel, last, len(gathered)), in_...  16.5 us
    unnamed x28, local copies, waits for them, and re-layouts  12.6 us
    pallas_call x1, Pallas kernels, state(): pl.pallas_call(state_kernel, in_specs=[SMEM] * 5 + [VMEM] * 2, out_specs=...  7.37 us
    pallas_call x1, Pallas kernels, margin_tiles(): pl.pallas_call(margin_kernel, in_specs=[VMEM, HBM], out_specs=HBM, out_sh...  7.23 us
    pallas_call x1, Pallas kernels, start(): pl.pallas_call(start_kernel, in_specs=[SMEM, SMEM, VMEM, VMEM], out_specs...  2.12 us
  transfers between devices with their start and end apart: 30, of which 11 were waited for; matrix products, arithmetic and copies ran while one was open for 0% of the time, Pallas kernels for 15%

profile of v4, /device:TPU:25, one launch (start us, length us, event | category | flops | bytes accessed | tf_op | source)
XLA Modules:
  0.0 96.1 jit_solution(16381950198533346953)
XLA Ops:
  0.6 2.1 %start.1.refs_0_ = bf16[8,64,128]{2,1,0:T(8,128)(2,1)} custom-call(s32[16]{0:T(128)} %count.3, f32[16]{0:T(128)} %occ.3, f32[16,4096]{1,0:T(8,128)} %right.3, f32[16,64]{1,0:T(8,128)} %energy.3), custom_call_target="tpu_custom_call" | custom-call | tf_op jit(solution)/shard_map/start/pallas_call | solution.py:87
  2.7 0.2 collective-permute-start.1
  2.9 1.1 %collective-permute-start = (bf16[8,64,128]{2,1,0:T(8,128)(2,1)}, bf16[8,64,128]{2,1,0:T(8,128)(2,1)S(1)}, u32[]{:S(2)}, u32[]{:S(2)}) collective-permute-start(bf16[8,64,128]{2,1,0:T(8,128)(2,1)} %start.1.refs_0_), channel_id=1, source_target_pairs={{0,12},{1,13},{2,14},{3,15},{4,8},{5,9},{6,10},{7,11},{8,4},{9,5},... | collective-permute-start | bytes 393224 | tf_op jit(solution)/shard_map/ppermute | solution.py:296
  4.0 3.3 %collective-permute-done.1.refs_4_ = bf16[8,64,128]{2,1,0:T(8,128)(2,1)S(1)} collective-permute-done((bf16[8,64,128]{2,1,0:T(8,128)(2,1)}, bf16[8,64,128]{2,1,0:T(8,128)(2,1)S(1)}, u32[]{:S(2)}, u32[]{:S(2)}) %collective-permute-start.1) | collective-permute-done | bytes 131104 | tf_op jit(solution)/shard_map/ppermute | solution.py:296
  7.3 1.2 %collective-permute-start.2 = (bf16[8,64,128]{2,1,0:T(8,128)(2,1)S(1)}, bf16[8,64,128]{2,1,0:T(8,128)(2,1)S(1)}, u32[]{:S(2)}, u32[]{:S(2)}) collective-permute-start(bf16[8,64,128]{2,1,0:T(8,128)(2,1)S(1)} %collective-permute-done.1.refs_4_), channel_id=1, source_target_pairs={{0,2},{1,3},{2,0},{3,1},{4,6},{5,7},{6,4},{7,5},{8,10},{9,11},{10,... | collective-permute-start | bytes 393224 | tf_op jit(solution)/shard_map/ppermute | solution.py:296
  8.6 0.2 collective-permute-start.5
  8.8 2.5 %copy-done.3 = bf16[16,40,4096]{2,1,0:T(8,128)(2,1)S(1)} copy-done((bf16[16,40,4096]{2,1,0:T(8,128)(2,1)S(1)}, bf16[16,40,4096]{2,1,0:T(8,128)(2,1)}, u32[]{:S(2)}) %copy-start.3) | copy-done | bytes 5242904
  11.3 0.8 copy-done.12
  12.1 7.2 %margin_tiles.1 = bf16[320,64,128]{2,1,0:T(8,128)(2,1)S(1)} custom-call(bf16[128,256]{1,0:T(8,128)(2,1)S(1)} %copy-done.12, bf16[640,4096]{1,0:T(8,128)(2,1)S(1)} %bitcast.5), custom_call_target="tpu_custom_call" | custom-call | bytes 10485760 | tf_op jit(solution)/shard_map/margin_tiles/pallas_call | solution.py:170
  19.4 2.3 %copy-done = bf16[320,64,128]{2,1,0:T(8,128)(2,1)} copy-done((bf16[320,64,128]{2,1,0:T(8,128)(2,1)}, bf16[320,64,128]{2,1,0:T(8,128)(2,1)S(1)}, u32[]{:S(2)}) %copy-start) | copy-done | bytes 5242904
  21.7 0.0 collective-permute-done.refs_12_
  21.7 0.0 collective-permute-done.2.refs_6_
  21.7 1.2 %collective-permute-start.3 = (bf16[8,64,128]{2,1,0:T(8,128)(2,1)S(1)}, bf16[8,64,128]{2,1,0:T(8,128)(2,1)S(1)}, u32[]{:S(2)}, u32[]{:S(2)}) collective-permute-start(bf16[8,64,128]{2,1,0:T(8,128)(2,1)S(1)} %collective-permute-done.refs_12_), channel_id=1, source_target_pairs={{0,2},{1,3},{2,0},{3,1},{4,6},{5,7},{6,4},{7,5},{8,10},{9,11},{10,... | collective-permute-start | bytes 393224 | tf_op jit(solution)/shard_map/ppermute | solution.py:296
  22.9 5.2 %collective-permute-start.4 = (bf16[8,64,128]{2,1,0:T(8,128)(2,1)S(1)}, bf16[8,64,128]{2,1,0:T(8,128)(2,1)S(1)}, u32[]{:S(2)}, u32[]{:S(2)}) collective-permute-start(bf16[8,64,128]{2,1,0:T(8,128)(2,1)S(1)} %copy-done.10), channel_id=1, source_target_pairs={{0,1},{1,0},{2,3},{3,2},{4,5},{5,4},{6,7},{7,6},{8,9},{9,8},{10,11... | collective-permute-start | bytes 393224 | tf_op jit(solution)/shard_map/ppermute | solution.py:296
  28.1 0.0 collective-permute-done.5.refs_2_
  28.1 0.1 collective-permute-start.6
  28.2 1.4 %collective-permute-start.9 = (bf16[8,64,128]{2,1,0:T(8,128)(2,1)S(1)}, bf16[8,64,128]{2,1,0:T(8,128)(2,1)S(1)}, u32[]{:S(2)}, u32[]{:S(2)}) collective-permute-start(bf16[8,64,128]{2,1,0:T(8,128)(2,1)S(1)} %collective-permute-done.refs_12_), channel_id=1, source_target_pairs={{0,4},{1,5},{2,6},{3,7},{4,0},{5,1},{6,2},{7,3},{8,12},{9,13},{10,... | collective-permute-start | bytes 393224 | tf_op jit(solution)/shard_map/ppermute | solution.py:296
  29.6 3.1 %collective-permute-start.7 = (bf16[8,64,128]{2,1,0:T(8,128)(2,1)S(1)}, bf16[8,64,128]{2,1,0:T(8,128)(2,1)S(1)}, u32[]{:S(2)}, u32[]{:S(2)}) collective-permute-start(bf16[8,64,128]{2,1,0:T(8,128)(2,1)S(1)} %collective-permute-done.1.refs_4_), channel_id=1, source_target_pairs={{0,1},{1,0},{2,3},{3,2},{4,5},{5,4},{6,7},{7,6},{8,9},{9,8},{10,11... | collective-permute-start | bytes 393224 | tf_op jit(solution)/shard_map/ppermute | solution.py:296
  32.7 7.4 %state.1 = (f32[8,64,128]{2,1,0:T(8,128)}, f32[8,64,128]{2,1,0:T(8,128)}, f32[8,64,128]{2,1,0:T(8,128)}, f32[8,64,128]{2,1,0:T(8,128)}, s32[16,40]{1,0:T(8,128)}) custom-call(s32[16]{0:T(128)} %count.3, f32[16]{0:T(128)} %occ.3, s32[1]{0:T(128)} %bitcast.2.twist, s32[16,40]{1,0:T(8,128)} %partners.1, s32[256]{0:T(256)} %slot_of.1, f32[16,4096]{1,0:T(8,128)} %right.3, ...), custom_call_target="tpu_custom_call" | custom-call | bytes 2097152 | tf_op jit(solution)/shard_map/state/pallas_call | solution.py:100
  40.1 0.1 collective-permute-start.13
  40.2 0.0 collective-permute-done.6.refs_3_
  40.2 0.5 collective-permute-start.8
  40.7 0.1 collective-permute-start.12
  40.8 0.4 collective-permute-start.10
  41.2 0.0 collective-permute-done.7.refs_5_
  41.2 0.1 collective-permute-start.14
  41.3 0.4 collective-permute-done.8.refs_7_
  41.7 0.3 collective-permute-done.12.refs_11_
  42.0 0.2 collective-permute-done.10.refs_9_
  42.2 0.3 collective-permute-done.14.refs_15_
  42.5 2.5 %copy-done.1 = bf16[320,64,128]{2,1,0:T(8,128)(2,1)S(1)} copy-done((bf16[320,64,128]{2,1,0:T(8,128)(2,1)S(1)}, bf16[320,64,128]{2,1,0:T(8,128)(2,1)}, u32[]{:S(2)}) %copy-start.1) | copy-done | bytes 5242904
  45.0 0.9 copy-done.4
  46.0 0.9 copy-done.6
  46.9 0.9 copy-done.8
  47.9 0.9 copy-done.11
  48.8 0.7 copy-done.13
  49.5 7.3 %couple.2 = (f32[8,64,128]{2,1,0:T(8,128)S(1)}, bf16[8,64,128]{2,1,0:T(8,128)(2,1)S(1)}) custom-call(s32[16,40]{1,0:T(8,128)S(1)} %copy-done.13, bf16[8,64,128]{2,1,0:T(8,128)(2,1)S(1)} %copy-done.10, bf16[8,64,128]{2,1,0:T(8,128)(2,1)S(1)} %collective-permute-done.4.refs_1_, bf16[8,64,128]{2,1,0:T(8,128)(2,1)S(1)} %collective-permute-done.5.refs_2_, ...), custom_call_target="tpu_custom_call" | custom-call | tf_op jit(solution)/shard_map/couple/pallas_call | solution.py:280
  56.9 0.1 collective-permute-start.16
  57.0 0.1 collective-permute-start.15
  57.1 7.6 %collective-permute-done.16.refs_4_ = bf16[8,64,128]{2,1,0:T(8,128)(2,1)S(1)} collective-permute-done((bf16[8,64,128]{2,1,0:T(8,128)(2,1)S(1)}, bf16[8,64,128]{2,1,0:T(8,128)(2,1)S(1)}, u32[]{:S(2)}, u32[]{:S(2)}) %collective-permute-start.16) | collective-permute-done | bytes 131104 | tf_op jit(solution)/shard_map/ppermute | solution.py:296
  64.7 2.3 %collective-permute-start.17 = (bf16[8,64,128]{2,1,0:T(8,128)(2,1)S(1)}, bf16[8,64,128]{2,1,0:T(8,128)(2,1)S(1)}, u32[]{:S(2)}, u32[]{:S(2)}) collective-permute-start(bf16[8,64,128]{2,1,0:T(8,128)(2,1)S(1)} %collective-permute-done.16.refs_4_), channel_id=1, source_target_pairs={{0,2},{1,3},{2,0},{3,1},{4,6},{5,7},{6,4},{7,5},{8,10},{9,11},{10,... | collective-permute-start | bytes 393224 | tf_op jit(solution)/shard_map/ppermute | solution.py:296
  67.0 0.0 collective-permute-start.20
  67.1 0.0 collective-permute-done.15.refs_12_
  67.1 2.8 %collective-permute-done.17.refs_6_ = bf16[8,64,128]{2,1,0:T(8,128)(2,1)S(1)} collective-permute-done((bf16[8,64,128]{2,1,0:T(8,128)(2,1)S(1)}, bf16[8,64,128]{2,1,0:T(8,128)(2,1)S(1)}, u32[]{:S(2)}, u32[]{:S(2)}) %collective-permute-start.17) | collective-permute-done | bytes 131104 | tf_op jit(solution)/shard_map/ppermute | solution.py:296
  69.9 1.0 collective-permute-start.18
  70.9 3.9 %collective-permute-start.19 = (bf16[8,64,128]{2,1,0:T(8,128)(2,1)S(1)}, bf16[8,64,128]{2,1,0:T(8,128)(2,1)S(1)}, u32[]{:S(2)}, u32[]{:S(2)}) collective-permute-start(bf16[8,64,128]{2,1,0:T(8,128)(2,1)S(1)} %get-tuple-element.41.refs_0_), channel_id=1, source_target_pairs={{0,1},{1,0},{2,3},{3,2},{4,5},{5,4},{6,7},{7,6},{8,9},{9,8},{10,11... | collective-permute-start | bytes 393224 | tf_op jit(solution)/shard_map/ppermute | solution.py:296
  74.7 0.0 collective-permute-done.20.refs_2_
  74.7 0.7 collective-permute-start.21
  75.5 2.9 %collective-permute-start.24 = (bf16[8,64,128]{2,1,0:T(8,128)(2,1)S(1)}, bf16[8,64,128]{2,1,0:T(8,128)(2,1)S(1)}, u32[]{:S(2)}, u32[]{:S(2)}) collective-permute-start(bf16[8,64,128]{2,1,0:T(8,128)(2,1)S(1)} %collective-permute-done.15.refs_12_), channel_id=1, source_target_pairs={{0,4},{1,5},{2,6},{3,7},{4,0},{5,1},{6,2},{7,3},{8,12},{9,13},{10,... | collective-permute-start | bytes 393224 | tf_op jit(solution)/shard_map/ppermute | solution.py:296
  78.3 0.6 collective-permute-start.22
  78.9 0.0 collective-permute-done.19.refs_1_
  78.9 0.1 collective-permute-start.28
  79.0 0.0 collective-permute-done.21.refs_3_
  79.0 0.4 collective-permute-start.23
  79.4 2.1 %collective-permute-done.26.refs_10_ = bf16[8,64,128]{2,1,0:T(8,128)(2,1)S(1)} collective-permute-done((bf16[8,64,128]{2,1,0:T(8,128)(2,1)S(1)}, bf16[8,64,128]{2,1,0:T(8,128)(2,1)S(1)}, u32[]{:S(2)}, u32[]{:S(2)}) %collective-permute-start.26) | collective-permute-done | bytes 131104 | tf_op jit(solution)/shard_map/ppermute | solution.py:296
  81.5 1.2 %collective-permute-start.27 = (bf16[8,64,128]{2,1,0:T(8,128)(2,1)S(1)}, bf16[8,64,128]{2,1,0:T(8,128)(2,1)S(1)}, u32[]{:S(2)}, u32[]{:S(2)}) collective-permute-start(bf16[8,64,128]{2,1,0:T(8,128)(2,1)S(1)} %collective-permute-done.26.refs_10_), channel_id=1, source_target_pairs={{0,1},{1,0},{2,3},{3,2},{4,5},{5,4},{6,7},{7,6},{8,9},{9,8},{10,11... | collective-permute-start | bytes 393224 | tf_op jit(solution)/shard_map/ppermute | solution.py:296
  82.7 2.1 %collective-permute-done.24.refs_8_ = bf16[8,64,128]{2,1,0:T(8,128)(2,1)S(1)} collective-permute-done((bf16[8,64,128]{2,1,0:T(8,128)(2,1)S(1)}, bf16[8,64,128]{2,1,0:T(8,128)(2,1)S(1)}, u32[]{:S(2)}, u32[]{:S(2)}) %collective-permute-start.24) | collective-permute-done | bytes 131104 | tf_op jit(solution)/shard_map/ppermute | solution.py:296
  84.8 0.8 collective-permute-start.25
  85.6 0.0 collective-permute-start.29
  85.6 0.0 collective-permute-done.28.refs_13_
  85.6 0.0 collective-permute-done.27.refs_11_
  85.6 1.0 collective-permute-done.25.refs_9_
  86.6 0.4 collective-permute-done.29.refs_15_
  87.0 9.2 %couple.3 = (f32[16,4096]{1,0:T(8,128)}, f32[16,4096]{1,0:T(8,128)}) custom-call(s32[16,40]{1,0:T(8,128)S(1)} %copy-done.13, bf16[8,64,128]{2,1,0:T(8,128)(2,1)S(1)} %get-tuple-element.41.refs_0_, bf16[8,64,128]{2,1,0:T(8,128)(2,1)S(1)} %collective-permute-done.19.refs_1_, bf16[8,64,128]{2,1,0:T(8,128)(2,1)S(1)} %collective-permute-done.20.refs_2_, ...), custom_call_target="tpu_custom_call" | custom-call | tf_op jit(solution)/shard_map/couple/pallas_call | solution.py:280
  (29 shorter events, 0.1 us)
Async XLA Ops:
  2.7 4.6 %collective-permute-start.1 = (bf16[8,64,128]{2,1,0:T(8,128)(2,1)}, bf16[8,64,128]{2,1,0:T(8,128)(2,1)S(1)}, u32[]{:S(2)}, u32[]{:S(2)}) collective-permute-start(bf16[8,64,128]{2,1,0:T(8,128)(2,1)} %start.1.refs_0_), channel_id=1, source_target_pairs={{0,4},{1,5},{2,6},{3,7},{4,0},{5,1},{6,2},{7,3},{8,12},{9,13},{10,... | collective-permute-start | bytes 393224 | tf_op jit(solution)/shard_map/ppermute | solution.py:296
  2.9 18.8 %collective-permute-start = (bf16[8,64,128]{2,1,0:T(8,128)(2,1)}, bf16[8,64,128]{2,1,0:T(8,128)(2,1)S(1)}, u32[]{:S(2)}, u32[]{:S(2)}) collective-permute-start(bf16[8,64,128]{2,1,0:T(8,128)(2,1)} %start.1.refs_0_), channel_id=1, source_target_pairs={{0,12},{1,13},{2,14},{3,15},{4,8},{5,9},{6,10},{7,11},{8,4},{9,5},... | collective-permute-start | bytes 393224 | tf_op jit(solution)/shard_map/ppermute | solution.py:296
  7.3 14.4 %collective-permute-start.2 = (bf16[8,64,128]{2,1,0:T(8,128)(2,1)S(1)}, bf16[8,64,128]{2,1,0:T(8,128)(2,1)S(1)}, u32[]{:S(2)}, u32[]{:S(2)}) collective-permute-start(bf16[8,64,128]{2,1,0:T(8,128)(2,1)S(1)} %collective-permute-done.1.refs_4_), channel_id=1, source_target_pairs={{0,2},{1,3},{2,0},{3,1},{4,6},{5,7},{6,4},{7,5},{8,10},{9,11},{10,... | collective-permute-start | bytes 393224 | tf_op jit(solution)/shard_map/ppermute | solution.py:296
  8.6 19.6 %collective-permute-start.5 = (bf16[8,64,128]{2,1,0:T(8,128)(2,1)}, bf16[8,64,128]{2,1,0:T(8,128)(2,1)S(1)}, u32[]{:S(2)}, u32[]{:S(2)}) collective-permute-start(bf16[8,64,128]{2,1,0:T(8,128)(2,1)} %start.1.refs_0_), channel_id=1, source_target_pairs={{0,2},{1,3},{2,0},{3,1},{4,6},{5,7},{6,4},{7,5},{8,10},{9,11},{10,... | collective-permute-start | bytes 393224 | tf_op jit(solution)/shard_map/ppermute | solution.py:296
  8.8 2.5 %copy-start.3 = (bf16[16,40,4096]{2,1,0:T(8,128)(2,1)S(1)}, bf16[16,40,4096]{2,1,0:T(8,128)(2,1)}, u32[]{:S(2)}) copy-start(bf16[16,40,4096]{2,1,0:T(8,128)(2,1)} %param.12) | copy-start | bytes 15728644
  11.3 0.8 copy-start.12
  12.1 10.8 %copy-start.10 = (bf16[8,64,128]{2,1,0:T(8,128)(2,1)S(1)}, bf16[8,64,128]{2,1,0:T(8,128)(2,1)}, u32[]{:S(2)}) copy-start(bf16[8,64,128]{2,1,0:T(8,128)(2,1)} %start.1.refs_0_) | copy-start | bytes 393220
  19.4 2.3 %copy-start = (bf16[320,64,128]{2,1,0:T(8,128)(2,1)}, bf16[320,64,128]{2,1,0:T(8,128)(2,1)S(1)}, u32[]{:S(2)}) copy-start(bf16[320,64,128]{2,1,0:T(8,128)(2,1)S(1)} %margin_tiles.1) | copy-start | bytes 15728644
  21.7 7.9 %collective-permute-start.3 = (bf16[8,64,128]{2,1,0:T(8,128)(2,1)S(1)}, bf16[8,64,128]{2,1,0:T(8,128)(2,1)S(1)}, u32[]{:S(2)}, u32[]{:S(2)}) collective-permute-start(bf16[8,64,128]{2,1,0:T(8,128)(2,1)S(1)} %collective-permute-done.refs_12_), channel_id=1, source_target_pairs={{0,2},{1,3},{2,0},{3,1},{4,6},{5,7},{6,4},{7,5},{8,10},{9,11},{10,... | collective-permute-start | bytes 393224 | tf_op jit(solution)/shard_map/ppermute | solution.py:296
  22.9 17.2 %collective-permute-start.4 = (bf16[8,64,128]{2,1,0:T(8,128)(2,1)S(1)}, bf16[8,64,128]{2,1,0:T(8,128)(2,1)S(1)}, u32[]{:S(2)}, u32[]{:S(2)}) collective-permute-start(bf16[8,64,128]{2,1,0:T(8,128)(2,1)S(1)} %copy-done.10), channel_id=1, source_target_pairs={{0,1},{1,0},{2,3},{3,2},{4,5},{5,4},{6,7},{7,6},{8,9},{9,8},{10,11... | collective-permute-start | bytes 393224 | tf_op jit(solution)/shard_map/ppermute | solution.py:296
  28.1 12.1 %collective-permute-start.6 = (bf16[8,64,128]{2,1,0:T(8,128)(2,1)S(1)}, bf16[8,64,128]{2,1,0:T(8,128)(2,1)S(1)}, u32[]{:S(2)}, u32[]{:S(2)}) collective-permute-start(bf16[8,64,128]{2,1,0:T(8,128)(2,1)S(1)} %collective-permute-done.5.refs_2_), channel_id=1, source_target_pairs={{0,1},{1,0},{2,3},{3,2},{4,5},{5,4},{6,7},{7,6},{8,9},{9,8},{10,11... | collective-permute-start | bytes 393224 | tf_op jit(solution)/shard_map/ppermute | solution.py:296
  28.2 12.5 %collective-permute-start.11 = (bf16[8,64,128]{2,1,0:T(8,128)(2,1)S(1)}, bf16[8,64,128]{2,1,0:T(8,128)(2,1)S(1)}, u32[]{:S(2)}, u32[]{:S(2)}) collective-permute-start(bf16[8,64,128]{2,1,0:T(8,128)(2,1)S(1)} %collective-permute-done.refs_12_), channel_id=1, source_target_pairs={{0,6},{1,7},{2,4},{3,5},{4,2},{5,3},{6,0},{7,1},{8,14},{9,15},{10,... | collective-permute-start | bytes 393224 | tf_op jit(solution)/shard_map/ppermute | solution.py:296
  28.2 12.6 %collective-permute-start.9 = (bf16[8,64,128]{2,1,0:T(8,128)(2,1)S(1)}, bf16[8,64,128]{2,1,0:T(8,128)(2,1)S(1)}, u32[]{:S(2)}, u32[]{:S(2)}) collective-permute-start(bf16[8,64,128]{2,1,0:T(8,128)(2,1)S(1)} %collective-permute-done.refs_12_), channel_id=1, source_target_pairs={{0,4},{1,5},{2,6},{3,7},{4,0},{5,1},{6,2},{7,3},{8,12},{9,13},{10,... | collective-permute-start | bytes 393224 | tf_op jit(solution)/shard_map/ppermute | solution.py:296
  29.6 11.6 %collective-permute-start.7 = (bf16[8,64,128]{2,1,0:T(8,128)(2,1)S(1)}, bf16[8,64,128]{2,1,0:T(8,128)(2,1)S(1)}, u32[]{:S(2)}, u32[]{:S(2)}) collective-permute-start(bf16[8,64,128]{2,1,0:T(8,128)(2,1)S(1)} %collective-permute-done.1.refs_4_), channel_id=1, source_target_pairs={{0,1},{1,0},{2,3},{3,2},{4,5},{5,4},{6,7},{7,6},{8,9},{9,8},{10,11... | collective-permute-start | bytes 393224 | tf_op jit(solution)/shard_map/ppermute | solution.py:296
  40.1 1.6 %collective-permute-start.13 = (bf16[8,64,128]{2,1,0:T(8,128)(2,1)S(1)}, bf16[8,64,128]{2,1,0:T(8,128)(2,1)S(1)}, u32[]{:S(2)}, u32[]{:S(2)}) collective-permute-start(bf16[8,64,128]{2,1,0:T(8,128)(2,1)S(1)} %collective-permute-done.refs_12_), channel_id=1, source_target_pairs={{0,1},{1,0},{2,3},{3,2},{4,5},{5,4},{6,7},{7,6},{8,9},{9,8},{10,11... | collective-permute-start | bytes 393224 | tf_op jit(solution)/shard_map/ppermute | solution.py:296
  40.2 1.5 %collective-permute-start.8 = (bf16[8,64,128]{2,1,0:T(8,128)(2,1)S(1)}, bf16[8,64,128]{2,1,0:T(8,128)(2,1)S(1)}, u32[]{:S(2)}, u32[]{:S(2)}) collective-permute-start(bf16[8,64,128]{2,1,0:T(8,128)(2,1)S(1)} %collective-permute-done.2.refs_6_), channel_id=1, source_target_pairs={{0,1},{1,0},{2,3},{3,2},{4,5},{5,4},{6,7},{7,6},{8,9},{9,8},{10,11... | collective-permute-start | bytes 393224 | tf_op jit(solution)/shard_map/ppermute | solution.py:296
  40.7 1.3 %collective-permute-start.12 = (bf16[8,64,128]{2,1,0:T(8,128)(2,1)S(1)}, bf16[8,64,128]{2,1,0:T(8,128)(2,1)S(1)}, u32[]{:S(2)}, u32[]{:S(2)}) collective-permute-start(bf16[8,64,128]{2,1,0:T(8,128)(2,1)S(1)} %collective-permute-done.11.refs_10_), channel_id=1, source_target_pairs={{0,1},{1,0},{2,3},{3,2},{4,5},{5,4},{6,7},{7,6},{8,9},{9,8},{10,11... | collective-permute-start | bytes 393224 | tf_op jit(solution)/shard_map/ppermute | solution.py:296
  40.8 1.4 %collective-permute-start.10 = (bf16[8,64,128]{2,1,0:T(8,128)(2,1)S(1)}, bf16[8,64,128]{2,1,0:T(8,128)(2,1)S(1)}, u32[]{:S(2)}, u32[]{:S(2)}) collective-permute-start(bf16[8,64,128]{2,1,0:T(8,128)(2,1)S(1)} %collective-permute-done.9.refs_8_), channel_id=1, source_target_pairs={{0,1},{1,0},{2,3},{3,2},{4,5},{5,4},{6,7},{7,6},{8,9},{9,8},{10,11... | collective-permute-start | bytes 393224 | tf_op jit(solution)/shard_map/ppermute | solution.py:296
  41.2 1.3 %collective-permute-start.14 = (bf16[8,64,128]{2,1,0:T(8,128)(2,1)S(1)}, bf16[8,64,128]{2,1,0:T(8,128)(2,1)S(1)}, u32[]{:S(2)}, u32[]{:S(2)}) collective-permute-start(bf16[8,64,128]{2,1,0:T(8,128)(2,1)S(1)} %collective-permute-done.3.refs_14_), channel_id=1, source_target_pairs={{0,1},{1,0},{2,3},{3,2},{4,5},{5,4},{6,7},{7,6},{8,9},{9,8},{10,11... | collective-permute-start | bytes 393224 | tf_op jit(solution)/shard_map/ppermute | solution.py:296
  42.5 2.5 %copy-start.1 = (bf16[320,64,128]{2,1,0:T(8,128)(2,1)S(1)}, bf16[320,64,128]{2,1,0:T(8,128)(2,1)}, u32[]{:S(2)}) copy-start(bf16[320,64,128]{2,1,0:T(8,128)(2,1)} %copy-done) | copy-start | bytes 15728644
  45.0 0.9 copy-start.4
  46.0 0.9 copy-start.6
  46.9 0.9 copy-start.8
  47.9 0.9 copy-start.11
  48.8 0.7 copy-start.13
  49.5 37.4 %copy-start.2 = (bf16[320,64,128]{2,1,0:T(8,128)(2,1)S(1)}, bf16[320,64,128]{2,1,0:T(8,128)(2,1)}, u32[]{:S(2)}) copy-start(bf16[320,64,128]{2,1,0:T(8,128)(2,1)} %copy-done) | copy-start | bytes 15728644
  49.5 37.4 %copy-start.5 = (f32[8,64,128]{2,1,0:T(8,128)S(1)}, f32[8,64,128]{2,1,0:T(8,128)}, u32[]{:S(2)}) copy-start(f32[8,64,128]{2,1,0:T(8,128)} %get-tuple-element.48.refs_17_) | copy-start | bytes 786436
  49.5 37.4 %copy-start.7 = (f32[8,64,128]{2,1,0:T(8,128)S(1)}, f32[8,64,128]{2,1,0:T(8,128)}, u32[]{:S(2)}) copy-start(f32[8,64,128]{2,1,0:T(8,128)} %get-tuple-element.49.refs_18_) | copy-start | bytes 786436
  49.5 37.4 %copy-start.9 = (f32[8,64,128]{2,1,0:T(8,128)S(1)}, f32[8,64,128]{2,1,0:T(8,128)}, u32[]{:S(2)}) copy-start(f32[8,64,128]{2,1,0:T(8,128)} %get-tuple-element.50.refs_19_) | copy-start | bytes 786436
  56.9 7.8 %collective-permute-start.16 = (bf16[8,64,128]{2,1,0:T(8,128)(2,1)S(1)}, bf16[8,64,128]{2,1,0:T(8,128)(2,1)S(1)}, u32[]{:S(2)}, u32[]{:S(2)}) collective-permute-start(bf16[8,64,128]{2,1,0:T(8,128)(2,1)S(1)} %get-tuple-element.41.refs_0_), channel_id=1, source_target_pairs={{0,4},{1,5},{2,6},{3,7},{4,0},{5,1},{6,2},{7,3},{8,12},{9,13},{10,... | collective-permute-start | bytes 393224 | tf_op jit(solution)/shard_map/ppermute | solution.py:296
  57.0 10.1 %collective-permute-start.15 = (bf16[8,64,128]{2,1,0:T(8,128)(2,1)S(1)}, bf16[8,64,128]{2,1,0:T(8,128)(2,1)S(1)}, u32[]{:S(2)}, u32[]{:S(2)}) collective-permute-start(bf16[8,64,128]{2,1,0:T(8,128)(2,1)S(1)} %get-tuple-element.41.refs_0_), channel_id=1, source_target_pairs={{0,12},{1,13},{2,14},{3,15},{4,8},{5,9},{6,10},{7,11},{8,4},{9,5},... | collective-permute-start | bytes 393224 | tf_op jit(solution)/shard_map/ppermute | solution.py:296
  64.7 5.2 %collective-permute-start.17 = (bf16[8,64,128]{2,1,0:T(8,128)(2,1)S(1)}, bf16[8,64,128]{2,1,0:T(8,128)(2,1)S(1)}, u32[]{:S(2)}, u32[]{:S(2)}) collective-permute-start(bf16[8,64,128]{2,1,0:T(8,128)(2,1)S(1)} %collective-permute-done.16.refs_4_), channel_id=1, source_target_pairs={{0,2},{1,3},{2,0},{3,1},{4,6},{5,7},{6,4},{7,5},{8,10},{9,11},{10,... | collective-permute-start | bytes 393224 | tf_op jit(solution)/shard_map/ppermute | solution.py:296
  67.0 7.7 %collective-permute-start.20 = (bf16[8,64,128]{2,1,0:T(8,128)(2,1)S(1)}, bf16[8,64,128]{2,1,0:T(8,128)(2,1)S(1)}, u32[]{:S(2)}, u32[]{:S(2)}) collective-permute-start(bf16[8,64,128]{2,1,0:T(8,128)(2,1)S(1)} %get-tuple-element.41.refs_0_), channel_id=1, source_target_pairs={{0,2},{1,3},{2,0},{3,1},{4,6},{5,7},{6,4},{7,5},{8,10},{9,11},{10,... | collective-permute-start | bytes 393224 | tf_op jit(solution)/shard_map/ppermute | solution.py:296
  69.9 8.5 %collective-permute-start.18 = (bf16[8,64,128]{2,1,0:T(8,128)(2,1)S(1)}, bf16[8,64,128]{2,1,0:T(8,128)(2,1)S(1)}, u32[]{:S(2)}, u32[]{:S(2)}) collective-permute-start(bf16[8,64,128]{2,1,0:T(8,128)(2,1)S(1)} %collective-permute-done.15.refs_12_), channel_id=1, source_target_pairs={{0,2},{1,3},{2,0},{3,1},{4,6},{5,7},{6,4},{7,5},{8,10},{9,11},{10,... | collective-permute-start | bytes 393224 | tf_op jit(solution)/shard_map/ppermute | solution.py:296
  70.9 8.1 %collective-permute-start.19 = (bf16[8,64,128]{2,1,0:T(8,128)(2,1)S(1)}, bf16[8,64,128]{2,1,0:T(8,128)(2,1)S(1)}, u32[]{:S(2)}, u32[]{:S(2)}) collective-permute-start(bf16[8,64,128]{2,1,0:T(8,128)(2,1)S(1)} %get-tuple-element.41.refs_0_), channel_id=1, source_target_pairs={{0,1},{1,0},{2,3},{3,2},{4,5},{5,4},{6,7},{7,6},{8,9},{9,8},{10,11... | collective-permute-start | bytes 393224 | tf_op jit(solution)/shard_map/ppermute | solution.py:296
  74.7 4.2 %collective-permute-start.21 = (bf16[8,64,128]{2,1,0:T(8,128)(2,1)S(1)}, bf16[8,64,128]{2,1,0:T(8,128)(2,1)S(1)}, u32[]{:S(2)}, u32[]{:S(2)}) collective-permute-start(bf16[8,64,128]{2,1,0:T(8,128)(2,1)S(1)} %collective-permute-done.20.refs_2_), channel_id=1, source_target_pairs={{0,1},{1,0},{2,3},{3,2},{4,5},{5,4},{6,7},{7,6},{8,9},{9,8},{10,11... | collective-permute-start | bytes 393224 | tf_op jit(solution)/shard_map/ppermute | solution.py:296
  75.5 6.0 %collective-permute-start.26 = (bf16[8,64,128]{2,1,0:T(8,128)(2,1)S(1)}, bf16[8,64,128]{2,1,0:T(8,128)(2,1)S(1)}, u32[]{:S(2)}, u32[]{:S(2)}) collective-permute-start(bf16[8,64,128]{2,1,0:T(8,128)(2,1)S(1)} %collective-permute-done.15.refs_12_), channel_id=1, source_target_pairs={{0,6},{1,7},{2,4},{3,5},{4,2},{5,3},{6,0},{7,1},{8,14},{9,15},{10,... | collective-permute-start | bytes 393224 | tf_op jit(solution)/shard_map/ppermute | solution.py:296
  75.5 9.3 %collective-permute-start.24 = (bf16[8,64,128]{2,1,0:T(8,128)(2,1)S(1)}, bf16[8,64,128]{2,1,0:T(8,128)(2,1)S(1)}, u32[]{:S(2)}, u32[]{:S(2)}) collective-permute-start(bf16[8,64,128]{2,1,0:T(8,128)(2,1)S(1)} %collective-permute-done.15.refs_12_), channel_id=1, source_target_pairs={{0,4},{1,5},{2,6},{3,7},{4,0},{5,1},{6,2},{7,3},{8,12},{9,13},{10,... | collective-permute-start | bytes 393224 | tf_op jit(solution)/shard_map/ppermute | solution.py:296
  78.3 7.3 %collective-permute-start.22 = (bf16[8,64,128]{2,1,0:T(8,128)(2,1)S(1)}, bf16[8,64,128]{2,1,0:T(8,128)(2,1)S(1)}, u32[]{:S(2)}, u32[]{:S(2)}) collective-permute-start(bf16[8,64,128]{2,1,0:T(8,128)(2,1)S(1)} %collective-permute-done.16.refs_4_), channel_id=1, source_target_pairs={{0,1},{1,0},{2,3},{3,2},{4,5},{5,4},{6,7},{7,6},{8,9},{9,8},{10,11... | collective-permute-start | bytes 393224 | tf_op jit(solution)/shard_map/ppermute | solution.py:296
  78.9 6.7 %collective-permute-start.28 = (bf16[8,64,128]{2,1,0:T(8,128)(2,1)S(1)}, bf16[8,64,128]{2,1,0:T(8,128)(2,1)S(1)}, u32[]{:S(2)}, u32[]{:S(2)}) collective-permute-start(bf16[8,64,128]{2,1,0:T(8,128)(2,1)S(1)} %collective-permute-done.15.refs_12_), channel_id=1, source_target_pairs={{0,1},{1,0},{2,3},{3,2},{4,5},{5,4},{6,7},{7,6},{8,9},{9,8},{10,11... | collective-permute-start | bytes 393224 | tf_op jit(solution)/shard_map/ppermute | solution.py:296
  79.0 6.6 %collective-permute-start.23 = (bf16[8,64,128]{2,1,0:T(8,128)(2,1)S(1)}, bf16[8,64,128]{2,1,0:T(8,128)(2,1)S(1)}, u32[]{:S(2)}, u32[]{:S(2)}) collective-permute-start(bf16[8,64,128]{2,1,0:T(8,128)(2,1)S(1)} %collective-permute-done.17.refs_6_), channel_id=1, source_target_pairs={{0,1},{1,0},{2,3},{3,2},{4,5},{5,4},{6,7},{7,6},{8,9},{9,8},{10,11... | collective-permute-start | bytes 393224 | tf_op jit(solution)/shard_map/ppermute | solution.py:296
  81.5 4.1 %collective-permute-start.27 = (bf16[8,64,128]{2,1,0:T(8,128)(2,1)S(1)}, bf16[8,64,128]{2,1,0:T(8,128)(2,1)S(1)}, u32[]{:S(2)}, u32[]{:S(2)}) collective-permute-start(bf16[8,64,128]{2,1,0:T(8,128)(2,1)S(1)} %collective-permute-done.26.refs_10_), channel_id=1, source_target_pairs={{0,1},{1,0},{2,3},{3,2},{4,5},{5,4},{6,7},{7,6},{8,9},{9,8},{10,11... | collective-permute-start | bytes 393224 | tf_op jit(solution)/shard_map/ppermute | solution.py:296
  84.8 1.8 %collective-permute-start.25 = (bf16[8,64,128]{2,1,0:T(8,128)(2,1)S(1)}, bf16[8,64,128]{2,1,0:T(8,128)(2,1)S(1)}, u32[]{:S(2)}, u32[]{:S(2)}) collective-permute-start(bf16[8,64,128]{2,1,0:T(8,128)(2,1)S(1)} %collective-permute-done.24.refs_8_), channel_id=1, source_target_pairs={{0,1},{1,0},{2,3},{3,2},{4,5},{5,4},{6,7},{7,6},{8,9},{9,8},{10,11... | collective-permute-start | bytes 393224 | tf_op jit(solution)/shard_map/ppermute | solution.py:296
  85.6 1.3 %collective-permute-start.29 = (bf16[8,64,128]{2,1,0:T(8,128)(2,1)S(1)}, bf16[8,64,128]{2,1,0:T(8,128)(2,1)S(1)}, u32[]{:S(2)}, u32[]{:S(2)}) collective-permute-start(bf16[8,64,128]{2,1,0:T(8,128)(2,1)S(1)} %collective-permute-done.18.refs_14_), channel_id=1, source_target_pairs={{0,1},{1,0},{2,3},{3,2},{4,5},{5,4},{6,7},{7,6},{8,9},{9,8},{10,11... | collective-permute-start | bytes 393224 | tf_op jit(solution)/shard_map/ppermute | solution.py:296

commit v5 on v4

--- a/solution.py
+++ b/solution.py
@@ -9,7 +9,6 @@
 from jax.experimental.pallas import tpu as pltpu
 from jax.sharding import PartitionSpec as P
 
-ITERS = 2
 FREQUENCY = 0.25
 SLOTS_AT_ONCE = 8
 ENTRIES = 16
@@ -17,6 +16,9 @@
 NT = (((1,), (1,)), ((), ()))
 VMEM = pl.BlockSpec(memory_space=pltpu.VMEM)
 SMEM = pl.BlockSpec(memory_space=pltpu.SMEM)
+VMEM_LIMIT = 58 * 2**20
+STATE_ROOM = 16
+COUPLE_LIMIT = 50 * 2**20
 HBM = pl.BlockSpec(memory_space=pltpu.HBM)
 
 
@@ -61,25 +63,15 @@
         blocks_out[u] = (mask * tile / denom).astype(jnp.bfloat16)
 
 
-def state_kernel(count, occ, twist, partners, slot_of, right, energy, right_out, denom_out, mask_out, solution_out, place_out, rows):
+def state_kernel(count, occ, right, energy, out_hbm, rows, out, done):
     for u, tile, denom, mask in begin(count, occ, right, energy, rows):
-        right_out[u] = tile
-        denom_out[u] = denom
-        mask_out[u] = mask
-        solution_out[u] = mask * tile / denom
-    slots, entries = partners.shape
-    half = slots // 2
-
-    def places(s, carry):
-        for k in range(entries):
-            target = slot_of[partners[s, k]] ^ (twist[0] * slots)
-            slot = lax.rem(target, slots)
-            side = lax.div(slot, half)
-            tile = lax.div(target, slots) * half + slot - side * half
-            place_out[s, k] = 4 * tile + 2 * side + k % 2
-        return carry
-
-    lax.fori_loop(0, slots, places, 0)
+        out[0, u] = tile
+        out[1, u] = denom
+        out[2, u] = mask
+        out[3, u] = mask * tile / denom
+    copy = pltpu.make_async_copy(out, out_hbm.at[:4], done)
+    copy.start()
+    copy.wait()
 
 
 def start(right_side, pno_energy, occ_energy, pno_count):
@@ -94,18 +86,28 @@
     )(pno_count, occ_energy, right_side, pno_energy)
 
 
-def state(twist, partners, slot_of, right_side, pno_energy, occ_energy, pno_count):
+def state(right_side, pno_energy, occ_energy, pno_count):
     slots, width = pno_energy.shape
-    tiles = jax.ShapeDtypeStruct((slots // 2, width, 2 * width), jnp.float32)
     return pl.pallas_call(
         state_kernel,
-        in_specs=[SMEM] * 5 + [VMEM] * 2,
-        out_specs=[VMEM] * 4 + [SMEM],
-        out_shape=[tiles] * 4 + [jax.ShapeDtypeStruct(partners.shape, jnp.int32)],
-        scratch_shapes=[pltpu.VMEM((slots * width, 2 * width), jnp.float32)],
+        in_specs=[SMEM] * 2 + [VMEM] * 2,
+        out_specs=HBM,
+        out_shape=jax.ShapeDtypeStruct((STATE_ROOM, slots // 2, width, 2 * width), jnp.float32),
+        scratch_shapes=[
+            pltpu.VMEM((slots * width, 2 * width), jnp.float32),
+            pltpu.VMEM((4, slots // 2, width, 2 * width), jnp.float32),
+            pltpu.SemaphoreType.DMA,
+        ],
         cost_estimate=pl.CostEstimate(flops=0, bytes_accessed=32 * right_side.size, transcendentals=0),
+        compiler_params=pltpu.CompilerParams(vmem_limit_bytes=VMEM_LIMIT),
         name="state",
-    )(pno_count, occ_energy, twist, partners, slot_of, right_side, pno_energy)
+    )(pno_count, occ_energy, right_side, pno_energy)
+
+
+def places(slot_of, slots, twist):
+    half = slots // 2
+    device, slot = slot_of // slots, slot_of % slots
+    return 4 * ((device ^ twist) * half + slot % half) + 2 * (slot // half)
 
 
 def picker():
@@ -179,17 +181,20 @@
             pltpu.SemaphoreType.DMA((entries // step,)),
         ],
         cost_estimate=pl.CostEstimate(flops=0, bytes_accessed=4 * margins.size, transcendentals=0),
-        compiler_params=pltpu.CompilerParams(vmem_limit_bytes=4 * margins.size + 2**20),
+        compiler_params=pltpu.CompilerParams(vmem_limit_bytes=VMEM_LIMIT),
         name="margin_tiles",
     )(picker(), margins.reshape(entries, flat))
     return tiles.reshape(slots, partners // 2, width, 2 * width)
 
 
-def couple_kernel(last, pieces, place, *refs):
+def couple_kernel(last, pieces, place, partners, *refs):
     gathered, refs = refs[:pieces], refs[pieces:]
-    margins, right, denom, mask, current = refs[:5]
-    outs, refs = refs[5:7], refs[7:]
-    expanded, held, halves, coupled, arrived = refs[-5:]
+    margins, state = refs[:2]
+    refs = refs[2:]
+    if last:
+        current, refs = refs[0], refs[1:]
+    outs, refs = refs[:2], refs[2:]
+    expanded, held, halves, coupled, steady, arrived = refs[-6:]
     slots, pairs, width, lanes = held.shape
     half = slots // 2
 
@@ -197,8 +202,10 @@
         some = pl.ds(i * SLOTS_AT_ONCE, SLOTS_AT_ONCE)
         return pltpu.make_async_copy(margins.at[some], held.at[some], arrived.at[i])
 
+    fetch_state = pltpu.make_async_copy(state.at[:4], steady, arrived.at[slots // SLOTS_AT_ONCE])
     for i in range(slots // SLOTS_AT_ONCE):
         fetch(i).start()
+    fetch_state.start()
 
     left = left_lanes(width)
     at = 0
@@ -218,7 +225,8 @@
 
     def one_slot(s, at):
         for k in range(pairs):
-            weights = jnp.concatenate([expanded[place[s, 2 * k]], expanded[place[s, 2 * k + 1]]], axis=0)
+            first, second = place[partners[s, 2 * k]], place[partners[s, 2 * k + 1]] + 1
+            weights = jnp.concatenate([expanded[first], expanded[second]], axis=0)
             product = jnp.dot(held[s, k], weights, preferred_element_type=jnp.float32)
             halves[at, :, k * lanes : (k + 1) * lanes] = product.astype(jnp.bfloat16)
         margin = jnp.concatenate([held[s, k] for k in range(pairs)], axis=1)
@@ -234,11 +242,13 @@
 
     if last:
         store = refs[0]
+    fetch_state.wait()
     for u in range(half):
         both = jnp.concatenate([coupled[u], coupled[u + half]], axis=1)
-        before = current[u]
-        residual = mask[u] * (right[u] - denom[u] * before - both)
-        after = before + residual / denom[u]
+        right, denom, mask = steady[0, u], steady[1, u], steady[2, u]
+        before = current[u] if last else steady[3, u]
+        residual = mask * (right - denom * before - both)
+        after = before + residual / denom
         if last:
             for n, tile in enumerate((after, residual)):
                 store[2 * n, u * width : (u + 1) * width] = tile
@@ -258,7 +268,8 @@
                 out[half:, j * lanes : (j + 1) * lanes] = jnp.where(keep, upper_turned, lower)
 
 
-def couple(last, place, gathered, margins, right, denom, mask, current):
+def couple(place, partners, gathered, margins, state, current):
+    last = current is not None
     slots, pairs, width, lanes = margins.shape
     half = slots // 2
     devices = sum(piece.shape[0] for piece in gathered) // half
@@ -274,18 +285,18 @@
     ]
     if last:
         scratch.insert(0, pltpu.VMEM((4, half * width, lanes), jnp.float32))
-    operands = [*gathered, margins, right, denom, mask, current]
-    size = sum(math.prod(x.shape) * x.dtype.itemsize for x in operands + outs + scratch)
-    scratch.append(pltpu.SemaphoreType.DMA((slots // SLOTS_AT_ONCE,)))
+    operands = [*gathered, margins, state] + [current] * last
+    scratch.append(pltpu.VMEM((4, *state.shape[1:]), jnp.float32))
+    scratch.append(pltpu.SemaphoreType.DMA((slots // SLOTS_AT_ONCE + 1,)))
     return pl.pallas_call(
         functools.partial(couple_kernel, last, len(gathered)),
-        in_specs=[SMEM] + [VMEM] * len(gathered) + [HBM] + [VMEM] * 4,
+        in_specs=[SMEM] * 2 + [VMEM] * len(gathered) + [HBM] * 2 + [VMEM] * last,
         out_specs=[VMEM] * len(outs),
         out_shape=outs,
         scratch_shapes=scratch,
-        compiler_params=pltpu.CompilerParams(vmem_limit_bytes=size + 4 * 2**20),
+        compiler_params=pltpu.CompilerParams(vmem_limit_bytes=COUPLE_LIMIT),
         name="couple",
-    )(place, *operands)
+    )(place, partners, *operands)
 
 
 def gather(blocks, devices, meanwhile):
@@ -299,34 +310,27 @@
     piece = {0: blocks}
     for other in (2, 4, 12):
         piece[other] = swap(blocks, other)
+    piece[12], first = lax.optimization_barrier((piece[12], first))
+    piece[8] = swap(piece[12], 4)
+    piece[10] = swap(piece[12], 6)
+    piece[14] = swap(piece[12], 2)
     piece[6] = swap(piece[4], 2)
-    piece[12], piece[6], first = lax.optimization_barrier((piece[12], piece[6], first))
-    piece[8] = swap(piece[12], 4)
-    piece[14] = swap(piece[12], 2)
-    piece[10] = swap(piece[12], 6)
-    for other in (0, 2, 4, 12, 6):
-        piece[other ^ 1] = swap(piece[other], 1)
-    piece[14], second = lax.optimization_barrier((piece[14], second))
-    for other in (14, 8, 10):
+    piece[10], second = lax.optimization_barrier((piece[10], second))
+    for other in (0, 2, 4, 12, 6, 14, 8, 10):
         piece[other ^ 1] = swap(piece[other], 1)
     return [piece[i] for i in range(devices)], (first, second)
 
 
 def shards(right_side, pno_energy, occ_energy, pno_count, margins, partners, slot_of):
     devices = lax.axis_size("pair")
-    twist = lax.axis_index("pair") if devices == 16 else 0
-    twist = jnp.full((1,), twist, jnp.int32)
+    place = places(slot_of, partners.shape[0], lax.axis_index("pair") if devices == 16 else 0)
     blocks = start(right_side, pno_energy, occ_energy, pno_count)
     tiles = margin_tiles(margins, pno_energy.shape[1])
-    states = state(twist, partners, slot_of, right_side, pno_energy, occ_energy, pno_count)
-    for step in range(ITERS):
-        gathered, (tiles, states) = gather(blocks, devices, (tiles, states))
-        right, denom, mask, current, place = states
-        outs = couple(step == ITERS - 1, place, gathered, tiles, right, denom, mask, current)
-        if step < ITERS - 1:
-            current, blocks = outs
-            states = right, denom, mask, current, place
-    return tuple(outs)
+    steady = state(right_side, pno_energy, occ_energy, pno_count)
+    gathered, (tiles, steady) = gather(blocks, devices, (tiles, steady))
+    current, blocks = couple(place, partners, gathered, tiles, steady, None)
+    gathered, (tiles, steady) = gather(blocks, devices, (tiles, steady))
+    return tuple(couple(place, partners, gathered, tiles, steady, current))
 
 
 def solution(mesh):

time: 96.6 us -> 70.2 us (0.73)
  the two profiles are of different devices: /device:TPU:25 before, /device:TPU:0 now
where the time goes in v5:
time: 70.2 us; the launch traced here: 70 us
  Pallas kernels  30.5 us (43%)
  starting transfers between devices  22.3 us (32%)
  waiting for transfers between devices  16.4 us (23%)
  between operations  0.74 us (1%)
    ppermute x30, starting transfers between devices, swap(): return lax.ppermute(piece, 'pair', [(i, i ^ other) for i in range(devices)])  22.3 us
    pallas_call x2, Pallas kernels, couple(): pl.pallas_call(functools.partial(couple_kernel, last, len(gathered)), in_...  19.2 us
    ppermute x30, waiting for transfers between devices, swap(): return lax.ppermute(piece, 'pair', [(i, i ^ other) for i in range(devices)])  16.4 us
    pallas_call x1, Pallas kernels, margin_tiles(): pl.pallas_call(margin_kernel, in_specs=[VMEM, HBM], out_specs=HBM, out_sh...  6.73 us
    pallas_call x1, Pallas kernels, state(): pl.pallas_call(state_kernel, in_specs=[SMEM] * 2 + [VMEM] * 2, out_specs=...  2.49 us
    pallas_call x1, Pallas kernels, start(): pl.pallas_call(start_kernel, in_specs=[SMEM, SMEM, VMEM, VMEM], out_specs...  2.12 us
  transfers between devices with their start and end apart: 30, of which 11 were waited for; matrix products, arithmetic and copies ran while one was open for 0% of the time, Pallas kernels for 13%

profile of v5, /device:TPU:0, one launch (start us, length us, event | category | flops | bytes accessed | tf_op | source)
XLA Modules:
  0.0 70.0 jit_solution(6188953642242559058)
XLA Ops:
  0.6 2.1 %start.1.refs_0_ = bf16[8,64,128]{2,1,0:T(8,128)(2,1)} custom-call(s32[16]{0:T(128)} %count.3, f32[16]{0:T(128)} %occ.3, f32[16,4096]{1,0:T(8,128)} %right.3, f32[16,64]{1,0:T(8,128)} %energy.3), custom_call_target="tpu_custom_call" | custom-call | tf_op jit(solution)/shard_map/start/pallas_call | solution.py:79
  2.7 5.0 %collective-permute-start.7 = (bf16[8,64,128]{2,1,0:T(8,128)(2,1)}, bf16[8,64,128]{2,1,0:T(8,128)(2,1)S(1)}, u32[]{:S(2)}, u32[]{:S(2)}) collective-permute-start(bf16[8,64,128]{2,1,0:T(8,128)(2,1)} %start.1.refs_0_), channel_id=1, source_target_pairs={{0,12},{1,13},{2,14},{3,15},{4,8},{5,9},{6,10},{7,11},{8,4},{9,5},... | collective-permute-start | bytes 393224 | tf_op jit(solution)/shard_map/ppermute | solution.py:307
  7.8 0.0 collective-permute-start.3
  7.8 1.5 %collective-permute-start.1 = (bf16[8,64,128]{2,1,0:T(8,128)(2,1)}, bf16[8,64,128]{2,1,0:T(8,128)(2,1)S(1)}, u32[]{:S(2)}, u32[]{:S(2)}) collective-permute-start(bf16[8,64,128]{2,1,0:T(8,128)(2,1)} %start.1.refs_0_), channel_id=1, source_target_pairs={{0,2},{1,3},{2,0},{3,1},{4,6},{5,7},{6,4},{7,5},{8,10},{9,11},{10,... | collective-permute-start | bytes 393224 | tf_op jit(solution)/shard_map/ppermute | solution.py:307
  9.3 0.0 collective-permute-start
  9.3 6.7 %margin_tiles.1 = bf16[320,64,128]{2,1,0:T(8,128)(2,1)} custom-call(bf16[128,256]{1,0:T(8,128)(2,1)} %constant.58.clone.pick, bf16[640,4096]{1,0:T(8,128)(2,1)} %bitcast.4), custom_call_target="tpu_custom_call" | custom-call | bytes 10485760 | tf_op jit(solution)/shard_map/margin_tiles/pallas_call | solution.py:172
  16.1 0.0 collective-permute-done.7.refs_12_
  16.1 2.0 %collective-permute-start.10 = (bf16[8,64,128]{2,1,0:T(8,128)(2,1)S(1)}, bf16[8,64,128]{2,1,0:T(8,128)(2,1)S(1)}, u32[]{:S(2)}, u32[]{:S(2)}) collective-permute-start(bf16[8,64,128]{2,1,0:T(8,128)(2,1)S(1)} %collective-permute-done.7.refs_12_), channel_id=1, source_target_pairs={{0,6},{1,7},{2,4},{3,5},{4,2},{5,3},{6,0},{7,1},{8,14},{9,15},{10,... | collective-permute-start | bytes 393224 | tf_op jit(solution)/shard_map/ppermute | solution.py:307
  18.1 0.0 collective-permute-done.3.refs_4_
  18.1 1.5 %collective-permute-start.5 = (bf16[8,64,128]{2,1,0:T(8,128)(2,1)S(1)}, bf16[8,64,128]{2,1,0:T(8,128)(2,1)S(1)}, u32[]{:S(2)}, u32[]{:S(2)}) collective-permute-start(bf16[8,64,128]{2,1,0:T(8,128)(2,1)S(1)} %collective-permute-done.3.refs_4_), channel_id=1, source_target_pairs={{0,2},{1,3},{2,0},{3,1},{4,6},{5,7},{6,4},{7,5},{8,10},{9,11},{10,... | collective-permute-start | bytes 393224 | tf_op jit(solution)/shard_map/ppermute | solution.py:307
  19.6 0.0 collective-permute-start.4
  19.6 0.0 collective-permute-done.1.refs_2_
  19.6 0.5 collective-permute-start.2
  20.1 0.0 collective-permute-done.refs_1_
  20.1 0.5 collective-permute-start.13
  20.7 2.4 %collective-permute-done.10.refs_10_ = bf16[8,64,128]{2,1,0:T(8,128)(2,1)S(1)} collective-permute-done((bf16[8,64,128]{2,1,0:T(8,128)(2,1)S(1)}, bf16[8,64,128]{2,1,0:T(8,128)(2,1)S(1)}, u32[]{:S(2)}, u32[]{:S(2)}) %collective-permute-start.10) | collective-permute-done | bytes 131104 | tf_op jit(solution)/shard_map/ppermute | solution.py:307
  23.0 2.1 %collective-permute-start.8 = (bf16[8,64,128]{2,1,0:T(8,128)(2,1)S(1)}, bf16[8,64,128]{2,1,0:T(8,128)(2,1)S(1)}, u32[]{:S(2)}, u32[]{:S(2)}) collective-permute-start(bf16[8,64,128]{2,1,0:T(8,128)(2,1)S(1)} %collective-permute-done.7.refs_12_), channel_id=1, source_target_pairs={{0,4},{1,5},{2,6},{3,7},{4,0},{5,1},{6,2},{7,3},{8,12},{9,13},{10,... | collective-permute-start | bytes 393224 | tf_op jit(solution)/shard_map/ppermute | solution.py:307
  25.1 2.5 %state.1.refs_17_ = f32[16,8,64,128]{3,2,1,0:T(8,128)} custom-call(s32[16]{0:T(128)} %count.3, f32[16]{0:T(128)} %occ.3, f32[16,4096]{1,0:T(8,128)} %right.3, f32[16,64]{1,0:T(8,128)} %energy.3), custom_call_target="tpu_custom_call" | custom-call | bytes 2097152 | tf_op jit(solution)/shard_map/state/pallas_call | solution.py:91
  27.6 0.0 collective-permute-done.5.refs_6_
  27.6 0.1 collective-permute-start.12
  27.7 0.0 collective-permute-done.4.refs_5_
  27.7 0.5 collective-permute-start.11
  28.2 0.0 collective-permute-done.2.refs_3_
  28.2 0.1 collective-permute-start.6
  28.3 0.3 collective-permute-done.13.refs_14_
  28.5 0.1 collective-permute-start.14
  28.7 0.0 collective-permute-done.8.refs_8_
  28.7 0.4 collective-permute-start.9
  29.1 0.0 collective-permute-done.12.refs_13_
  29.1 0.4 collective-permute-done.6.refs_7_
  29.5 0.4 collective-permute-done.14.refs_15_
  29.9 0.0 collective-permute-done.11.refs_11_
  29.9 0.2 collective-permute-done.9.refs_9_
  30.1 8.7 %couple.2 = (f32[8,64,128]{2,1,0:T(8,128)S(1)}, bf16[8,64,128]{2,1,0:T(8,128)(2,1)S(1)}) custom-call(s32[256]{0:T(256)S(1)} %multiply_add_fusion.place, s32[16,40]{1,0:T(8,128)S(1)} %copy-done.1, bf16[8,64,128]{2,1,0:T(8,128)(2,1)S(1)} %copy-done, bf16[8,64,128]{2,1,0:T(8,128)(2,1)S(1)} %collective-permute-done.refs_1_, ...), custom_call_target="tpu_custom_call" | custom-call | tf_op jit(solution)/shard_map/couple/pallas_call | solution.py:291
  38.8 0.9 %collective-permute-start.22 = (bf16[8,64,128]{2,1,0:T(8,128)(2,1)S(1)}, bf16[8,64,128]{2,1,0:T(8,128)(2,1)S(1)}, u32[]{:S(2)}, u32[]{:S(2)}) collective-permute-start(bf16[8,64,128]{2,1,0:T(8,128)(2,1)S(1)} %get-tuple-element.16.refs_0_), channel_id=1, source_target_pairs={{0,12},{1,13},{2,14},{3,15},{4,8},{5,9},{6,10},{7,11},{8,4},{9,5},... | collective-permute-start | bytes 393224 | tf_op jit(solution)/shard_map/ppermute | solution.py:307
  39.6 0.7 collective-permute-start.18
  40.3 0.9 %collective-permute-start.16 = (bf16[8,64,128]{2,1,0:T(8,128)(2,1)S(1)}, bf16[8,64,128]{2,1,0:T(8,128)(2,1)S(1)}, u32[]{:S(2)}, u32[]{:S(2)}) collective-permute-start(bf16[8,64,128]{2,1,0:T(8,128)(2,1)S(1)} %get-tuple-element.16.refs_0_), channel_id=1, source_target_pairs={{0,2},{1,3},{2,0},{3,1},{4,6},{5,7},{6,4},{7,5},{8,10},{9,11},{10,... | collective-permute-start | bytes 393224 | tf_op jit(solution)/shard_map/ppermute | solution.py:307
  41.2 0.0 collective-permute-start.15
  41.2 5.8 %collective-permute-done.22.refs_12_ = bf16[8,64,128]{2,1,0:T(8,128)(2,1)S(1)} collective-permute-done((bf16[8,64,128]{2,1,0:T(8,128)(2,1)S(1)}, bf16[8,64,128]{2,1,0:T(8,128)(2,1)S(1)}, u32[]{:S(2)}, u32[]{:S(2)}) %collective-permute-start.22) | collective-permute-done | bytes 131104 | tf_op jit(solution)/shard_map/ppermute | solution.py:307
  47.0 2.1 %collective-permute-start.25 = (bf16[8,64,128]{2,1,0:T(8,128)(2,1)S(1)}, bf16[8,64,128]{2,1,0:T(8,128)(2,1)S(1)}, u32[]{:S(2)}, u32[]{:S(2)}) collective-permute-start(bf16[8,64,128]{2,1,0:T(8,128)(2,1)S(1)} %collective-permute-done.22.refs_12_), channel_id=1, source_target_pairs={{0,6},{1,7},{2,4},{3,5},{4,2},{5,3},{6,0},{7,1},{8,14},{9,15},{10,... | collective-permute-start | bytes 393224 | tf_op jit(solution)/shard_map/ppermute | solution.py:307
  49.1 1.0 %collective-permute-start.28 = (bf16[8,64,128]{2,1,0:T(8,128)(2,1)S(1)}, bf16[8,64,128]{2,1,0:T(8,128)(2,1)S(1)}, u32[]{:S(2)}, u32[]{:S(2)}) collective-permute-start(bf16[8,64,128]{2,1,0:T(8,128)(2,1)S(1)} %collective-permute-done.22.refs_12_), channel_id=1, source_target_pairs={{0,2},{1,3},{2,0},{3,1},{4,6},{5,7},{6,4},{7,5},{8,10},{9,11},{10,... | collective-permute-start | bytes 393224 | tf_op jit(solution)/shard_map/ppermute | solution.py:307
  50.1 0.0 collective-permute-done.18.refs_4_
  50.1 0.0 collective-permute-start.27
  50.1 0.0 collective-permute-done.16.refs_2_
  50.1 0.5 collective-permute-start.23
  50.6 0.9 %collective-permute-start.20 = (bf16[8,64,128]{2,1,0:T(8,128)(2,1)S(1)}, bf16[8,64,128]{2,1,0:T(8,128)(2,1)S(1)}, u32[]{:S(2)}, u32[]{:S(2)}) collective-permute-start(bf16[8,64,128]{2,1,0:T(8,128)(2,1)S(1)} %collective-permute-done.18.refs_4_), channel_id=1, source_target_pairs={{0,2},{1,3},{2,0},{3,1},{4,6},{5,7},{6,4},{7,5},{8,10},{9,11},{10,... | collective-permute-start | bytes 393224 | tf_op jit(solution)/shard_map/ppermute | solution.py:307
  51.4 1.5 %collective-permute-done.25.refs_10_ = bf16[8,64,128]{2,1,0:T(8,128)(2,1)S(1)} collective-permute-done((bf16[8,64,128]{2,1,0:T(8,128)(2,1)S(1)}, bf16[8,64,128]{2,1,0:T(8,128)(2,1)S(1)}, u32[]{:S(2)}, u32[]{:S(2)}) %collective-permute-start.25) | collective-permute-done | bytes 131104 | tf_op jit(solution)/shard_map/ppermute | solution.py:307
  53.0 0.0 collective-permute-start.19
  53.0 2.9 %collective-permute-done.28.refs_14_ = bf16[8,64,128]{2,1,0:T(8,128)(2,1)S(1)} collective-permute-done((bf16[8,64,128]{2,1,0:T(8,128)(2,1)S(1)}, bf16[8,64,128]{2,1,0:T(8,128)(2,1)S(1)}, u32[]{:S(2)}, u32[]{:S(2)}) %collective-permute-start.28) | collective-permute-done | bytes 131104 | tf_op jit(solution)/shard_map/ppermute | solution.py:307
  55.8 0.0 collective-permute-start.17
  55.8 0.0 collective-permute-done.27.refs_13_
  55.8 0.5 collective-permute-start.26
  56.3 0.0 collective-permute-done.23.refs_8_
  56.3 0.1 collective-permute-start.29
  56.4 1.6 %collective-permute-done.20.refs_6_ = bf16[8,64,128]{2,1,0:T(8,128)(2,1)S(1)} collective-permute-done((bf16[8,64,128]{2,1,0:T(8,128)(2,1)S(1)}, bf16[8,64,128]{2,1,0:T(8,128)(2,1)S(1)}, u32[]{:S(2)}, u32[]{:S(2)}) %collective-permute-start.20) | collective-permute-done | bytes 131104 | tf_op jit(solution)/shard_map/ppermute | solution.py:307
  58.0 0.0 collective-permute-start.24
  58.0 0.0 collective-permute-done.19.refs_5_
  58.0 0.5 collective-permute-start.21
  58.5 0.0 collective-permute-done.17.refs_3_
  58.5 0.0 collective-permute-done.29.refs_15_
  58.5 0.0 collective-permute-done.26.refs_11_
  58.5 0.8 %collective-permute-done.24.refs_9_ = bf16[8,64,128]{2,1,0:T(8,128)(2,1)S(1)} collective-permute-done((bf16[8,64,128]{2,1,0:T(8,128)(2,1)S(1)}, bf16[8,64,128]{2,1,0:T(8,128)(2,1)S(1)}, u32[]{:S(2)}, u32[]{:S(2)}) %collective-permute-start.24) | collective-permute-done | bytes 131104 | tf_op jit(solution)/shard_map/ppermute | solution.py:307
  59.3 0.2 collective-permute-done.21.refs_7_
  59.5 10.5 %couple.3 = (f32[16,4096]{1,0:T(8,128)}, f32[16,4096]{1,0:T(8,128)}) custom-call(s32[256]{0:T(256)S(1)} %multiply_add_fusion.place, s32[16,40]{1,0:T(8,128)S(1)} %copy-done.1, bf16[8,64,128]{2,1,0:T(8,128)(2,1)S(1)} %get-tuple-element.16.refs_0_, bf16[8,64,128]{2,1,0:T(8,128)(2,1)S(1)} %collective-permute-done.15.refs_1_, ...), custom_call_target="tpu_custom_call" | custom-call | tf_op jit(solution)/shard_map/couple/pallas_call | solution.py:291
  (8 shorter events, 0.0 us)
Async XLA Ops:
  2.7 13.3 %collective-permute-start.7 = (bf16[8,64,128]{2,1,0:T(8,128)(2,1)}, bf16[8,64,128]{2,1,0:T(8,128)(2,1)S(1)}, u32[]{:S(2)}, u32[]{:S(2)}) collective-permute-start(bf16[8,64,128]{2,1,0:T(8,128)(2,1)} %start.1.refs_0_), channel_id=1, source_target_pairs={{0,12},{1,13},{2,14},{3,15},{4,8},{5,9},{6,10},{7,11},{8,4},{9,5},... | collective-permute-start | bytes 393224 | tf_op jit(solution)/shard_map/ppermute | solution.py:307
  7.8 10.3 %collective-permute-start.3 = (bf16[8,64,128]{2,1,0:T(8,128)(2,1)}, bf16[8,64,128]{2,1,0:T(8,128)(2,1)S(1)}, u32[]{:S(2)}, u32[]{:S(2)}) collective-permute-start(bf16[8,64,128]{2,1,0:T(8,128)(2,1)} %start.1.refs_0_), channel_id=1, source_target_pairs={{0,4},{1,5},{2,6},{3,7},{4,0},{5,1},{6,2},{7,3},{8,12},{9,13},{10,... | collective-permute-start | bytes 393224 | tf_op jit(solution)/shard_map/ppermute | solution.py:307
  7.8 11.8 %collective-permute-start.1 = (bf16[8,64,128]{2,1,0:T(8,128)(2,1)}, bf16[8,64,128]{2,1,0:T(8,128)(2,1)S(1)}, u32[]{:S(2)}, u32[]{:S(2)}) collective-permute-start(bf16[8,64,128]{2,1,0:T(8,128)(2,1)} %start.1.refs_0_), channel_id=1, source_target_pairs={{0,2},{1,3},{2,0},{3,1},{4,6},{5,7},{6,4},{7,5},{8,10},{9,11},{10,... | collective-permute-start | bytes 393224 | tf_op jit(solution)/shard_map/ppermute | solution.py:307
  9.3 10.8 %collective-permute-start = (bf16[8,64,128]{2,1,0:T(8,128)(2,1)}, bf16[8,64,128]{2,1,0:T(8,128)(2,1)S(1)}, u32[]{:S(2)}, u32[]{:S(2)}) collective-permute-start(bf16[8,64,128]{2,1,0:T(8,128)(2,1)} %start.1.refs_0_), channel_id=1, source_target_pairs={{0,1},{1,0},{2,3},{3,2},{4,5},{5,4},{6,7},{7,6},{8,9},{9,8},{10,11... | collective-permute-start | bytes 393224 | tf_op jit(solution)/shard_map/ppermute | solution.py:307
  9.3 19.7 %copy-start.2 = (s32[256]{0:T(256)S(1)}, s32[256]{0:T(256)}, u32[]{:S(2)}) copy-start(s32[256]{0:T(256)} %param.14) | copy-start | bytes 3076
  9.3 20.8 %copy-start = (bf16[8,64,128]{2,1,0:T(8,128)(2,1)S(1)}, bf16[8,64,128]{2,1,0:T(8,128)(2,1)}, u32[]{:S(2)}) copy-start(bf16[8,64,128]{2,1,0:T(8,128)(2,1)} %start.1.refs_0_) | copy-start | bytes 393220
  9.3 20.8 %copy-start.1 = (s32[16,40]{1,0:T(8,128)S(1)}, s32[16,40]{1,0:T(8,128)}, u32[]{:S(2)}) copy-start(s32[16,40]{1,0:T(8,128)} %partners.3) | copy-start | bytes 7684
  16.1 6.9 %collective-permute-start.10 = (bf16[8,64,128]{2,1,0:T(8,128)(2,1)S(1)}, bf16[8,64,128]{2,1,0:T(8,128)(2,1)S(1)}, u32[]{:S(2)}, u32[]{:S(2)}) collective-permute-start(bf16[8,64,128]{2,1,0:T(8,128)(2,1)S(1)} %collective-permute-done.7.refs_12_), channel_id=1, source_target_pairs={{0,6},{1,7},{2,4},{3,5},{4,2},{5,3},{6,0},{7,1},{8,14},{9,15},{10,... | collective-permute-start | bytes 393224 | tf_op jit(solution)/shard_map/ppermute | solution.py:307
  18.1 9.5 %collective-permute-start.5 = (bf16[8,64,128]{2,1,0:T(8,128)(2,1)S(1)}, bf16[8,64,128]{2,1,0:T(8,128)(2,1)S(1)}, u32[]{:S(2)}, u32[]{:S(2)}) collective-permute-start(bf16[8,64,128]{2,1,0:T(8,128)(2,1)S(1)} %collective-permute-done.3.refs_4_), channel_id=1, source_target_pairs={{0,2},{1,3},{2,0},{3,1},{4,6},{5,7},{6,4},{7,5},{8,10},{9,11},{10,... | collective-permute-start | bytes 393224 | tf_op jit(solution)/shard_map/ppermute | solution.py:307
  19.6 8.1 %collective-permute-start.4 = (bf16[8,64,128]{2,1,0:T(8,128)(2,1)S(1)}, bf16[8,64,128]{2,1,0:T(8,128)(2,1)S(1)}, u32[]{:S(2)}, u32[]{:S(2)}) collective-permute-start(bf16[8,64,128]{2,1,0:T(8,128)(2,1)S(1)} %collective-permute-done.3.refs_4_), channel_id=1, source_target_pairs={{0,1},{1,0},{2,3},{3,2},{4,5},{5,4},{6,7},{7,6},{8,9},{9,8},{10,11... | collective-permute-start | bytes 393224 | tf_op jit(solution)/shard_map/ppermute | solution.py:307
  19.6 8.5 %collective-permute-start.2 = (bf16[8,64,128]{2,1,0:T(8,128)(2,1)S(1)}, bf16[8,64,128]{2,1,0:T(8,128)(2,1)S(1)}, u32[]{:S(2)}, u32[]{:S(2)}) collective-permute-start(bf16[8,64,128]{2,1,0:T(8,128)(2,1)S(1)} %collective-permute-done.1.refs_2_), channel_id=1, source_target_pairs={{0,1},{1,0},{2,3},{3,2},{4,5},{5,4},{6,7},{7,6},{8,9},{9,8},{10,11... | collective-permute-start | bytes 393224 | tf_op jit(solution)/shard_map/ppermute | solution.py:307
  20.1 8.4 %collective-permute-start.13 = (bf16[8,64,128]{2,1,0:T(8,128)(2,1)S(1)}, bf16[8,64,128]{2,1,0:T(8,128)(2,1)S(1)}, u32[]{:S(2)}, u32[]{:S(2)}) collective-permute-start(bf16[8,64,128]{2,1,0:T(8,128)(2,1)S(1)} %collective-permute-done.7.refs_12_), channel_id=1, source_target_pairs={{0,2},{1,3},{2,0},{3,1},{4,6},{5,7},{6,4},{7,5},{8,10},{9,11},{10,... | collective-permute-start | bytes 393224 | tf_op jit(solution)/shard_map/ppermute | solution.py:307
  23.0 5.7 %collective-permute-start.8 = (bf16[8,64,128]{2,1,0:T(8,128)(2,1)S(1)}, bf16[8,64,128]{2,1,0:T(8,128)(2,1)S(1)}, u32[]{:S(2)}, u32[]{:S(2)}) collective-permute-start(bf16[8,64,128]{2,1,0:T(8,128)(2,1)S(1)} %collective-permute-done.7.refs_12_), channel_id=1, source_target_pairs={{0,4},{1,5},{2,6},{3,7},{4,0},{5,1},{6,2},{7,3},{8,12},{9,13},{10,... | collective-permute-start | bytes 393224 | tf_op jit(solution)/shard_map/ppermute | solution.py:307
  27.6 1.5 %collective-permute-start.12 = (bf16[8,64,128]{2,1,0:T(8,128)(2,1)S(1)}, bf16[8,64,128]{2,1,0:T(8,128)(2,1)S(1)}, u32[]{:S(2)}, u32[]{:S(2)}) collective-permute-start(bf16[8,64,128]{2,1,0:T(8,128)(2,1)S(1)} %collective-permute-done.7.refs_12_), channel_id=1, source_target_pairs={{0,1},{1,0},{2,3},{3,2},{4,5},{5,4},{6,7},{7,6},{8,9},{9,8},{10,11... | collective-permute-start | bytes 393224 | tf_op jit(solution)/shard_map/ppermute | solution.py:307
  27.7 2.2 %collective-permute-start.11 = (bf16[8,64,128]{2,1,0:T(8,128)(2,1)S(1)}, bf16[8,64,128]{2,1,0:T(8,128)(2,1)S(1)}, u32[]{:S(2)}, u32[]{:S(2)}) collective-permute-start(bf16[8,64,128]{2,1,0:T(8,128)(2,1)S(1)} %collective-permute-done.10.refs_10_), channel_id=1, source_target_pairs={{0,1},{1,0},{2,3},{3,2},{4,5},{5,4},{6,7},{7,6},{8,9},{9,8},{10,11... | collective-permute-start | bytes 393224 | tf_op jit(solution)/shard_map/ppermute | solution.py:307
  28.2 1.3 %collective-permute-start.6 = (bf16[8,64,128]{2,1,0:T(8,128)(2,1)S(1)}, bf16[8,64,128]{2,1,0:T(8,128)(2,1)S(1)}, u32[]{:S(2)}, u32[]{:S(2)}) collective-permute-start(bf16[8,64,128]{2,1,0:T(8,128)(2,1)S(1)} %collective-permute-done.5.refs_6_), channel_id=1, source_target_pairs={{0,1},{1,0},{2,3},{3,2},{4,5},{5,4},{6,7},{7,6},{8,9},{9,8},{10,11... | collective-permute-start | bytes 393224 | tf_op jit(solution)/shard_map/ppermute | solution.py:307
  28.5 1.3 %collective-permute-start.14 = (bf16[8,64,128]{2,1,0:T(8,128)(2,1)S(1)}, bf16[8,64,128]{2,1,0:T(8,128)(2,1)S(1)}, u32[]{:S(2)}, u32[]{:S(2)}) collective-permute-start(bf16[8,64,128]{2,1,0:T(8,128)(2,1)S(1)} %collective-permute-done.13.refs_14_), channel_id=1, source_target_pairs={{0,1},{1,0},{2,3},{3,2},{4,5},{5,4},{6,7},{7,6},{8,9},{9,8},{10,11... | collective-permute-start | bytes 393224 | tf_op jit(solution)/shard_map/ppermute | solution.py:307
  28.7 1.4 %collective-permute-start.9 = (bf16[8,64,128]{2,1,0:T(8,128)(2,1)S(1)}, bf16[8,64,128]{2,1,0:T(8,128)(2,1)S(1)}, u32[]{:S(2)}, u32[]{:S(2)}) collective-permute-start(bf16[8,64,128]{2,1,0:T(8,128)(2,1)S(1)} %collective-permute-done.8.refs_8_), channel_id=1, source_target_pairs={{0,1},{1,0},{2,3},{3,2},{4,5},{5,4},{6,7},{7,6},{8,9},{9,8},{10,11... | collective-permute-start | bytes 393224 | tf_op jit(solution)/shard_map/ppermute | solution.py:307
  38.8 8.2 %collective-permute-start.22 = (bf16[8,64,128]{2,1,0:T(8,128)(2,1)S(1)}, bf16[8,64,128]{2,1,0:T(8,128)(2,1)S(1)}, u32[]{:S(2)}, u32[]{:S(2)}) collective-permute-start(bf16[8,64,128]{2,1,0:T(8,128)(2,1)S(1)} %get-tuple-element.16.refs_0_), channel_id=1, source_target_pairs={{0,12},{1,13},{2,14},{3,15},{4,8},{5,9},{6,10},{7,11},{8,4},{9,5},... | collective-permute-start | bytes 393224 | tf_op jit(solution)/shard_map/ppermute | solution.py:307
  39.6 10.4 %collective-permute-start.18 = (bf16[8,64,128]{2,1,0:T(8,128)(2,1)S(1)}, bf16[8,64,128]{2,1,0:T(8,128)(2,1)S(1)}, u32[]{:S(2)}, u32[]{:S(2)}) collective-permute-start(bf16[8,64,128]{2,1,0:T(8,128)(2,1)S(1)} %get-tuple-element.16.refs_0_), channel_id=1, source_target_pairs={{0,4},{1,5},{2,6},{3,7},{4,0},{5,1},{6,2},{7,3},{8,12},{9,13},{10,... | collective-permute-start | bytes 393224 | tf_op jit(solution)/shard_map/ppermute | solution.py:307
  40.3 9.8 %collective-permute-start.16 = (bf16[8,64,128]{2,1,0:T(8,128)(2,1)S(1)}, bf16[8,64,128]{2,1,0:T(8,128)(2,1)S(1)}, u32[]{:S(2)}, u32[]{:S(2)}) collective-permute-start(bf16[8,64,128]{2,1,0:T(8,128)(2,1)S(1)} %get-tuple-element.16.refs_0_), channel_id=1, source_target_pairs={{0,2},{1,3},{2,0},{3,1},{4,6},{5,7},{6,4},{7,5},{8,10},{9,11},{10,... | collective-permute-start | bytes 393224 | tf_op jit(solution)/shard_map/ppermute | solution.py:307
  41.2 9.3 %collective-permute-start.15 = (bf16[8,64,128]{2,1,0:T(8,128)(2,1)S(1)}, bf16[8,64,128]{2,1,0:T(8,128)(2,1)S(1)}, u32[]{:S(2)}, u32[]{:S(2)}) collective-permute-start(bf16[8,64,128]{2,1,0:T(8,128)(2,1)S(1)} %get-tuple-element.16.refs_0_), channel_id=1, source_target_pairs={{0,1},{1,0},{2,3},{3,2},{4,5},{5,4},{6,7},{7,6},{8,9},{9,8},{10,11... | collective-permute-start | bytes 393224 | tf_op jit(solution)/shard_map/ppermute | solution.py:307
  47.0 6.0 %collective-permute-start.25 = (bf16[8,64,128]{2,1,0:T(8,128)(2,1)S(1)}, bf16[8,64,128]{2,1,0:T(8,128)(2,1)S(1)}, u32[]{:S(2)}, u32[]{:S(2)}) collective-permute-start(bf16[8,64,128]{2,1,0:T(8,128)(2,1)S(1)} %collective-permute-done.22.refs_12_), channel_id=1, source_target_pairs={{0,6},{1,7},{2,4},{3,5},{4,2},{5,3},{6,0},{7,1},{8,14},{9,15},{10,... | collective-permute-start | bytes 393224 | tf_op jit(solution)/shard_map/ppermute | solution.py:307
  49.1 6.7 %collective-permute-start.28 = (bf16[8,64,128]{2,1,0:T(8,128)(2,1)S(1)}, bf16[8,64,128]{2,1,0:T(8,128)(2,1)S(1)}, u32[]{:S(2)}, u32[]{:S(2)}) collective-permute-start(bf16[8,64,128]{2,1,0:T(8,128)(2,1)S(1)} %collective-permute-done.22.refs_12_), channel_id=1, source_target_pairs={{0,2},{1,3},{2,0},{3,1},{4,6},{5,7},{6,4},{7,5},{8,10},{9,11},{10,... | collective-permute-start | bytes 393224 | tf_op jit(solution)/shard_map/ppermute | solution.py:307
  50.1 5.8 %collective-permute-start.27 = (bf16[8,64,128]{2,1,0:T(8,128)(2,1)S(1)}, bf16[8,64,128]{2,1,0:T(8,128)(2,1)S(1)}, u32[]{:S(2)}, u32[]{:S(2)}) collective-permute-start(bf16[8,64,128]{2,1,0:T(8,128)(2,1)S(1)} %collective-permute-done.22.refs_12_), channel_id=1, source_target_pairs={{0,1},{1,0},{2,3},{3,2},{4,5},{5,4},{6,7},{7,6},{8,9},{9,8},{10,11... | collective-permute-start | bytes 393224 | tf_op jit(solution)/shard_map/ppermute | solution.py:307
  50.1 6.3 %collective-permute-start.23 = (bf16[8,64,128]{2,1,0:T(8,128)(2,1)S(1)}, bf16[8,64,128]{2,1,0:T(8,128)(2,1)S(1)}, u32[]{:S(2)}, u32[]{:S(2)}) collective-permute-start(bf16[8,64,128]{2,1,0:T(8,128)(2,1)S(1)} %collective-permute-done.22.refs_12_), channel_id=1, source_target_pairs={{0,4},{1,5},{2,6},{3,7},{4,0},{5,1},{6,2},{7,3},{8,12},{9,13},{10,... | collective-permute-start | bytes 393224 | tf_op jit(solution)/shard_map/ppermute | solution.py:307
  50.6 7.4 %collective-permute-start.20 = (bf16[8,64,128]{2,1,0:T(8,128)(2,1)S(1)}, bf16[8,64,128]{2,1,0:T(8,128)(2,1)S(1)}, u32[]{:S(2)}, u32[]{:S(2)}) collective-permute-start(bf16[8,64,128]{2,1,0:T(8,128)(2,1)S(1)} %collective-permute-done.18.refs_4_), channel_id=1, source_target_pairs={{0,2},{1,3},{2,0},{3,1},{4,6},{5,7},{6,4},{7,5},{8,10},{9,11},{10,... | collective-permute-start | bytes 393224 | tf_op jit(solution)/shard_map/ppermute | solution.py:307
  53.0 5.0 %collective-permute-start.19 = (bf16[8,64,128]{2,1,0:T(8,128)(2,1)S(1)}, bf16[8,64,128]{2,1,0:T(8,128)(2,1)S(1)}, u32[]{:S(2)}, u32[]{:S(2)}) collective-permute-start(bf16[8,64,128]{2,1,0:T(8,128)(2,1)S(1)} %collective-permute-done.18.refs_4_), channel_id=1, source_target_pairs={{0,1},{1,0},{2,3},{3,2},{4,5},{5,4},{6,7},{7,6},{8,9},{9,8},{10,11... | collective-permute-start | bytes 393224 | tf_op jit(solution)/shard_map/ppermute | solution.py:307
  55.8 2.7 %collective-permute-start.17 = (bf16[8,64,128]{2,1,0:T(8,128)(2,1)S(1)}, bf16[8,64,128]{2,1,0:T(8,128)(2,1)S(1)}, u32[]{:S(2)}, u32[]{:S(2)}) collective-permute-start(bf16[8,64,128]{2,1,0:T(8,128)(2,1)S(1)} %collective-permute-done.16.refs_2_), channel_id=1, source_target_pairs={{0,1},{1,0},{2,3},{3,2},{4,5},{5,4},{6,7},{7,6},{8,9},{9,8},{10,11... | collective-permute-start | bytes 393224 | tf_op jit(solution)/shard_map/ppermute | solution.py:307
  55.8 2.7 %collective-permute-start.26 = (bf16[8,64,128]{2,1,0:T(8,128)(2,1)S(1)}, bf16[8,64,128]{2,1,0:T(8,128)(2,1)S(1)}, u32[]{:S(2)}, u32[]{:S(2)}) collective-permute-start(bf16[8,64,128]{2,1,0:T(8,128)(2,1)S(1)} %collective-permute-done.25.refs_10_), channel_id=1, source_target_pairs={{0,1},{1,0},{2,3},{3,2},{4,5},{5,4},{6,7},{7,6},{8,9},{9,8},{10,11... | collective-permute-start | bytes 393224 | tf_op jit(solution)/shard_map/ppermute | solution.py:307
  56.3 2.1 %collective-permute-start.29 = (bf16[8,64,128]{2,1,0:T(8,128)(2,1)S(1)}, bf16[8,64,128]{2,1,0:T(8,128)(2,1)S(1)}, u32[]{:S(2)}, u32[]{:S(2)}) collective-permute-start(bf16[8,64,128]{2,1,0:T(8,128)(2,1)S(1)} %collective-permute-done.28.refs_14_), channel_id=1, source_target_pairs={{0,1},{1,0},{2,3},{3,2},{4,5},{5,4},{6,7},{7,6},{8,9},{9,8},{10,11... | collective-permute-start | bytes 393224 | tf_op jit(solution)/shard_map/ppermute | solution.py:307
  58.0 1.3 %collective-permute-start.24 = (bf16[8,64,128]{2,1,0:T(8,128)(2,1)S(1)}, bf16[8,64,128]{2,1,0:T(8,128)(2,1)S(1)}, u32[]{:S(2)}, u32[]{:S(2)}) collective-permute-start(bf16[8,64,128]{2,1,0:T(8,128)(2,1)S(1)} %collective-permute-done.23.refs_8_), channel_id=1, source_target_pairs={{0,1},{1,0},{2,3},{3,2},{4,5},{5,4},{6,7},{7,6},{8,9},{9,8},{10,11... | collective-permute-start | bytes 393224 | tf_op jit(solution)/shard_map/ppermute | solution.py:307
  58.0 1.5 %collective-permute-start.21 = (bf16[8,64,128]{2,1,0:T(8,128)(2,1)S(1)}, bf16[8,64,128]{2,1,0:T(8,128)(2,1)S(1)}, u32[]{:S(2)}, u32[]{:S(2)}) collective-permute-start(bf16[8,64,128]{2,1,0:T(8,128)(2,1)S(1)} %collective-permute-done.20.refs_6_), channel_id=1, source_target_pairs={{0,1},{1,0},{2,3},{3,2},{4,5},{5,4},{6,7},{7,6},{8,9},{9,8},{10,11... | collective-permute-start | bytes 393224 | tf_op jit(solution)/shard_map/ppermute | solution.py:307

commit v6 on v5

v6 whole, which is shorter than its diff:
```python
import functools
import math

import jax
import jax.numpy as jnp
import numpy as np
from jax import lax
from jax.experimental import pallas as pl
from jax.experimental.pallas import tpu as pltpu
from jax.sharding import PartitionSpec as P

FREQUENCY = 0.25
SLOTS_AT_ONCE = 8
ENTRIES = 16
TILES = 8
FIRST = 6
AHEAD = 4
CUTS = 2
NT = (((1,), (1,)), ((), ()))
VMEM = pl.BlockSpec(memory_space=pltpu.VMEM)
SMEM = pl.BlockSpec(memory_space=pltpu.SMEM)
VMEM_LIMIT = 58 * 2**20
STATE_ROOM = 16
COUPLE_LIMIT = 50 * 2**20
HBM = pl.BlockSpec(memory_space=pltpu.HBM)


def left_lanes(width):
    return lax.broadcasted_iota(jnp.int32, (width, 2 * width), 1) < width


def swap_halves(tile):
    width = tile.shape[1] // 2
    return jnp.concatenate([tile[:, width:], tile[:, :width]], axis=1)


def begin(count, occ, right, energy, rows):
    slots, width = energy.shape
    half = slots // 2
    lanes = 2 * width
    slot = lax.broadcasted_iota(jnp.int32, (slots, lanes), 0)
    for j in range(width // 2):
        part = right[:, j * lanes : (j + 1) * lanes]
        turned = swap_halves(part)
        rows[pl.ds(2 * j, slots, stride=width), :] = jnp.where(slot < half, part, turned)
        rows[pl.ds(2 * j + 1, slots, stride=width), :] = jnp.where(slot < half, turned, part)
    left = left_lanes(width)
    row = lax.broadcasted_iota(jnp.int32, (width, lanes), 0)
    column = lax.broadcasted_iota(jnp.int32, (width, lanes), 1) % width
    across = energy[...]
    down = across.T
    for u in range(half):
        v = u + half
        first = jnp.broadcast_to(down[:, u : u + 1], (width, lanes))
        second = jnp.broadcast_to(down[:, v : v + 1], (width, lanes))
        along = jnp.concatenate([across[u : u + 1], across[v : v + 1]], axis=1)
        shift = jnp.where(left, occ[u], occ[v])
        denom = jnp.where(left, first, second) + along - shift - FREQUENCY
        most = jnp.where(left, count[u], count[v])
        mask = jnp.where((row < most) & (column < most), 1.0, 0.0)
        yield u, jnp.where(left, rows[u * width : (u + 1) * width], rows[v * width : (v + 1) * width]), denom, mask


def start_kernel(count, occ, right, energy, blocks_out, rows):
    for u, tile, denom, mask in begin(count, occ, right, energy, rows):
        blocks_out[u] = (mask * tile / denom).astype(jnp.bfloat16)


def start(right_side, pno_energy, occ_energy, pno_count):
    slots, width = pno_energy.shape
    return pl.pallas_call(
        start_kernel,
        in_specs=[SMEM, SMEM, VMEM, VMEM],
        out_specs=VMEM,
        out_shape=jax.ShapeDtypeStruct((slots // 2, width, 2 * width), jnp.bfloat16),
        scratch_shapes=[pltpu.VMEM((slots * width, 2 * width), jnp.float32)],
        name="start",
    )(pno_count, occ_energy, right_side, pno_energy)


def places(slot_of, slots, twist):
    half = slots // 2
    device, slot = slot_of // slots, slot_of % slots
    return 4 * ((device ^ twist) * half + slot % half) + 2 * (slot // half)


def picker():
    pair, line = np.divmod(np.arange(ENTRIES * TILES), 2 * TILES)
    ones = np.zeros((ENTRIES * TILES, 2 * TILES * ENTRIES), np.float32)
    for side in range(2):
        ones[np.arange(ENTRIES * TILES), (line % 2) * TILES * ENTRIES + (line // 2) * ENTRIES + 2 * pair + side] = 1
    return jnp.asarray(ones, jnp.bfloat16)


def repack(i, ones, held, made):
    step, width, lanes = held.shape[1], *made.shape[2:]
    left = lax.broadcasted_iota(jnp.int32, (ENTRIES, lanes), 1) < width
    even = lax.broadcasted_iota(jnp.int32, (ENTRIES, lanes), 0) % 2 == 0
    for group in range(step // ENTRIES):
        rows = slice(group * ENTRIES, (group + 1) * ENTRIES)
        for n in range(0, width // 2, 2 * TILES):
            sides = []
            for part in (n, n + TILES):
                upper, lower = [], []
                for j in range(part, part + TILES):
                    here = held[i, rows, j * lanes : (j + 1) * lanes]
                    turned = swap_halves(here)
                    zero = jnp.zeros_like(here)
                    upper.append(jnp.where(left & even, here, jnp.where(left | even, zero, turned)))
                    lower.append(jnp.where(left & even, turned, jnp.where(left | even, zero, here)))
                sides.append(jnp.concatenate(upper + lower, axis=0))
            both = jnp.concatenate(sides, axis=1)
            found = jnp.dot(ones, both, preferred_element_type=jnp.float32).astype(jnp.bfloat16)
            for pair in range(ENTRIES // 2):
                for side in range(2):
                    line = 2 * (n + side * TILES)
                    made[i, group * (ENTRIES // 2) + pair, line : line + 2 * TILES] = found[
                        pair * 2 * TILES : (pair + 1) * 2 * TILES, side * lanes : (side + 1) * lanes
                    ]


def margin_kernel(offset, pick, margins, *refs):
    if offset > 0:
        _, count, occ, right, energy, tiles, state, *refs, rows, out, done = refs
        refs = tiles, *refs
    tiles, held, made, arrived, left_for = refs
    steps, step = held.shape[:2]

    def fetch(i):
        return pltpu.make_async_copy(margins.at[pl.ds((offset + i) * step, step)], held.at[i], arrived.at[i])

    def store(i):
        some = pl.ds((offset + i) * (step // 2), step // 2)
        return pltpu.make_async_copy(made.at[i], tiles.at[some], left_for.at[i])

    for i in range(min(AHEAD, steps)):
        fetch(i).start()
    if offset > 0:
        for u, tile, denom, mask in begin(count, occ, right, energy, rows):
            out[0, u] = tile
            out[1, u] = denom
            out[2, u] = mask
            out[3, u] = mask * tile / denom
        state_copy = pltpu.make_async_copy(out, state.at[:4], done)
        state_copy.start()
    ones = pick[...]

    def some(i, carry):
        fetch(i).wait()

        @pl.when(i + AHEAD < steps)
        def _():
            fetch(i + AHEAD).start()

        repack(i, ones, held, made)
        store(i).start()
        return carry

    lax.fori_loop(0, steps, some, 0)
    for i in range(steps):
        store(i).wait()
    if offset > 0:
        state_copy.wait()


def margin_scratch(steps, step, flat, width):
    return [
        pltpu.VMEM((steps, step, flat), jnp.bfloat16),
        pltpu.VMEM((steps, step // 2, width, 2 * width), jnp.bfloat16),
        pltpu.SemaphoreType.DMA((steps,)),
        pltpu.SemaphoreType.DMA((steps,)),
    ]


def margin_tiles(margins, width):
    slots, partners, flat = margins.shape
    entries = slots * partners
    step = math.lcm(partners, ENTRIES)
    return pl.pallas_call(
        functools.partial(margin_kernel, 0),
        in_specs=[VMEM, HBM],
        out_specs=HBM,
        out_shape=jax.ShapeDtypeStruct((entries // 2, width, 2 * width), jnp.bfloat16),
        scratch_shapes=margin_scratch(FIRST, step, flat, width),
        cost_estimate=pl.CostEstimate(flops=0, bytes_accessed=4 * margins.size, transcendentals=0),
        compiler_params=pltpu.CompilerParams(vmem_limit_bytes=VMEM_LIMIT),
        name="margin_tiles",
    )(picker(), margins.reshape(entries, flat))


def more_tiles(tiles, margins, right_side, pno_energy, occ_energy, pno_count):
    slots, partners, flat = margins.shape
    width = pno_energy.shape[1]
    entries = slots * partners
    step = math.lcm(partners, ENTRIES)
    return pl.pallas_call(
        functools.partial(margin_kernel, FIRST),
        in_specs=[VMEM, HBM, HBM, SMEM, SMEM, VMEM, VMEM],
        out_specs=[HBM, HBM],
        out_shape=[
            jax.ShapeDtypeStruct(tiles.shape, tiles.dtype),
            jax.ShapeDtypeStruct((STATE_ROOM, slots // 2, width, 2 * width), jnp.float32),
        ],
        scratch_shapes=[
            *margin_scratch(entries // step - FIRST, step, flat, width),
            pltpu.VMEM((slots * width, 2 * width), jnp.float32),
            pltpu.VMEM((4, slots // 2, width, 2 * width), jnp.float32),
            pltpu.SemaphoreType.DMA,
        ],
        input_output_aliases={2: 0},
        cost_estimate=pl.CostEstimate(flops=0, bytes_accessed=4 * margins.size, transcendentals=0),
        compiler_params=pltpu.CompilerParams(vmem_limit_bytes=VMEM_LIMIT),
        name="more_tiles",
    )(picker(), margins.reshape(entries, flat), tiles, pno_count, occ_energy, right_side, pno_energy)


def flat_kernel(count, occ, current, right, energy, out_hbm, store, out, done):
    slots, width = energy.shape
    half, lanes = slots // 2, 2 * width
    for u in range(half):
        tile = current[u]
        store[0, u * width : (u + 1) * width] = tile
        store[1, u * width : (u + 1) * width] = swap_halves(tile)
    slot = lax.broadcasted_iota(jnp.int32, (slots, lanes), 0)
    lane = lax.broadcasted_iota(jnp.int32, (slots, lanes), 1)
    shift = jnp.zeros((slots, lanes), jnp.float32)
    most = jnp.zeros((slots, lanes), jnp.int32)
    for s in range(slots):
        shift = jnp.where(slot == s, occ[s], shift)
        most = jnp.where(slot == s, count[s], most)
    left = lane < width
    across = energy[...]
    along = jnp.concatenate([across, across], axis=1)
    inside = lane % width < most
    for j in range(width // 2):
        columns = slice(j * lanes, (j + 1) * lanes)
        first = jnp.broadcast_to(across[:, 2 * j : 2 * j + 1], (slots, lanes))
        second = jnp.broadcast_to(across[:, 2 * j + 1 : 2 * j + 2], (slots, lanes))
        row = 2 * j + jnp.where(left, 0, 1)
        out[0, :, columns] = right[:, columns]
        out[1, :, columns] = jnp.where(left, first, second) + along - shift - FREQUENCY
        out[2, :, columns] = jnp.where(inside & (row < most), 1.0, 0.0)
        upper, lower = (store[0, pl.ds(2 * j + i, half, stride=width), :] for i in range(2))
        upper_turned, lower_turned = (store[1, pl.ds(2 * j + i, half, stride=width), :] for i in range(2))
        out[3, :half, columns] = jnp.where(left[:half], upper, lower_turned)
        out[3, half:, columns] = jnp.where(left[:half], upper_turned, lower)
    copy = pltpu.make_async_copy(out, out_hbm.at[:4], done)
    copy.start()
    copy.wait()


def flat_state(current, right_side, pno_energy, occ_energy, pno_count):
    slots, flat = right_side.shape
    width = pno_energy.shape[1]
    return pl.pallas_call(
        flat_kernel,
        in_specs=[SMEM, SMEM, VMEM, VMEM, VMEM],
        out_specs=HBM,
        out_shape=jax.ShapeDtypeStruct((STATE_ROOM, slots, flat), jnp.float32),
        scratch_shapes=[
            pltpu.VMEM((2, slots // 2 * width, 2 * width), jnp.float32),
            pltpu.VMEM((4, slots, flat), jnp.float32),
            pltpu.SemaphoreType.DMA,
        ],
        cost_estimate=pl.CostEstimate(flops=0, bytes_accessed=32 * right_side.size, transcendentals=0),
        name="flat_state",
    )(pno_count, occ_energy, current, right_side, pno_energy)


def couple_kernel(last, pieces, place, partners, *refs):
    gathered, refs = refs[:pieces], refs[pieces:]
    margins, state, *outs = refs[:4]
    expanded, held, halves, coupled, steady, arrived = refs[4:10]
    slots, pairs, width, lanes = held.shape
    half = slots // 2

    def fetch(i):
        return pltpu.make_async_copy(margins.at[i], held.at[i], arrived.at[i])

    fetch_state = pltpu.make_async_copy(state.at[:4], steady, arrived.at[slots])
    for i in range(SLOTS_AT_ONCE):
        fetch(i).start()
    left = left_lanes(width)
    at = 0
    for piece in gathered:

        def expand(i, at, piece=piece):
            tile = piece[i]
            turned = swap_halves(tile)
            zero = jnp.zeros_like(tile)
            expanded[at] = jnp.where(left, tile, zero)
            expanded[at + 1] = jnp.where(left, zero, turned)
            expanded[at + 2] = jnp.where(left, turned, zero)
            expanded[at + 3] = jnp.where(left, zero, tile)
            return at + 4

        at = lax.fori_loop(0, piece.shape[0], expand, at, unroll=half)

    def one_slot(s, at):
        for k in range(pairs):
            first, second = place[partners[s, 2 * k]], place[partners[s, 2 * k + 1]] + 1
            weights = jnp.concatenate([expanded[first], expanded[second]], axis=0)
            product = jnp.dot(held[s, k], weights, preferred_element_type=jnp.float32)
            halves[at, :, k * lanes : (k + 1) * lanes] = product.astype(jnp.bfloat16)
        margin = jnp.concatenate([held[s, k] for k in range(pairs)], axis=1)
        coupled[pl.ds(s * width, width)] = lax.dot_general(halves[at], margin, NT, preferred_element_type=jnp.float32)

    for i in range(SLOTS_AT_ONCE, slots):
        fetch(i).start()
    fetch_state.start()

    def some_slots(i, carry):
        for at in range(SLOTS_AT_ONCE):
            fetch(i * SLOTS_AT_ONCE + at).wait()
        for at in range(SLOTS_AT_ONCE):
            one_slot(i * SLOTS_AT_ONCE + at, at)
        return carry

    lax.fori_loop(0, slots // SLOTS_AT_ONCE, some_slots, 0)

    fetch_state.wait()
    if not last:
        for u in range(half):
            v = u + half
            both = jnp.concatenate(
                [coupled[u * width : (u + 1) * width], coupled[v * width : (v + 1) * width]], axis=1
            )
            right, denom, mask, before = (steady[i, u] for i in range(4))
            after = before + mask * (right - denom * before - both) / denom
            outs[0][u] = after
            outs[1][u] = after.astype(jnp.bfloat16)
        return
    made, sent = refs[10:]
    columns = width // 2 // CUTS * lanes

    def send(i, cut):
        some = pl.ds(cut * columns, columns)
        return pltpu.make_async_copy(made.at[i, :, some], outs[i].at[:, some], sent.at[i, cut])

    for cut in range(CUTS):
        for j in range(cut * width // 2 // CUTS, (cut + 1) * width // 2 // CUTS):
            here = slice(j * lanes, (j + 1) * lanes)
            both = jnp.concatenate([coupled[pl.ds(2 * j + i, slots, stride=width), :] for i in range(2)], axis=1)
            right, denom, mask, before = (steady[i, :, here] for i in range(4))
            residual = mask * (right - denom * before - both)
            made[0, :, here] = before + residual / denom
            made[1, :, here] = residual
        for i in range(2):
            send(i, cut).start()
    for cut in range(CUTS):
        for i in range(2):
            send(i, cut).wait()


def couple(place, partners, gathered, margins, state, last):
    slots, pairs, width, lanes = margins.shape
    half = slots // 2
    devices = sum(piece.shape[0] for piece in gathered) // half
    packed = jax.ShapeDtypeStruct((half, width, lanes), jnp.float32)
    flat = jax.ShapeDtypeStruct((slots, width * width), jnp.float32)
    blocks = jax.ShapeDtypeStruct((half, width, lanes), jnp.bfloat16)
    scratch = [
        pltpu.VMEM((2 * devices * slots, width, lanes), jnp.bfloat16),
        pltpu.VMEM((slots, pairs, width, lanes), jnp.bfloat16),
        pltpu.VMEM((SLOTS_AT_ONCE, width, pairs * lanes), jnp.bfloat16),
        pltpu.VMEM((slots * width, width), jnp.float32),
        pltpu.VMEM((4, *state.shape[1:]), jnp.float32),
        pltpu.SemaphoreType.DMA((slots + 1,)),
    ]
    if last:
        scratch += [pltpu.VMEM((2, slots, width * width), jnp.float32), pltpu.SemaphoreType.DMA((2, CUTS))]
    return pl.pallas_call(
        functools.partial(couple_kernel, last, len(gathered)),
        in_specs=[SMEM] * 2 + [VMEM] * len(gathered) + [HBM] * 2,
        out_specs=[HBM] * 2 if last else [VMEM] * 2,
        out_shape=[flat, flat] if last else [packed, blocks],
        scratch_shapes=scratch,
        compiler_params=pltpu.CompilerParams(vmem_limit_bytes=COUPLE_LIMIT),
        name="couple",
    )(place, partners, *gathered, margins, state)


def gather(blocks, devices, first, second):
    work = first()
    if devices != 16:
        return [lax.all_gather(blocks, "pair", axis=0, tiled=True)], second(work)

    def swap(piece, other):
        return lax.ppermute(piece, "pair", [(i, i ^ other) for i in range(devices)])

    piece = {0: blocks}
    for other in (2, 4, 12):
        piece[other] = swap(blocks, other)
    piece[12], work = lax.optimization_barrier((piece[12], work))
    work = second(work)
    piece[8] = swap(piece[12], 4)
    piece[10] = swap(piece[12], 6)
    piece[14] = swap(piece[12], 2)
    piece[6] = swap(piece[4], 2)
    piece[10], work = lax.optimization_barrier((piece[10], work))
    for other in (0, 2, 4, 12, 6, 14, 8, 10):
        piece[other ^ 1] = swap(piece[other], 1)
    return [piece[i] for i in range(devices)], work


def shards(right_side, pno_energy, occ_energy, pno_count, margins, partners, slot_of):
    devices = lax.axis_size("pair")
    slots, entries = partners.shape
    width = pno_energy.shape[1]
    own = right_side, pno_energy, occ_energy, pno_count
    place = places(slot_of, slots, lax.axis_index("pair") if devices == 16 else 0)
    gathered, (tiles, state) = gather(
        start(*own), devices, lambda: margin_tiles(margins, width), lambda tiles: more_tiles(tiles, margins, *own)
    )
    tiles = tiles.reshape(slots, entries // 2, width, 2 * width)
    current, blocks = couple(place, partners, gathered, tiles, state, False)
    gathered, state = gather(blocks, devices, lambda: flat_state(current, *own), lambda state: state)
    return tuple(couple(place, partners, gathered, tiles, state, True))


def solution(mesh):
    placed = (
        P(("groups", "pair"), None),
        P(("groups", "pair"), None),
        P(("groups", "pair")),
        P(("groups", "pair")),
        P(("groups", "pair"), None, None),
        P(("groups", "pair"), None),
        P("groups"),
    )
    return jax.shard_map(
        shards,
        mesh=mesh,
        in_specs=placed,
        out_specs=(P(("groups", "pair"), None), P(("groups", "pair"), None)),
        check_vma=False,
    )
```

time: 70.2 us -> 69.6 us (level)
  Pallas kernels: 30.5 us -> 32.9 us
  waiting for transfers between devices: 16.4 us -> 14.3 us
  starting transfers between devices: 22.3 us -> 20.5 us
    pallas_call x2 -> x3, Pallas kernels: 9.22 us -> 12.5 us  [the longest x1 5.71 us: margin_tiles(): pl.pallas_call(functools.partial(margin_kernel, 0), in_specs=[VMEM, HBM],...]
    ppermute x30, waiting for transfers between devices: 16.4 us -> 14.3 us  [swap(): return lax.ppermute(piece, 'pair', [(i, i ^ other) for i in range(devices)])]
    ppermute x30, starting transfers between devices: 22.3 us -> 20.5 us  [swap(): return lax.ppermute(piece, 'pair', [(i, i ^ other) for i in range(devices)])]
    pallas_call x2, Pallas kernels: 19.2 us -> 18.3 us  [couple(): pl.pallas_call(functools.partial(couple_kernel, last, len(gathered)), in_...]
  transfers between devices with their start and end apart: 30 -> 30, of which waited for: 11 -> 12; matrix products, arithmetic and copies ran while one was open for 0% -> 0% of each run, Pallas kernels for 13% -> 18%
where the time goes in v6:
time: 69.6 us; the launch traced here: 69.2 us
  Pallas kernels  32.9 us (47%)
  starting transfers between devices  20.5 us (29%)
  waiting for transfers between devices  14.3 us (21%)
  between operations  0.75 us (1%)
  local copies, waits for them, and re-layouts  0.71 us (1%)
    ppermute x30, starting transfers between devices, swap(): return lax.ppermute(piece, 'pair', [(i, i ^ other) for i in range(devices)])  20.5 us
    pallas_call x2, Pallas kernels, couple(): pl.pallas_call(functools.partial(couple_kernel, last, len(gathered)), in_...  18.3 us
    ppermute x30, waiting for transfers between devices, swap(): return lax.ppermute(piece, 'pair', [(i, i ^ other) for i in range(devices)])  14.3 us
    pallas_call x1, Pallas kernels, margin_tiles(): pl.pallas_call(functools.partial(margin_kernel, 0), in_specs=[VMEM, HBM],...  5.71 us
    pallas_call x1, Pallas kernels, more_tiles(): pl.pallas_call(functools.partial(margin_kernel, FIRST), in_specs=[VMEM, H...  4.09 us
    pallas_call x1, Pallas kernels, flat_state(): pl.pallas_call(flat_kernel, in_specs=[SMEM, SMEM, VMEM, VMEM, VMEM], out_...  2.73 us
    pallas_call x1, Pallas kernels, start(): pl.pallas_call(start_kernel, in_specs=[SMEM, SMEM, VMEM, VMEM], out_specs...  2.12 us
  transfers between devices with their start and end apart: 30, of which 12 were waited for; matrix products, arithmetic and copies ran while one was open for 0% of the time, Pallas kernels for 18%

profile of v6, /device:TPU:0, one launch (start us, length us, event | category | flops | bytes accessed | tf_op | source)
XLA Modules:
  0.0 69.2 jit_solution(10235265312696542392)
XLA Ops:
  0.6 2.1 %start.1.refs_0_ = bf16[8,64,128]{2,1,0:T(8,128)(2,1)} custom-call(s32[16]{0:T(128)} %count.3, f32[16]{0:T(128)} %occ.3, f32[16,4096]{1,0:T(8,128)} %right.3, f32[16,64]{1,0:T(8,128)} %energy.3), custom_call_target="tpu_custom_call" | custom-call | tf_op jit(solution)/shard_map/start/pallas_call | solution.py:71
  2.7 5.0 %collective-permute-start.7 = (bf16[8,64,128]{2,1,0:T(8,128)(2,1)}, bf16[8,64,128]{2,1,0:T(8,128)(2,1)S(1)}, u32[]{:S(2)}, u32[]{:S(2)}) collective-permute-start(bf16[8,64,128]{2,1,0:T(8,128)(2,1)} %start.1.refs_0_), channel_id=1, source_target_pairs={{0,12},{1,13},{2,14},{3,15},{4,8},{5,9},{6,10},{7,11},{8,4},{9,5},... | collective-permute-start | bytes 393224 | tf_op jit(solution)/shard_map/ppermute | solution.py:389
  7.8 0.0 collective-permute-start.3
  7.8 1.5 %collective-permute-start.1 = (bf16[8,64,128]{2,1,0:T(8,128)(2,1)}, bf16[8,64,128]{2,1,0:T(8,128)(2,1)S(1)}, u32[]{:S(2)}, u32[]{:S(2)}) collective-permute-start(bf16[8,64,128]{2,1,0:T(8,128)(2,1)} %start.1.refs_0_), channel_id=1, source_target_pairs={{0,2},{1,3},{2,0},{3,1},{4,6},{5,7},{6,4},{7,5},{8,10},{9,11},{10,... | collective-permute-start | bytes 393224 | tf_op jit(solution)/shard_map/ppermute | solution.py:389
  9.3 0.0 collective-permute-start
  9.3 5.7 %margin_tiles.1.refs_0_ = bf16[320,64,128]{2,1,0:T(8,128)(2,1)} custom-call(bf16[128,256]{1,0:T(8,128)(2,1)} %constant.58.clone.pick, bf16[640,4096]{1,0:T(8,128)(2,1)} %bitcast.4), custom_call_target="tpu_custom_call" | custom-call | bytes 10485760 | tf_op jit(solution)/shard_map/margin_tiles/pallas_call | solution.py:179
  15.0 0.0 collective-permute-done.7.refs_12_
  15.1 2.0 %collective-permute-start.10 = (bf16[8,64,128]{2,1,0:T(8,128)(2,1)S(1)}, bf16[8,64,128]{2,1,0:T(8,128)(2,1)S(1)}, u32[]{:S(2)}, u32[]{:S(2)}) collective-permute-start(bf16[8,64,128]{2,1,0:T(8,128)(2,1)S(1)} %collective-permute-done.7.refs_12_), channel_id=1, source_target_pairs={{0,6},{1,7},{2,4},{3,5},{4,2},{5,3},{6,0},{7,1},{8,14},{9,15},{10,... | collective-permute-start | bytes 393224 | tf_op jit(solution)/shard_map/ppermute | solution.py:389
  17.1 1.5 %collective-permute-start.13 = (bf16[8,64,128]{2,1,0:T(8,128)(2,1)S(1)}, bf16[8,64,128]{2,1,0:T(8,128)(2,1)S(1)}, u32[]{:S(2)}, u32[]{:S(2)}) collective-permute-start(bf16[8,64,128]{2,1,0:T(8,128)(2,1)S(1)} %collective-permute-done.7.refs_12_), channel_id=1, source_target_pairs={{0,2},{1,3},{2,0},{3,1},{4,6},{5,7},{6,4},{7,5},{8,10},{9,11},{10,... | collective-permute-start | bytes 393224 | tf_op jit(solution)/shard_map/ppermute | solution.py:389
  18.6 0.0 collective-permute-done.3.refs_4_
  18.6 0.0 collective-permute-done.1.refs_2_
  18.6 0.1 collective-permute-start.12
  18.7 0.0 collective-permute-done.refs_1_
  18.7 0.6 collective-permute-start.5
  19.3 3.0 %collective-permute-done.10.refs_10_ = bf16[8,64,128]{2,1,0:T(8,128)(2,1)S(1)} collective-permute-done((bf16[8,64,128]{2,1,0:T(8,128)(2,1)S(1)}, bf16[8,64,128]{2,1,0:T(8,128)(2,1)S(1)}, u32[]{:S(2)}, u32[]{:S(2)}) %collective-permute-start.10) | collective-permute-done | bytes 131104 | tf_op jit(solution)/shard_map/ppermute | solution.py:389
  22.3 0.0 collective-permute-start.4
  22.3 4.1 %more_tiles.1 = (bf16[320,64,128]{2,1,0:T(8,128)(2,1)}, f32[16,8,64,128]{3,2,1,0:T(8,128)}) custom-call(bf16[128,256]{1,0:T(8,128)(2,1)} %constant.58.clone.pick, bf16[640,4096]{1,0:T(8,128)(2,1)} %bitcast.5, bf16[320,64,128]{2,1,0:T(8,128)(2,1)} %margin_tiles.1.refs_0_, s32[16]{0:T(128)} %count.3, f32[16]{0:T(128)} %occ.3, ...), custom_call_target="tpu_custom_call", output_to_operand_aliasing={{0}: (2, {})} | custom-call | bytes 10485760 | tf_op jit(solution)/shard_map/more_tiles/pallas_call | solution.py:196
  26.4 0.0 collective-permute-done.13.refs_14_
  26.5 0.6 collective-permute-start.2
  27.0 0.0 collective-permute-done.8.refs_8_
  27.0 0.1 collective-permute-start.11
  27.1 0.0 collective-permute-done.12.refs_13_
  27.1 0.4 collective-permute-start.14
  27.5 0.0 collective-permute-done.5.refs_6_
  27.5 0.1 collective-permute-start.9
  27.6 0.0 collective-permute-done.4.refs_5_
  27.6 0.4 collective-permute-start.6
  28.1 0.0 collective-permute-done.2.refs_3_
  28.1 0.3 collective-permute-done.11.refs_11_
  28.4 0.2 collective-permute-done.14.refs_15_
  28.6 0.3 collective-permute-done.9.refs_9_
  28.9 0.2 collective-permute-done.6.refs_7_
  29.1 8.6 %couple.2 = (f32[8,64,128]{2,1,0:T(8,128)S(1)}, bf16[8,64,128]{2,1,0:T(8,128)(2,1)S(1)}) custom-call(s32[256]{0:T(256)S(1)} %multiply_add_fusion.place, s32[16,40]{1,0:T(8,128)S(1)} %copy-done.2, bf16[8,64,128]{2,1,0:T(8,128)(2,1)S(1)} %copy-done, bf16[8,64,128]{2,1,0:T(8,128)(2,1)S(1)} %collective-permute-done.refs_1_, ...), custom_call_target="tpu_custom_call" | custom-call | tf_op jit(solution)/shard_map/couple/pallas_call | solution.py:372
  37.7 0.0 copy-start.1
  37.7 0.7 %copy-done.1 = f32[8,64,128]{2,1,0:T(8,128)} copy-done((f32[8,64,128]{2,1,0:T(8,128)}, f32[8,64,128]{2,1,0:T(8,128)S(1)}, u32[]{:S(2)}) %copy-start.1) | copy-done | bytes 262168
  38.4 1.1 %collective-permute-start.22 = (bf16[8,64,128]{2,1,0:T(8,128)(2,1)S(1)}, bf16[8,64,128]{2,1,0:T(8,128)(2,1)S(1)}, u32[]{:S(2)}, u32[]{:S(2)}) collective-permute-start(bf16[8,64,128]{2,1,0:T(8,128)(2,1)S(1)} %get-tuple-element.22.refs_0_), channel_id=1, source_target_pairs={{0,12},{1,13},{2,14},{3,15},{4,8},{5,9},{6,10},{7,11},{8,4},{9,5},... | collective-permute-start | bytes 393224 | tf_op jit(solution)/shard_map/ppermute | solution.py:389
  39.5 0.9 %collective-permute-start.18 = (bf16[8,64,128]{2,1,0:T(8,128)(2,1)S(1)}, bf16[8,64,128]{2,1,0:T(8,128)(2,1)S(1)}, u32[]{:S(2)}, u32[]{:S(2)}) collective-permute-start(bf16[8,64,128]{2,1,0:T(8,128)(2,1)S(1)} %get-tuple-element.22.refs_0_), channel_id=1, source_target_pairs={{0,4},{1,5},{2,6},{3,7},{4,0},{5,1},{6,2},{7,3},{8,12},{9,13},{10,... | collective-permute-start | bytes 393224 | tf_op jit(solution)/shard_map/ppermute | solution.py:389
  40.5 0.5 collective-permute-start.16
  41.0 0.0 collective-permute-start.15
  41.0 2.7 %flat_state.1.refs_17_ = f32[16,16,4096]{2,1,0:T(8,128)} custom-call(s32[16]{0:T(128)} %count.3, f32[16]{0:T(128)} %occ.3, f32[8,64,128]{2,1,0:T(8,128)} %copy-done.1, f32[16,4096]{1,0:T(8,128)} %right.3, f32[16,64]{1,0:T(8,128)} %energy.3), custom_call_target="tpu_custom_call" | custom-call | bytes 2097152 | tf_op jit(solution)/shard_map/flat_state/pallas_call | solution.py:255
  43.7 2.9 %collective-permute-done.22.refs_12_ = bf16[8,64,128]{2,1,0:T(8,128)(2,1)S(1)} collective-permute-done((bf16[8,64,128]{2,1,0:T(8,128)(2,1)S(1)}, bf16[8,64,128]{2,1,0:T(8,128)(2,1)S(1)}, u32[]{:S(2)}, u32[]{:S(2)}) %collective-permute-start.22) | collective-permute-done | bytes 131104 | tf_op jit(solution)/shard_map/ppermute | solution.py:389
  46.6 2.4 %collective-permute-start.25 = (bf16[8,64,128]{2,1,0:T(8,128)(2,1)S(1)}, bf16[8,64,128]{2,1,0:T(8,128)(2,1)S(1)}, u32[]{:S(2)}, u32[]{:S(2)}) collective-permute-start(bf16[8,64,128]{2,1,0:T(8,128)(2,1)S(1)} %collective-permute-done.22.refs_12_), channel_id=1, source_target_pairs={{0,6},{1,7},{2,4},{3,5},{4,2},{5,3},{6,0},{7,1},{8,14},{9,15},{10,... | collective-permute-start | bytes 393224 | tf_op jit(solution)/shard_map/ppermute | solution.py:389
  48.9 0.1 collective-permute-start.23
  49.0 0.0 collective-permute-done.18.refs_4_
  49.0 1.5 %collective-permute-start.28 = (bf16[8,64,128]{2,1,0:T(8,128)(2,1)S(1)}, bf16[8,64,128]{2,1,0:T(8,128)(2,1)S(1)}, u32[]{:S(2)}, u32[]{:S(2)}) collective-permute-start(bf16[8,64,128]{2,1,0:T(8,128)(2,1)S(1)} %collective-permute-done.22.refs_12_), channel_id=1, source_target_pairs={{0,2},{1,3},{2,0},{3,1},{4,6},{5,7},{6,4},{7,5},{8,10},{9,11},{10,... | collective-permute-start | bytes 393224 | tf_op jit(solution)/shard_map/ppermute | solution.py:389
  50.5 0.0 collective-permute-done.16.refs_2_
  50.5 0.0 collective-permute-start.27
  50.5 0.0 collective-permute-done.15.refs_1_
  50.5 0.6 collective-permute-start.20
  51.1 1.8 %collective-permute-done.25.refs_10_ = bf16[8,64,128]{2,1,0:T(8,128)(2,1)S(1)} collective-permute-done((bf16[8,64,128]{2,1,0:T(8,128)(2,1)S(1)}, bf16[8,64,128]{2,1,0:T(8,128)(2,1)S(1)}, u32[]{:S(2)}, u32[]{:S(2)}) %collective-permute-start.25) | collective-permute-done | bytes 131104 | tf_op jit(solution)/shard_map/ppermute | solution.py:389
  52.9 0.0 collective-permute-start.17
  52.9 2.3 %collective-permute-done.23.refs_8_ = bf16[8,64,128]{2,1,0:T(8,128)(2,1)S(1)} collective-permute-done((bf16[8,64,128]{2,1,0:T(8,128)(2,1)S(1)}, bf16[8,64,128]{2,1,0:T(8,128)(2,1)S(1)}, u32[]{:S(2)}, u32[]{:S(2)}) %collective-permute-start.23) | collective-permute-done | bytes 131104 | tf_op jit(solution)/shard_map/ppermute | solution.py:389
  55.2 0.0 collective-permute-start.19
  55.2 0.3 collective-permute-done.28.refs_14_
  55.6 0.2 collective-permute-start.26
  55.7 0.3 collective-permute-start.24
  56.1 2.0 %collective-permute-done.20.refs_6_ = bf16[8,64,128]{2,1,0:T(8,128)(2,1)S(1)} collective-permute-done((bf16[8,64,128]{2,1,0:T(8,128)(2,1)S(1)}, bf16[8,64,128]{2,1,0:T(8,128)(2,1)S(1)}, u32[]{:S(2)}, u32[]{:S(2)}) %collective-permute-start.20) | collective-permute-done | bytes 131104 | tf_op jit(solution)/shard_map/ppermute | solution.py:389
  58.1 0.5 collective-permute-start.21
  58.6 0.0 collective-permute-done.19.refs_5_
  58.6 0.0 collective-permute-done.26.refs_11_
  58.6 0.0 collective-permute-done.24.refs_9_
  58.6 0.8 %collective-permute-done.29.refs_15_ = bf16[8,64,128]{2,1,0:T(8,128)(2,1)S(1)} collective-permute-done((bf16[8,64,128]{2,1,0:T(8,128)(2,1)S(1)}, bf16[8,64,128]{2,1,0:T(8,128)(2,1)S(1)}, u32[]{:S(2)}, u32[]{:S(2)}) %collective-permute-start.29) | collective-permute-done | bytes 131104 | tf_op jit(solution)/shard_map/ppermute | solution.py:389
  59.4 0.2 collective-permute-done.21.refs_7_
  59.6 9.6 %couple.3 = (f32[16,4096]{1,0:T(8,128)}, f32[16,4096]{1,0:T(8,128)}) custom-call(s32[256]{0:T(256)S(1)} %multiply_add_fusion.place, s32[16,40]{1,0:T(8,128)S(1)} %copy-done.2, bf16[8,64,128]{2,1,0:T(8,128)(2,1)S(1)} %get-tuple-element.22.refs_0_, bf16[8,64,128]{2,1,0:T(8,128)(2,1)S(1)} %collective-permute-done.15.refs_1_, ...), custom_call_target="tpu_custom_call" | custom-call | tf_op jit(solution)/shard_map/couple/pallas_call | solution.py:372
  (11 shorter events, 0.0 us)
Async XLA Ops:
  2.7 12.3 %collective-permute-start.7 = (bf16[8,64,128]{2,1,0:T(8,128)(2,1)}, bf16[8,64,128]{2,1,0:T(8,128)(2,1)S(1)}, u32[]{:S(2)}, u32[]{:S(2)}) collective-permute-start(bf16[8,64,128]{2,1,0:T(8,128)(2,1)} %start.1.refs_0_), channel_id=1, source_target_pairs={{0,12},{1,13},{2,14},{3,15},{4,8},{5,9},{6,10},{7,11},{8,4},{9,5},... | collective-permute-start | bytes 393224 | tf_op jit(solution)/shard_map/ppermute | solution.py:389
  7.8 10.8 %collective-permute-start.3 = (bf16[8,64,128]{2,1,0:T(8,128)(2,1)}, bf16[8,64,128]{2,1,0:T(8,128)(2,1)S(1)}, u32[]{:S(2)}, u32[]{:S(2)}) collective-permute-start(bf16[8,64,128]{2,1,0:T(8,128)(2,1)} %start.1.refs_0_), channel_id=1, source_target_pairs={{0,4},{1,5},{2,6},{3,7},{4,0},{5,1},{6,2},{7,3},{8,12},{9,13},{10,... | collective-permute-start | bytes 393224 | tf_op jit(solution)/shard_map/ppermute | solution.py:389
  7.8 10.8 %collective-permute-start.1 = (bf16[8,64,128]{2,1,0:T(8,128)(2,1)}, bf16[8,64,128]{2,1,0:T(8,128)(2,1)S(1)}, u32[]{:S(2)}, u32[]{:S(2)}) collective-permute-start(bf16[8,64,128]{2,1,0:T(8,128)(2,1)} %start.1.refs_0_), channel_id=1, source_target_pairs={{0,2},{1,3},{2,0},{3,1},{4,6},{5,7},{6,4},{7,5},{8,10},{9,11},{10,... | collective-permute-start | bytes 393224 | tf_op jit(solution)/shard_map/ppermute | solution.py:389
  9.3 9.4 %collective-permute-start = (bf16[8,64,128]{2,1,0:T(8,128)(2,1)}, bf16[8,64,128]{2,1,0:T(8,128)(2,1)S(1)}, u32[]{:S(2)}, u32[]{:S(2)}) collective-permute-start(bf16[8,64,128]{2,1,0:T(8,128)(2,1)} %start.1.refs_0_), channel_id=1, source_target_pairs={{0,1},{1,0},{2,3},{3,2},{4,5},{5,4},{6,7},{7,6},{8,9},{9,8},{10,11... | collective-permute-start | bytes 393224 | tf_op jit(solution)/shard_map/ppermute | solution.py:389
  15.1 7.3 %collective-permute-start.10 = (bf16[8,64,128]{2,1,0:T(8,128)(2,1)S(1)}, bf16[8,64,128]{2,1,0:T(8,128)(2,1)S(1)}, u32[]{:S(2)}, u32[]{:S(2)}) collective-permute-start(bf16[8,64,128]{2,1,0:T(8,128)(2,1)S(1)} %collective-permute-done.7.refs_12_), channel_id=1, source_target_pairs={{0,6},{1,7},{2,4},{3,5},{4,2},{5,3},{6,0},{7,1},{8,14},{9,15},{10,... | collective-permute-start | bytes 393224 | tf_op jit(solution)/shard_map/ppermute | solution.py:389
  17.1 9.4 %collective-permute-start.13 = (bf16[8,64,128]{2,1,0:T(8,128)(2,1)S(1)}, bf16[8,64,128]{2,1,0:T(8,128)(2,1)S(1)}, u32[]{:S(2)}, u32[]{:S(2)}) collective-permute-start(bf16[8,64,128]{2,1,0:T(8,128)(2,1)S(1)} %collective-permute-done.7.refs_12_), channel_id=1, source_target_pairs={{0,2},{1,3},{2,0},{3,1},{4,6},{5,7},{6,4},{7,5},{8,10},{9,11},{10,... | collective-permute-start | bytes 393224 | tf_op jit(solution)/shard_map/ppermute | solution.py:389
  18.6 8.4 %collective-permute-start.8 = (bf16[8,64,128]{2,1,0:T(8,128)(2,1)S(1)}, bf16[8,64,128]{2,1,0:T(8,128)(2,1)S(1)}, u32[]{:S(2)}, u32[]{:S(2)}) collective-permute-start(bf16[8,64,128]{2,1,0:T(8,128)(2,1)S(1)} %collective-permute-done.7.refs_12_), channel_id=1, source_target_pairs={{0,4},{1,5},{2,6},{3,7},{4,0},{5,1},{6,2},{7,3},{8,12},{9,13},{10,... | collective-permute-start | bytes 393224 | tf_op jit(solution)/shard_map/ppermute | solution.py:389
  18.6 8.5 %collective-permute-start.12 = (bf16[8,64,128]{2,1,0:T(8,128)(2,1)S(1)}, bf16[8,64,128]{2,1,0:T(8,128)(2,1)S(1)}, u32[]{:S(2)}, u32[]{:S(2)}) collective-permute-start(bf16[8,64,128]{2,1,0:T(8,128)(2,1)S(1)} %collective-permute-done.7.refs_12_), channel_id=1, source_target_pairs={{0,1},{1,0},{2,3},{3,2},{4,5},{5,4},{6,7},{7,6},{8,9},{9,8},{10,11... | collective-permute-start | bytes 393224 | tf_op jit(solution)/shard_map/ppermute | solution.py:389
  18.7 8.8 %collective-permute-start.5 = (bf16[8,64,128]{2,1,0:T(8,128)(2,1)S(1)}, bf16[8,64,128]{2,1,0:T(8,128)(2,1)S(1)}, u32[]{:S(2)}, u32[]{:S(2)}) collective-permute-start(bf16[8,64,128]{2,1,0:T(8,128)(2,1)S(1)} %collective-permute-done.3.refs_4_), channel_id=1, source_target_pairs={{0,2},{1,3},{2,0},{3,1},{4,6},{5,7},{6,4},{7,5},{8,10},{9,11},{10,... | collective-permute-start | bytes 393224 | tf_op jit(solution)/shard_map/ppermute | solution.py:389
  22.3 5.3 %collective-permute-start.4 = (bf16[8,64,128]{2,1,0:T(8,128)(2,1)S(1)}, bf16[8,64,128]{2,1,0:T(8,128)(2,1)S(1)}, u32[]{:S(2)}, u32[]{:S(2)}) collective-permute-start(bf16[8,64,128]{2,1,0:T(8,128)(2,1)S(1)} %collective-permute-done.3.refs_4_), channel_id=1, source_target_pairs={{0,1},{1,0},{2,3},{3,2},{4,5},{5,4},{6,7},{7,6},{8,9},{9,8},{10,11... | collective-permute-start | bytes 393224 | tf_op jit(solution)/shard_map/ppermute | solution.py:389
  22.3 5.7 %copy-start.3 = (s32[256]{0:T(256)S(1)}, s32[256]{0:T(256)}, u32[]{:S(2)}) copy-start(s32[256]{0:T(256)} %param.15) | copy-start | bytes 3076
  22.3 6.7 %copy-start = (bf16[8,64,128]{2,1,0:T(8,128)(2,1)S(1)}, bf16[8,64,128]{2,1,0:T(8,128)(2,1)}, u32[]{:S(2)}) copy-start(bf16[8,64,128]{2,1,0:T(8,128)(2,1)} %start.1.refs_0_) | copy-start | bytes 393220
  22.3 6.7 %copy-start.2 = (s32[16,40]{1,0:T(8,128)S(1)}, s32[16,40]{1,0:T(8,128)}, u32[]{:S(2)}) copy-start(s32[16,40]{1,0:T(8,128)} %partners.3) | copy-start | bytes 7684
  26.5 1.6 %collective-permute-start.2 = (bf16[8,64,128]{2,1,0:T(8,128)(2,1)S(1)}, bf16[8,64,128]{2,1,0:T(8,128)(2,1)S(1)}, u32[]{:S(2)}, u32[]{:S(2)}) collective-permute-start(bf16[8,64,128]{2,1,0:T(8,128)(2,1)S(1)} %collective-permute-done.1.refs_2_), channel_id=1, source_target_pairs={{0,1},{1,0},{2,3},{3,2},{4,5},{5,4},{6,7},{7,6},{8,9},{9,8},{10,11... | collective-permute-start | bytes 393224 | tf_op jit(solution)/shard_map/ppermute | solution.py:389
  27.0 1.3 %collective-permute-start.11 = (bf16[8,64,128]{2,1,0:T(8,128)(2,1)S(1)}, bf16[8,64,128]{2,1,0:T(8,128)(2,1)S(1)}, u32[]{:S(2)}, u32[]{:S(2)}) collective-permute-start(bf16[8,64,128]{2,1,0:T(8,128)(2,1)S(1)} %collective-permute-done.10.refs_10_), channel_id=1, source_target_pairs={{0,1},{1,0},{2,3},{3,2},{4,5},{5,4},{6,7},{7,6},{8,9},{9,8},{10,11... | collective-permute-start | bytes 393224 | tf_op jit(solution)/shard_map/ppermute | solution.py:389
  27.1 1.4 %collective-permute-start.14 = (bf16[8,64,128]{2,1,0:T(8,128)(2,1)S(1)}, bf16[8,64,128]{2,1,0:T(8,128)(2,1)S(1)}, u32[]{:S(2)}, u32[]{:S(2)}) collective-permute-start(bf16[8,64,128]{2,1,0:T(8,128)(2,1)S(1)} %collective-permute-done.13.refs_14_), channel_id=1, source_target_pairs={{0,1},{1,0},{2,3},{3,2},{4,5},{5,4},{6,7},{7,6},{8,9},{9,8},{10,11... | collective-permute-start | bytes 393224 | tf_op jit(solution)/shard_map/ppermute | solution.py:389
  27.5 1.3 %collective-permute-start.9 = (bf16[8,64,128]{2,1,0:T(8,128)(2,1)S(1)}, bf16[8,64,128]{2,1,0:T(8,128)(2,1)S(1)}, u32[]{:S(2)}, u32[]{:S(2)}) collective-permute-start(bf16[8,64,128]{2,1,0:T(8,128)(2,1)S(1)} %collective-permute-done.8.refs_8_), channel_id=1, source_target_pairs={{0,1},{1,0},{2,3},{3,2},{4,5},{5,4},{6,7},{7,6},{8,9},{9,8},{10,11... | collective-permute-start | bytes 393224 | tf_op jit(solution)/shard_map/ppermute | solution.py:389
  27.6 1.4 %collective-permute-start.6 = (bf16[8,64,128]{2,1,0:T(8,128)(2,1)S(1)}, bf16[8,64,128]{2,1,0:T(8,128)(2,1)S(1)}, u32[]{:S(2)}, u32[]{:S(2)}) collective-permute-start(bf16[8,64,128]{2,1,0:T(8,128)(2,1)S(1)} %collective-permute-done.5.refs_6_), channel_id=1, source_target_pairs={{0,1},{1,0},{2,3},{3,2},{4,5},{5,4},{6,7},{7,6},{8,9},{9,8},{10,11... | collective-permute-start | bytes 393224 | tf_op jit(solution)/shard_map/ppermute | solution.py:389
  37.7 0.7 %copy-start.1 = (f32[8,64,128]{2,1,0:T(8,128)}, f32[8,64,128]{2,1,0:T(8,128)S(1)}, u32[]{:S(2)}) copy-start(f32[8,64,128]{2,1,0:T(8,128)S(1)} %get-tuple-element.23.current) | copy-start | bytes 786436
  38.4 8.2 %collective-permute-start.22 = (bf16[8,64,128]{2,1,0:T(8,128)(2,1)S(1)}, bf16[8,64,128]{2,1,0:T(8,128)(2,1)S(1)}, u32[]{:S(2)}, u32[]{:S(2)}) collective-permute-start(bf16[8,64,128]{2,1,0:T(8,128)(2,1)S(1)} %get-tuple-element.22.refs_0_), channel_id=1, source_target_pairs={{0,12},{1,13},{2,14},{3,15},{4,8},{5,9},{6,10},{7,11},{8,4},{9,5},... | collective-permute-start | bytes 393224 | tf_op jit(solution)/shard_map/ppermute | solution.py:389
  39.5 9.5 %collective-permute-start.18 = (bf16[8,64,128]{2,1,0:T(8,128)(2,1)S(1)}, bf16[8,64,128]{2,1,0:T(8,128)(2,1)S(1)}, u32[]{:S(2)}, u32[]{:S(2)}) collective-permute-start(bf16[8,64,128]{2,1,0:T(8,128)(2,1)S(1)} %get-tuple-element.22.refs_0_), channel_id=1, source_target_pairs={{0,4},{1,5},{2,6},{3,7},{4,0},{5,1},{6,2},{7,3},{8,12},{9,13},{10,... | collective-permute-start | bytes 393224 | tf_op jit(solution)/shard_map/ppermute | solution.py:389
  40.5 10.0 %collective-permute-start.16 = (bf16[8,64,128]{2,1,0:T(8,128)(2,1)S(1)}, bf16[8,64,128]{2,1,0:T(8,128)(2,1)S(1)}, u32[]{:S(2)}, u32[]{:S(2)}) collective-permute-start(bf16[8,64,128]{2,1,0:T(8,128)(2,1)S(1)} %get-tuple-element.22.refs_0_), channel_id=1, source_target_pairs={{0,2},{1,3},{2,0},{3,1},{4,6},{5,7},{6,4},{7,5},{8,10},{9,11},{10,... | collective-permute-start | bytes 393224 | tf_op jit(solution)/shard_map/ppermute | solution.py:389
  41.0 9.5 %collective-permute-start.15 = (bf16[8,64,128]{2,1,0:T(8,128)(2,1)S(1)}, bf16[8,64,128]{2,1,0:T(8,128)(2,1)S(1)}, u32[]{:S(2)}, u32[]{:S(2)}) collective-permute-start(bf16[8,64,128]{2,1,0:T(8,128)(2,1)S(1)} %get-tuple-element.22.refs_0_), channel_id=1, source_target_pairs={{0,1},{1,0},{2,3},{3,2},{4,5},{5,4},{6,7},{7,6},{8,9},{9,8},{10,11... | collective-permute-start | bytes 393224 | tf_op jit(solution)/shard_map/ppermute | solution.py:389
  46.6 6.4 %collective-permute-start.25 = (bf16[8,64,128]{2,1,0:T(8,128)(2,1)S(1)}, bf16[8,64,128]{2,1,0:T(8,128)(2,1)S(1)}, u32[]{:S(2)}, u32[]{:S(2)}) collective-permute-start(bf16[8,64,128]{2,1,0:T(8,128)(2,1)S(1)} %collective-permute-done.22.refs_12_), channel_id=1, source_target_pairs={{0,6},{1,7},{2,4},{3,5},{4,2},{5,3},{6,0},{7,1},{8,14},{9,15},{10,... | collective-permute-start | bytes 393224 | tf_op jit(solution)/shard_map/ppermute | solution.py:389
  48.9 6.3 %collective-permute-start.23 = (bf16[8,64,128]{2,1,0:T(8,128)(2,1)S(1)}, bf16[8,64,128]{2,1,0:T(8,128)(2,1)S(1)}, u32[]{:S(2)}, u32[]{:S(2)}) collective-permute-start(bf16[8,64,128]{2,1,0:T(8,128)(2,1)S(1)} %collective-permute-done.22.refs_12_), channel_id=1, source_target_pairs={{0,4},{1,5},{2,6},{3,7},{4,0},{5,1},{6,2},{7,3},{8,12},{9,13},{10,... | collective-permute-start | bytes 393224 | tf_op jit(solution)/shard_map/ppermute | solution.py:389
  49.0 6.6 %collective-permute-start.28 = (bf16[8,64,128]{2,1,0:T(8,128)(2,1)S(1)}, bf16[8,64,128]{2,1,0:T(8,128)(2,1)S(1)}, u32[]{:S(2)}, u32[]{:S(2)}) collective-permute-start(bf16[8,64,128]{2,1,0:T(8,128)(2,1)S(1)} %collective-permute-done.22.refs_12_), channel_id=1, source_target_pairs={{0,2},{1,3},{2,0},{3,1},{4,6},{5,7},{6,4},{7,5},{8,10},{9,11},{10,... | collective-permute-start | bytes 393224 | tf_op jit(solution)/shard_map/ppermute | solution.py:389
  50.5 5.3 %collective-permute-start.27 = (bf16[8,64,128]{2,1,0:T(8,128)(2,1)S(1)}, bf16[8,64,128]{2,1,0:T(8,128)(2,1)S(1)}, u32[]{:S(2)}, u32[]{:S(2)}) collective-permute-start(bf16[8,64,128]{2,1,0:T(8,128)(2,1)S(1)} %collective-permute-done.22.refs_12_), channel_id=1, source_target_pairs={{0,1},{1,0},{2,3},{3,2},{4,5},{5,4},{6,7},{7,6},{8,9},{9,8},{10,11... | collective-permute-start | bytes 393224 | tf_op jit(solution)/shard_map/ppermute | solution.py:389
  50.5 7.6 %collective-permute-start.20 = (bf16[8,64,128]{2,1,0:T(8,128)(2,1)S(1)}, bf16[8,64,128]{2,1,0:T(8,128)(2,1)S(1)}, u32[]{:S(2)}, u32[]{:S(2)}) collective-permute-start(bf16[8,64,128]{2,1,0:T(8,128)(2,1)S(1)} %collective-permute-done.18.refs_4_), channel_id=1, source_target_pairs={{0,2},{1,3},{2,0},{3,1},{4,6},{5,7},{6,4},{7,5},{8,10},{9,11},{10,... | collective-permute-start | bytes 393224 | tf_op jit(solution)/shard_map/ppermute | solution.py:389
  52.9 5.1 %collective-permute-start.17 = (bf16[8,64,128]{2,1,0:T(8,128)(2,1)S(1)}, bf16[8,64,128]{2,1,0:T(8,128)(2,1)S(1)}, u32[]{:S(2)}, u32[]{:S(2)}) collective-permute-start(bf16[8,64,128]{2,1,0:T(8,128)(2,1)S(1)} %collective-permute-done.16.refs_2_), channel_id=1, source_target_pairs={{0,1},{1,0},{2,3},{3,2},{4,5},{5,4},{6,7},{7,6},{8,9},{9,8},{10,11... | collective-permute-start | bytes 393224 | tf_op jit(solution)/shard_map/ppermute | solution.py:389
  55.2 3.4 %collective-permute-start.19 = (bf16[8,64,128]{2,1,0:T(8,128)(2,1)S(1)}, bf16[8,64,128]{2,1,0:T(8,128)(2,1)S(1)}, u32[]{:S(2)}, u32[]{:S(2)}) collective-permute-start(bf16[8,64,128]{2,1,0:T(8,128)(2,1)S(1)} %collective-permute-done.18.refs_4_), channel_id=1, source_target_pairs={{0,1},{1,0},{2,3},{3,2},{4,5},{5,4},{6,7},{7,6},{8,9},{9,8},{10,11... | collective-permute-start | bytes 393224 | tf_op jit(solution)/shard_map/ppermute | solution.py:389
  55.6 3.0 %collective-permute-start.26 = (bf16[8,64,128]{2,1,0:T(8,128)(2,1)S(1)}, bf16[8,64,128]{2,1,0:T(8,128)(2,1)S(1)}, u32[]{:S(2)}, u32[]{:S(2)}) collective-permute-start(bf16[8,64,128]{2,1,0:T(8,128)(2,1)S(1)} %collective-permute-done.25.refs_10_), channel_id=1, source_target_pairs={{0,1},{1,0},{2,3},{3,2},{4,5},{5,4},{6,7},{7,6},{8,9},{9,8},{10,11... | collective-permute-start | bytes 393224 | tf_op jit(solution)/shard_map/ppermute | solution.py:389
  55.7 2.8 %collective-permute-start.24 = (bf16[8,64,128]{2,1,0:T(8,128)(2,1)S(1)}, bf16[8,64,128]{2,1,0:T(8,128)(2,1)S(1)}, u32[]{:S(2)}, u32[]{:S(2)}) collective-permute-start(bf16[8,64,128]{2,1,0:T(8,128)(2,1)S(1)} %collective-permute-done.23.refs_8_), channel_id=1, source_target_pairs={{0,1},{1,0},{2,3},{3,2},{4,5},{5,4},{6,7},{7,6},{8,9},{9,8},{10,11... | collective-permute-start | bytes 393224 | tf_op jit(solution)/shard_map/ppermute | solution.py:389
  58.1 1.3 %collective-permute-start.29 = (bf16[8,64,128]{2,1,0:T(8,128)(2,1)S(1)}, bf16[8,64,128]{2,1,0:T(8,128)(2,1)S(1)}, u32[]{:S(2)}, u32[]{:S(2)}) collective-permute-start(bf16[8,64,128]{2,1,0:T(8,128)(2,1)S(1)} %collective-permute-done.28.refs_14_), channel_id=1, source_target_pairs={{0,1},{1,0},{2,3},{3,2},{4,5},{5,4},{6,7},{7,6},{8,9},{9,8},{10,11... | collective-permute-start | bytes 393224 | tf_op jit(solution)/shard_map/ppermute | solution.py:389
  58.1 1.5 %collective-permute-start.21 = (bf16[8,64,128]{2,1,0:T(8,128)(2,1)S(1)}, bf16[8,64,128]{2,1,0:T(8,128)(2,1)S(1)}, u32[]{:S(2)}, u32[]{:S(2)}) collective-permute-start(bf16[8,64,128]{2,1,0:T(8,128)(2,1)S(1)} %collective-permute-done.20.refs_6_), channel_id=1, source_target_pairs={{0,1},{1,0},{2,3},{3,2},{4,5},{5,4},{6,7},{7,6},{8,9},{9,8},{10,11... | collective-permute-start | bytes 393224 | tf_op jit(solution)/shard_map/ppermute | solution.py:389

commit v7 on v6

--- a/solution.py
+++ b/solution.py
@@ -10,17 +10,18 @@
 from jax.sharding import PartitionSpec as P
 
 FREQUENCY = 0.25
-SLOTS_AT_ONCE = 8
+BUFFERS = 8
 ENTRIES = 16
 TILES = 8
 FIRST = 6
-AHEAD = 4
+AHEAD = 8
 CUTS = 2
 NT = (((1,), (1,)), ((), ()))
 VMEM = pl.BlockSpec(memory_space=pltpu.VMEM)
 SMEM = pl.BlockSpec(memory_space=pltpu.SMEM)
 VMEM_LIMIT = 58 * 2**20
 STATE_ROOM = 16
+FLAT_LIMIT = 8 * 2**20
 COUPLE_LIMIT = 50 * 2**20
 HBM = pl.BlockSpec(memory_space=pltpu.HBM)
 
@@ -263,6 +264,7 @@
             pltpu.SemaphoreType.DMA,
         ],
         cost_estimate=pl.CostEstimate(flops=0, bytes_accessed=32 * right_side.size, transcendentals=0),
+        compiler_params=pltpu.CompilerParams(vmem_limit_bytes=FLAT_LIMIT),
         name="flat_state",
     )(pno_count, occ_energy, current, right_side, pno_energy)
 
@@ -274,12 +276,16 @@
     slots, pairs, width, lanes = held.shape
     half = slots // 2
 
+    parts = ((0, slots // 4), (slots // 4, slots - slots // 4))
+
     def fetch(i):
-        return pltpu.make_async_copy(margins.at[i], held.at[i], arrived.at[i])
-
-    fetch_state = pltpu.make_async_copy(state.at[:4], steady, arrived.at[slots])
-    for i in range(SLOTS_AT_ONCE):
+        some = pl.ds(*parts[i])
+        return pltpu.make_async_copy(margins.at[some], held.at[some], arrived.at[i])
+
+    fetch_state = pltpu.make_async_copy(state.at[:4], steady, arrived.at[len(parts)])
+    for i in range(len(parts)):
         fetch(i).start()
+    fetch_state.start()
     left = left_lanes(width)
     at = 0
     for piece in gathered:
@@ -303,20 +309,12 @@
             product = jnp.dot(held[s, k], weights, preferred_element_type=jnp.float32)
             halves[at, :, k * lanes : (k + 1) * lanes] = product.astype(jnp.bfloat16)
         margin = jnp.concatenate([held[s, k] for k in range(pairs)], axis=1)
-        coupled[pl.ds(s * width, width)] = lax.dot_general(halves[at], margin, NT, preferred_element_type=jnp.float32)
-
-    for i in range(SLOTS_AT_ONCE, slots):
-        fetch(i).start()
-    fetch_state.start()
-
-    def some_slots(i, carry):
-        for at in range(SLOTS_AT_ONCE):
-            fetch(i * SLOTS_AT_ONCE + at).wait()
-        for at in range(SLOTS_AT_ONCE):
-            one_slot(i * SLOTS_AT_ONCE + at, at)
-        return carry
-
-    lax.fori_loop(0, slots // SLOTS_AT_ONCE, some_slots, 0)
+        coupled[s * width : (s + 1) * width] = lax.dot_general(halves[at], margin, NT, preferred_element_type=jnp.float32)
+
+    for i, (first, some) in enumerate(parts):
+        fetch(i).wait()
+        for s in range(first, first + some):
+            one_slot(s, s % BUFFERS)
 
     fetch_state.wait()
     if not last:
@@ -362,10 +360,10 @@
     scratch = [
         pltpu.VMEM((2 * devices * slots, width, lanes), jnp.bfloat16),
         pltpu.VMEM((slots, pairs, width, lanes), jnp.bfloat16),
-        pltpu.VMEM((SLOTS_AT_ONCE, width, pairs * lanes), jnp.bfloat16),
+        pltpu.VMEM((BUFFERS, width, pairs * lanes), jnp.bfloat16),
         pltpu.VMEM((slots * width, width), jnp.float32),
         pltpu.VMEM((4, *state.shape[1:]), jnp.float32),
-        pltpu.SemaphoreType.DMA((slots + 1,)),
+        pltpu.SemaphoreType.DMA((3,)),
     ]
     if last:
         scratch += [pltpu.VMEM((2, slots, width * width), jnp.float32), pltpu.SemaphoreType.DMA((2, CUTS))]

time: 69.6 us -> 68.1 us (0.978)
  Pallas kernels: 32.9 us -> 30.8 us
  local copies, waits for them, and re-layouts: 0.71 us -> 2.04 us
  waiting for transfers between devices: 14.3 us -> 13.5 us
    unnamed x8 -> x16, local copies, waits for them, and re-layouts: 0.71 us -> 2.04 us
    pallas_call x1, Pallas kernels: 2.73 us -> 1.52 us  [flat_state(): pl.pallas_call(flat_kernel, in_specs=[SMEM, SMEM, VMEM, VMEM, VMEM], out_...]
    pallas_call x2, Pallas kernels: 18.3 us -> 17.3 us  [couple(): pl.pallas_call(functools.partial(couple_kernel, last, len(gathered)), in_...]
    ppermute x30, waiting for transfers between devices: 14.3 us -> 13.5 us  [swap(): return lax.ppermute(piece, 'pair', [(i, i ^ other) for i in range(devices)])]
  transfers between devices with their start and end apart: 30 -> 30, of which waited for: 12 -> 12; matrix products, arithmetic and copies ran while one was open for 0% -> 0% of each run, Pallas kernels for 18% -> 17%
where the time goes in v7:
time: 68.1 us; the launch traced here: 67.9 us
  Pallas kernels  30.8 us (45%)
  starting transfers between devices  20.6 us (30%)
  waiting for transfers between devices  13.5 us (20%)
  local copies, waits for them, and re-layouts  2.04 us (3%)
  between operations  0.95 us (1%)
    ppermute x30, starting transfers between devices, swap(): return lax.ppermute(piece, 'pair', [(i, i ^ other) for i in range(devices)])  20.6 us
    pallas_call x2, Pallas kernels, couple(): pl.pallas_call(functools.partial(couple_kernel, last, len(gathered)), in_...  17.3 us
    ppermute x30, waiting for transfers between devices, swap(): return lax.ppermute(piece, 'pair', [(i, i ^ other) for i in range(devices)])  13.5 us
    pallas_call x1, Pallas kernels, margin_tiles(): pl.pallas_call(functools.partial(margin_kernel, 0), in_specs=[VMEM, HBM],...  5.73 us
    pallas_call x1, Pallas kernels, more_tiles(): pl.pallas_call(functools.partial(margin_kernel, FIRST), in_specs=[VMEM, H...  4.09 us
    pallas_call x1, Pallas kernels, start(): pl.pallas_call(start_kernel, in_specs=[SMEM, SMEM, VMEM, VMEM], out_specs...  2.12 us
    unnamed x16, local copies, waits for them, and re-layouts  2.04 us
    pallas_call x1, Pallas kernels, flat_state(): pl.pallas_call(flat_kernel, in_specs=[SMEM, SMEM, VMEM, VMEM, VMEM], out_...  1.52 us
  transfers between devices with their start and end apart: 30, of which 12 were waited for; matrix products, arithmetic and copies ran while one was open for 0% of the time, Pallas kernels for 17%

profile of v7, /device:TPU:0, one launch (start us, length us, event | category | flops | bytes accessed | tf_op | source)
XLA Modules:
  0.0 67.9 jit_solution(3945751569735431196)
XLA Ops:
  0.6 2.1 %start.1.refs_0_ = bf16[8,64,128]{2,1,0:T(8,128)(2,1)} custom-call(s32[16]{0:T(128)} %count.3, f32[16]{0:T(128)} %occ.3, f32[16,4096]{1,0:T(8,128)} %right.3, f32[16,64]{1,0:T(8,128)} %energy.3), custom_call_target="tpu_custom_call" | custom-call | tf_op jit(solution)/shard_map/start/pallas_call | solution.py:72
  2.7 5.0 %collective-permute-start.7 = (bf16[8,64,128]{2,1,0:T(8,128)(2,1)}, bf16[8,64,128]{2,1,0:T(8,128)(2,1)S(1)}, u32[]{:S(2)}, u32[]{:S(2)}) collective-permute-start(bf16[8,64,128]{2,1,0:T(8,128)(2,1)} %start.1.refs_0_), channel_id=1, source_target_pairs={{0,12},{1,13},{2,14},{3,15},{4,8},{5,9},{6,10},{7,11},{8,4},{9,5},... | collective-permute-start | bytes 393224 | tf_op jit(solution)/shard_map/ppermute | solution.py:387
  7.8 0.0 collective-permute-start.3
  7.8 1.5 %collective-permute-start.1 = (bf16[8,64,128]{2,1,0:T(8,128)(2,1)}, bf16[8,64,128]{2,1,0:T(8,128)(2,1)S(1)}, u32[]{:S(2)}, u32[]{:S(2)}) collective-permute-start(bf16[8,64,128]{2,1,0:T(8,128)(2,1)} %start.1.refs_0_), channel_id=1, source_target_pairs={{0,2},{1,3},{2,0},{3,1},{4,6},{5,7},{6,4},{7,5},{8,10},{9,11},{10,... | collective-permute-start | bytes 393224 | tf_op jit(solution)/shard_map/ppermute | solution.py:387
  9.3 0.0 collective-permute-start
  9.3 5.7 %margin_tiles.1.refs_0_ = bf16[320,64,128]{2,1,0:T(8,128)(2,1)} custom-call(bf16[128,256]{1,0:T(8,128)(2,1)} %constant.58.clone.pick, bf16[640,4096]{1,0:T(8,128)(2,1)} %bitcast.4), custom_call_target="tpu_custom_call" | custom-call | bytes 10485760 | tf_op jit(solution)/shard_map/margin_tiles/pallas_call | solution.py:180
  15.1 0.0 collective-permute-done.7.refs_12_
  15.1 2.0 %collective-permute-start.10 = (bf16[8,64,128]{2,1,0:T(8,128)(2,1)S(1)}, bf16[8,64,128]{2,1,0:T(8,128)(2,1)S(1)}, u32[]{:S(2)}, u32[]{:S(2)}) collective-permute-start(bf16[8,64,128]{2,1,0:T(8,128)(2,1)S(1)} %collective-permute-done.7.refs_12_), channel_id=1, source_target_pairs={{0,6},{1,7},{2,4},{3,5},{4,2},{5,3},{6,0},{7,1},{8,14},{9,15},{10,... | collective-permute-start | bytes 393224 | tf_op jit(solution)/shard_map/ppermute | solution.py:387
  17.1 1.5 %collective-permute-start.13 = (bf16[8,64,128]{2,1,0:T(8,128)(2,1)S(1)}, bf16[8,64,128]{2,1,0:T(8,128)(2,1)S(1)}, u32[]{:S(2)}, u32[]{:S(2)}) collective-permute-start(bf16[8,64,128]{2,1,0:T(8,128)(2,1)S(1)} %collective-permute-done.7.refs_12_), channel_id=1, source_target_pairs={{0,2},{1,3},{2,0},{3,1},{4,6},{5,7},{6,4},{7,5},{8,10},{9,11},{10,... | collective-permute-start | bytes 393224 | tf_op jit(solution)/shard_map/ppermute | solution.py:387
  18.6 0.0 collective-permute-done.3.refs_4_
  18.6 0.0 collective-permute-start.8
  18.6 0.0 collective-permute-done.1.refs_2_
  18.6 0.1 collective-permute-start.12
  18.7 0.0 collective-permute-done.refs_1_
  18.7 0.6 collective-permute-start.5
  19.3 3.0 %collective-permute-done.10.refs_10_ = bf16[8,64,128]{2,1,0:T(8,128)(2,1)S(1)} collective-permute-done((bf16[8,64,128]{2,1,0:T(8,128)(2,1)S(1)}, bf16[8,64,128]{2,1,0:T(8,128)(2,1)S(1)}, u32[]{:S(2)}, u32[]{:S(2)}) %collective-permute-start.10) | collective-permute-done | bytes 131104 | tf_op jit(solution)/shard_map/ppermute | solution.py:387
  22.3 0.0 collective-permute-start.4
  22.4 4.1 %more_tiles.1 = (bf16[320,64,128]{2,1,0:T(8,128)(2,1)}, f32[16,8,64,128]{3,2,1,0:T(8,128)}) custom-call(bf16[128,256]{1,0:T(8,128)(2,1)} %constant.58.clone.pick, bf16[640,4096]{1,0:T(8,128)(2,1)} %bitcast.5, bf16[320,64,128]{2,1,0:T(8,128)(2,1)} %margin_tiles.1.refs_0_, s32[16]{0:T(128)} %count.3, f32[16]{0:T(128)} %occ.3, ...), custom_call_target="tpu_custom_call", output_to_operand_aliasing={{0}: (2, {})} | custom-call | bytes 10485760 | tf_op jit(solution)/shard_map/more_tiles/pallas_call | solution.py:197
  26.5 0.0 collective-permute-done.13.refs_14_
  26.5 0.6 collective-permute-start.2
  27.0 0.0 collective-permute-done.8.refs_8_
  27.0 0.1 collective-permute-start.11
  27.1 0.0 collective-permute-done.12.refs_13_
  27.1 0.4 collective-permute-start.14
  27.5 0.0 collective-permute-done.5.refs_6_
  27.5 0.1 collective-permute-start.9
  27.6 0.0 collective-permute-done.4.refs_5_
  27.6 0.4 collective-permute-start.6
  28.1 0.0 collective-permute-done.2.refs_3_
  28.1 0.3 collective-permute-done.11.refs_11_
  28.4 0.2 collective-permute-done.14.refs_15_
  28.6 0.3 collective-permute-done.9.refs_9_
  28.9 0.2 collective-permute-done.6.refs_7_
  29.1 0.0 copy-start.5
  29.1 0.0 copy-start.6
  29.1 8.2 %couple.2 = (f32[8,64,128]{2,1,0:T(8,128)S(1)}, bf16[8,64,128]{2,1,0:T(8,128)(2,1)S(1)}) custom-call(s32[256]{0:T(256)S(1)} %multiply_add_fusion.place, s32[16,40]{1,0:T(8,128)S(1)} %copy-done.4, bf16[8,64,128]{2,1,0:T(8,128)(2,1)S(1)} %copy-done.2, bf16[8,64,128]{2,1,0:T(8,128)(2,1)S(1)} %collective-permute-done.refs_1_, ...), custom_call_target="tpu_custom_call" | custom-call | tf_op jit(solution)/shard_map/couple/pallas_call | solution.py:370
  37.3 1.2 %collective-permute-start.22 = (bf16[8,64,128]{2,1,0:T(8,128)(2,1)S(1)}, bf16[8,64,128]{2,1,0:T(8,128)(2,1)S(1)}, u32[]{:S(2)}, u32[]{:S(2)}) collective-permute-start(bf16[8,64,128]{2,1,0:T(8,128)(2,1)S(1)} %get-tuple-element.22.refs_0_), channel_id=1, source_target_pairs={{0,12},{1,13},{2,14},{3,15},{4,8},{5,9},{6,10},{7,11},{8,4},{9,5},... | collective-permute-start | bytes 393224 | tf_op jit(solution)/shard_map/ppermute | solution.py:387
  38.5 1.0 %collective-permute-start.18 = (bf16[8,64,128]{2,1,0:T(8,128)(2,1)S(1)}, bf16[8,64,128]{2,1,0:T(8,128)(2,1)S(1)}, u32[]{:S(2)}, u32[]{:S(2)}) collective-permute-start(bf16[8,64,128]{2,1,0:T(8,128)(2,1)S(1)} %get-tuple-element.22.refs_0_), channel_id=1, source_target_pairs={{0,4},{1,5},{2,6},{3,7},{4,0},{5,1},{6,2},{7,3},{8,12},{9,13},{10,... | collective-permute-start | bytes 393224 | tf_op jit(solution)/shard_map/ppermute | solution.py:387
  39.5 0.5 collective-permute-start.16
  40.0 0.0 collective-permute-start.15
  40.0 1.5 %flat_state.1.refs_17_ = f32[16,16,4096]{2,1,0:T(8,128)S(1)} custom-call(s32[16]{0:T(128)S(1)} %copy-done.5, f32[16]{0:T(128)S(1)} %copy-done.6, f32[8,64,128]{2,1,0:T(8,128)S(1)} %get-tuple-element.23.current, f32[16,4096]{1,0:T(8,128)S(1)} %copy-done.1, f32[16,64]{1,0:T(8,128)S(1)} %copy-done.3), custom_call_target="tpu_custom_call" | custom-call | bytes 2097152 | tf_op jit(solution)/shard_map/flat_state/pallas_call | solution.py:256
  41.6 2.0 %copy-done = f32[16,16,4096]{2,1,0:T(8,128)} copy-done((f32[16,16,4096]{2,1,0:T(8,128)}, f32[16,16,4096]{2,1,0:T(8,128)S(1)}, u32[]{:S(2)}) %copy-start) | copy-done | bytes 4194328
  43.6 2.0 %collective-permute-done.22.refs_12_ = bf16[8,64,128]{2,1,0:T(8,128)(2,1)S(1)} collective-permute-done((bf16[8,64,128]{2,1,0:T(8,128)(2,1)S(1)}, bf16[8,64,128]{2,1,0:T(8,128)(2,1)S(1)}, u32[]{:S(2)}, u32[]{:S(2)}) %collective-permute-start.22) | collective-permute-done | bytes 131104 | tf_op jit(solution)/shard_map/ppermute | solution.py:387
  45.6 2.3 %collective-permute-start.25 = (bf16[8,64,128]{2,1,0:T(8,128)(2,1)S(1)}, bf16[8,64,128]{2,1,0:T(8,128)(2,1)S(1)}, u32[]{:S(2)}, u32[]{:S(2)}) collective-permute-start(bf16[8,64,128]{2,1,0:T(8,128)(2,1)S(1)} %collective-permute-done.22.refs_12_), channel_id=1, source_target_pairs={{0,6},{1,7},{2,4},{3,5},{4,2},{5,3},{6,0},{7,1},{8,14},{9,15},{10,... | collective-permute-start | bytes 393224 | tf_op jit(solution)/shard_map/ppermute | solution.py:387
  47.9 0.1 collective-permute-start.23
  48.0 1.5 %collective-permute-start.28 = (bf16[8,64,128]{2,1,0:T(8,128)(2,1)S(1)}, bf16[8,64,128]{2,1,0:T(8,128)(2,1)S(1)}, u32[]{:S(2)}, u32[]{:S(2)}) collective-permute-start(bf16[8,64,128]{2,1,0:T(8,128)(2,1)S(1)} %collective-permute-done.22.refs_12_), channel_id=1, source_target_pairs={{0,2},{1,3},{2,0},{3,1},{4,6},{5,7},{6,4},{7,5},{8,10},{9,11},{10,... | collective-permute-start | bytes 393224 | tf_op jit(solution)/shard_map/ppermute | solution.py:387
  49.4 0.0 collective-permute-done.15.refs_1_
  49.5 0.6 collective-permute-start.20
  50.1 1.9 %collective-permute-done.25.refs_10_ = bf16[8,64,128]{2,1,0:T(8,128)(2,1)S(1)} collective-permute-done((bf16[8,64,128]{2,1,0:T(8,128)(2,1)S(1)}, bf16[8,64,128]{2,1,0:T(8,128)(2,1)S(1)}, u32[]{:S(2)}, u32[]{:S(2)}) %collective-permute-start.25) | collective-permute-done | bytes 131104 | tf_op jit(solution)/shard_map/ppermute | solution.py:387
  52.0 0.0 collective-permute-start.17
  52.0 2.2 %collective-permute-done.23.refs_8_ = bf16[8,64,128]{2,1,0:T(8,128)(2,1)S(1)} collective-permute-done((bf16[8,64,128]{2,1,0:T(8,128)(2,1)S(1)}, bf16[8,64,128]{2,1,0:T(8,128)(2,1)S(1)}, u32[]{:S(2)}, u32[]{:S(2)}) %collective-permute-start.23) | collective-permute-done | bytes 131104 | tf_op jit(solution)/shard_map/ppermute | solution.py:387
  54.2 0.0 collective-permute-start.19
  54.2 0.4 collective-permute-done.28.refs_14_
  54.6 0.1 collective-permute-start.26
  54.7 0.4 collective-permute-start.24
  55.1 2.0 %collective-permute-done.20.refs_6_ = bf16[8,64,128]{2,1,0:T(8,128)(2,1)S(1)} collective-permute-done((bf16[8,64,128]{2,1,0:T(8,128)(2,1)S(1)}, bf16[8,64,128]{2,1,0:T(8,128)(2,1)S(1)}, u32[]{:S(2)}, u32[]{:S(2)}) %collective-permute-start.20) | collective-permute-done | bytes 131104 | tf_op jit(solution)/shard_map/ppermute | solution.py:387
  57.0 0.0 collective-permute-start.29
  57.1 0.0 collective-permute-done.17.refs_3_
  57.1 0.5 collective-permute-start.21
  57.6 0.0 collective-permute-done.19.refs_5_
  57.6 0.0 collective-permute-done.26.refs_11_
  57.6 0.8 %collective-permute-done.29.refs_15_ = bf16[8,64,128]{2,1,0:T(8,128)(2,1)S(1)} collective-permute-done((bf16[8,64,128]{2,1,0:T(8,128)(2,1)S(1)}, bf16[8,64,128]{2,1,0:T(8,128)(2,1)S(1)}, u32[]{:S(2)}, u32[]{:S(2)}) %collective-permute-start.29) | collective-permute-done | bytes 131104 | tf_op jit(solution)/shard_map/ppermute | solution.py:387
  58.4 0.2 collective-permute-done.21.refs_7_
  58.6 9.1 %couple.3 = (f32[16,4096]{1,0:T(8,128)}, f32[16,4096]{1,0:T(8,128)}) custom-call(s32[256]{0:T(256)S(1)} %multiply_add_fusion.place, s32[16,40]{1,0:T(8,128)S(1)} %copy-done.4, bf16[8,64,128]{2,1,0:T(8,128)(2,1)S(1)} %get-tuple-element.22.refs_0_, bf16[8,64,128]{2,1,0:T(8,128)(2,1)S(1)} %collective-permute-done.15.refs_1_, ...), custom_call_target="tpu_custom_call" | custom-call | tf_op jit(solution)/shard_map/couple/pallas_call | solution.py:370
  (19 shorter events, 0.1 us)
Async XLA Ops:
  2.7 12.3 %collective-permute-start.7 = (bf16[8,64,128]{2,1,0:T(8,128)(2,1)}, bf16[8,64,128]{2,1,0:T(8,128)(2,1)S(1)}, u32[]{:S(2)}, u32[]{:S(2)}) collective-permute-start(bf16[8,64,128]{2,1,0:T(8,128)(2,1)} %start.1.refs_0_), channel_id=1, source_target_pairs={{0,12},{1,13},{2,14},{3,15},{4,8},{5,9},{6,10},{7,11},{8,4},{9,5},... | collective-permute-start | bytes 393224 | tf_op jit(solution)/shard_map/ppermute | solution.py:387
  7.8 10.8 %collective-permute-start.3 = (bf16[8,64,128]{2,1,0:T(8,128)(2,1)}, bf16[8,64,128]{2,1,0:T(8,128)(2,1)S(1)}, u32[]{:S(2)}, u32[]{:S(2)}) collective-permute-start(bf16[8,64,128]{2,1,0:T(8,128)(2,1)} %start.1.refs_0_), channel_id=1, source_target_pairs={{0,4},{1,5},{2,6},{3,7},{4,0},{5,1},{6,2},{7,3},{8,12},{9,13},{10,... | collective-permute-start | bytes 393224 | tf_op jit(solution)/shard_map/ppermute | solution.py:387
  7.8 10.8 %collective-permute-start.1 = (bf16[8,64,128]{2,1,0:T(8,128)(2,1)}, bf16[8,64,128]{2,1,0:T(8,128)(2,1)S(1)}, u32[]{:S(2)}, u32[]{:S(2)}) collective-permute-start(bf16[8,64,128]{2,1,0:T(8,128)(2,1)} %start.1.refs_0_), channel_id=1, source_target_pairs={{0,2},{1,3},{2,0},{3,1},{4,6},{5,7},{6,4},{7,5},{8,10},{9,11},{10,... | collective-permute-start | bytes 393224 | tf_op jit(solution)/shard_map/ppermute | solution.py:387
  9.3 9.4 %collective-permute-start = (bf16[8,64,128]{2,1,0:T(8,128)(2,1)}, bf16[8,64,128]{2,1,0:T(8,128)(2,1)S(1)}, u32[]{:S(2)}, u32[]{:S(2)}) collective-permute-start(bf16[8,64,128]{2,1,0:T(8,128)(2,1)} %start.1.refs_0_), channel_id=1, source_target_pairs={{0,1},{1,0},{2,3},{3,2},{4,5},{5,4},{6,7},{7,6},{8,9},{9,8},{10,11... | collective-permute-start | bytes 393224 | tf_op jit(solution)/shard_map/ppermute | solution.py:387
  15.1 7.3 %collective-permute-start.10 = (bf16[8,64,128]{2,1,0:T(8,128)(2,1)S(1)}, bf16[8,64,128]{2,1,0:T(8,128)(2,1)S(1)}, u32[]{:S(2)}, u32[]{:S(2)}) collective-permute-start(bf16[8,64,128]{2,1,0:T(8,128)(2,1)S(1)} %collective-permute-done.7.refs_12_), channel_id=1, source_target_pairs={{0,6},{1,7},{2,4},{3,5},{4,2},{5,3},{6,0},{7,1},{8,14},{9,15},{10,... | collective-permute-start | bytes 393224 | tf_op jit(solution)/shard_map/ppermute | solution.py:387
  17.1 9.4 %collective-permute-start.13 = (bf16[8,64,128]{2,1,0:T(8,128)(2,1)S(1)}, bf16[8,64,128]{2,1,0:T(8,128)(2,1)S(1)}, u32[]{:S(2)}, u32[]{:S(2)}) collective-permute-start(bf16[8,64,128]{2,1,0:T(8,128)(2,1)S(1)} %collective-permute-done.7.refs_12_), channel_id=1, source_target_pairs={{0,2},{1,3},{2,0},{3,1},{4,6},{5,7},{6,4},{7,5},{8,10},{9,11},{10,... | collective-permute-start | bytes 393224 | tf_op jit(solution)/shard_map/ppermute | solution.py:387
  18.6 8.4 %collective-permute-start.8 = (bf16[8,64,128]{2,1,0:T(8,128)(2,1)S(1)}, bf16[8,64,128]{2,1,0:T(8,128)(2,1)S(1)}, u32[]{:S(2)}, u32[]{:S(2)}) collective-permute-start(bf16[8,64,128]{2,1,0:T(8,128)(2,1)S(1)} %collective-permute-done.7.refs_12_), channel_id=1, source_target_pairs={{0,4},{1,5},{2,6},{3,7},{4,0},{5,1},{6,2},{7,3},{8,12},{9,13},{10,... | collective-permute-start | bytes 393224 | tf_op jit(solution)/shard_map/ppermute | solution.py:387
  18.6 8.5 %collective-permute-start.12 = (bf16[8,64,128]{2,1,0:T(8,128)(2,1)S(1)}, bf16[8,64,128]{2,1,0:T(8,128)(2,1)S(1)}, u32[]{:S(2)}, u32[]{:S(2)}) collective-permute-start(bf16[8,64,128]{2,1,0:T(8,128)(2,1)S(1)} %collective-permute-done.7.refs_12_), channel_id=1, source_target_pairs={{0,1},{1,0},{2,3},{3,2},{4,5},{5,4},{6,7},{7,6},{8,9},{9,8},{10,11... | collective-permute-start | bytes 393224 | tf_op jit(solution)/shard_map/ppermute | solution.py:387
  18.7 8.8 %collective-permute-start.5 = (bf16[8,64,128]{2,1,0:T(8,128)(2,1)S(1)}, bf16[8,64,128]{2,1,0:T(8,128)(2,1)S(1)}, u32[]{:S(2)}, u32[]{:S(2)}) collective-permute-start(bf16[8,64,128]{2,1,0:T(8,128)(2,1)S(1)} %collective-permute-done.3.refs_4_), channel_id=1, source_target_pairs={{0,2},{1,3},{2,0},{3,1},{4,6},{5,7},{6,4},{7,5},{8,10},{9,11},{10,... | collective-permute-start | bytes 393224 | tf_op jit(solution)/shard_map/ppermute | solution.py:387
  22.3 5.3 %collective-permute-start.4 = (bf16[8,64,128]{2,1,0:T(8,128)(2,1)S(1)}, bf16[8,64,128]{2,1,0:T(8,128)(2,1)S(1)}, u32[]{:S(2)}, u32[]{:S(2)}) collective-permute-start(bf16[8,64,128]{2,1,0:T(8,128)(2,1)S(1)} %collective-permute-done.3.refs_4_), channel_id=1, source_target_pairs={{0,1},{1,0},{2,3},{3,2},{4,5},{5,4},{6,7},{7,6},{8,9},{9,8},{10,11... | collective-permute-start | bytes 393224 | tf_op jit(solution)/shard_map/ppermute | solution.py:387
  22.3 5.7 %copy-start.7 = (s32[256]{0:T(256)S(1)}, s32[256]{0:T(256)}, u32[]{:S(2)}) copy-start(s32[256]{0:T(256)} %param.15) | copy-start | bytes 3076
  22.3 6.7 %copy-start.2 = (bf16[8,64,128]{2,1,0:T(8,128)(2,1)S(1)}, bf16[8,64,128]{2,1,0:T(8,128)(2,1)}, u32[]{:S(2)}) copy-start(bf16[8,64,128]{2,1,0:T(8,128)(2,1)} %start.1.refs_0_) | copy-start | bytes 393220
  22.3 6.7 %copy-start.4 = (s32[16,40]{1,0:T(8,128)S(1)}, s32[16,40]{1,0:T(8,128)}, u32[]{:S(2)}) copy-start(s32[16,40]{1,0:T(8,128)} %partners.3) | copy-start | bytes 7684
  26.5 1.6 %collective-permute-start.2 = (bf16[8,64,128]{2,1,0:T(8,128)(2,1)S(1)}, bf16[8,64,128]{2,1,0:T(8,128)(2,1)S(1)}, u32[]{:S(2)}, u32[]{:S(2)}) collective-permute-start(bf16[8,64,128]{2,1,0:T(8,128)(2,1)S(1)} %collective-permute-done.1.refs_2_), channel_id=1, source_target_pairs={{0,1},{1,0},{2,3},{3,2},{4,5},{5,4},{6,7},{7,6},{8,9},{9,8},{10,11... | collective-permute-start | bytes 393224 | tf_op jit(solution)/shard_map/ppermute | solution.py:387
  27.0 1.3 %collective-permute-start.11 = (bf16[8,64,128]{2,1,0:T(8,128)(2,1)S(1)}, bf16[8,64,128]{2,1,0:T(8,128)(2,1)S(1)}, u32[]{:S(2)}, u32[]{:S(2)}) collective-permute-start(bf16[8,64,128]{2,1,0:T(8,128)(2,1)S(1)} %collective-permute-done.10.refs_10_), channel_id=1, source_target_pairs={{0,1},{1,0},{2,3},{3,2},{4,5},{5,4},{6,7},{7,6},{8,9},{9,8},{10,11... | collective-permute-start | bytes 393224 | tf_op jit(solution)/shard_map/ppermute | solution.py:387
  27.1 1.4 %collective-permute-start.14 = (bf16[8,64,128]{2,1,0:T(8,128)(2,1)S(1)}, bf16[8,64,128]{2,1,0:T(8,128)(2,1)S(1)}, u32[]{:S(2)}, u32[]{:S(2)}) collective-permute-start(bf16[8,64,128]{2,1,0:T(8,128)(2,1)S(1)} %collective-permute-done.13.refs_14_), channel_id=1, source_target_pairs={{0,1},{1,0},{2,3},{3,2},{4,5},{5,4},{6,7},{7,6},{8,9},{9,8},{10,11... | collective-permute-start | bytes 393224 | tf_op jit(solution)/shard_map/ppermute | solution.py:387
  27.5 1.3 %collective-permute-start.9 = (bf16[8,64,128]{2,1,0:T(8,128)(2,1)S(1)}, bf16[8,64,128]{2,1,0:T(8,128)(2,1)S(1)}, u32[]{:S(2)}, u32[]{:S(2)}) collective-permute-start(bf16[8,64,128]{2,1,0:T(8,128)(2,1)S(1)} %collective-permute-done.8.refs_8_), channel_id=1, source_target_pairs={{0,1},{1,0},{2,3},{3,2},{4,5},{5,4},{6,7},{7,6},{8,9},{9,8},{10,11... | collective-permute-start | bytes 393224 | tf_op jit(solution)/shard_map/ppermute | solution.py:387
  27.6 1.5 %collective-permute-start.6 = (bf16[8,64,128]{2,1,0:T(8,128)(2,1)S(1)}, bf16[8,64,128]{2,1,0:T(8,128)(2,1)S(1)}, u32[]{:S(2)}, u32[]{:S(2)}) collective-permute-start(bf16[8,64,128]{2,1,0:T(8,128)(2,1)S(1)} %collective-permute-done.5.refs_6_), channel_id=1, source_target_pairs={{0,1},{1,0},{2,3},{3,2},{4,5},{5,4},{6,7},{7,6},{8,9},{9,8},{10,11... | collective-permute-start | bytes 393224 | tf_op jit(solution)/shard_map/ppermute | solution.py:387
  29.1 10.9 %copy-start.1 = (f32[16,4096]{1,0:T(8,128)S(1)}, f32[16,4096]{1,0:T(8,128)}, u32[]{:S(2)}) copy-start(f32[16,4096]{1,0:T(8,128)} %right.3) | copy-start | bytes 786436
  29.1 10.9 %copy-start.3 = (f32[16,64]{1,0:T(8,128)S(1)}, f32[16,64]{1,0:T(8,128)}, u32[]{:S(2)}) copy-start(f32[16,64]{1,0:T(8,128)} %energy.3) | copy-start | bytes 12292
  29.1 10.9 %copy-start.5 = (s32[16]{0:T(128)S(1)}, s32[16]{0:T(128)}, u32[]{:S(2)}) copy-start(s32[16]{0:T(128)} %count.3) | copy-start | bytes 196
  29.1 10.9 %copy-start.6 = (f32[16]{0:T(128)S(1)}, f32[16]{0:T(128)}, u32[]{:S(2)}) copy-start(f32[16]{0:T(128)} %occ.3) | copy-start | bytes 196
  37.3 8.2 %collective-permute-start.22 = (bf16[8,64,128]{2,1,0:T(8,128)(2,1)S(1)}, bf16[8,64,128]{2,1,0:T(8,128)(2,1)S(1)}, u32[]{:S(2)}, u32[]{:S(2)}) collective-permute-start(bf16[8,64,128]{2,1,0:T(8,128)(2,1)S(1)} %get-tuple-element.22.refs_0_), channel_id=1, source_target_pairs={{0,12},{1,13},{2,14},{3,15},{4,8},{5,9},{6,10},{7,11},{8,4},{9,5},... | collective-permute-start | bytes 393224 | tf_op jit(solution)/shard_map/ppermute | solution.py:387
  38.5 9.5 %collective-permute-start.18 = (bf16[8,64,128]{2,1,0:T(8,128)(2,1)S(1)}, bf16[8,64,128]{2,1,0:T(8,128)(2,1)S(1)}, u32[]{:S(2)}, u32[]{:S(2)}) collective-permute-start(bf16[8,64,128]{2,1,0:T(8,128)(2,1)S(1)} %get-tuple-element.22.refs_0_), channel_id=1, source_target_pairs={{0,4},{1,5},{2,6},{3,7},{4,0},{5,1},{6,2},{7,3},{8,12},{9,13},{10,... | collective-permute-start | bytes 393224 | tf_op jit(solution)/shard_map/ppermute | solution.py:387
  39.5 9.9 %collective-permute-start.16 = (bf16[8,64,128]{2,1,0:T(8,128)(2,1)S(1)}, bf16[8,64,128]{2,1,0:T(8,128)(2,1)S(1)}, u32[]{:S(2)}, u32[]{:S(2)}) collective-permute-start(bf16[8,64,128]{2,1,0:T(8,128)(2,1)S(1)} %get-tuple-element.22.refs_0_), channel_id=1, source_target_pairs={{0,2},{1,3},{2,0},{3,1},{4,6},{5,7},{6,4},{7,5},{8,10},{9,11},{10,... | collective-permute-start | bytes 393224 | tf_op jit(solution)/shard_map/ppermute | solution.py:387
  40.0 9.4 %collective-permute-start.15 = (bf16[8,64,128]{2,1,0:T(8,128)(2,1)S(1)}, bf16[8,64,128]{2,1,0:T(8,128)(2,1)S(1)}, u32[]{:S(2)}, u32[]{:S(2)}) collective-permute-start(bf16[8,64,128]{2,1,0:T(8,128)(2,1)S(1)} %get-tuple-element.22.refs_0_), channel_id=1, source_target_pairs={{0,1},{1,0},{2,3},{3,2},{4,5},{5,4},{6,7},{7,6},{8,9},{9,8},{10,11... | collective-permute-start | bytes 393224 | tf_op jit(solution)/shard_map/ppermute | solution.py:387
  41.6 2.0 %copy-start = (f32[16,16,4096]{2,1,0:T(8,128)}, f32[16,16,4096]{2,1,0:T(8,128)S(1)}, u32[]{:S(2)}) copy-start(f32[16,16,4096]{2,1,0:T(8,128)S(1)} %flat_state.1.refs_17_) | copy-start | bytes 12582916
  45.6 6.4 %collective-permute-start.25 = (bf16[8,64,128]{2,1,0:T(8,128)(2,1)S(1)}, bf16[8,64,128]{2,1,0:T(8,128)(2,1)S(1)}, u32[]{:S(2)}, u32[]{:S(2)}) collective-permute-start(bf16[8,64,128]{2,1,0:T(8,128)(2,1)S(1)} %collective-permute-done.22.refs_12_), channel_id=1, source_target_pairs={{0,6},{1,7},{2,4},{3,5},{4,2},{5,3},{6,0},{7,1},{8,14},{9,15},{10,... | collective-permute-start | bytes 393224 | tf_op jit(solution)/shard_map/ppermute | solution.py:387
  47.9 6.3 %collective-permute-start.23 = (bf16[8,64,128]{2,1,0:T(8,128)(2,1)S(1)}, bf16[8,64,128]{2,1,0:T(8,128)(2,1)S(1)}, u32[]{:S(2)}, u32[]{:S(2)}) collective-permute-start(bf16[8,64,128]{2,1,0:T(8,128)(2,1)S(1)} %collective-permute-done.22.refs_12_), channel_id=1, source_target_pairs={{0,4},{1,5},{2,6},{3,7},{4,0},{5,1},{6,2},{7,3},{8,12},{9,13},{10,... | collective-permute-start | bytes 393224 | tf_op jit(solution)/shard_map/ppermute | solution.py:387
  48.0 6.6 %collective-permute-start.28 = (bf16[8,64,128]{2,1,0:T(8,128)(2,1)S(1)}, bf16[8,64,128]{2,1,0:T(8,128)(2,1)S(1)}, u32[]{:S(2)}, u32[]{:S(2)}) collective-permute-start(bf16[8,64,128]{2,1,0:T(8,128)(2,1)S(1)} %collective-permute-done.22.refs_12_), channel_id=1, source_target_pairs={{0,2},{1,3},{2,0},{3,1},{4,6},{5,7},{6,4},{7,5},{8,10},{9,11},{10,... | collective-permute-start | bytes 393224 | tf_op jit(solution)/shard_map/ppermute | solution.py:387
  49.4 5.2 %collective-permute-start.27 = (bf16[8,64,128]{2,1,0:T(8,128)(2,1)S(1)}, bf16[8,64,128]{2,1,0:T(8,128)(2,1)S(1)}, u32[]{:S(2)}, u32[]{:S(2)}) collective-permute-start(bf16[8,64,128]{2,1,0:T(8,128)(2,1)S(1)} %collective-permute-done.22.refs_12_), channel_id=1, source_target_pairs={{0,1},{1,0},{2,3},{3,2},{4,5},{5,4},{6,7},{7,6},{8,9},{9,8},{10,11... | collective-permute-start | bytes 393224 | tf_op jit(solution)/shard_map/ppermute | solution.py:387
  49.5 7.6 %collective-permute-start.20 = (bf16[8,64,128]{2,1,0:T(8,128)(2,1)S(1)}, bf16[8,64,128]{2,1,0:T(8,128)(2,1)S(1)}, u32[]{:S(2)}, u32[]{:S(2)}) collective-permute-start(bf16[8,64,128]{2,1,0:T(8,128)(2,1)S(1)} %collective-permute-done.18.refs_4_), channel_id=1, source_target_pairs={{0,2},{1,3},{2,0},{3,1},{4,6},{5,7},{6,4},{7,5},{8,10},{9,11},{10,... | collective-permute-start | bytes 393224 | tf_op jit(solution)/shard_map/ppermute | solution.py:387
  52.0 5.1 %collective-permute-start.17 = (bf16[8,64,128]{2,1,0:T(8,128)(2,1)S(1)}, bf16[8,64,128]{2,1,0:T(8,128)(2,1)S(1)}, u32[]{:S(2)}, u32[]{:S(2)}) collective-permute-start(bf16[8,64,128]{2,1,0:T(8,128)(2,1)S(1)} %collective-permute-done.16.refs_2_), channel_id=1, source_target_pairs={{0,1},{1,0},{2,3},{3,2},{4,5},{5,4},{6,7},{7,6},{8,9},{9,8},{10,11... | collective-permute-start | bytes 393224 | tf_op jit(solution)/shard_map/ppermute | solution.py:387
  54.2 3.4 %collective-permute-start.19 = (bf16[8,64,128]{2,1,0:T(8,128)(2,1)S(1)}, bf16[8,64,128]{2,1,0:T(8,128)(2,1)S(1)}, u32[]{:S(2)}, u32[]{:S(2)}) collective-permute-start(bf16[8,64,128]{2,1,0:T(8,128)(2,1)S(1)} %collective-permute-done.18.refs_4_), channel_id=1, source_target_pairs={{0,1},{1,0},{2,3},{3,2},{4,5},{5,4},{6,7},{7,6},{8,9},{9,8},{10,11... | collective-permute-start | bytes 393224 | tf_op jit(solution)/shard_map/ppermute | solution.py:387
  54.6 3.0 %collective-permute-start.26 = (bf16[8,64,128]{2,1,0:T(8,128)(2,1)S(1)}, bf16[8,64,128]{2,1,0:T(8,128)(2,1)S(1)}, u32[]{:S(2)}, u32[]{:S(2)}) collective-permute-start(bf16[8,64,128]{2,1,0:T(8,128)(2,1)S(1)} %collective-permute-done.25.refs_10_), channel_id=1, source_target_pairs={{0,1},{1,0},{2,3},{3,2},{4,5},{5,4},{6,7},{7,6},{8,9},{9,8},{10,11... | collective-permute-start | bytes 393224 | tf_op jit(solution)/shard_map/ppermute | solution.py:387
  54.7 2.9 %collective-permute-start.24 = (bf16[8,64,128]{2,1,0:T(8,128)(2,1)S(1)}, bf16[8,64,128]{2,1,0:T(8,128)(2,1)S(1)}, u32[]{:S(2)}, u32[]{:S(2)}) collective-permute-start(bf16[8,64,128]{2,1,0:T(8,128)(2,1)S(1)} %collective-permute-done.23.refs_8_), channel_id=1, source_target_pairs={{0,1},{1,0},{2,3},{3,2},{4,5},{5,4},{6,7},{7,6},{8,9},{9,8},{10,11... | collective-permute-start | bytes 393224 | tf_op jit(solution)/shard_map/ppermute | solution.py:387
  57.0 1.3 %collective-permute-start.29 = (bf16[8,64,128]{2,1,0:T(8,128)(2,1)S(1)}, bf16[8,64,128]{2,1,0:T(8,128)(2,1)S(1)}, u32[]{:S(2)}, u32[]{:S(2)}) collective-permute-start(bf16[8,64,128]{2,1,0:T(8,128)(2,1)S(1)} %collective-permute-done.28.refs_14_), channel_id=1, source_target_pairs={{0,1},{1,0},{2,3},{3,2},{4,5},{5,4},{6,7},{7,6},{8,9},{9,8},{10,11... | collective-permute-start | bytes 393224 | tf_op jit(solution)/shard_map/ppermute | solution.py:387
  57.1 1.5 %collective-permute-start.21 = (bf16[8,64,128]{2,1,0:T(8,128)(2,1)S(1)}, bf16[8,64,128]{2,1,0:T(8,128)(2,1)S(1)}, u32[]{:S(2)}, u32[]{:S(2)}) collective-permute-start(bf16[8,64,128]{2,1,0:T(8,128)(2,1)S(1)} %collective-permute-done.20.refs_6_), channel_id=1, source_target_pairs={{0,1},{1,0},{2,3},{3,2},{4,5},{5,4},{6,7},{7,6},{8,9},{9,8},{10,11... | collective-permute-start | bytes 393224 | tf_op jit(solution)/shard_map/ppermute | solution.py:387

commit v8 on v7

--- a/solution.py
+++ b/solution.py
@@ -285,7 +285,6 @@
     fetch_state = pltpu.make_async_copy(state.at[:4], steady, arrived.at[len(parts)])
     for i in range(len(parts)):
         fetch(i).start()
-    fetch_state.start()
     left = left_lanes(width)
     at = 0
     for piece in gathered:
@@ -313,6 +312,8 @@
 
     for i, (first, some) in enumerate(parts):
         fetch(i).wait()
+        if i == 0:
+            fetch_state.start()
         for s in range(first, first + some):
             one_slot(s, s % BUFFERS)
 

time: 68.1 us -> 68.1 us (level)
  no operation moved by 1% of the time
where the time goes in v8:
time: 68.1 us; the launch traced here: 67.9 us
  Pallas kernels  30.8 us (45%)
  starting transfers between devices  20.6 us (30%)
  waiting for transfers between devices  13.5 us (20%)
  local copies, waits for them, and re-layouts  2.04 us (3%)
  between operations  0.95 us (1%)
    ppermute x30, starting transfers between devices, swap(): return lax.ppermute(piece, 'pair', [(i, i ^ other) for i in range(devices)])  20.6 us
    pallas_call x2, Pallas kernels, couple(): pl.pallas_call(functools.partial(couple_kernel, last, len(gathered)), in_...  17.3 us
    ppermute x30, waiting for transfers between devices, swap(): return lax.ppermute(piece, 'pair', [(i, i ^ other) for i in range(devices)])  13.5 us
    pallas_call x1, Pallas kernels, margin_tiles(): pl.pallas_call(functools.partial(margin_kernel, 0), in_specs=[VMEM, HBM],...  5.73 us
    pallas_call x1, Pallas kernels, more_tiles(): pl.pallas_call(functools.partial(margin_kernel, FIRST), in_specs=[VMEM, H...  4.09 us
    pallas_call x1, Pallas kernels, start(): pl.pallas_call(start_kernel, in_specs=[SMEM, SMEM, VMEM, VMEM], out_specs...  2.12 us
    unnamed x16, local copies, waits for them, and re-layouts  2.04 us
    pallas_call x1, Pallas kernels, flat_state(): pl.pallas_call(flat_kernel, in_specs=[SMEM, SMEM, VMEM, VMEM, VMEM], out_...  1.52 us
  transfers between devices with their start and end apart: 30, of which 12 were waited for; matrix products, arithmetic and copies ran while one was open for 0% of the time, Pallas kernels for 17%

profile of v8, /device:TPU:0, one launch (start us, length us, event | category | flops | bytes accessed | tf_op | source)
XLA Modules:
  0.0 67.9 jit_solution(4104427142797387467)
XLA Ops:
  0.6 2.1 %start.1.refs_0_ = bf16[8,64,128]{2,1,0:T(8,128)(2,1)} custom-call(s32[16]{0:T(128)} %count.3, f32[16]{0:T(128)} %occ.3, f32[16,4096]{1,0:T(8,128)} %right.3, f32[16,64]{1,0:T(8,128)} %energy.3), custom_call_target="tpu_custom_call" | custom-call | tf_op jit(solution)/shard_map/start/pallas_call | solution.py:72
  2.7 5.0 %collective-permute-start.7 = (bf16[8,64,128]{2,1,0:T(8,128)(2,1)}, bf16[8,64,128]{2,1,0:T(8,128)(2,1)S(1)}, u32[]{:S(2)}, u32[]{:S(2)}) collective-permute-start(bf16[8,64,128]{2,1,0:T(8,128)(2,1)} %start.1.refs_0_), channel_id=1, source_target_pairs={{0,12},{1,13},{2,14},{3,15},{4,8},{5,9},{6,10},{7,11},{8,4},{9,5},... | collective-permute-start | bytes 393224 | tf_op jit(solution)/shard_map/ppermute | solution.py:388
  7.8 0.0 collective-permute-start.3
  7.8 1.5 %collective-permute-start.1 = (bf16[8,64,128]{2,1,0:T(8,128)(2,1)}, bf16[8,64,128]{2,1,0:T(8,128)(2,1)S(1)}, u32[]{:S(2)}, u32[]{:S(2)}) collective-permute-start(bf16[8,64,128]{2,1,0:T(8,128)(2,1)} %start.1.refs_0_), channel_id=1, source_target_pairs={{0,2},{1,3},{2,0},{3,1},{4,6},{5,7},{6,4},{7,5},{8,10},{9,11},{10,... | collective-permute-start | bytes 393224 | tf_op jit(solution)/shard_map/ppermute | solution.py:388
  9.3 0.0 collective-permute-start
  9.3 5.7 %margin_tiles.1.refs_0_ = bf16[320,64,128]{2,1,0:T(8,128)(2,1)} custom-call(bf16[128,256]{1,0:T(8,128)(2,1)} %constant.58.clone.pick, bf16[640,4096]{1,0:T(8,128)(2,1)} %bitcast.4), custom_call_target="tpu_custom_call" | custom-call | bytes 10485760 | tf_op jit(solution)/shard_map/margin_tiles/pallas_call | solution.py:180
  15.1 0.0 collective-permute-done.7.refs_12_
  15.1 2.0 %collective-permute-start.10 = (bf16[8,64,128]{2,1,0:T(8,128)(2,1)S(1)}, bf16[8,64,128]{2,1,0:T(8,128)(2,1)S(1)}, u32[]{:S(2)}, u32[]{:S(2)}) collective-permute-start(bf16[8,64,128]{2,1,0:T(8,128)(2,1)S(1)} %collective-permute-done.7.refs_12_), channel_id=1, source_target_pairs={{0,6},{1,7},{2,4},{3,5},{4,2},{5,3},{6,0},{7,1},{8,14},{9,15},{10,... | collective-permute-start | bytes 393224 | tf_op jit(solution)/shard_map/ppermute | solution.py:388
  17.1 1.5 %collective-permute-start.13 = (bf16[8,64,128]{2,1,0:T(8,128)(2,1)S(1)}, bf16[8,64,128]{2,1,0:T(8,128)(2,1)S(1)}, u32[]{:S(2)}, u32[]{:S(2)}) collective-permute-start(bf16[8,64,128]{2,1,0:T(8,128)(2,1)S(1)} %collective-permute-done.7.refs_12_), channel_id=1, source_target_pairs={{0,2},{1,3},{2,0},{3,1},{4,6},{5,7},{6,4},{7,5},{8,10},{9,11},{10,... | collective-permute-start | bytes 393224 | tf_op jit(solution)/shard_map/ppermute | solution.py:388
  18.6 0.0 collective-permute-done.3.refs_4_
  18.6 0.0 collective-permute-start.8
  18.6 0.0 collective-permute-done.1.refs_2_
  18.6 0.1 collective-permute-start.12
  18.7 0.0 collective-permute-done.refs_1_
  18.7 0.6 collective-permute-start.5
  19.3 3.0 %collective-permute-done.10.refs_10_ = bf16[8,64,128]{2,1,0:T(8,128)(2,1)S(1)} collective-permute-done((bf16[8,64,128]{2,1,0:T(8,128)(2,1)S(1)}, bf16[8,64,128]{2,1,0:T(8,128)(2,1)S(1)}, u32[]{:S(2)}, u32[]{:S(2)}) %collective-permute-start.10) | collective-permute-done | bytes 131104 | tf_op jit(solution)/shard_map/ppermute | solution.py:388
  22.3 0.0 collective-permute-start.4
  22.4 4.1 %more_tiles.1 = (bf16[320,64,128]{2,1,0:T(8,128)(2,1)}, f32[16,8,64,128]{3,2,1,0:T(8,128)}) custom-call(bf16[128,256]{1,0:T(8,128)(2,1)} %constant.58.clone.pick, bf16[640,4096]{1,0:T(8,128)(2,1)} %bitcast.5, bf16[320,64,128]{2,1,0:T(8,128)(2,1)} %margin_tiles.1.refs_0_, s32[16]{0:T(128)} %count.3, f32[16]{0:T(128)} %occ.3, ...), custom_call_target="tpu_custom_call", output_to_operand_aliasing={{0}: (2, {})} | custom-call | bytes 10485760 | tf_op jit(solution)/shard_map/more_tiles/pallas_call | solution.py:197
  26.5 0.0 collective-permute-done.13.refs_14_
  26.5 0.6 collective-permute-start.2
  27.0 0.0 collective-permute-done.8.refs_8_
  27.0 0.1 collective-permute-start.11
  27.1 0.0 collective-permute-done.12.refs_13_
  27.1 0.4 collective-permute-start.14
  27.5 0.0 collective-permute-done.5.refs_6_
  27.5 0.1 collective-permute-start.9
  27.6 0.0 collective-permute-done.4.refs_5_
  27.6 0.4 collective-permute-start.6
  28.1 0.0 collective-permute-done.2.refs_3_
  28.1 0.3 collective-permute-done.11.refs_11_
  28.4 0.2 collective-permute-done.14.refs_15_
  28.6 0.3 collective-permute-done.9.refs_9_
  28.9 0.2 collective-permute-done.6.refs_7_
  29.1 0.0 copy-start.5
  29.1 0.0 copy-start.6
  29.1 8.2 %couple.2 = (f32[8,64,128]{2,1,0:T(8,128)S(1)}, bf16[8,64,128]{2,1,0:T(8,128)(2,1)S(1)}) custom-call(s32[256]{0:T(256)S(1)} %multiply_add_fusion.place, s32[16,40]{1,0:T(8,128)S(1)} %copy-done.4, bf16[8,64,128]{2,1,0:T(8,128)(2,1)S(1)} %copy-done.2, bf16[8,64,128]{2,1,0:T(8,128)(2,1)S(1)} %collective-permute-done.refs_1_, ...), custom_call_target="tpu_custom_call" | custom-call | tf_op jit(solution)/shard_map/couple/pallas_call | solution.py:371
  37.3 1.2 %collective-permute-start.22 = (bf16[8,64,128]{2,1,0:T(8,128)(2,1)S(1)}, bf16[8,64,128]{2,1,0:T(8,128)(2,1)S(1)}, u32[]{:S(2)}, u32[]{:S(2)}) collective-permute-start(bf16[8,64,128]{2,1,0:T(8,128)(2,1)S(1)} %get-tuple-element.22.refs_0_), channel_id=1, source_target_pairs={{0,12},{1,13},{2,14},{3,15},{4,8},{5,9},{6,10},{7,11},{8,4},{9,5},... | collective-permute-start | bytes 393224 | tf_op jit(solution)/shard_map/ppermute | solution.py:388
  38.5 1.0 %collective-permute-start.18 = (bf16[8,64,128]{2,1,0:T(8,128)(2,1)S(1)}, bf16[8,64,128]{2,1,0:T(8,128)(2,1)S(1)}, u32[]{:S(2)}, u32[]{:S(2)}) collective-permute-start(bf16[8,64,128]{2,1,0:T(8,128)(2,1)S(1)} %get-tuple-element.22.refs_0_), channel_id=1, source_target_pairs={{0,4},{1,5},{2,6},{3,7},{4,0},{5,1},{6,2},{7,3},{8,12},{9,13},{10,... | collective-permute-start | bytes 393224 | tf_op jit(solution)/shard_map/ppermute | solution.py:388
  39.5 0.5 collective-permute-start.16
  40.0 0.0 collective-permute-start.15
  40.0 1.5 %flat_state.1.refs_17_ = f32[16,16,4096]{2,1,0:T(8,128)S(1)} custom-call(s32[16]{0:T(128)S(1)} %copy-done.5, f32[16]{0:T(128)S(1)} %copy-done.6, f32[8,64,128]{2,1,0:T(8,128)S(1)} %get-tuple-element.23.current, f32[16,4096]{1,0:T(8,128)S(1)} %copy-done.1, f32[16,64]{1,0:T(8,128)S(1)} %copy-done.3), custom_call_target="tpu_custom_call" | custom-call | bytes 2097152 | tf_op jit(solution)/shard_map/flat_state/pallas_call | solution.py:256
  41.6 2.0 %copy-done = f32[16,16,4096]{2,1,0:T(8,128)} copy-done((f32[16,16,4096]{2,1,0:T(8,128)}, f32[16,16,4096]{2,1,0:T(8,128)S(1)}, u32[]{:S(2)}) %copy-start) | copy-done | bytes 4194328
  43.6 2.0 %collective-permute-done.22.refs_12_ = bf16[8,64,128]{2,1,0:T(8,128)(2,1)S(1)} collective-permute-done((bf16[8,64,128]{2,1,0:T(8,128)(2,1)S(1)}, bf16[8,64,128]{2,1,0:T(8,128)(2,1)S(1)}, u32[]{:S(2)}, u32[]{:S(2)}) %collective-permute-start.22) | collective-permute-done | bytes 131104 | tf_op jit(solution)/shard_map/ppermute | solution.py:388
  45.6 2.3 %collective-permute-start.25 = (bf16[8,64,128]{2,1,0:T(8,128)(2,1)S(1)}, bf16[8,64,128]{2,1,0:T(8,128)(2,1)S(1)}, u32[]{:S(2)}, u32[]{:S(2)}) collective-permute-start(bf16[8,64,128]{2,1,0:T(8,128)(2,1)S(1)} %collective-permute-done.22.refs_12_), channel_id=1, source_target_pairs={{0,6},{1,7},{2,4},{3,5},{4,2},{5,3},{6,0},{7,1},{8,14},{9,15},{10,... | collective-permute-start | bytes 393224 | tf_op jit(solution)/shard_map/ppermute | solution.py:388
  47.9 0.1 collective-permute-start.23
  48.0 1.5 %collective-permute-start.28 = (bf16[8,64,128]{2,1,0:T(8,128)(2,1)S(1)}, bf16[8,64,128]{2,1,0:T(8,128)(2,1)S(1)}, u32[]{:S(2)}, u32[]{:S(2)}) collective-permute-start(bf16[8,64,128]{2,1,0:T(8,128)(2,1)S(1)} %collective-permute-done.22.refs_12_), channel_id=1, source_target_pairs={{0,2},{1,3},{2,0},{3,1},{4,6},{5,7},{6,4},{7,5},{8,10},{9,11},{10,... | collective-permute-start | bytes 393224 | tf_op jit(solution)/shard_map/ppermute | solution.py:388
  49.4 0.0 collective-permute-done.15.refs_1_
  49.5 0.6 collective-permute-start.20
  50.1 1.9 %collective-permute-done.25.refs_10_ = bf16[8,64,128]{2,1,0:T(8,128)(2,1)S(1)} collective-permute-done((bf16[8,64,128]{2,1,0:T(8,128)(2,1)S(1)}, bf16[8,64,128]{2,1,0:T(8,128)(2,1)S(1)}, u32[]{:S(2)}, u32[]{:S(2)}) %collective-permute-start.25) | collective-permute-done | bytes 131104 | tf_op jit(solution)/shard_map/ppermute | solution.py:388
  52.0 0.0 collective-permute-start.17
  52.0 2.2 %collective-permute-done.23.refs_8_ = bf16[8,64,128]{2,1,0:T(8,128)(2,1)S(1)} collective-permute-done((bf16[8,64,128]{2,1,0:T(8,128)(2,1)S(1)}, bf16[8,64,128]{2,1,0:T(8,128)(2,1)S(1)}, u32[]{:S(2)}, u32[]{:S(2)}) %collective-permute-start.23) | collective-permute-done | bytes 131104 | tf_op jit(solution)/shard_map/ppermute | solution.py:388
  54.2 0.0 collective-permute-start.19
  54.2 0.4 collective-permute-done.28.refs_14_
  54.6 0.1 collective-permute-start.26
  54.7 0.4 collective-permute-start.24
  55.1 2.0 %collective-permute-done.20.refs_6_ = bf16[8,64,128]{2,1,0:T(8,128)(2,1)S(1)} collective-permute-done((bf16[8,64,128]{2,1,0:T(8,128)(2,1)S(1)}, bf16[8,64,128]{2,1,0:T(8,128)(2,1)S(1)}, u32[]{:S(2)}, u32[]{:S(2)}) %collective-permute-start.20) | collective-permute-done | bytes 131104 | tf_op jit(solution)/shard_map/ppermute | solution.py:388
  57.0 0.0 collective-permute-start.29
  57.1 0.0 collective-permute-done.17.refs_3_
  57.1 0.5 collective-permute-start.21
  57.6 0.0 collective-permute-done.19.refs_5_
  57.6 0.0 collective-permute-done.26.refs_11_
  57.6 0.8 %collective-permute-done.29.refs_15_ = bf16[8,64,128]{2,1,0:T(8,128)(2,1)S(1)} collective-permute-done((bf16[8,64,128]{2,1,0:T(8,128)(2,1)S(1)}, bf16[8,64,128]{2,1,0:T(8,128)(2,1)S(1)}, u32[]{:S(2)}, u32[]{:S(2)}) %collective-permute-start.29) | collective-permute-done | bytes 131104 | tf_op jit(solution)/shard_map/ppermute | solution.py:388
  58.4 0.2 collective-permute-done.21.refs_7_
  58.6 9.1 %couple.3 = (f32[16,4096]{1,0:T(8,128)}, f32[16,4096]{1,0:T(8,128)}) custom-call(s32[256]{0:T(256)S(1)} %multiply_add_fusion.place, s32[16,40]{1,0:T(8,128)S(1)} %copy-done.4, bf16[8,64,128]{2,1,0:T(8,128)(2,1)S(1)} %get-tuple-element.22.refs_0_, bf16[8,64,128]{2,1,0:T(8,128)(2,1)S(1)} %collective-permute-done.15.refs_1_, ...), custom_call_target="tpu_custom_call" | custom-call | tf_op jit(solution)/shard_map/couple/pallas_call | solution.py:371
  (19 shorter events, 0.1 us)
Async XLA Ops:
  2.7 12.3 %collective-permute-start.7 = (bf16[8,64,128]{2,1,0:T(8,128)(2,1)}, bf16[8,64,128]{2,1,0:T(8,128)(2,1)S(1)}, u32[]{:S(2)}, u32[]{:S(2)}) collective-permute-start(bf16[8,64,128]{2,1,0:T(8,128)(2,1)} %start.1.refs_0_), channel_id=1, source_target_pairs={{0,12},{1,13},{2,14},{3,15},{4,8},{5,9},{6,10},{7,11},{8,4},{9,5},... | collective-permute-start | bytes 393224 | tf_op jit(solution)/shard_map/ppermute | solution.py:388
  7.8 10.8 %collective-permute-start.3 = (bf16[8,64,128]{2,1,0:T(8,128)(2,1)}, bf16[8,64,128]{2,1,0:T(8,128)(2,1)S(1)}, u32[]{:S(2)}, u32[]{:S(2)}) collective-permute-start(bf16[8,64,128]{2,1,0:T(8,128)(2,1)} %start.1.refs_0_), channel_id=1, source_target_pairs={{0,4},{1,5},{2,6},{3,7},{4,0},{5,1},{6,2},{7,3},{8,12},{9,13},{10,... | collective-permute-start | bytes 393224 | tf_op jit(solution)/shard_map/ppermute | solution.py:388
  7.8 10.8 %collective-permute-start.1 = (bf16[8,64,128]{2,1,0:T(8,128)(2,1)}, bf16[8,64,128]{2,1,0:T(8,128)(2,1)S(1)}, u32[]{:S(2)}, u32[]{:S(2)}) collective-permute-start(bf16[8,64,128]{2,1,0:T(8,128)(2,1)} %start.1.refs_0_), channel_id=1, source_target_pairs={{0,2},{1,3},{2,0},{3,1},{4,6},{5,7},{6,4},{7,5},{8,10},{9,11},{10,... | collective-permute-start | bytes 393224 | tf_op jit(solution)/shard_map/ppermute | solution.py:388
  9.3 9.4 %collective-permute-start = (bf16[8,64,128]{2,1,0:T(8,128)(2,1)}, bf16[8,64,128]{2,1,0:T(8,128)(2,1)S(1)}, u32[]{:S(2)}, u32[]{:S(2)}) collective-permute-start(bf16[8,64,128]{2,1,0:T(8,128)(2,1)} %start.1.refs_0_), channel_id=1, source_target_pairs={{0,1},{1,0},{2,3},{3,2},{4,5},{5,4},{6,7},{7,6},{8,9},{9,8},{10,11... | collective-permute-start | bytes 393224 | tf_op jit(solution)/shard_map/ppermute | solution.py:388
  15.1 7.3 %collective-permute-start.10 = (bf16[8,64,128]{2,1,0:T(8,128)(2,1)S(1)}, bf16[8,64,128]{2,1,0:T(8,128)(2,1)S(1)}, u32[]{:S(2)}, u32[]{:S(2)}) collective-permute-start(bf16[8,64,128]{2,1,0:T(8,128)(2,1)S(1)} %collective-permute-done.7.refs_12_), channel_id=1, source_target_pairs={{0,6},{1,7},{2,4},{3,5},{4,2},{5,3},{6,0},{7,1},{8,14},{9,15},{10,... | collective-permute-start | bytes 393224 | tf_op jit(solution)/shard_map/ppermute | solution.py:388
  17.1 9.4 %collective-permute-start.13 = (bf16[8,64,128]{2,1,0:T(8,128)(2,1)S(1)}, bf16[8,64,128]{2,1,0:T(8,128)(2,1)S(1)}, u32[]{:S(2)}, u32[]{:S(2)}) collective-permute-start(bf16[8,64,128]{2,1,0:T(8,128)(2,1)S(1)} %collective-permute-done.7.refs_12_), channel_id=1, source_target_pairs={{0,2},{1,3},{2,0},{3,1},{4,6},{5,7},{6,4},{7,5},{8,10},{9,11},{10,... | collective-permute-start | bytes 393224 | tf_op jit(solution)/shard_map/ppermute | solution.py:388
  18.6 8.4 %collective-permute-start.8 = (bf16[8,64,128]{2,1,0:T(8,128)(2,1)S(1)}, bf16[8,64,128]{2,1,0:T(8,128)(2,1)S(1)}, u32[]{:S(2)}, u32[]{:S(2)}) collective-permute-start(bf16[8,64,128]{2,1,0:T(8,128)(2,1)S(1)} %collective-permute-done.7.refs_12_), channel_id=1, source_target_pairs={{0,4},{1,5},{2,6},{3,7},{4,0},{5,1},{6,2},{7,3},{8,12},{9,13},{10,... | collective-permute-start | bytes 393224 | tf_op jit(solution)/shard_map/ppermute | solution.py:388
  18.6 8.5 %collective-permute-start.12 = (bf16[8,64,128]{2,1,0:T(8,128)(2,1)S(1)}, bf16[8,64,128]{2,1,0:T(8,128)(2,1)S(1)}, u32[]{:S(2)}, u32[]{:S(2)}) collective-permute-start(bf16[8,64,128]{2,1,0:T(8,128)(2,1)S(1)} %collective-permute-done.7.refs_12_), channel_id=1, source_target_pairs={{0,1},{1,0},{2,3},{3,2},{4,5},{5,4},{6,7},{7,6},{8,9},{9,8},{10,11... | collective-permute-start | bytes 393224 | tf_op jit(solution)/shard_map/ppermute | solution.py:388
  18.7 8.8 %collective-permute-start.5 = (bf16[8,64,128]{2,1,0:T(8,128)(2,1)S(1)}, bf16[8,64,128]{2,1,0:T(8,128)(2,1)S(1)}, u32[]{:S(2)}, u32[]{:S(2)}) collective-permute-start(bf16[8,64,128]{2,1,0:T(8,128)(2,1)S(1)} %collective-permute-done.3.refs_4_), channel_id=1, source_target_pairs={{0,2},{1,3},{2,0},{3,1},{4,6},{5,7},{6,4},{7,5},{8,10},{9,11},{10,... | collective-permute-start | bytes 393224 | tf_op jit(solution)/shard_map/ppermute | solution.py:388
  22.3 5.3 %collective-permute-start.4 = (bf16[8,64,128]{2,1,0:T(8,128)(2,1)S(1)}, bf16[8,64,128]{2,1,0:T(8,128)(2,1)S(1)}, u32[]{:S(2)}, u32[]{:S(2)}) collective-permute-start(bf16[8,64,128]{2,1,0:T(8,128)(2,1)S(1)} %collective-permute-done.3.refs_4_), channel_id=1, source_target_pairs={{0,1},{1,0},{2,3},{3,2},{4,5},{5,4},{6,7},{7,6},{8,9},{9,8},{10,11... | collective-permute-start | bytes 393224 | tf_op jit(solution)/shard_map/ppermute | solution.py:388
  22.3 5.7 %copy-start.7 = (s32[256]{0:T(256)S(1)}, s32[256]{0:T(256)}, u32[]{:S(2)}) copy-start(s32[256]{0:T(256)} %param.15) | copy-start | bytes 3076
  22.3 6.7 %copy-start.2 = (bf16[8,64,128]{2,1,0:T(8,128)(2,1)S(1)}, bf16[8,64,128]{2,1,0:T(8,128)(2,1)}, u32[]{:S(2)}) copy-start(bf16[8,64,128]{2,1,0:T(8,128)(2,1)} %start.1.refs_0_) | copy-start | bytes 393220
  22.3 6.7 %copy-start.4 = (s32[16,40]{1,0:T(8,128)S(1)}, s32[16,40]{1,0:T(8,128)}, u32[]{:S(2)}) copy-start(s32[16,40]{1,0:T(8,128)} %partners.3) | copy-start | bytes 7684
  26.5 1.6 %collective-permute-start.2 = (bf16[8,64,128]{2,1,0:T(8,128)(2,1)S(1)}, bf16[8,64,128]{2,1,0:T(8,128)(2,1)S(1)}, u32[]{:S(2)}, u32[]{:S(2)}) collective-permute-start(bf16[8,64,128]{2,1,0:T(8,128)(2,1)S(1)} %collective-permute-done.1.refs_2_), channel_id=1, source_target_pairs={{0,1},{1,0},{2,3},{3,2},{4,5},{5,4},{6,7},{7,6},{8,9},{9,8},{10,11... | collective-permute-start | bytes 393224 | tf_op jit(solution)/shard_map/ppermute | solution.py:388
  27.0 1.3 %collective-permute-start.11 = (bf16[8,64,128]{2,1,0:T(8,128)(2,1)S(1)}, bf16[8,64,128]{2,1,0:T(8,128)(2,1)S(1)}, u32[]{:S(2)}, u32[]{:S(2)}) collective-permute-start(bf16[8,64,128]{2,1,0:T(8,128)(2,1)S(1)} %collective-permute-done.10.refs_10_), channel_id=1, source_target_pairs={{0,1},{1,0},{2,3},{3,2},{4,5},{5,4},{6,7},{7,6},{8,9},{9,8},{10,11... | collective-permute-start | bytes 393224 | tf_op jit(solution)/shard_map/ppermute | solution.py:388
  27.1 1.4 %collective-permute-start.14 = (bf16[8,64,128]{2,1,0:T(8,128)(2,1)S(1)}, bf16[8,64,128]{2,1,0:T(8,128)(2,1)S(1)}, u32[]{:S(2)}, u32[]{:S(2)}) collective-permute-start(bf16[8,64,128]{2,1,0:T(8,128)(2,1)S(1)} %collective-permute-done.13.refs_14_), channel_id=1, source_target_pairs={{0,1},{1,0},{2,3},{3,2},{4,5},{5,4},{6,7},{7,6},{8,9},{9,8},{10,11... | collective-permute-start | bytes 393224 | tf_op jit(solution)/shard_map/ppermute | solution.py:388
  27.5 1.3 %collective-permute-start.9 = (bf16[8,64,128]{2,1,0:T(8,128)(2,1)S(1)}, bf16[8,64,128]{2,1,0:T(8,128)(2,1)S(1)}, u32[]{:S(2)}, u32[]{:S(2)}) collective-permute-start(bf16[8,64,128]{2,1,0:T(8,128)(2,1)S(1)} %collective-permute-done.8.refs_8_), channel_id=1, source_target_pairs={{0,1},{1,0},{2,3},{3,2},{4,5},{5,4},{6,7},{7,6},{8,9},{9,8},{10,11... | collective-permute-start | bytes 393224 | tf_op jit(solution)/shard_map/ppermute | solution.py:388
  27.6 1.5 %collective-permute-start.6 = (bf16[8,64,128]{2,1,0:T(8,128)(2,1)S(1)}, bf16[8,64,128]{2,1,0:T(8,128)(2,1)S(1)}, u32[]{:S(2)}, u32[]{:S(2)}) collective-permute-start(bf16[8,64,128]{2,1,0:T(8,128)(2,1)S(1)} %collective-permute-done.5.refs_6_), channel_id=1, source_target_pairs={{0,1},{1,0},{2,3},{3,2},{4,5},{5,4},{6,7},{7,6},{8,9},{9,8},{10,11... | collective-permute-start | bytes 393224 | tf_op jit(solution)/shard_map/ppermute | solution.py:388
  29.1 10.9 %copy-start.1 = (f32[16,4096]{1,0:T(8,128)S(1)}, f32[16,4096]{1,0:T(8,128)}, u32[]{:S(2)}) copy-start(f32[16,4096]{1,0:T(8,128)} %right.3) | copy-start | bytes 786436
  29.1 10.9 %copy-start.3 = (f32[16,64]{1,0:T(8,128)S(1)}, f32[16,64]{1,0:T(8,128)}, u32[]{:S(2)}) copy-start(f32[16,64]{1,0:T(8,128)} %energy.3) | copy-start | bytes 12292
  29.1 10.9 %copy-start.5 = (s32[16]{0:T(128)S(1)}, s32[16]{0:T(128)}, u32[]{:S(2)}) copy-start(s32[16]{0:T(128)} %count.3) | copy-start | bytes 196
  29.1 10.9 %copy-start.6 = (f32[16]{0:T(128)S(1)}, f32[16]{0:T(128)}, u32[]{:S(2)}) copy-start(f32[16]{0:T(128)} %occ.3) | copy-start | bytes 196
  37.3 8.2 %collective-permute-start.22 = (bf16[8,64,128]{2,1,0:T(8,128)(2,1)S(1)}, bf16[8,64,128]{2,1,0:T(8,128)(2,1)S(1)}, u32[]{:S(2)}, u32[]{:S(2)}) collective-permute-start(bf16[8,64,128]{2,1,0:T(8,128)(2,1)S(1)} %get-tuple-element.22.refs_0_), channel_id=1, source_target_pairs={{0,12},{1,13},{2,14},{3,15},{4,8},{5,9},{6,10},{7,11},{8,4},{9,5},... | collective-permute-start | bytes 393224 | tf_op jit(solution)/shard_map/ppermute | solution.py:388
  38.5 9.5 %collective-permute-start.18 = (bf16[8,64,128]{2,1,0:T(8,128)(2,1)S(1)}, bf16[8,64,128]{2,1,0:T(8,128)(2,1)S(1)}, u32[]{:S(2)}, u32[]{:S(2)}) collective-permute-start(bf16[8,64,128]{2,1,0:T(8,128)(2,1)S(1)} %get-tuple-element.22.refs_0_), channel_id=1, source_target_pairs={{0,4},{1,5},{2,6},{3,7},{4,0},{5,1},{6,2},{7,3},{8,12},{9,13},{10,... | collective-permute-start | bytes 393224 | tf_op jit(solution)/shard_map/ppermute | solution.py:388
  39.5 9.9 %collective-permute-start.16 = (bf16[8,64,128]{2,1,0:T(8,128)(2,1)S(1)}, bf16[8,64,128]{2,1,0:T(8,128)(2,1)S(1)}, u32[]{:S(2)}, u32[]{:S(2)}) collective-permute-start(bf16[8,64,128]{2,1,0:T(8,128)(2,1)S(1)} %get-tuple-element.22.refs_0_), channel_id=1, source_target_pairs={{0,2},{1,3},{2,0},{3,1},{4,6},{5,7},{6,4},{7,5},{8,10},{9,11},{10,... | collective-permute-start | bytes 393224 | tf_op jit(solution)/shard_map/ppermute | solution.py:388
  40.0 9.4 %collective-permute-start.15 = (bf16[8,64,128]{2,1,0:T(8,128)(2,1)S(1)}, bf16[8,64,128]{2,1,0:T(8,128)(2,1)S(1)}, u32[]{:S(2)}, u32[]{:S(2)}) collective-permute-start(bf16[8,64,128]{2,1,0:T(8,128)(2,1)S(1)} %get-tuple-element.22.refs_0_), channel_id=1, source_target_pairs={{0,1},{1,0},{2,3},{3,2},{4,5},{5,4},{6,7},{7,6},{8,9},{9,8},{10,11... | collective-permute-start | bytes 393224 | tf_op jit(solution)/shard_map/ppermute | solution.py:388
  41.6 2.0 %copy-start = (f32[16,16,4096]{2,1,0:T(8,128)}, f32[16,16,4096]{2,1,0:T(8,128)S(1)}, u32[]{:S(2)}) copy-start(f32[16,16,4096]{2,1,0:T(8,128)S(1)} %flat_state.1.refs_17_) | copy-start | bytes 12582916
  45.6 6.4 %collective-permute-start.25 = (bf16[8,64,128]{2,1,0:T(8,128)(2,1)S(1)}, bf16[8,64,128]{2,1,0:T(8,128)(2,1)S(1)}, u32[]{:S(2)}, u32[]{:S(2)}) collective-permute-start(bf16[8,64,128]{2,1,0:T(8,128)(2,1)S(1)} %collective-permute-done.22.refs_12_), channel_id=1, source_target_pairs={{0,6},{1,7},{2,4},{3,5},{4,2},{5,3},{6,0},{7,1},{8,14},{9,15},{10,... | collective-permute-start | bytes 393224 | tf_op jit(solution)/shard_map/ppermute | solution.py:388
  47.9 6.3 %collective-permute-start.23 = (bf16[8,64,128]{2,1,0:T(8,128)(2,1)S(1)}, bf16[8,64,128]{2,1,0:T(8,128)(2,1)S(1)}, u32[]{:S(2)}, u32[]{:S(2)}) collective-permute-start(bf16[8,64,128]{2,1,0:T(8,128)(2,1)S(1)} %collective-permute-done.22.refs_12_), channel_id=1, source_target_pairs={{0,4},{1,5},{2,6},{3,7},{4,0},{5,1},{6,2},{7,3},{8,12},{9,13},{10,... | collective-permute-start | bytes 393224 | tf_op jit(solution)/shard_map/ppermute | solution.py:388
  48.0 6.6 %collective-permute-start.28 = (bf16[8,64,128]{2,1,0:T(8,128)(2,1)S(1)}, bf16[8,64,128]{2,1,0:T(8,128)(2,1)S(1)}, u32[]{:S(2)}, u32[]{:S(2)}) collective-permute-start(bf16[8,64,128]{2,1,0:T(8,128)(2,1)S(1)} %collective-permute-done.22.refs_12_), channel_id=1, source_target_pairs={{0,2},{1,3},{2,0},{3,1},{4,6},{5,7},{6,4},{7,5},{8,10},{9,11},{10,... | collective-permute-start | bytes 393224 | tf_op jit(solution)/shard_map/ppermute | solution.py:388
  49.4 5.2 %collective-permute-start.27 = (bf16[8,64,128]{2,1,0:T(8,128)(2,1)S(1)}, bf16[8,64,128]{2,1,0:T(8,128)(2,1)S(1)}, u32[]{:S(2)}, u32[]{:S(2)}) collective-permute-start(bf16[8,64,128]{2,1,0:T(8,128)(2,1)S(1)} %collective-permute-done.22.refs_12_), channel_id=1, source_target_pairs={{0,1},{1,0},{2,3},{3,2},{4,5},{5,4},{6,7},{7,6},{8,9},{9,8},{10,11... | collective-permute-start | bytes 393224 | tf_op jit(solution)/shard_map/ppermute | solution.py:388
  49.5 7.6 %collective-permute-start.20 = (bf16[8,64,128]{2,1,0:T(8,128)(2,1)S(1)}, bf16[8,64,128]{2,1,0:T(8,128)(2,1)S(1)}, u32[]{:S(2)}, u32[]{:S(2)}) collective-permute-start(bf16[8,64,128]{2,1,0:T(8,128)(2,1)S(1)} %collective-permute-done.18.refs_4_), channel_id=1, source_target_pairs={{0,2},{1,3},{2,0},{3,1},{4,6},{5,7},{6,4},{7,5},{8,10},{9,11},{10,... | collective-permute-start | bytes 393224 | tf_op jit(solution)/shard_map/ppermute | solution.py:388
  52.0 5.1 %collective-permute-start.17 = (bf16[8,64,128]{2,1,0:T(8,128)(2,1)S(1)}, bf16[8,64,128]{2,1,0:T(8,128)(2,1)S(1)}, u32[]{:S(2)}, u32[]{:S(2)}) collective-permute-start(bf16[8,64,128]{2,1,0:T(8,128)(2,1)S(1)} %collective-permute-done.16.refs_2_), channel_id=1, source_target_pairs={{0,1},{1,0},{2,3},{3,2},{4,5},{5,4},{6,7},{7,6},{8,9},{9,8},{10,11... | collective-permute-start | bytes 393224 | tf_op jit(solution)/shard_map/ppermute | solution.py:388
  54.2 3.4 %collective-permute-start.19 = (bf16[8,64,128]{2,1,0:T(8,128)(2,1)S(1)}, bf16[8,64,128]{2,1,0:T(8,128)(2,1)S(1)}, u32[]{:S(2)}, u32[]{:S(2)}) collective-permute-start(bf16[8,64,128]{2,1,0:T(8,128)(2,1)S(1)} %collective-permute-done.18.refs_4_), channel_id=1, source_target_pairs={{0,1},{1,0},{2,3},{3,2},{4,5},{5,4},{6,7},{7,6},{8,9},{9,8},{10,11... | collective-permute-start | bytes 393224 | tf_op jit(solution)/shard_map/ppermute | solution.py:388
  54.6 3.0 %collective-permute-start.26 = (bf16[8,64,128]{2,1,0:T(8,128)(2,1)S(1)}, bf16[8,64,128]{2,1,0:T(8,128)(2,1)S(1)}, u32[]{:S(2)}, u32[]{:S(2)}) collective-permute-start(bf16[8,64,128]{2,1,0:T(8,128)(2,1)S(1)} %collective-permute-done.25.refs_10_), channel_id=1, source_target_pairs={{0,1},{1,0},{2,3},{3,2},{4,5},{5,4},{6,7},{7,6},{8,9},{9,8},{10,11... | collective-permute-start | bytes 393224 | tf_op jit(solution)/shard_map/ppermute | solution.py:388
  54.7 2.9 %collective-permute-start.24 = (bf16[8,64,128]{2,1,0:T(8,128)(2,1)S(1)}, bf16[8,64,128]{2,1,0:T(8,128)(2,1)S(1)}, u32[]{:S(2)}, u32[]{:S(2)}) collective-permute-start(bf16[8,64,128]{2,1,0:T(8,128)(2,1)S(1)} %collective-permute-done.23.refs_8_), channel_id=1, source_target_pairs={{0,1},{1,0},{2,3},{3,2},{4,5},{5,4},{6,7},{7,6},{8,9},{9,8},{10,11... | collective-permute-start | bytes 393224 | tf_op jit(solution)/shard_map/ppermute | solution.py:388
  57.0 1.3 %collective-permute-start.29 = (bf16[8,64,128]{2,1,0:T(8,128)(2,1)S(1)}, bf16[8,64,128]{2,1,0:T(8,128)(2,1)S(1)}, u32[]{:S(2)}, u32[]{:S(2)}) collective-permute-start(bf16[8,64,128]{2,1,0:T(8,128)(2,1)S(1)} %collective-permute-done.28.refs_14_), channel_id=1, source_target_pairs={{0,1},{1,0},{2,3},{3,2},{4,5},{5,4},{6,7},{7,6},{8,9},{9,8},{10,11... | collective-permute-start | bytes 393224 | tf_op jit(solution)/shard_map/ppermute | solution.py:388
  57.1 1.5 %collective-permute-start.21 = (bf16[8,64,128]{2,1,0:T(8,128)(2,1)S(1)}, bf16[8,64,128]{2,1,0:T(8,128)(2,1)S(1)}, u32[]{:S(2)}, u32[]{:S(2)}) collective-permute-start(bf16[8,64,128]{2,1,0:T(8,128)(2,1)S(1)} %collective-permute-done.20.refs_6_), channel_id=1, source_target_pairs={{0,1},{1,0},{2,3},{3,2},{4,5},{5,4},{6,7},{7,6},{8,9},{9,8},{10,11... | collective-permute-start | bytes 393224 | tf_op jit(solution)/shard_map/ppermute | solution.py:388
